TPU v7x, 256 devices: a whole 4x4x8 slice. The times are simulated.
256 devices in a mesh: dp: 16 (over x, y), seq: 16 (over z, core).
Axes of the slice: x: 4, y: 4, z: 8, core: 2. Of those that a mesh axis runs over, the one named last changes fastest.
Arguments:
- layer_input: bfloat16 [16, 2048, 4096], P('dp', 'seq'), may hold values from -6 to 6
- queries: bfloat16 [16, 2048, 2048], P('dp', 'seq'), may hold values from -12.5 to 12.5
- keys: bfloat16 [16, 2048, 512], P('dp', 'seq'), may hold values from -5 to 5
- values: bfloat16 [16, 2048, 512], P('dp', 'seq'), may hold values from -6 to 6
- output_grads: bfloat16 [16, 2048, 2048], P('dp', 'seq'), may hold values from -6 to 6
- block_links: int32 [16, 16, 8], P('dp'), may hold values from 0 to 15, as said below
- segment_ids: int32 [16, 2048], P('dp'), may hold values from 0 to 2, never falling along the last dimension, each value on 1 to 1024 neighbouring positions
Outputs:
- query_grads: bfloat16 [16, 2048, 2048], P('dp', 'seq')
- key_grads: bfloat16 [16, 2048, 512], P('dp', 'seq')
- value_grads: bfloat16 [16, 2048, 512], P('dp', 'seq')
- key_weight_grads: float32 [4096, 512], P(('dp', 'seq'))
- value_weight_grads: float32 [4096, 512], P(('dp', 'seq'))
Inputs may be any that keep to these rules, and one draw needn't show every extreme that they name: `block_links`: each row of 8 entries names distinct key blocks of its sequence, among them the row's own block, the two blocks beside it (block 15 counting as beside block 0) and block 0.
All inputs are finite; a program needn't handle non-finite values.
Results may differ from a plain program's by a relative error of at most 0.018.
Values may be sent and summed in bfloat16 or wider, within the bound.
No kernel may reach another device: no remote copies, remote signals or barrier semaphores. Data moves between devices by JAX's collectives and lax.ppermute only.
A program may use at most 128 MiB of HBM per device.

v0:
```python
import math

import jax
import jax.numpy as jnp
from jax import lax
from jax.sharding import PartitionSpec as P

HEAD_DIM = 128


def product(einsum_form, first_operand, second_operand):
    return jnp.einsum(
        einsum_form, first_operand, second_operand, preferred_element_type=jnp.float32
    )


def block_grads(query_blocks, key_tiles, grad_blocks, allowed, keep_rows, score_scale):
    head_width = query_blocks.shape[-1]
    key_part = key_tiles[..., :head_width]
    value_part = key_tiles[..., head_width:]
    scores = product("brhe,bce->bhrc", query_blocks, key_part) * score_scale
    scores = jnp.where(allowed[:, None], scores, -1e30)
    highest = jnp.max(scores, axis=-1, keepdims=True)
    log_totals = highest + jnp.log(jnp.sum(jnp.exp(scores - highest), axis=-1, keepdims=True))
    probs = jnp.exp(scores - log_totals) * keep_rows[:, None, None, None]
    attention = probs.astype(jnp.bfloat16)
    attended = product("bhrc,bce->brhe", attention, value_part)
    delta_rows = jnp.sum(grad_blocks.astype(jnp.float32) * attended, axis=-1)
    prob_grads = product("brhe,bce->bhrc", grad_blocks, value_part)
    score_grads = (probs * (prob_grads - jnp.transpose(delta_rows, (0, 2, 1))[..., None])).astype(
        jnp.bfloat16
    )
    query_part = product("bhrc,bce->brhe", score_grads, key_part) * score_scale
    key_grads = product("bhrc,brhe->bce", score_grads, query_blocks) * score_scale
    value_grads = product("bhrc,brhe->bce", attention, grad_blocks)
    return (query_part, jnp.concatenate([key_grads, value_grads], axis=-1))


def sequence_grads(query_rows, pair_rows, grad_rows, segment_rows, link_rows, score_scale):
    length = query_rows.shape[0]
    block_count = link_rows.shape[0]
    block_rows = length // block_count
    heads_here = query_rows.shape[1]
    head_width = query_rows.shape[2]
    link_count = link_rows.shape[1]
    steps_count = block_count // 4

    def to_steps(array):
        return array.reshape((steps_count, 4, block_rows) + array.shape[1:])

    tile_pairs = pair_rows.reshape(block_count, block_rows, 2 * head_width)
    tile_segments = segment_rows.reshape(block_count, block_rows)
    keep_all = (jnp.arange(block_count) != 0).astype(jnp.float32).reshape(steps_count, 4)

    def one_step(totals, pieces):
        query_part, grad_part, link_part, segment_part, keep_part = pieces
        gathered = jnp.take(tile_pairs, link_part, axis=0).reshape(
            4, link_count * block_rows, 2 * head_width
        )
        gathered_segments = jnp.take(tile_segments, link_part, axis=0).reshape(
            4, link_count * block_rows
        )
        allowed = segment_part[:, :, None] == gathered_segments[:, None, :]
        query_part_grads, pair_part_grads = block_grads(
            query_part, gathered, grad_part, allowed, keep_part, score_scale
        )
        totals = totals.at[link_part.reshape(-1)].add(
            pair_part_grads.reshape(4 * link_count, block_rows, 2 * head_width)
        )
        return (totals, query_part_grads)

    initial = jnp.zeros((block_count, block_rows, 2 * head_width), jnp.float32)
    totals, query_steps = lax.scan(
        one_step,
        initial,
        (
            to_steps(query_rows),
            to_steps(grad_rows),
            link_rows.reshape(steps_count, 4, link_count),
            tile_segments.reshape(steps_count, 4, block_rows),
            keep_all,
        ),
    )
    first_allowed = (segment_rows[:block_rows][:, None] == segment_rows[None, :])[None]
    first_query, first_pair = block_grads(
        query_rows[:block_rows][None],
        pair_rows[None],
        grad_rows[:block_rows][None],
        first_allowed,
        jnp.ones((1,), jnp.float32),
        score_scale,
    )
    query_all = jnp.concatenate(
        [first_query[0], query_steps.reshape(length, heads_here, head_width)[block_rows:]], axis=0
    )
    pair_all = totals.reshape(length, 2 * head_width) + first_pair[0]
    return (query_all, pair_all)


def local(layer_input, queries, keys, values, output_grads, block_links, segment_ids):
    parties = lax.axis_size("seq")
    local_tokens = queries.shape[1]
    head_width = HEAD_DIM
    heads_total = queries.shape[2] // head_width
    kv_total = keys.shape[2] // head_width
    per_device = heads_total // parties
    sharing = parties // kv_total
    score_scale = 1.0 / math.sqrt(head_width)
    query_local = queries[0].reshape(local_tokens, parties, per_device * head_width)
    grad_local = output_grads[0].reshape(local_tokens, parties, per_device * head_width)
    pair_local = jnp.concatenate(
        [
            keys[0].reshape(local_tokens, kv_total, head_width),
            values[0].reshape(local_tokens, kv_total, head_width),
        ],
        axis=-1,
    )
    pair_slots = jnp.repeat(pair_local, sharing, axis=1)
    query_seq, grad_seq, pair_seq = (
        lax.all_to_all(query_local, "seq", split_axis=1, concat_axis=0, tiled=True),
        lax.all_to_all(grad_local, "seq", split_axis=1, concat_axis=0, tiled=True),
        lax.all_to_all(pair_slots, "seq", split_axis=1, concat_axis=0, tiled=True),
    )
    seq_length = local_tokens * parties
    query_part, pair_part = sequence_grads(
        query_seq,
        pair_seq.reshape(seq_length, 2 * head_width),
        grad_seq,
        segment_ids[0],
        block_links[0],
        score_scale,
    )
    query_back = lax.all_to_all(
        query_part.astype(jnp.bfloat16), "seq", split_axis=0, concat_axis=1, tiled=True
    )
    pair_back = lax.all_to_all(
        pair_part.reshape(seq_length, 1, 2 * head_width),
        "seq",
        split_axis=0,
        concat_axis=1,
        tiled=True,
    )
    pair_total = jnp.sum(pair_back.reshape(local_tokens, kv_total, sharing, 2 * head_width), axis=2)
    key_width = kv_total * head_width
    key_grads = pair_total[..., :head_width].reshape(local_tokens, key_width).astype(jnp.bfloat16)
    value_grads = pair_total[..., head_width:].reshape(local_tokens, key_width).astype(jnp.bfloat16)
    joined = jnp.concatenate([key_grads, value_grads], axis=-1)
    inputs_local = layer_input[0]
    contract = (((0,), (0,)), ((), ()))
    weight_grads = lax.psum_scatter(
        lax.dot_general(inputs_local, joined, contract, preferred_element_type=jnp.float32),
        ("dp", "seq"),
        scatter_dimension=0,
        tiled=True,
    )
    query_grads = query_back.reshape(local_tokens, heads_total * head_width)
    return (
        query_grads[None],
        key_grads[None],
        value_grads[None],
        weight_grads[:, :key_width],
        weight_grads[:, key_width:],
    )


def solution(mesh):
    return jax.shard_map(
        local,
        mesh=mesh,
        in_specs=(
            P("dp", "seq", None),
            P("dp", "seq", None),
            P("dp", "seq", None),
            P("dp", "seq", None),
            P("dp", "seq", None),
            P("dp", None, None),
            P("dp", None),
        ),
        out_specs=(
            P("dp", "seq", None),
            P("dp", "seq", None),
            P("dp", "seq", None),
            P(("dp", "seq"), None),
            P(("dp", "seq"), None),
        ),
        check_vma=False,
    )
```

profile of v0, /device:TPU:1, one launch (start us, length us, event | category | flops | bytes accessed | tf_op | source)
XLA Modules:
  0.0 1591.6 jit_solution(6923438288982903675)
XLA Ops:
  9.4 10.0 all-to-all-start.1
  19.7 17.0 %all-to-all-done.1 = bf16[128,16,128]{2,0,1:T(8,128)(2,1)S(1)} async-done(((bf16[128,16,128]{2,0,1:T(8,128)(2,1)}), bf16[128,16,128]{2,0,1:T(8,128)(2,1)S(1)}, u32[]{:S(2)}, u32[]{:S(2)}) %all-to-all-start.1) | async-done | bytes 524320 | tf_op jit(solution)/shard_map/all_to_all | solution.py:120
  37.9 3.7 all-to-all-start
  42.6 26.2 %all-to-all-done = bf16[128,16,256]{2,0,1:T(8,128)(2,1)S(1)} async-done(((bf16[128,16,256]{2,0,1:T(8,128)(2,1)}), bf16[128,16,256]{2,0,1:T(8,128)(2,1)S(1)}, u32[]{:S(2)}, u32[]{:S(2)}) %all-to-all-start) | async-done | bytes 1048608 | tf_op jit(solution)/shard_map/all_to_all | solution.py:122
  68.9 4.1 all-to-all-start.2
  74.7 15.1 all-to-all-done.2
  90.9 2.0 convolution_bitcast_fusion.2
  94.0 2.1 fusion.28
  96.3 108.5 %while.12 = (s32[]{:T(128)}, f32[16,128,256]{2,1,0:T(8,128)S(1)}, bf16[4,4,128,1,128]{4,2,1,0,3:T(8,128)(2,1)}, s32[4,4,8]{2,1,0:T(4,128)S(1)}, s32[4,4,128]{2,1...) while((s32[]{:T(128)}, f32[16,128,256]{2,1,0:T(8,128)S(1)}, ...), condition=%wide.region_8.9_spmd, body=%wide.region_3.8_spmd.sunk | while | flops 818221440 | bytes 65444928 | solution.py:73
  97.3 3.3 gather_fusion
  100.5 1.9 bitcast_select_fusion.3
  102.5 2.5 fusion.91
  105.3 1.7 fusion.94
  109.5 2.7 fusion.93
  113.0 1.7 convolution_multiply_fusion.6
  114.7 2.2 pad_maximum_fusion.4
  116.9 6.5 scatter_fusion
  124.4 3.3 gather_fusion
  127.6 1.9 bitcast_select_fusion.3
  129.6 2.5 fusion.91
  132.4 1.7 fusion.94
  136.6 2.7 fusion.93
  140.2 1.7 convolution_multiply_fusion.6
  141.8 2.2 pad_maximum_fusion.4
  144.0 6.5 scatter_fusion
  151.5 3.3 gather_fusion
  154.7 1.9 bitcast_select_fusion.3
  156.7 2.5 fusion.91
  159.5 1.7 fusion.94
  163.7 2.7 fusion.93
  167.3 1.7 convolution_multiply_fusion.6
  169.0 2.2 pad_maximum_fusion.4
  171.2 6.5 scatter_fusion
  178.6 3.3 gather_fusion
  181.9 1.9 bitcast_select_fusion.3
  183.8 2.5 fusion.91
  186.6 1.7 fusion.94
  190.8 2.7 fusion.93
  194.4 1.7 convolution_multiply_fusion.6
  196.1 2.2 pad_maximum_fusion.4
  198.3 6.5 scatter_fusion
  204.8 1.7 fusion.36
  206.5 8.6 copy.123
  215.1 53.8 %all_to_all.75 = f32[2048,1,256]{2,1,0:T(1,128)S(1)} all-to-all(f32[2048,1,256]{2,1,0:T(1,128)S(1)} %copy.123), channel_id=1, replica_groups=mesh['dp'=16,'seq'=16] {'seq'}, dimensions={0} | all-to-all | bytes 4194304 | tf_op jit(solution)/shard_map/all_to_all | solution.py:136
  269.5 8.0 convolution_bitcast_fusion.1
  277.6 17.5 %copy.147 = f32[4096,1024]{1,0:T(8,128)} copy(f32[4096,1024]{0,1:T(8,128)} %convolution_bitcast_fusion.1) | data formatting | bytes 33554432
  298.6 21.0 %all_to_all.76 = bf16[16,2,8192]{2,1,0:T(2,128)(2,1)S(1)} all-to-all(bf16[16,2,8192]{2,1,0:T(2,128)(2,1)S(1)} %reshape.436), channel_id=1, replica_groups=mesh['dp'=16,'seq'=16] {'seq'}, dimensions={0} | all-to-all | bytes 1048576 | tf_op jit(solution)/shard_map/all_to_all | solution.py:133
  323.0 1260.3 %reduce-scatter.4.cloned.1.call-done = f32[16,1024]{1,0:T(8,128)} async-done(((f32[4096,1024]{1,0:T(8,128)}), f32[16,1024]{1,0:T(8,128)}) %reduce-scatter.4.cloned.1.call-update) | async-done | bytes 65552
  (154 shorter events, 35.7 us)
Async XLA Ops:
  7.2 262.4 %copy-start = (bf16[1,128,4096]{2,1,0:T(8,128)(2,1)S(1)}, bf16[1,128,4096]{2,1,0:T(8,128)(2,1)}, u32[]{:S(2)}) copy-start(bf16[1,128,4096]{2,1,0:T(8,128)(2,1)} %param.9) | copy-start | bytes 3145732
  7.2 12.2 copy-start.11
  7.2 12.2 copy-start.12
  9.4 27.3 %all-to-all-start.1 = ((bf16[128,16,128]{2,0,1:T(8,128)(2,1)}), bf16[128,16,128]{2,0,1:T(8,128)(2,1)S(1)}, u32[]{:S(2)}, u32[]{:S(2)}) async-start(bf16[128,16,128]{2,0,1:T(8,128)(2,1)} %copy.114), calls=%async_computation.1 | async-start | bytes 1048576 | tf_op jit(solution)/shard_map/all_to_all | solution.py:120
  19.6 22.0 %copy-start.9 = (bf16[1,128,2048]{2,1,0:T(8,128)(2,1)S(1)}, bf16[1,128,2048]{2,1,0:T(8,128)(2,1)}, u32[]{:S(2)}) copy-start(bf16[1,128,2048]{2,1,0:T(8,128)(2,1)} %param.13) | copy-start | bytes 1572868
  36.7 5.9 copy-start.6
  37.9 35.2 %copy-start.13 = (s32[1,16,8]{1,2,0:T(8,128)S(1)}, s32[1,16,8]{1,2,0:T(8,128)}, u32[]{:S(2)}) copy-start(s32[1,16,8]{1,2,0:T(8,128)} %param.14) | copy-start | bytes 1540
  37.9 35.3 %copy-start.5 = (s32[1,2048]{1,0:T(1,128)S(1)}, s32[1,2048]{1,0:T(1,128)}, u32[]{:S(2)}) copy-start(s32[1,2048]{1,0:T(1,128)} %param.15) | copy-start | bytes 24580
  37.9 31.0 %all-to-all-start = ((bf16[128,16,256]{2,0,1:T(8,128)(2,1)}), bf16[128,16,256]{2,0,1:T(8,128)(2,1)S(1)}, u32[]{:S(2)}, u32[]{:S(2)}) async-start(bf16[128,16,256]{2,0,1:T(8,128)(2,1)} %bitcast.22), calls=%async_computation | async-start | bytes 2097152 | tf_op jit(solution)/shard_map/all_to_all | solution.py:122
  68.8 24.1 %copy-start.2 = (bf16[128,16,256]{2,0,1:T(8,128)(2,1)}, bf16[128,16,256]{2,0,1:T(8,128)(2,1)S(1)}, u32[]{:S(2)}) copy-start(bf16[128,16,256]{2,0,1:T(8,128)(2,1)S(1)} %all-to-all-done) | copy-start | bytes 3145732
  68.9 20.9 %all-to-all-start.2 = ((bf16[128,16,128]{0,2,1:T(8,128)(2,1)}), bf16[128,16,128]{0,2,1:T(8,128)(2,1)}, u32[]{:S(2)}, u32[]{:S(2)}) async-start(bf16[128,16,128]{0,2,1:T(8,128)(2,1)} %bitcast.37), calls=%async_computation.2 | async-start | bytes 1048576 | tf_op jit(solution)/shard_map/all_to_all | solution.py:121
  73.0 1510.4 %reduce-scatter.4.cloned.1.call-start = ((), (), s32[]{:S(2)}) async-start(), calls=%async_computation.6 | async-start | bytes 16842752
  94.0 2.1 copy-start.7
  108.5 1.0 copy-start.4
  112.4 2.4 copy-start.1
  135.6 1.0 copy-start.4
  139.5 2.4 copy-start.1
  162.7 1.0 copy-start.4
  166.6 2.4 copy-start.1
  189.9 1.0 copy-start.4
  193.7 2.4 copy-start.1
  295.0 1.0 copy-start.10
  295.0 1.4 copy-start.3
  295.0 1.5 copy-start.8
Sparse Core Ops, SparseCore 0:
  295.2 1288.1 reduce-scatter.3
where the time goes:
time: 1600 us; the launch traced here: 1590 us
  waiting for transfers between devices  1320 us (82%)
  blocking collectives  74.8 us (5%)
  local copies, waits for them, and re-layouts  59.9 us (4%)
  matrix products  58.4 us (4%)
  other arithmetic  47.2 us (3%)
  starting transfers between devices  17.8 us (1%)
    unnamed x2, waiting for transfers between devices  1260 us
    all_to_all x1, blocking collectives, local(): lax.all_to_all(pair_part.reshape(seq_length, 1, 2 * head_width), 'seq', s...  53.8 us
    dot_general x30, matrix products, product(): jnp.einsum(einsum_form, first_operand, second_operand, preferred_element_...  50.3 us
  transfers between devices with their start and end apart: 4, of which 4 were waited for; matrix products, arithmetic and copies ran while one was open for 1% of the time, Pallas kernels for 0%

commit v1 on v0

v1 whole, which is shorter than its diff:
```python
import math

import jax
import jax.numpy as jnp
from jax import lax
from jax.experimental import pallas as pl
from jax.experimental.pallas import tpu as pltpu
from jax.sharding import Mesh, PartitionSpec as P

NX, NY, NZ, NC = 4, 4, 8, 2
HEAD = 128
BLOCK = 128
BLOCKS = NZ * NC
LINKS = 8
KV_HEADS = 4
MIB = 1 << 20
SCALE = 1.0 / math.sqrt(HEAD)
LOG2E = math.log2(math.e)
MASKED = -1e30


def dot(a, b):
    return lax.dot_general(
        a, b, (((1,), (0,)), ((), ())), preferred_element_type=jnp.float32
    )


def attention_kernel(
    links_ref, core_ref, rows_ref, other_ref, seg_cols_ref, seg_rows_ref,
    dq_ref, own_ref, away_ref, pair_ref, keys_t_ref, total_ref,
):
    core = core_ref[0]

    def load_pairs(i, carry):
        for block, pair in ((2 * i + core, rows_ref[i, :, 4 * HEAD:]), (2 * i + 1 - core, other_ref[i])):
            pair_ref[block] = pair
            keys_t_ref[block] = pair[:, :HEAD].T
        return carry

    lax.fori_loop(0, NZ, load_pairs, 0)
    total_ref[...] = jnp.zeros_like(total_ref)

    def query_block(i, key_blocks):
        block = 2 * i + core
        rows = rows_ref[i]
        queries = jnp.concatenate([rows[:, :HEAD], rows[:, HEAD : 2 * HEAD]], axis=0)
        grads = jnp.concatenate([rows[:, 2 * HEAD : 3 * HEAD], rows[:, 3 * HEAD : 4 * HEAD]], axis=0)
        queries_t, grads_t = queries.T, grads.T
        seg = seg_rows_ref[pl.ds(block, 1), :]
        scores = []
        highest = None
        for j in key_blocks:
            allowed = seg_cols_ref[j] == seg
            s = dot(pair_ref[j, :, :HEAD], queries_t) * (SCALE * LOG2E)
            s = jnp.where(jnp.concatenate([allowed, allowed], axis=1), s, MASKED)
            top = jnp.max(s, axis=0, keepdims=True)
            highest = top if highest is None else jnp.maximum(highest, top)
            scores.append(s)
        weights = []
        norm = None
        for s in scores:
            e = jnp.exp2(s - highest)
            part = jnp.sum(e, axis=0, keepdims=True)
            norm = part if norm is None else norm + part
            weights.append(e)
        inverse = 1.0 / norm
        probs, prob_grads = [], []
        delta = None
        for j, e in zip(key_blocks, weights):
            p = e * inverse
            attention = p.astype(jnp.bfloat16)
            g = dot(pair_ref[j, :, HEAD:], grads_t)
            part = jnp.sum(attention.astype(jnp.float32) * g, axis=0, keepdims=True)
            delta = part if delta is None else delta + part
            total_ref[j, :, HEAD:] += dot(attention, grads)
            probs.append(p)
            prob_grads.append(g)
        dq_t = None
        for j, p, g in zip(key_blocks, probs, prob_grads):
            score_grads = (p * (g - delta)).astype(jnp.bfloat16)
            total_ref[j, :, :HEAD] += dot(score_grads, queries)
            part = dot(keys_t_ref[j], score_grads)
            dq_t = part if dq_t is None else dq_t + part
        dq = (dq_t * SCALE).T
        dq_ref[i, :, :HEAD] = dq[:BLOCK].astype(jnp.bfloat16)
        dq_ref[i, :, HEAD:] = dq[BLOCK:].astype(jnp.bfloat16)

    def linked(i, carry):
        query_block(i, [links_ref[2 * i + core, t] for t in range(LINKS)])
        return carry

    @pl.when(core == 0)
    def _():
        query_block(0, list(range(BLOCKS)))

    lax.fori_loop(1 - core, NZ, linked, 0)

    def store(i, carry):
        for ref, block in ((own_ref, 2 * i + core), (away_ref, 2 * i + 1 - core)):
            ref[i, :, :HEAD] = total_ref[block, :, :HEAD] * SCALE
            ref[i, :, HEAD:] = total_ref[block, :, HEAD:]
        return carry

    lax.fori_loop(0, NZ, store, 0)


def attention_grads(links, core, rows, other, seg_cols, seg_rows):
    vmem = pl.BlockSpec(memory_space=pltpu.VMEM)
    smem = pl.BlockSpec(memory_space=pltpu.SMEM)
    return pl.pallas_call(
        attention_kernel,
        out_shape=(
            jax.ShapeDtypeStruct((NZ, BLOCK, 2 * HEAD), jnp.bfloat16),
            jax.ShapeDtypeStruct((NZ, BLOCK, 2 * HEAD), jnp.float32),
            jax.ShapeDtypeStruct((NZ, BLOCK, 2 * HEAD), jnp.float32),
        ),
        in_specs=[smem, smem, vmem, vmem, vmem, vmem],
        out_specs=(vmem, vmem, vmem),
        scratch_shapes=[
            pltpu.VMEM((BLOCKS, BLOCK, 2 * HEAD), jnp.bfloat16),
            pltpu.VMEM((BLOCKS, HEAD, BLOCK), jnp.bfloat16),
            pltpu.VMEM((BLOCKS, BLOCK, 2 * HEAD), jnp.float32),
        ],
        compiler_params=pltpu.CompilerParams(vmem_limit_bytes=48 * MIB),
        cost_estimate=pl.CostEstimate(
            flops=4_000_000_000, bytes_accessed=8 * MIB, transcendentals=2_500_000
        ),
    )(links, core, rows, other, seg_cols, seg_rows)


def weight_kernel(place_ref, grads_ref, own_ref, other_ref, out_ref, total_ref):
    step = pl.program_id(0)
    x, core = place_ref[0], place_ref[1]

    @pl.when(step == 0)
    def _():
        total_ref[...] = jnp.zeros_like(total_ref)

    total = total_ref[...]
    for s in range(NX):
        source = (lax.rem(x - s + NX, NX) * NY + step) * NC
        grads = jnp.concatenate([grads_ref[source + core], grads_ref[source + 1 - core]], axis=0)
        inputs = jnp.concatenate([own_ref[0, s], other_ref[0, s]], axis=0)
        total = total + dot(grads.T, inputs)
    total_ref[...] = total

    @pl.when(step == NY - 1)
    def _():
        out_ref[...] = total_ref[...].T.astype(jnp.bfloat16)


def weight_grads_part(place, grads, own, other):
    width = own.shape[-1]
    return pl.pallas_call(
        weight_kernel,
        grid=(NY,),
        out_shape=jax.ShapeDtypeStruct((width, HEAD), jnp.bfloat16),
        in_specs=[
            pl.BlockSpec(memory_space=pltpu.SMEM),
            pl.BlockSpec(memory_space=pltpu.VMEM),
            pl.BlockSpec((1, NX, BLOCK, width), lambda i: (i, 0, 0, 0)),
            pl.BlockSpec((1, NX, BLOCK, width), lambda i: (i, 0, 0, 0)),
        ],
        out_specs=pl.BlockSpec((width, HEAD), lambda i: (0, 0)),
        scratch_shapes=[pltpu.VMEM((HEAD, width), jnp.float32)],
        compiler_params=pltpu.CompilerParams(vmem_limit_bytes=32 * MIB),
        cost_estimate=pl.CostEstimate(
            flops=1_100_000_000, bytes_accessed=9 * MIB, transcendentals=0
        ),
    )(place, grads, own, other)


def ring(size, shift):
    return [(i, (i + shift) % size) for i in range(size)]


def swap_cores(a):
    return lax.ppermute(a, "c", [(0, 1), (1, 0)])


def local(layer_input, queries, keys, values, output_grads, block_links, segment_ids):
    x, core = lax.axis_index("x"), lax.axis_index("c")
    bf16 = jnp.bfloat16

    inputs = layer_input[0]
    width = inputs.shape[1] // NX
    pieces = []
    for s in range(NX):
        piece = lax.dynamic_slice_in_dim(inputs, lax.rem(x + s, NX) * width, width, axis=1)
        pieces.append(piece if s == 0 else lax.ppermute(piece, "x", ring(NX, s)))
    inputs_own = lax.all_gather(jnp.stack(pieces), "y", axis=0)

    def by_chip(a):
        return jnp.transpose(a.reshape(BLOCK, NZ, 2 * HEAD), (1, 0, 2))

    def by_key_head(a):
        heads = jnp.transpose(a.reshape(BLOCK, KV_HEADS, HEAD), (1, 0, 2))
        return jnp.repeat(heads, NZ // KV_HEADS, axis=0)

    outgoing = jnp.concatenate(
        [by_chip(queries[0]), by_chip(output_grads[0]), by_key_head(keys[0]), by_key_head(values[0])],
        axis=-1,
    )
    rows = lax.all_to_all(outgoing, "z", split_axis=0, concat_axis=0, tiled=True)
    other = swap_cores(rows[..., 4 * HEAD :])

    seg_rows = segment_ids[0].reshape(BLOCKS, BLOCK)
    seg_cols = jnp.broadcast_to(seg_rows[:, :, None], (BLOCKS, BLOCK, BLOCK))
    dq, own, away = attention_grads(
        block_links[0], core.reshape(1).astype(jnp.int32), rows, other, seg_cols, seg_rows
    )

    pair = (own + swap_cores(away)).astype(bf16)
    pair = lax.all_to_all(pair, "z", split_axis=0, concat_axis=0, tiled=True)
    pair = pair.reshape(KV_HEADS, NZ // KV_HEADS, BLOCK, 2, HEAD).astype(jnp.float32)
    pair = jnp.sum(pair, axis=1).astype(bf16)
    key_grads = jnp.transpose(pair[:, :, 0], (1, 0, 2)).reshape(BLOCK, KV_HEADS * HEAD)
    value_grads = jnp.transpose(pair[:, :, 1], (1, 0, 2)).reshape(BLOCK, KV_HEADS * HEAD)

    dq = lax.all_to_all(dq, "z", split_axis=0, concat_axis=0, tiled=True)
    query_grads = jnp.transpose(dq, (1, 0, 2)).reshape(BLOCK, NZ * 2 * HEAD)

    chunks = jnp.transpose(pair, (0, 2, 1, 3)).reshape(1, NY * NC, BLOCK, HEAD)
    chunks = jnp.broadcast_to(chunks, (NX, NY * NC, BLOCK, HEAD)).reshape(-1, BLOCK, HEAD)
    grads = lax.all_to_all(chunks, ("x", "y", "c"), split_axis=0, concat_axis=0, tiled=True)
    inputs_other = swap_cores(inputs_own)
    place = jnp.stack([x, core]).astype(jnp.int32)
    part = weight_grads_part(place, grads, inputs_own, inputs_other)

    part = part.reshape(NY * NZ * NC, -1, HEAD)
    part = lax.all_to_all(part, ("y", "z", "c"), split_axis=0, concat_axis=0, tiled=True)
    part = part.reshape(NY, NZ, NC, -1, HEAD).astype(jnp.float32)
    part = jnp.transpose(jnp.sum(part, axis=1), (1, 2, 0, 3))
    part = part.reshape(NC, -1, NY * HEAD)
    return query_grads[None], key_grads[None], value_grads[None], part[0], part[1]


def solution(mesh):
    chips = Mesh(mesh.devices.reshape(NX, NY, NZ, NC), ("x", "y", "z", "c"))
    dp, seq = ("x", "y"), ("z", "c")
    by_position = P(dp, seq, None)
    return jax.shard_map(
        local,
        mesh=chips,
        in_specs=(by_position,) * 5 + (P(dp, None, None), P(dp, None)),
        out_specs=(by_position,) * 3 + (P(dp + seq, None),) * 2,
        check_vma=False,
    )
```

time: 1600 us -> 191 us (0.12)
  waiting for transfers between devices: 1320 us -> 34.1 us
  matrix products: 58.4 us -> 0 us
  local copies, waits for them, and re-layouts: 59.9 us -> 9.68 us
  other arithmetic: 47.2 us -> 2.51 us
  Pallas kernels: 0 us -> 18.2 us
  blocking collectives: 74.8 us -> 92.8 us
    unnamed x2 -> x1, waiting for transfers between devices: 1260 us -> 0.02 us
    dot_general x31 -> x0, matrix products: 58.4 us -> none  [the longest x30 50.3 us: product(): jnp.einsum(einsum_form, first_operand, second_operand, preferred_element_...]
    all_to_all x3 -> x2, waiting for transfers between devices: 58.4 us -> 17.7 us  [the longest x1 9.26 us: local(): dq = lax.all_to_all(dq, 'z', split_axis=0, concat_axis=0, tiled=True)]
    scatter-add x4 -> x0, other arithmetic: 25.9 us -> none  [one_step(): totals.at[link_part.reshape(-1)]]
    unnamed x35 -> x19, local copies, waits for them, and re-layouts: 24.7 us -> 5.32 us
    pallas_call x0 -> x2, Pallas kernels: none -> 18.2 us  [the longest x1 13.3 us: attention_grads(): pl.pallas_call(attention_kernel, out_shape=(jax.ShapeDtypeStruct((NZ, BLO...]
    all_to_all x2 -> x3, blocking collectives: 74.8 us -> 92.8 us  [the longest x1 45.2 us: local(): lax.all_to_all(outgoing, 'z', split_axis=0, concat_axis=0, tiled=True)]
  transfers between devices with their start and end apart: 4 -> 9, of which waited for: 4 -> 7; matrix products, arithmetic and copies ran while one was open for 1% -> 4% of each run, Pallas kernels for 0% -> 10%
where the time goes in v1:
time: 191 us
  blocking collectives  92.8 us (49%)
  waiting for transfers between devices  34.1 us (18%)
  starting transfers between devices  19.4 us (10%)
  Pallas kernels  18.2 us (10%)
  between operations  14.3 us (7%)
  local copies, waits for them, and re-layouts  9.68 us (5%)
  other arithmetic  2.51 us (1%)
    all_to_all x1, blocking collectives, local(): lax.all_to_all(outgoing, 'z', split_axis=0, concat_axis=0, tiled=True)  45.2 us
    all_to_all x1, blocking collectives, local(): lax.all_to_all(chunks, ('x', 'y', 'c'), split_axis=0, concat_axis=0, tile...  24.4 us
    all_to_all x1, blocking collectives, local(): pair = lax.all_to_all(pair, 'z', split_axis=0, concat_axis=0, tiled=True)  23.2 us
    pallas_call x1, Pallas kernels, attention_grads(): pl.pallas_call(attention_kernel, out_shape=(jax.ShapeDtypeStruct((NZ, BLO...  13.3 us
    ppermute x3, waiting for transfers between devices, local(): pieces.append(piece if s == 0 else lax.ppermute(piece, 'x', ring(NX, s)))  10.8 us
    all_to_all x1, waiting for transfers between devices, local(): dq = lax.all_to_all(dq, 'z', split_axis=0, concat_axis=0, tiled=True)  9.26 us
    all_to_all x1, waiting for transfers between devices, local(): lax.all_to_all(part, ('y', 'z', 'c'), split_axis=0, concat_axis=0, tiled=...  8.49 us
    ppermute x3, starting transfers between devices, swap_cores(): return lax.ppermute(a, 'c', [(0, 1), (1, 0)])  5.46 us
  transfers between devices with their start and end apart: 9, of which 7 were waited for; matrix products, arithmetic and copies ran while one was open for 4% of the time, Pallas kernels for 10%

profile of v1, /device:TPU:1, one launch (start us, length us, event | category | flops | bytes accessed | tf_op | source)
XLA Modules:
  0.0 191.0 jit_solution(9688501995416460030)
XLA Ops:
  7.2 0.0 all-gather.3.cloned.1.call-start
  7.3 1.3 constant_dynamic-slice_fusion
  8.6 2.1 %collective-permute-start.2 = (bf16[128,1024]{1,0:T(8,128)(2,1)S(1)}, bf16[128,1024]{1,0:T(8,128)(2,1)S(1)}, u32[]{:S(2)}, u32[]{:S(2)}) collective-permute-start(bf16[128,1024]{1,0:T(8,128)(2,1)S(1)} %get-tuple-element.32), channel_id=1, source_target_pairs={{0,64},{64,128},{128,192},{192,0},{1,65},{65,129},{129,193},{193,1... | collective-permute-start | bytes 786440 | tf_op jit(solution)/shard_map/ppermute | solution.py:190
  10.7 1.4 collective-permute-start.4
  12.1 1.6 collective-permute-start.3
  13.7 2.0 %collective-permute-done.2 = bf16[128,1024]{1,0:T(8,128)(2,1)S(1)} collective-permute-done((bf16[128,1024]{1,0:T(8,128)(2,1)S(1)}, bf16[128,1024]{1,0:T(8,128)(2,1)S(1)}, u32[]{:S(2)}, u32[]{:S(2)}) %collective-permute-start.2) | collective-permute-done | bytes 262176 | tf_op jit(solution)/shard_map/ppermute | solution.py:190
  15.8 1.5 collective-permute-done.4
  17.2 7.3 %collective-permute-done.3 = bf16[128,1024]{1,0:T(8,128)(2,1)S(1)} collective-permute-done((bf16[128,1024]{1,0:T(8,128)(2,1)S(1)}, bf16[128,1024]{1,0:T(8,128)(2,1)S(1)}, u32[]{:S(2)}, u32[]{:S(2)}) %collective-permute-start.3) | collective-permute-done | bytes 262176 | tf_op jit(solution)/shard_map/ppermute | solution.py:190
  24.5 1.1 pad_maximum_fusion.1
  25.6 0.0 all-gather.3.cloned.1.call-update
  25.8 0.3 copy.50
  26.1 0.2 copy.51
  26.3 0.3 copy.52
  26.6 0.2 copy.53
  26.9 0.0 copy-start.6
  26.9 0.0 copy-start.1
  26.9 0.1 pad_maximum_fusion
  27.1 45.2 %all_to_all.25.rows_ref = bf16[8,128,768]{2,1,0:T(8,128)(2,1)S(1)} all-to-all(bf16[8,128,768]{2,1,0:T(8,128)(2,1)S(1)} %pad_maximum_fusion), channel_id=1, replica_groups=mesh['x'=4,'y'=4,'z'=8,'c'=2] {'z'}, dimensions={0} | all-to-all | bytes 3145728 | tf_op jit(solution)/shard_map/all_to_all | solution.py:204
  72.3 3.8 %collective-permute-start = (bf16[8,128,256]{2,1,0:T(8,128)(2,1)S(1)}, bf16[8,128,256]{2,1,0:T(8,128)(2,1)S(1)}, u32[]{:S(2)}, u32[]{:S(2)}) collective-permute-start(bf16[8,128,256]{2,1,0:T(8,128)(2,1)S(1)} %slice.22), channel_id=1, source_target_pairs={{0,1},{1,0},{2,3},{3,2},{4,5},{5,4},{6,7},{7,6},{8,9},{9,8},{10,11... | collective-permute-start | bytes 1572872 | tf_op jit(solution)/shard_map/ppermute | solution.py:178
  76.1 0.1 copy.56.links_ref
  76.2 3.3 %all-gather.3.cloned.1.call-done = bf16[16,128,1024]{2,1,0:T(8,128)(2,1)} async-done(((bf16[4,128,1024]{2,1,0:T(8,128)(2,1)}), bf16[16,128,1024]{2,1,0:T(8,128)(2,1)}) %all-gather.3.cloned.1.call-update) | async-done | bytes 4194320 | tf_op jit(solution)/shard_map/all_gather | solution.py:191
  79.4 0.7 collective-permute-start.5
  80.1 0.0 collective-permute-done.other_ref
  80.1 0.3 broadcast_in_dim.23.seg_cols_ref
  80.4 13.3 %shard_map.110 = (bf16[8,128,256]{2,1,0:T(8,128)(2,1)}, f32[8,128,256]{2,1,0:T(8,128)S(1)}, f32[8,128,256]{2,1,0:T(8,128)S(1)}) custom-call(s32[16,8]{1,0:T(8,128)S(1)} %copy.56.links_ref, s32[1]{0:T(128)} %bitcast.1.core_ref, bf16[8,128,768]{2,1,0:T(8,128)(2,1)S(1)} %all_to_all.25.rows_ref, bf16[8,128,256]{2,1,0:T(8,128)(2,1)S(1)} %collective-permute-done.other_ref, ...), custom_call_target="tpu_custom_call" | custom-call | flops 4000000000 | bytes 8388608 | tf_op jit(solution)/shard_map/pallas_call | solution.py:110
  93.7 1.0 collective-permute-start.1
  94.7 2.3 %collective-permute-done.1 = f32[8,128,256]{2,1,0:T(8,128)S(1)} collective-permute-done((f32[8,128,256]{2,1,0:T(8,128)S(1)}, f32[8,128,256]{2,1,0:T(8,128)S(1)}, u32[]{:S(2)}, u32[]{:S(2)}) %collective-permute-start.1) | collective-permute-done | bytes 1048608 | tf_op jit(solution)/shard_map/ppermute | solution.py:178
  97.0 0.2 add_convert_fusion
  97.2 23.2 %all_to_all.26 = bf16[8,128,256]{2,1,0:T(8,128)(2,1)S(1)} all-to-all(bf16[8,128,256]{2,1,0:T(8,128)(2,1)S(1)} %add_convert_fusion), channel_id=1, replica_groups=mesh['x'=4,'y'=4,'z'=8,'c'=2] {'z'}, dimensions={0} | all-to-all | bytes 1048576 | tf_op jit(solution)/shard_map/all_to_all | solution.py:214
  120.4 0.1 reshape.47
  120.6 1.0 reduce_sum.21
  121.6 0.2 broadcast_in_dim.25
  121.8 24.4 %all_to_all.27.grads_ref = bf16[32,128,128]{2,1,0:T(8,128)(2,1)S(1)} all-to-all(bf16[32,128,128]{2,1,0:T(8,128)(2,1)S(1)} %bitcast.55), channel_id=1, replica_groups=mesh['x'=4,'y'=4,'z'=8,'c'=2] {'x','y','c'}, dimensions={0} | all-to-all | bytes 2097152 | tf_op jit(solution)/shard_map/all_to_all | solution.py:225
  146.2 3.7 %all-to-all-start.1 = ((bf16[8,128,256]{2,1,0:T(8,128)(2,1)}), bf16[8,128,256]{2,1,0:T(8,128)(2,1)S(1)}, u32[]{:S(2)}, u32[]{:S(2)}) async-start(bf16[8,128,256]{2,1,0:T(8,128)(2,1)} %get-tuple-element.8), calls=%async_computation.1 | async-start | bytes 1048576 | tf_op jit(solution)/shard_map/all_to_all | solution.py:220
  149.9 0.1 pad_add_fusion.place_ref
  150.0 2.2 %copy-done = bf16[16,128,1024]{2,1,0:T(8,128)(2,1)S(1)} copy-done((bf16[16,128,1024]{2,1,0:T(8,128)(2,1)S(1)}, bf16[16,128,1024]{2,1,0:T(8,128)(2,1)}, u32[]{:S(2)}) %copy-start) | copy-done | bytes 4194328
  152.1 4.9 %shard_map.111 = bf16[1024,128]{1,0:T(8,128)(2,1)} custom-call(s32[2]{0:T(128)S(1)} %pad_add_fusion.place_ref, bf16[32,128,128]{2,1,0:T(8,128)(2,1)S(1)} %all_to_all.27.grads_ref, bf16[4,4,128,1024]{3,2,1,0:T(8,128)(2,1)S(1)} %bitcast.52, bf16[4,4,128,1024]{3,2,1,0:T(8,128)(2,1)} %collective-permute-done.5.other_ref), custom_call_target="tpu_custom_call" | custom-call | flops 1100000000 | bytes 9437184 | tf_op jit(solution)/shard_map/pallas_call | solution.py:154
  157.0 9.3 %all-to-all-done.1 = bf16[8,128,256]{2,1,0:T(8,128)(2,1)S(1)} async-done(((bf16[8,128,256]{2,1,0:T(8,128)(2,1)}), bf16[8,128,256]{2,1,0:T(8,128)(2,1)S(1)}, u32[]{:S(2)}, u32[]{:S(2)}) %all-to-all-start.1) | async-done | bytes 524320 | tf_op jit(solution)/shard_map/all_to_all | solution.py:220
  166.3 5.1 %all-to-all-start.4 = ((bf16[64,16,128]{2,1,0:T(8,128)(2,1)}), bf16[64,16,128]{2,1,0:T(8,128)(2,1)S(1)}, u32[]{:S(2)}, u32[]{:S(2)}) async-start(bf16[64,16,128]{2,1,0:T(8,128)(2,1)} %bitcast.28), calls=%async_computation.4 | async-start | bytes 524288 | tf_op jit(solution)/shard_map/all_to_all | solution.py:231
  171.4 0.3 copy.57
  171.7 1.0 copy.63
  172.7 0.4 fusion
  173.1 0.1 copy.69
  173.2 0.8 copy.65
  174.0 0.1 copy.68
  174.2 0.8 copy.64
  174.9 8.5 %all-to-all-done.4 = bf16[64,16,128]{2,1,0:T(8,128)(2,1)S(1)} async-done(((bf16[64,16,128]{2,1,0:T(8,128)(2,1)}), bf16[64,16,128]{2,1,0:T(8,128)(2,1)S(1)}, u32[]{:S(2)}, u32[]{:S(2)}) %all-to-all-start.4) | async-done | bytes 262176 | tf_op jit(solution)/shard_map/all_to_all | solution.py:231
  183.5 0.6 copy_bitcast_fusion
  (24 shorter events, 0.4 us)
Async XLA Ops:
  7.2 18.5 %copy-start.4 = (bf16[1,128,512]{2,1,0:T(8,128)(2,1)S(1)}, bf16[1,128,512]{2,1,0:T(8,128)(2,1)}, u32[]{:S(2)}) copy-start(bf16[1,128,512]{2,1,0:T(8,128)(2,1)} %param.9) | copy-start | bytes 393220
  7.2 18.5 %copy-start.5 = (bf16[1,128,512]{2,1,0:T(8,128)(2,1)S(1)}, bf16[1,128,512]{2,1,0:T(8,128)(2,1)}, u32[]{:S(2)}) copy-start(bf16[1,128,512]{2,1,0:T(8,128)(2,1)} %param.10) | copy-start | bytes 393220
  7.2 72.2 %all-gather.3.cloned.1.call-start = ((), (), s32[]{:S(2)}) async-start(), calls=%async_computation.5 | async-start | bytes 5242880 | tf_op jit(solution)/shard_map/all_gather | solution.py:191
  7.3 18.5 %copy-start.2 = (bf16[1,128,2048]{2,1,0:T(8,128)(2,1)S(1)}, bf16[1,128,2048]{2,1,0:T(8,128)(2,1)}, u32[]{:S(2)}) copy-start(bf16[1,128,2048]{2,1,0:T(8,128)(2,1)} %param.8) | copy-start | bytes 1572868
  8.6 7.1 %collective-permute-start.2 = (bf16[128,1024]{1,0:T(8,128)(2,1)S(1)}, bf16[128,1024]{1,0:T(8,128)(2,1)S(1)}, u32[]{:S(2)}, u32[]{:S(2)}) collective-permute-start(bf16[128,1024]{1,0:T(8,128)(2,1)S(1)} %get-tuple-element.32), channel_id=1, source_target_pairs={{0,64},{64,128},{128,192},{192,0},{1,65},{65,129},{129,193},{193,1... | collective-permute-start | bytes 786440 | tf_op jit(solution)/shard_map/ppermute | solution.py:190
  10.7 6.5 %collective-permute-start.4 = (bf16[128,1024]{1,0:T(8,128)(2,1)S(1)}, bf16[128,1024]{1,0:T(8,128)(2,1)S(1)}, u32[]{:S(2)}, u32[]{:S(2)}) collective-permute-start(bf16[128,1024]{1,0:T(8,128)(2,1)S(1)} %get-tuple-element.33), channel_id=1, source_target_pairs={{0,192},{64,0},{128,64},{192,128},{1,193},{65,1},{129,65},{193,129... | collective-permute-start | bytes 786440 | tf_op jit(solution)/shard_map/ppermute | solution.py:190
  12.1 12.4 %collective-permute-start.3 = (bf16[128,1024]{1,0:T(8,128)(2,1)S(1)}, bf16[128,1024]{1,0:T(8,128)(2,1)S(1)}, u32[]{:S(2)}, u32[]{:S(2)}) collective-permute-start(bf16[128,1024]{1,0:T(8,128)(2,1)S(1)} %get-tuple-element.34), channel_id=1, source_target_pairs={{0,128},{64,192},{128,0},{192,64},{1,129},{65,193},{129,1},{193,65... | collective-permute-start | bytes 786440 | tf_op jit(solution)/shard_map/ppermute | solution.py:190
  24.5 1.8 copy-start.3
  26.9 49.2 %copy-start.6 = (s32[1,16,8]{1,2,0:T(8,128)S(1)}, s32[1,16,8]{1,2,0:T(8,128)}, u32[]{:S(2)}) copy-start(s32[1,16,8]{1,2,0:T(8,128)} %param.12) | copy-start | bytes 1540
  26.9 53.2 %copy-start.1 = (s32[1,2048]{1,0:T(1,128)S(1)}, s32[1,2048]{1,0:T(1,128)}, u32[]{:S(2)}) copy-start(s32[1,2048]{1,0:T(1,128)} %param.13) | copy-start | bytes 24580
  72.3 7.8 %collective-permute-start = (bf16[8,128,256]{2,1,0:T(8,128)(2,1)S(1)}, bf16[8,128,256]{2,1,0:T(8,128)(2,1)S(1)}, u32[]{:S(2)}, u32[]{:S(2)}) collective-permute-start(bf16[8,128,256]{2,1,0:T(8,128)(2,1)S(1)} %slice.22), channel_id=1, source_target_pairs={{0,1},{1,0},{2,3},{3,2},{4,5},{5,4},{6,7},{7,6},{8,9},{9,8},{10,11... | collective-permute-start | bytes 1572872 | tf_op jit(solution)/shard_map/ppermute | solution.py:178
  79.4 70.5 %collective-permute-start.5 = (bf16[4,4,128,1024]{3,2,1,0:T(8,128)(2,1)}, bf16[4,4,128,1024]{3,2,1,0:T(8,128)(2,1)}, u32[]{:S(2)}, u32[]{:S(2)}) collective-permute-start(bf16[4,4,128,1024]{3,2,1,0:T(8,128)(2,1)} %bitcast.51), channel_id=1, source_target_pairs={{0,1},{1,0},{2,3},{3,2},{4,5},{5,4},{6,7},{7,6},{8,9},{9,8},{10,11... | collective-permute-start | bytes 12582920 | tf_op jit(solution)/shard_map/ppermute | solution.py:178
  93.7 3.3 %collective-permute-start.1 = (f32[8,128,256]{2,1,0:T(8,128)S(1)}, f32[8,128,256]{2,1,0:T(8,128)S(1)}, u32[]{:S(2)}, u32[]{:S(2)}) collective-permute-start(f32[8,128,256]{2,1,0:T(8,128)S(1)} %get-tuple-element.10), channel_id=1, source_target_pairs={{0,1},{1,0},{2,3},{3,2},{4,5},{5,4},{6,7},{7,6},{8,9},{9,8},{10,11... | collective-permute-start | bytes 3145736 | tf_op jit(solution)/shard_map/ppermute | solution.py:178
  146.2 20.1 %all-to-all-start.1 = ((bf16[8,128,256]{2,1,0:T(8,128)(2,1)}), bf16[8,128,256]{2,1,0:T(8,128)(2,1)S(1)}, u32[]{:S(2)}, u32[]{:S(2)}) async-start(bf16[8,128,256]{2,1,0:T(8,128)(2,1)} %get-tuple-element.8), calls=%async_computation.1 | async-start | bytes 1048576 | tf_op jit(solution)/shard_map/all_to_all | solution.py:220
  150.0 2.2 %copy-start = (bf16[16,128,1024]{2,1,0:T(8,128)(2,1)S(1)}, bf16[16,128,1024]{2,1,0:T(8,128)(2,1)}, u32[]{:S(2)}) copy-start(bf16[16,128,1024]{2,1,0:T(8,128)(2,1)} %all-gather.3.cloned.1.call-done) | copy-start | bytes 12582916
  166.3 17.1 %all-to-all-start.4 = ((bf16[64,16,128]{2,1,0:T(8,128)(2,1)}), bf16[64,16,128]{2,1,0:T(8,128)(2,1)S(1)}, u32[]{:S(2)}, u32[]{:S(2)}) async-start(bf16[64,16,128]{2,1,0:T(8,128)(2,1)} %bitcast.28), calls=%async_computation.4 | async-start | bytes 524288 | tf_op jit(solution)/shard_map/all_to_all | solution.py:231
Sparse Core Ops, SparseCore 0:
  25.7 53.6 all-gather.2

commit v2 on v1

--- a/solution.py
+++ b/solution.py
@@ -26,10 +26,10 @@
 
 
 def attention_kernel(
-    links_ref, core_ref, rows_ref, other_ref, seg_cols_ref, seg_rows_ref,
+    links_ref, place_ref, rows_ref, other_ref, seg_cols_ref, seg_rows_ref,
     dq_ref, own_ref, away_ref, pair_ref, keys_t_ref, total_ref,
 ):
-    core = core_ref[0]
+    z, core = place_ref[1], place_ref[2]
 
     def load_pairs(i, carry):
         for block, pair in ((2 * i + core, rows_ref[i, :, 4 * HEAD:]), (2 * i + 1 - core, other_ref[i])):
@@ -82,8 +82,9 @@
             part = dot(keys_t_ref[j], score_grads)
             dq_t = part if dq_t is None else dq_t + part
         dq = (dq_t * SCALE).T
-        dq_ref[i, :, :HEAD] = dq[:BLOCK].astype(jnp.bfloat16)
-        dq_ref[i, :, HEAD:] = dq[BLOCK:].astype(jnp.bfloat16)
+        slot = lax.rem(i - z + NZ, NZ)
+        dq_ref[slot, :, :HEAD] = dq[:BLOCK].astype(jnp.bfloat16)
+        dq_ref[slot, :, HEAD:] = dq[BLOCK:].astype(jnp.bfloat16)
 
     def linked(i, carry):
         query_block(i, [links_ref[2 * i + core, t] for t in range(LINKS)])
@@ -104,7 +105,7 @@
     lax.fori_loop(0, NZ, store, 0)
 
 
-def attention_grads(links, core, rows, other, seg_cols, seg_rows):
+def attention_grads(links, place, rows, other, seg_cols, seg_rows):
     vmem = pl.BlockSpec(memory_space=pltpu.VMEM)
     smem = pl.BlockSpec(memory_space=pltpu.SMEM)
     return pl.pallas_call(
@@ -125,49 +126,117 @@
         cost_estimate=pl.CostEstimate(
             flops=4_000_000_000, bytes_accessed=8 * MIB, transcendentals=2_500_000
         ),
-    )(links, core, rows, other, seg_cols, seg_rows)
-
-
-def weight_kernel(place_ref, grads_ref, own_ref, other_ref, out_ref, total_ref):
-    step = pl.program_id(0)
-    x, core = place_ref[0], place_ref[1]
-
-    @pl.when(step == 0)
-    def _():
-        total_ref[...] = jnp.zeros_like(total_ref)
-
-    total = total_ref[...]
-    for s in range(NX):
-        source = (lax.rem(x - s + NX, NX) * NY + step) * NC
-        grads = jnp.concatenate([grads_ref[source + core], grads_ref[source + 1 - core]], axis=0)
-        inputs = jnp.concatenate([own_ref[0, s], other_ref[0, s]], axis=0)
-        total = total + dot(grads.T, inputs)
-    total_ref[...] = total
-
-    @pl.when(step == NY - 1)
-    def _():
-        out_ref[...] = total_ref[...].T.astype(jnp.bfloat16)
+    )(links, place, rows, other, seg_cols, seg_rows)
+
+
+PARTS = tuple((shift, first) for shift in (0, -1, 1, 2) for first in (0, NX // 2))
+
+
+def weight_kernel(place_ref, grads_ref, *refs):
+    count = len(PARTS)
+    out_ref, own_ref, other_ref, sems = refs[2 * count :]
+    copies = []
+    for p in range(count):
+        for side, held in enumerate((own_ref, other_ref)):
+            copy = pltpu.make_async_copy(refs[side * count + p], held.at[p], sems.at[side, p])
+            copy.start()
+            copies.append(copy)
+    x, y, core = place_ref[0], place_ref[3], place_ref[2]
+    total = None
+    for p, (shift, first) in enumerate(PARTS):
+        copies[2 * p].wait()
+        copies[2 * p + 1].wait()
+        for s in range(NX // 2):
+            source = (lax.rem(x - first - s + NX, NX) * NY + lax.rem(y + shift + NY, NY)) * NC
+            grads = jnp.concatenate([grads_ref[source + core], grads_ref[source + 1 - core]], axis=0)
+            inputs = jnp.concatenate([own_ref[p, s], other_ref[p, s]], axis=0)
+            part = dot(grads.T, inputs)
+            total = part if total is None else total + part
+    out_ref[...] = total.T.astype(jnp.bfloat16)
 
 
 def weight_grads_part(place, grads, own, other):
-    width = own.shape[-1]
+    shape = own[0].shape
+    vmem = pl.BlockSpec(memory_space=pltpu.VMEM)
+    held = pltpu.VMEM((len(PARTS),) + shape, jnp.bfloat16)
     return pl.pallas_call(
         weight_kernel,
-        grid=(NY,),
-        out_shape=jax.ShapeDtypeStruct((width, HEAD), jnp.bfloat16),
-        in_specs=[
-            pl.BlockSpec(memory_space=pltpu.SMEM),
-            pl.BlockSpec(memory_space=pltpu.VMEM),
-            pl.BlockSpec((1, NX, BLOCK, width), lambda i: (i, 0, 0, 0)),
-            pl.BlockSpec((1, NX, BLOCK, width), lambda i: (i, 0, 0, 0)),
-        ],
-        out_specs=pl.BlockSpec((width, HEAD), lambda i: (0, 0)),
-        scratch_shapes=[pltpu.VMEM((HEAD, width), jnp.float32)],
-        compiler_params=pltpu.CompilerParams(vmem_limit_bytes=32 * MIB),
+        out_shape=jax.ShapeDtypeStruct((shape[-1], HEAD), jnp.bfloat16),
+        in_specs=[pl.BlockSpec(memory_space=pltpu.SMEM), vmem]
+        + [pl.BlockSpec(memory_space=pl.ANY)] * (2 * len(PARTS)),
+        out_specs=vmem,
+        scratch_shapes=[held, held, pltpu.SemaphoreType.DMA((2, len(PARTS)))],
+        compiler_params=pltpu.CompilerParams(vmem_limit_bytes=24 * MIB),
         cost_estimate=pl.CostEstimate(
             flops=1_100_000_000, bytes_accessed=9 * MIB, transcendentals=0
         ),
-    )(place, grads, own, other)
+    )(place, grads, *own, *other)
+
+
+def pack_kernel(queries_ref, grads_ref, keys_ref, values_ref, out_ref):
+    for i in range(NZ):
+        heads = slice(2 * HEAD * i, 2 * HEAD * (i + 1))
+        shared = slice(HEAD * (i * KV_HEADS // NZ), HEAD * (i * KV_HEADS // NZ + 1))
+        out_ref[i, :, : 2 * HEAD] = queries_ref[:, heads]
+        out_ref[i, :, 2 * HEAD : 4 * HEAD] = grads_ref[:, heads]
+        out_ref[i, :, 4 * HEAD : 5 * HEAD] = keys_ref[:, shared]
+        out_ref[i, :, 5 * HEAD :] = values_ref[:, shared]
+
+
+def packed(queries, grads, keys, values):
+    vmem = pl.BlockSpec(memory_space=pltpu.VMEM)
+    return pl.pallas_call(
+        pack_kernel,
+        out_shape=jax.ShapeDtypeStruct((NZ, BLOCK, 6 * HEAD), jnp.bfloat16),
+        in_specs=[vmem] * 4,
+        out_specs=vmem,
+        compiler_params=pltpu.CompilerParams(vmem_limit_bytes=16 * MIB),
+        cost_estimate=pl.CostEstimate(flops=0, bytes_accessed=3 * MIB, transcendentals=0),
+    )(queries, grads, keys, values)
+
+
+def pair_kernel(partials_ref, keys_ref, values_ref, chunks_ref):
+    for g in range(KV_HEADS):
+        pair = partials_ref[2 * g].astype(jnp.float32) + partials_ref[2 * g + 1].astype(jnp.float32)
+        pair = pair.astype(jnp.bfloat16)
+        for kind, ref in enumerate((keys_ref, values_ref)):
+            part = pair[:, kind * HEAD : (kind + 1) * HEAD]
+            ref[:, g * HEAD : (g + 1) * HEAD] = part
+            for x in range(NX):
+                chunks_ref[(x * NY + g) * NC + kind] = part
+
+
+def pair_grads(partials):
+    vmem = pl.BlockSpec(memory_space=pltpu.VMEM)
+    out = jax.ShapeDtypeStruct((BLOCK, KV_HEADS * HEAD), jnp.bfloat16)
+    return pl.pallas_call(
+        pair_kernel,
+        out_shape=(out, out, jax.ShapeDtypeStruct((NX * NY * NC, BLOCK, HEAD), jnp.bfloat16)),
+        in_specs=[vmem],
+        out_specs=(vmem, vmem, vmem),
+        compiler_params=pltpu.CompilerParams(vmem_limit_bytes=16 * MIB),
+        cost_estimate=pl.CostEstimate(flops=0, bytes_accessed=2 * MIB, transcendentals=0),
+    )(partials)
+
+
+def join_kernel(place_ref, *refs):
+    out_ref = refs[-1]
+    z = place_ref[1]
+    for s in range(NZ):
+        column = lax.rem(z - s + NZ, NZ) * (2 * HEAD)
+        out_ref[:, pl.ds(pl.multiple_of(column, 2 * HEAD), 2 * HEAD)] = refs[s][...]
+
+
+def joined(place, pieces):
+    vmem = pl.BlockSpec(memory_space=pltpu.VMEM)
+    return pl.pallas_call(
+        join_kernel,
+        out_shape=jax.ShapeDtypeStruct((BLOCK, NZ * 2 * HEAD), jnp.bfloat16),
+        in_specs=[pl.BlockSpec(memory_space=pltpu.SMEM)] + [vmem] * NZ,
+        out_specs=vmem,
+        compiler_params=pltpu.CompilerParams(vmem_limit_bytes=16 * MIB),
+        cost_estimate=pl.CostEstimate(flops=0, bytes_accessed=MIB, transcendentals=0),
+    )(place, *pieces)
 
 
 def ring(size, shift):
@@ -179,7 +248,8 @@
 
 
 def local(layer_input, queries, keys, values, output_grads, block_links, segment_ids):
-    x, core = lax.axis_index("x"), lax.axis_index("c")
+    x, y, z, core = (lax.axis_index(axis) for axis in ("x", "y", "z", "c"))
+    place = jnp.stack([x, z, core, y]).astype(jnp.int32)
     bf16 = jnp.bfloat16
 
     inputs = layer_input[0]
@@ -188,44 +258,42 @@
     for s in range(NX):
         piece = lax.dynamic_slice_in_dim(inputs, lax.rem(x + s, NX) * width, width, axis=1)
         pieces.append(piece if s == 0 else lax.ppermute(piece, "x", ring(NX, s)))
-    inputs_own = lax.all_gather(jnp.stack(pieces), "y", axis=0)
-
-    def by_chip(a):
-        return jnp.transpose(a.reshape(BLOCK, NZ, 2 * HEAD), (1, 0, 2))
-
-    def by_key_head(a):
-        heads = jnp.transpose(a.reshape(BLOCK, KV_HEADS, HEAD), (1, 0, 2))
-        return jnp.repeat(heads, NZ // KV_HEADS, axis=0)
-
-    outgoing = jnp.concatenate(
-        [by_chip(queries[0]), by_chip(output_grads[0]), by_key_head(keys[0]), by_key_head(values[0])],
-        axis=-1,
-    )
+    half = NX // 2
+    mine = (jnp.stack(pieces[:half]), jnp.stack(pieces[half:]))
+    before, after = (
+        tuple(lax.ppermute(a, "y", ring(NY, shift)) for a in mine) for shift in (1, -1)
+    )
+
+    outgoing = packed(queries[0], output_grads[0], keys[0], values[0])
     rows = lax.all_to_all(outgoing, "z", split_axis=0, concat_axis=0, tiled=True)
+    rows, mine = lax.optimization_barrier((rows, mine))
     other = swap_cores(rows[..., 4 * HEAD :])
 
     seg_rows = segment_ids[0].reshape(BLOCKS, BLOCK)
     seg_cols = jnp.broadcast_to(seg_rows[:, :, None], (BLOCKS, BLOCK, BLOCK))
     dq, own, away = attention_grads(
-        block_links[0], core.reshape(1).astype(jnp.int32), rows, other, seg_cols, seg_rows
-    )
+        block_links[0], place, rows, other, seg_cols, seg_rows
+    )
+
+    dq, own, away, before, after = lax.optimization_barrier((dq, own, away, before, after))
+    far = (
+        lax.ppermute(before[0], "y", ring(NY, 1)),
+        lax.ppermute(after[1], "y", ring(NY, -1)),
+    )
+    inputs_own = mine + before + after
+    inputs_other = tuple(swap_cores(a) for a in inputs_own)
 
     pair = (own + swap_cores(away)).astype(bf16)
     pair = lax.all_to_all(pair, "z", split_axis=0, concat_axis=0, tiled=True)
-    pair = pair.reshape(KV_HEADS, NZ // KV_HEADS, BLOCK, 2, HEAD).astype(jnp.float32)
-    pair = jnp.sum(pair, axis=1).astype(bf16)
-    key_grads = jnp.transpose(pair[:, :, 0], (1, 0, 2)).reshape(BLOCK, KV_HEADS * HEAD)
-    value_grads = jnp.transpose(pair[:, :, 1], (1, 0, 2)).reshape(BLOCK, KV_HEADS * HEAD)
-
-    dq = lax.all_to_all(dq, "z", split_axis=0, concat_axis=0, tiled=True)
-    query_grads = jnp.transpose(dq, (1, 0, 2)).reshape(BLOCK, NZ * 2 * HEAD)
-
-    chunks = jnp.transpose(pair, (0, 2, 1, 3)).reshape(1, NY * NC, BLOCK, HEAD)
-    chunks = jnp.broadcast_to(chunks, (NX, NY * NC, BLOCK, HEAD)).reshape(-1, BLOCK, HEAD)
+    dq, pair, inputs_other, far = lax.optimization_barrier((dq, pair, inputs_other, far))
+    far_other = tuple(swap_cores(a) for a in far)
+    key_grads, value_grads, chunks = pair_grads(pair)
+
     grads = lax.all_to_all(chunks, ("x", "y", "c"), split_axis=0, concat_axis=0, tiled=True)
-    inputs_other = swap_cores(inputs_own)
-    place = jnp.stack([x, core]).astype(jnp.int32)
-    part = weight_grads_part(place, grads, inputs_own, inputs_other)
+    dq = (dq[0],) + tuple(lax.ppermute(dq[s], "z", ring(NZ, s)) for s in range(1, NZ))
+    grads, dq, far_other = lax.optimization_barrier((grads, dq, far_other))
+    query_grads = joined(place, dq)
+    part = weight_grads_part(place, grads, inputs_own + far, inputs_other + far_other)
 
     part = part.reshape(NY * NZ * NC, -1, HEAD)
     part = lax.all_to_all(part, ("y", "z", "c"), split_axis=0, concat_axis=0, tiled=True)

time: 191 us -> 177 us (0.927)
  blocking collectives: 92.8 us -> 0 us
  starting transfers between devices: 19.4 us -> 62.7 us
  waiting for transfers between devices: 34.1 us -> 66.2 us
  local copies, waits for them, and re-layouts: 9.68 us -> 24 us
  between operations: 14.3 us -> 0.81 us
  Pallas kernels: 18.2 us -> 21.1 us
    all_to_all x3 -> x0, blocking collectives: 92.8 us -> none  [the longest x1 45.2 us: local(): lax.all_to_all(outgoing, 'z', split_axis=0, concat_axis=0, tiled=True)]
    ppermute x0 -> x13, starting transfers between devices: none -> 23.1 us  [the longest x7 14.9 us: local(): lax.ppermute(dq[s], 'z', ring(NZ, s))]
    ppermute x0 -> x13, waiting for transfers between devices: none -> 21 us  [the longest x1 7.96 us: local(): lax.ppermute(before[0], 'y', ring(NY, 1))]
    all_to_all x1 -> x3, starting transfers between devices: 3.68 us -> 19.8 us  [the longest x1 9.01 us: local(): lax.all_to_all(outgoing, 'z', split_axis=0, concat_axis=0, tiled=True)]
    unnamed x19 -> x50, local copies, waits for them, and re-layouts: 5.32 us -> 19.7 us
    all_to_all x1 -> x3, waiting for transfers between devices: 9.26 us -> 23.6 us  [the longest x1 22 us: local(): lax.all_to_all(outgoing, 'z', split_axis=0, concat_axis=0, tiled=True)]
    all_to_all x1, starting transfers between devices: 5.13 us -> 9.78 us  [local(): lax.all_to_all(part, ('y', 'z', 'c'), split_axis=0, concat_axis=0, tiled=...]
    pallas_call x1 -> x4, Pallas kernels: 4.88 us -> 8.21 us  [the longest x1 4.29 us: weight_grads_part(): pl.pallas_call(weight_kernel, out_shape=jax.ShapeDtypeStruct((shape[-1],...]
  transfers between devices with their start and end apart: 9 -> 30, of which waited for: 7 -> 16; matrix products, arithmetic and copies ran while one was open for 4% -> 2% of each run, Pallas kernels for 10% -> 8%
where the time goes in v2:
time: 177 us; the launch traced here: 176 us
  waiting for transfers between devices  66.2 us (37%)
  starting transfers between devices  62.7 us (35%)
  local copies, waits for them, and re-layouts  24 us (14%)
  Pallas kernels  21.1 us (12%)
    all_to_all x1, waiting for transfers between devices, local(): lax.all_to_all(outgoing, 'z', split_axis=0, concat_axis=0, tiled=True)  22 us
    unnamed x50, local copies, waits for them, and re-layouts  19.7 us
    ppermute x7, starting transfers between devices, local(): lax.ppermute(dq[s], 'z', ring(NZ, s))  14.9 us
    pallas_call x1, Pallas kernels, attention_grads(): pl.pallas_call(attention_kernel, out_shape=(jax.ShapeDtypeStruct((NZ, BLO...  12.9 us
    ppermute x3, waiting for transfers between devices, local(): pieces.append(piece if s == 0 else lax.ppermute(piece, 'x', ring(NX, s)))  10.5 us
    all_to_all x1, starting transfers between devices, local(): lax.all_to_all(part, ('y', 'z', 'c'), split_axis=0, concat_axis=0, tiled=...  9.78 us
    all_to_all x1, starting transfers between devices, local(): lax.all_to_all(outgoing, 'z', split_axis=0, concat_axis=0, tiled=True)  9.01 us
    all_to_all x1, waiting for transfers between devices, local(): lax.all_to_all(part, ('y', 'z', 'c'), split_axis=0, concat_axis=0, tiled=...  8.92 us
  transfers between devices with their start and end apart: 30, of which 16 were waited for; matrix products, arithmetic and copies ran while one was open for 2% of the time, Pallas kernels for 8%

profile of v2, /device:TPU:1, one launch (start us, length us, event | category | flops | bytes accessed | tf_op | source)
XLA Modules:
  0.0 175.8 jit_solution(9553405772214164550)
XLA Ops:
  0.6 1.0 copy-done.15
  1.7 1.0 copy-done.16
  2.7 0.9 copy-done.17
  3.6 0.9 copy-done.18
  4.5 1.3 shard_map.110
  5.9 9.0 %all-to-all-start = ((bf16[8,128,768]{2,1,0:T(8,128)(2,1)}), bf16[8,128,768]{2,1,0:T(8,128)(2,1)S(1)}, u32[]{:S(2)}, u32[]{:S(2)}) async-start(bf16[8,128,768]{2,1,0:T(8,128)(2,1)} %shard_map.110), calls=%async_computation | async-start | bytes 3145728 | tf_op jit(solution)/shard_map/all_to_all | solution.py:268
  14.9 1.3 dynamic-slice_bitcast_fusion.1
  16.2 2.8 %collective-permute-start.1 = (bf16[128,1024]{1,0:T(8,128)(2,1)S(1)}, bf16[128,1024]{1,0:T(8,128)(2,1)S(1)}, u32[]{:S(2)}, u32[]{:S(2)}) collective-permute-start(bf16[128,1024]{1,0:T(8,128)(2,1)S(1)} %get-tuple-element.79), channel_id=1, source_target_pairs={{0,128},{64,192},{128,0},{192,64},{1,129},{65,193},{129,1},{193,65... | collective-permute-start | bytes 786440 | tf_op jit(solution)/shard_map/ppermute | solution.py:260
  19.0 0.9 collective-permute-start.2
  20.5 4.1 %collective-permute-done.1 = bf16[128,1024]{1,0:T(8,128)(2,1)S(1)} collective-permute-done((bf16[128,1024]{1,0:T(8,128)(2,1)S(1)}, bf16[128,1024]{1,0:T(8,128)(2,1)S(1)}, u32[]{:S(2)}, u32[]{:S(2)}) %collective-permute-start.1) | collective-permute-done | bytes 262176 | tf_op jit(solution)/shard_map/ppermute | solution.py:260
  24.6 6.1 %collective-permute-done.2 = bf16[128,1024]{1,0:T(8,128)(2,1)S(1)} collective-permute-done((bf16[128,1024]{1,0:T(8,128)(2,1)S(1)}, bf16[128,1024]{1,0:T(8,128)(2,1)S(1)}, u32[]{:S(2)}, u32[]{:S(2)}) %collective-permute-start.2) | collective-permute-done | bytes 262176 | tf_op jit(solution)/shard_map/ppermute | solution.py:260
  31.1 22.0 %all-to-all-done.rows_ref = bf16[8,128,768]{2,1,0:T(8,128)(2,1)S(1)} async-done(((bf16[8,128,768]{2,1,0:T(8,128)(2,1)}), bf16[8,128,768]{2,1,0:T(8,128)(2,1)S(1)}, u32[]{:S(2)}, u32[]{:S(2)}) %all-to-all-start) | async-done | bytes 1572896 | tf_op jit(solution)/shard_map/all_to_all | solution.py:268
  54.0 2.7 %collective-permute-start.3 = (bf16[8,128,256]{2,1,0:T(8,128)(2,1)}, bf16[8,128,256]{2,1,0:T(8,128)(2,1)}, u32[]{:S(2)}, u32[]{:S(2)}) collective-permute-start(bf16[8,128,256]{2,1,0:T(8,128)(2,1)} %slice.35), channel_id=1, source_target_pairs={{0,1},{1,0},{2,3},{3,2},{4,5},{5,4},{6,7},{7,6},{8,9},{9,8},{10,11... | collective-permute-start | bytes 1572872 | tf_op jit(solution)/shard_map/ppermute | solution.py:247
  56.6 1.3 collective-permute-start.5
  57.9 1.4 collective-permute-start.7
  59.4 2.7 %collective-permute-start.6 = (bf16[2,128,1024]{2,1,0:T(8,128)(2,1)S(1)}, bf16[2,128,1024]{2,1,0:T(8,128)(2,1)}, u32[]{:S(2)}, u32[]{:S(2)}) collective-permute-start(bf16[2,128,1024]{2,1,0:T(8,128)(2,1)S(1)} %pad_maximum_fusion.refs_0_), channel_id=1, source_target_pairs={{0,48},{16,0},{32,16},{48,32},{1,49},{17,1},{33,17},{49,33},{2,50}... | collective-permute-start | bytes 1572872 | tf_op jit(solution)/shard_map/ppermute | solution.py:264
  62.5 12.9 %shard_map.111 = (bf16[8,128,256]{2,1,0:T(8,128)(2,1)S(1)}, f32[8,128,256]{2,1,0:T(8,128)S(1)}, f32[8,128,256]{2,1,0:T(8,128)S(1)}) custom-call(s32[16,8]{1,0:T(8,128)S(1)} %copy.14.links_ref, s32[4]{0:T(128)S(1)} %pad_add_fusion.place_ref, bf16[8,128,768]{2,1,0:T(8,128)(2,1)S(1)} %all-to-all-done.rows_ref, ...), custom_call_target="tpu_custom_call" | custom-call | flops 4000000000 | bytes 8388608 | tf_op jit(solution)/shard_map/pallas_call | solution.py:111
  76.2 6.7 %collective-permute-done.4.refs_2_ = bf16[2,128,1024]{2,1,0:T(8,128)(2,1)} collective-permute-done((bf16[2,128,1024]{2,1,0:T(8,128)(2,1)S(1)}, bf16[2,128,1024]{2,1,0:T(8,128)(2,1)}, u32[]{:S(2)}, u32[]{:S(2)}) %collective-permute-start.4) | collective-permute-done | bytes 524320 | tf_op jit(solution)/shard_map/ppermute | solution.py:264
  84.1 1.8 %collective-permute-done.8 = f32[8,128,256]{2,1,0:T(8,128)S(1)} collective-permute-done((f32[8,128,256]{2,1,0:T(8,128)S(1)}, f32[8,128,256]{2,1,0:T(8,128)S(1)}, u32[]{:S(2)}, u32[]{:S(2)}) %collective-permute-start.8) | collective-permute-done | bytes 1048608 | tf_op jit(solution)/shard_map/ppermute | solution.py:247
  85.9 0.9 add_convert_fusion
  86.8 3.5 %all-to-all-start.1 = ((bf16[8,128,256]{2,1,0:T(8,128)(2,1)}), bf16[8,128,256]{2,1,0:T(8,128)(2,1)S(1)}, u32[]{:S(2)}, u32[]{:S(2)}) async-start(bf16[8,128,256]{2,1,0:T(8,128)(2,1)} %add_convert_fusion), calls=%async_computation.1 | async-start | bytes 1048576 | tf_op jit(solution)/shard_map/all_to_all | solution.py:287
  90.3 1.4 collective-permute-start.15
  92.9 1.4 collective-permute-start.16
  97.0 8.0 %collective-permute-done.15.refs_6_ = bf16[2,128,1024]{2,1,0:T(8,128)(2,1)S(1)} collective-permute-done((bf16[2,128,1024]{2,1,0:T(8,128)(2,1)}, bf16[2,128,1024]{2,1,0:T(8,128)(2,1)S(1)}, u32[]{:S(2)}, u32[]{:S(2)}) %collective-permute-start.15) | collective-permute-done | bytes 524320 | tf_op jit(solution)/shard_map/ppermute | solution.py:280
  105.8 0.9 collective-permute-done.16.refs_7_
  106.7 1.6 all-to-all-done.1.partials_ref
  108.2 1.2 shard_map.112
  109.4 7.3 %all-to-all-start.2 = ((bf16[32,128,128]{2,1,0:T(8,128)(2,1)}), bf16[32,128,128]{2,1,0:T(8,128)(2,1)S(1)}, u32[]{:S(2)}, u32[]{:S(2)}) async-start(bf16[32,128,128]{2,1,0:T(8,128)(2,1)} %get-tuple-element.56), calls=%async_computation.2 | async-start | bytes 2097152 | tf_op jit(solution)/shard_map/all_to_all | solution.py:292
  117.3 1.1 slice_bitcast_fusion
  118.8 2.1 %collective-permute-start.18 = (bf16[128,256]{1,0:T(8,128)(2,1)S(1)}, bf16[128,256]{1,0:T(8,128)(2,1)S(1)}, u32[]{:S(2)}, u32[]{:S(2)}) collective-permute-start(bf16[128,256]{1,0:T(8,128)(2,1)S(1)} %get-tuple-element.88), channel_id=1, source_target_pairs={{0,4},{2,6},{4,8},{6,10},{8,12},{10,14},{12,0},{14,2},{1,5},{3,7},... | collective-permute-start | bytes 196616 | tf_op jit(solution)/shard_map/ppermute | solution.py:293
  120.9 2.4 %collective-permute-start.19 = (bf16[128,256]{1,0:T(8,128)(2,1)S(1)}, bf16[128,256]{1,0:T(8,128)(2,1)S(1)}, u32[]{:S(2)}, u32[]{:S(2)}) collective-permute-start(bf16[128,256]{1,0:T(8,128)(2,1)S(1)} %get-tuple-element.87), channel_id=1, source_target_pairs={{0,6},{2,8},{4,10},{6,12},{8,14},{10,0},{12,2},{14,4},{1,7},{3,9},... | collective-permute-start | bytes 196616 | tf_op jit(solution)/shard_map/ppermute | solution.py:293
  123.3 4.1 %collective-permute-start.20 = (bf16[128,256]{1,0:T(8,128)(2,1)S(1)}, bf16[128,256]{1,0:T(8,128)(2,1)S(1)}, u32[]{:S(2)}, u32[]{:S(2)}) collective-permute-start(bf16[128,256]{1,0:T(8,128)(2,1)S(1)} %get-tuple-element.86), channel_id=1, source_target_pairs={{0,8},{2,10},{4,12},{6,14},{8,0},{10,2},{12,4},{14,6},{1,9},{3,11}... | collective-permute-start | bytes 196616 | tf_op jit(solution)/shard_map/ppermute | solution.py:293
  127.4 2.6 %collective-permute-start.21 = (bf16[128,256]{1,0:T(8,128)(2,1)S(1)}, bf16[128,256]{1,0:T(8,128)(2,1)S(1)}, u32[]{:S(2)}, u32[]{:S(2)}) collective-permute-start(bf16[128,256]{1,0:T(8,128)(2,1)S(1)} %get-tuple-element.85), channel_id=1, source_target_pairs={{0,10},{2,12},{4,14},{6,0},{8,2},{10,4},{12,6},{14,8},{1,11},{3,13... | collective-permute-start | bytes 196616 | tf_op jit(solution)/shard_map/ppermute | solution.py:293
  130.3 1.6 collective-permute-start.22
  132.2 1.8 %collective-permute-start.23 = (bf16[128,256]{1,0:T(8,128)(2,1)S(1)}, bf16[128,256]{1,0:T(8,128)(2,1)S(1)}, u32[]{:S(2)}, u32[]{:S(2)}) collective-permute-start(bf16[128,256]{1,0:T(8,128)(2,1)S(1)} %get-tuple-element.83), channel_id=1, source_target_pairs={{0,14},{2,0},{4,2},{6,4},{8,6},{10,8},{12,10},{14,12},{1,15},{3,1}... | collective-permute-start | bytes 196616 | tf_op jit(solution)/shard_map/ppermute | solution.py:293
  134.1 3.7 %collective-permute-done.22.refs_6_ = bf16[128,256]{1,0:T(8,128)(2,1)S(1)} collective-permute-done((bf16[128,256]{1,0:T(8,128)(2,1)S(1)}, bf16[128,256]{1,0:T(8,128)(2,1)S(1)}, u32[]{:S(2)}, u32[]{:S(2)}) %collective-permute-start.22) | collective-permute-done | bytes 65568 | tf_op jit(solution)/shard_map/ppermute | solution.py:293
  138.5 1.0 collective-permute-done.23.refs_7_
  141.7 1.0 copy-done.1
  142.8 1.0 copy-done.3
  143.8 1.0 copy-done.5
  144.8 1.0 copy-done.7
  145.9 1.0 copy-done.9
  146.9 1.0 copy-done.11
  148.0 1.0 copy-done.13
  149.0 4.3 %shard_map.114 = bf16[1024,128]{1,0:T(8,128)(2,1)} custom-call(s32[4]{0:T(128)S(1)} %pad_add_fusion.place_ref, bf16[32,128,128]{2,1,0:T(8,128)(2,1)S(1)} %all-to-all-done.2.grads_ref, bf16[2,128,1024]{2,1,0:T(8,128)(2,1)S(1)} %pad_maximum_fusion.refs_0_, bf16[2,128,1024]{2,1,0:T(8,128)(2,1)S(1)} %pad_maximum_fusion.1.refs_1_, ...), custom_call_target="tpu_custom_call" | custom-call | flops 1100000000 | bytes 9437184 | tf_op jit(solution)/shard_map/pallas_call | solution.py:162
  153.3 9.8 %all-to-all-start.3 = ((bf16[64,16,128]{2,1,0:T(8,128)(2,1)}), bf16[64,16,128]{2,1,0:T(8,128)(2,1)S(1)}, u32[]{:S(2)}, u32[]{:S(2)}) async-start(bf16[64,16,128]{2,1,0:T(8,128)(2,1)} %bitcast.27), calls=%async_computation.3 | async-start | bytes 524288 | tf_op jit(solution)/shard_map/all_to_all | solution.py:299
  164.8 1.4 shard_map.113
  166.2 8.9 %all-to-all-done.3 = bf16[64,16,128]{2,1,0:T(8,128)(2,1)S(1)} async-done(((bf16[64,16,128]{2,1,0:T(8,128)(2,1)}), bf16[64,16,128]{2,1,0:T(8,128)(2,1)S(1)}, u32[]{:S(2)}, u32[]{:S(2)}) %all-to-all-start.3) | async-done | bytes 262176 | tf_op jit(solution)/shard_map/all_to_all | solution.py:299
  (81 shorter events, 16.1 us)
Async XLA Ops:
  0.6 1.0 copy-start.15
  1.7 1.0 copy-start.16
  2.7 0.9 copy-start.17
  3.6 0.9 copy-start.18
  5.9 47.3 %all-to-all-start = ((bf16[8,128,768]{2,1,0:T(8,128)(2,1)}), bf16[8,128,768]{2,1,0:T(8,128)(2,1)S(1)}, u32[]{:S(2)}, u32[]{:S(2)}) async-start(bf16[8,128,768]{2,1,0:T(8,128)(2,1)} %shard_map.110), calls=%async_computation | async-start | bytes 3145728 | tf_op jit(solution)/shard_map/all_to_all | solution.py:268
  16.2 8.4 %collective-permute-start.1 = (bf16[128,1024]{1,0:T(8,128)(2,1)S(1)}, bf16[128,1024]{1,0:T(8,128)(2,1)S(1)}, u32[]{:S(2)}, u32[]{:S(2)}) collective-permute-start(bf16[128,1024]{1,0:T(8,128)(2,1)S(1)} %get-tuple-element.79), channel_id=1, source_target_pairs={{0,128},{64,192},{128,0},{192,64},{1,129},{65,193},{129,1},{193,65... | collective-permute-start | bytes 786440 | tf_op jit(solution)/shard_map/ppermute | solution.py:260
  19.0 11.7 %collective-permute-start.2 = (bf16[128,1024]{1,0:T(8,128)(2,1)S(1)}, bf16[128,1024]{1,0:T(8,128)(2,1)S(1)}, u32[]{:S(2)}, u32[]{:S(2)}) collective-permute-start(bf16[128,1024]{1,0:T(8,128)(2,1)S(1)} %get-tuple-element.82), channel_id=1, source_target_pairs={{0,192},{64,0},{128,64},{192,128},{1,193},{65,1},{129,65},{193,129... | collective-permute-start | bytes 786440 | tf_op jit(solution)/shard_map/ppermute | solution.py:260
  19.9 11.2 %collective-permute-start = (bf16[128,1024]{1,0:T(8,128)(2,1)S(1)}, bf16[128,1024]{1,0:T(8,128)(2,1)S(1)}, u32[]{:S(2)}, u32[]{:S(2)}) collective-permute-start(bf16[128,1024]{1,0:T(8,128)(2,1)S(1)} %get-tuple-element.80), channel_id=1, source_target_pairs={{0,64},{64,128},{128,192},{192,0},{1,65},{65,129},{129,193},{193,1... | collective-permute-start | bytes 786440 | tf_op jit(solution)/shard_map/ppermute | solution.py:260
  30.7 31.4 %copy-start.24 = (s32[1,16,8]{1,2,0:T(8,128)S(1)}, s32[1,16,8]{1,2,0:T(8,128)}, u32[]{:S(2)}) copy-start(s32[1,16,8]{1,2,0:T(8,128)} %param.12) | copy-start | bytes 1540
  30.7 31.5 %copy-start.23 = (s32[1,2048]{1,0:T(1,128)S(1)}, s32[1,2048]{1,0:T(1,128)}, u32[]{:S(2)}) copy-start(s32[1,2048]{1,0:T(1,128)} %param.13) | copy-start | bytes 24580
  54.0 8.2 %collective-permute-start.3 = (bf16[8,128,256]{2,1,0:T(8,128)(2,1)}, bf16[8,128,256]{2,1,0:T(8,128)(2,1)}, u32[]{:S(2)}, u32[]{:S(2)}) collective-permute-start(bf16[8,128,256]{2,1,0:T(8,128)(2,1)} %slice.35), channel_id=1, source_target_pairs={{0,1},{1,0},{2,3},{3,2},{4,5},{5,4},{6,7},{7,6},{8,9},{9,8},{10,11... | collective-permute-start | bytes 1572872 | tf_op jit(solution)/shard_map/ppermute | solution.py:247
  56.6 19.6 %collective-permute-start.5 = (bf16[2,128,1024]{2,1,0:T(8,128)(2,1)S(1)}, bf16[2,128,1024]{2,1,0:T(8,128)(2,1)S(1)}, u32[]{:S(2)}, u32[]{:S(2)}) collective-permute-start(bf16[2,128,1024]{2,1,0:T(8,128)(2,1)S(1)} %pad_maximum_fusion.1.refs_1_), channel_id=1, source_target_pairs={{0,16},{16,32},{32,48},{48,0},{1,17},{17,33},{33,49},{49,1},{2,18}... | collective-permute-start | bytes 1572872 | tf_op jit(solution)/shard_map/ppermute | solution.py:264
  57.9 18.3 %collective-permute-start.7 = (bf16[2,128,1024]{2,1,0:T(8,128)(2,1)S(1)}, bf16[2,128,1024]{2,1,0:T(8,128)(2,1)}, u32[]{:S(2)}, u32[]{:S(2)}) collective-permute-start(bf16[2,128,1024]{2,1,0:T(8,128)(2,1)S(1)} %pad_maximum_fusion.1.refs_1_), channel_id=1, source_target_pairs={{0,48},{16,0},{32,16},{48,32},{1,49},{17,1},{33,17},{49,33},{2,50}... | collective-permute-start | bytes 1572872 | tf_op jit(solution)/shard_map/ppermute | solution.py:264
  59.4 23.5 %collective-permute-start.4 = (bf16[2,128,1024]{2,1,0:T(8,128)(2,1)S(1)}, bf16[2,128,1024]{2,1,0:T(8,128)(2,1)}, u32[]{:S(2)}, u32[]{:S(2)}) collective-permute-start(bf16[2,128,1024]{2,1,0:T(8,128)(2,1)S(1)} %pad_maximum_fusion.refs_0_), channel_id=1, source_target_pairs={{0,16},{16,32},{32,48},{48,0},{1,17},{17,33},{33,49},{49,1},{2,18}... | collective-permute-start | bytes 1572872 | tf_op jit(solution)/shard_map/ppermute | solution.py:264
  59.4 23.5 %collective-permute-start.6 = (bf16[2,128,1024]{2,1,0:T(8,128)(2,1)S(1)}, bf16[2,128,1024]{2,1,0:T(8,128)(2,1)}, u32[]{:S(2)}, u32[]{:S(2)}) collective-permute-start(bf16[2,128,1024]{2,1,0:T(8,128)(2,1)S(1)} %pad_maximum_fusion.refs_0_), channel_id=1, source_target_pairs={{0,48},{16,0},{32,16},{48,32},{1,49},{17,1},{33,17},{49,33},{2,50}... | collective-permute-start | bytes 1572872 | tf_op jit(solution)/shard_map/ppermute | solution.py:264
  82.9 3.0 %collective-permute-start.8 = (f32[8,128,256]{2,1,0:T(8,128)S(1)}, f32[8,128,256]{2,1,0:T(8,128)S(1)}, u32[]{:S(2)}, u32[]{:S(2)}) collective-permute-start(f32[8,128,256]{2,1,0:T(8,128)S(1)} %get-tuple-element.48), channel_id=1, source_target_pairs={{0,1},{1,0},{2,3},{3,2},{4,5},{5,4},{6,7},{7,6},{8,9},{9,8},{10,11... | collective-permute-start | bytes 3145736 | tf_op jit(solution)/shard_map/ppermute | solution.py:247
  83.6 8.7 %collective-permute-start.10 = (bf16[2,128,1024]{2,1,0:T(8,128)(2,1)S(1)}, bf16[2,128,1024]{2,1,0:T(8,128)(2,1)S(1)}, u32[]{:S(2)}, u32[]{:S(2)}) collective-permute-start(bf16[2,128,1024]{2,1,0:T(8,128)(2,1)S(1)} %pad_maximum_fusion.1.refs_1_), channel_id=1, source_target_pairs={{0,1},{1,0},{2,3},{3,2},{4,5},{5,4},{6,7},{7,6},{8,9},{9,8},{10,11... | collective-permute-start | bytes 1572872 | tf_op jit(solution)/shard_map/ppermute | solution.py:247
  83.6 8.7 %collective-permute-start.9 = (bf16[2,128,1024]{2,1,0:T(8,128)(2,1)S(1)}, bf16[2,128,1024]{2,1,0:T(8,128)(2,1)S(1)}, u32[]{:S(2)}, u32[]{:S(2)}) collective-permute-start(bf16[2,128,1024]{2,1,0:T(8,128)(2,1)S(1)} %pad_maximum_fusion.refs_0_), channel_id=1, source_target_pairs={{0,1},{1,0},{2,3},{3,2},{4,5},{5,4},{6,7},{7,6},{8,9},{9,8},{10,11... | collective-permute-start | bytes 1572872 | tf_op jit(solution)/shard_map/ppermute | solution.py:247
  84.1 8.7 %collective-permute-start.11 = (bf16[2,128,1024]{2,1,0:T(8,128)(2,1)}, bf16[2,128,1024]{2,1,0:T(8,128)(2,1)}, u32[]{:S(2)}, u32[]{:S(2)}) collective-permute-start(bf16[2,128,1024]{2,1,0:T(8,128)(2,1)} %collective-permute-done.4.refs_2_), channel_id=1, source_target_pairs={{0,1},{1,0},{2,3},{3,2},{4,5},{5,4},{6,7},{7,6},{8,9},{9,8},{10,11... | collective-permute-start | bytes 1572872 | tf_op jit(solution)/shard_map/ppermute | solution.py:247
  86.8 21.4 %all-to-all-start.1 = ((bf16[8,128,256]{2,1,0:T(8,128)(2,1)}), bf16[8,128,256]{2,1,0:T(8,128)(2,1)S(1)}, u32[]{:S(2)}, u32[]{:S(2)}) async-start(bf16[8,128,256]{2,1,0:T(8,128)(2,1)} %add_convert_fusion), calls=%async_computation.1 | async-start | bytes 1048576 | tf_op jit(solution)/shard_map/all_to_all | solution.py:287
  90.3 14.6 %collective-permute-start.15 = (bf16[2,128,1024]{2,1,0:T(8,128)(2,1)}, bf16[2,128,1024]{2,1,0:T(8,128)(2,1)S(1)}, u32[]{:S(2)}, u32[]{:S(2)}) collective-permute-start(bf16[2,128,1024]{2,1,0:T(8,128)(2,1)} %collective-permute-done.4.refs_2_), channel_id=1, source_target_pairs={{0,16},{16,32},{32,48},{48,0},{1,17},{17,33},{33,49},{49,1},{2,18}... | collective-permute-start | bytes 1572872 | tf_op jit(solution)/shard_map/ppermute | solution.py:280
  91.7 2.9 %collective-permute-start.12 = (bf16[2,128,1024]{2,1,0:T(8,128)(2,1)S(1)}, bf16[2,128,1024]{2,1,0:T(8,128)(2,1)S(1)}, u32[]{:S(2)}, u32[]{:S(2)}) collective-permute-start(bf16[2,128,1024]{2,1,0:T(8,128)(2,1)S(1)} %collective-permute-done.5.refs_3_), channel_id=1, source_target_pairs={{0,1},{1,0},{2,3},{3,2},{4,5},{5,4},{6,7},{7,6},{8,9},{9,8},{10,11... | collective-permute-start | bytes 1572872 | tf_op jit(solution)/shard_map/ppermute | solution.py:247
  92.3 3.0 %collective-permute-start.13 = (bf16[2,128,1024]{2,1,0:T(8,128)(2,1)}, bf16[2,128,1024]{2,1,0:T(8,128)(2,1)S(1)}, u32[]{:S(2)}, u32[]{:S(2)}) collective-permute-start(bf16[2,128,1024]{2,1,0:T(8,128)(2,1)} %collective-permute-done.6.refs_4_), channel_id=1, source_target_pairs={{0,1},{1,0},{2,3},{3,2},{4,5},{5,4},{6,7},{7,6},{8,9},{9,8},{10,11... | collective-permute-start | bytes 1572872 | tf_op jit(solution)/shard_map/ppermute | solution.py:247
  92.3 17.1 %copy-start = (bf16[2,128,1024]{2,1,0:T(8,128)(2,1)}, bf16[2,128,1024]{2,1,0:T(8,128)(2,1)S(1)}, u32[]{:S(2)}) copy-start(bf16[2,128,1024]{2,1,0:T(8,128)(2,1)S(1)} %collective-permute-done.9.refs_8_) | copy-start | bytes 1572868
  92.4 3.8 %collective-permute-start.14 = (bf16[2,128,1024]{2,1,0:T(8,128)(2,1)}, bf16[2,128,1024]{2,1,0:T(8,128)(2,1)S(1)}, u32[]{:S(2)}, u32[]{:S(2)}) collective-permute-start(bf16[2,128,1024]{2,1,0:T(8,128)(2,1)} %collective-permute-done.7.refs_5_), channel_id=1, source_target_pairs={{0,1},{1,0},{2,3},{3,2},{4,5},{5,4},{6,7},{7,6},{8,9},{9,8},{10,11... | collective-permute-start | bytes 1572872 | tf_op jit(solution)/shard_map/ppermute | solution.py:247
  92.9 13.8 %collective-permute-start.16 = (bf16[2,128,1024]{2,1,0:T(8,128)(2,1)}, bf16[2,128,1024]{2,1,0:T(8,128)(2,1)}, u32[]{:S(2)}, u32[]{:S(2)}) collective-permute-start(bf16[2,128,1024]{2,1,0:T(8,128)(2,1)} %collective-permute-done.7.refs_5_), channel_id=1, source_target_pairs={{0,48},{16,0},{32,16},{48,32},{1,49},{17,1},{33,17},{49,33},{2,50}... | collective-permute-start | bytes 1572872 | tf_op jit(solution)/shard_map/ppermute | solution.py:281
  94.5 0.8 copy-start.4
  104.9 0.8 copy-start.2
  109.4 32.3 %all-to-all-start.2 = ((bf16[32,128,128]{2,1,0:T(8,128)(2,1)}), bf16[32,128,128]{2,1,0:T(8,128)(2,1)S(1)}, u32[]{:S(2)}, u32[]{:S(2)}) async-start(bf16[32,128,128]{2,1,0:T(8,128)(2,1)} %get-tuple-element.56), calls=%async_computation.2 | async-start | bytes 2097152 | tf_op jit(solution)/shard_map/all_to_all | solution.py:292
  116.7 23.4 %collective-permute-start.24 = (bf16[2,128,1024]{2,1,0:T(8,128)(2,1)}, bf16[2,128,1024]{2,1,0:T(8,128)(2,1)S(1)}, u32[]{:S(2)}, u32[]{:S(2)}) collective-permute-start(bf16[2,128,1024]{2,1,0:T(8,128)(2,1)} %copy-done.2), channel_id=1, source_target_pairs={{0,1},{1,0},{2,3},{3,2},{4,5},{5,4},{6,7},{7,6},{8,9},{9,8},{10,11... | collective-permute-start | bytes 1572872 | tf_op jit(solution)/shard_map/ppermute | solution.py:247
  117.1 23.9 %collective-permute-start.25 = (bf16[2,128,1024]{2,1,0:T(8,128)(2,1)}, bf16[2,128,1024]{2,1,0:T(8,128)(2,1)S(1)}, u32[]{:S(2)}, u32[]{:S(2)}) collective-permute-start(bf16[2,128,1024]{2,1,0:T(8,128)(2,1)} %collective-permute-done.16.refs_7_), channel_id=1, source_target_pairs={{0,1},{1,0},{2,3},{3,2},{4,5},{5,4},{6,7},{7,6},{8,9},{9,8},{10,11... | collective-permute-start | bytes 1572872 | tf_op jit(solution)/shard_map/ppermute | solution.py:247
  118.4 4.9 %collective-permute-start.17 = (bf16[128,256]{1,0:T(8,128)(2,1)S(1)}, bf16[128,256]{1,0:T(8,128)(2,1)S(1)}, u32[]{:S(2)}, u32[]{:S(2)}) collective-permute-start(bf16[128,256]{1,0:T(8,128)(2,1)S(1)} %get-tuple-element.89), channel_id=1, source_target_pairs={{0,2},{2,4},{4,6},{6,8},{8,10},{10,12},{12,14},{14,0},{1,3},{3,5},... | collective-permute-start | bytes 196616 | tf_op jit(solution)/shard_map/ppermute | solution.py:293
  118.8 8.6 %collective-permute-start.18 = (bf16[128,256]{1,0:T(8,128)(2,1)S(1)}, bf16[128,256]{1,0:T(8,128)(2,1)S(1)}, u32[]{:S(2)}, u32[]{:S(2)}) collective-permute-start(bf16[128,256]{1,0:T(8,128)(2,1)S(1)} %get-tuple-element.88), channel_id=1, source_target_pairs={{0,4},{2,6},{4,8},{6,10},{8,12},{10,14},{12,0},{14,2},{1,5},{3,7},... | collective-permute-start | bytes 196616 | tf_op jit(solution)/shard_map/ppermute | solution.py:293
  120.9 9.4 %collective-permute-start.19 = (bf16[128,256]{1,0:T(8,128)(2,1)S(1)}, bf16[128,256]{1,0:T(8,128)(2,1)S(1)}, u32[]{:S(2)}, u32[]{:S(2)}) collective-permute-start(bf16[128,256]{1,0:T(8,128)(2,1)S(1)} %get-tuple-element.87), channel_id=1, source_target_pairs={{0,6},{2,8},{4,10},{6,12},{8,14},{10,0},{12,2},{14,4},{1,7},{3,9},... | collective-permute-start | bytes 196616 | tf_op jit(solution)/shard_map/ppermute | solution.py:293
  123.3 8.9 %collective-permute-start.20 = (bf16[128,256]{1,0:T(8,128)(2,1)S(1)}, bf16[128,256]{1,0:T(8,128)(2,1)S(1)}, u32[]{:S(2)}, u32[]{:S(2)}) collective-permute-start(bf16[128,256]{1,0:T(8,128)(2,1)S(1)} %get-tuple-element.86), channel_id=1, source_target_pairs={{0,8},{2,10},{4,12},{6,14},{8,0},{10,2},{12,4},{14,6},{1,9},{3,11}... | collective-permute-start | bytes 196616 | tf_op jit(solution)/shard_map/ppermute | solution.py:293
  127.4 6.7 %collective-permute-start.21 = (bf16[128,256]{1,0:T(8,128)(2,1)S(1)}, bf16[128,256]{1,0:T(8,128)(2,1)S(1)}, u32[]{:S(2)}, u32[]{:S(2)}) collective-permute-start(bf16[128,256]{1,0:T(8,128)(2,1)S(1)} %get-tuple-element.85), channel_id=1, source_target_pairs={{0,10},{2,12},{4,14},{6,0},{8,2},{10,4},{12,6},{14,8},{1,11},{3,13... | collective-permute-start | bytes 196616 | tf_op jit(solution)/shard_map/ppermute | solution.py:293
  130.3 7.6 %collective-permute-start.22 = (bf16[128,256]{1,0:T(8,128)(2,1)S(1)}, bf16[128,256]{1,0:T(8,128)(2,1)S(1)}, u32[]{:S(2)}, u32[]{:S(2)}) collective-permute-start(bf16[128,256]{1,0:T(8,128)(2,1)S(1)} %get-tuple-element.84), channel_id=1, source_target_pairs={{0,12},{2,14},{4,0},{6,2},{8,4},{10,6},{12,8},{14,10},{1,13},{3,15... | collective-permute-start | bytes 196616 | tf_op jit(solution)/shard_map/ppermute | solution.py:293
  132.2 7.3 %collective-permute-start.23 = (bf16[128,256]{1,0:T(8,128)(2,1)S(1)}, bf16[128,256]{1,0:T(8,128)(2,1)S(1)}, u32[]{:S(2)}, u32[]{:S(2)}) collective-permute-start(bf16[128,256]{1,0:T(8,128)(2,1)S(1)} %get-tuple-element.83), channel_id=1, source_target_pairs={{0,14},{2,0},{4,2},{6,4},{8,6},{10,8},{12,10},{14,12},{1,15},{3,1}... | collective-permute-start | bytes 196616 | tf_op jit(solution)/shard_map/ppermute | solution.py:293
  141.7 1.0 copy-start.1
  142.8 1.0 copy-start.3
  143.8 1.0 copy-start.5
  144.8 1.0 copy-start.7
  145.9 1.0 copy-start.9
  146.9 1.0 copy-start.11
  148.0 1.0 copy-start.13
  153.3 21.8 %all-to-all-start.3 = ((bf16[64,16,128]{2,1,0:T(8,128)(2,1)}), bf16[64,16,128]{2,1,0:T(8,128)(2,1)S(1)}, u32[]{:S(2)}, u32[]{:S(2)}) async-start(bf16[64,16,128]{2,1,0:T(8,128)(2,1)} %bitcast.27), calls=%async_computation.3 | async-start | bytes 524288 | tf_op jit(solution)/shard_map/all_to_all | solution.py:299
  163.1 0.8 copy-start.20
  163.9 0.8 copy-start.22
  (7 other events, 5.2 us)

commit v3 on v2

v3 whole, which is shorter than its diff:
```python
import math

import jax
import jax.numpy as jnp
from jax import lax
from jax.experimental import pallas as pl
from jax.experimental.pallas import tpu as pltpu
from jax.sharding import Mesh, PartitionSpec as P

NX, NY, NZ, NC = 4, 4, 8, 2
HEAD = 128
BLOCK = 128
BLOCKS = NZ * NC
LINKS = 8
KV_HEADS = 4
MIB = 1 << 20
SCALE = 1.0 / math.sqrt(HEAD)
LOG2E = math.log2(math.e)
MASKED = -1e30


def placed(arrays, space):
    return tuple(pltpu.with_memory_space_constraint(a, space) for a in arrays)


def dot(a, b):
    return lax.dot_general(
        a, b, (((1,), (0,)), ((), ())), preferred_element_type=jnp.float32
    )


def attention_kernel(
    links_ref, place_ref, rows_ref, other_ref, seg_cols_ref, seg_rows_ref,
    dq_ref, own_ref, away_ref, pair_ref, keys_t_ref, total_ref, near_ref, near_t_ref,
):
    z, core = place_ref[1], place_ref[2]

    def at(block):
        return pl.ds(pl.multiple_of(block * BLOCK, BLOCK), BLOCK)

    def load_pairs(i, carry):
        for block, pair in ((2 * i + core, rows_ref[i, :, 4 * HEAD:]), (2 * i + 1 - core, other_ref[i])):
            pair_ref[at(block), :] = pair
            keys_t_ref[:, at(block)] = pair[:, :HEAD].T
        return carry

    lax.fori_loop(0, NZ, load_pairs, 0)
    total_ref[...] = jnp.zeros_like(total_ref)

    def query_block(i, key_blocks, pairs, keys_t):
        rows = rows_ref[i]
        queries = jnp.concatenate([rows[:, :HEAD], rows[:, HEAD : 2 * HEAD]], axis=0)
        grads = jnp.concatenate([rows[:, 2 * HEAD : 3 * HEAD], rows[:, 3 * HEAD : 4 * HEAD]], axis=0)
        queries_t, grads_t = queries.T, grads.T
        seg = seg_rows_ref[pl.ds(2 * i + core, 1), :]
        allowed = jnp.concatenate([seg_cols_ref[j] == seg for j in key_blocks], axis=0)
        scores = dot(pairs[:, :HEAD], queries_t) * (SCALE * LOG2E)
        scores = jnp.where(jnp.concatenate([allowed, allowed], axis=1), scores, MASKED)
        weights = jnp.exp2(scores - jnp.max(scores, axis=0, keepdims=True))
        probs = weights * (1.0 / jnp.sum(weights, axis=0, keepdims=True))
        attention = probs.astype(jnp.bfloat16)
        prob_grads = dot(pairs[:, HEAD:], grads_t)
        delta = jnp.sum(attention.astype(jnp.float32) * prob_grads, axis=0, keepdims=True)
        score_grads = (probs * (prob_grads - delta)).astype(jnp.bfloat16)
        value_part = dot(attention, grads)
        key_part = dot(score_grads, queries)
        for t, j in enumerate(key_blocks):
            here = slice(t * BLOCK, (t + 1) * BLOCK)
            total_ref[at(j), :HEAD] += key_part[here]
            total_ref[at(j), HEAD:] += value_part[here]
        dq = (dot(keys_t, score_grads) * SCALE).T
        slot = lax.rem(i - z + NZ, NZ)
        dq_ref[slot, :, :HEAD] = dq[:BLOCK].astype(jnp.bfloat16)
        dq_ref[slot, :, HEAD:] = dq[BLOCK:].astype(jnp.bfloat16)

    def linked(i, carry):
        key_blocks = [links_ref[2 * i + core, t] for t in range(LINKS)]
        for t, j in enumerate(key_blocks):
            here = slice(t * BLOCK, (t + 1) * BLOCK)
            near_ref[here, :] = pair_ref[at(j), :]
            near_t_ref[:, here] = keys_t_ref[:, at(j)]
        query_block(i, key_blocks, near_ref[...], near_t_ref[...])
        return carry

    @pl.when(core == 0)
    def _():
        query_block(0, list(range(BLOCKS)), pair_ref[...], keys_t_ref[...])

    lax.fori_loop(1 - core, NZ, linked, 0)

    def store(i, carry):
        for ref, block in ((own_ref, 2 * i + core), (away_ref, 2 * i + 1 - core)):
            ref[i, :, :HEAD] = total_ref[at(block), :HEAD] * SCALE
            ref[i, :, HEAD:] = total_ref[at(block), HEAD:]
        return carry

    lax.fori_loop(0, NZ, store, 0)


def attention_grads(links, place, rows, other, seg_cols, seg_rows):
    vmem = pl.BlockSpec(memory_space=pltpu.VMEM)
    smem = pl.BlockSpec(memory_space=pltpu.SMEM)
    return pl.pallas_call(
        attention_kernel,
        out_shape=(
            jax.ShapeDtypeStruct((NZ, BLOCK, 2 * HEAD), jnp.bfloat16),
            jax.ShapeDtypeStruct((NZ, BLOCK, 2 * HEAD), jnp.float32),
            jax.ShapeDtypeStruct((NZ, BLOCK, 2 * HEAD), jnp.float32),
        ),
        in_specs=[smem, smem, vmem, vmem, vmem, vmem],
        out_specs=(vmem, vmem, vmem),
        scratch_shapes=[
            pltpu.VMEM((BLOCKS * BLOCK, 2 * HEAD), jnp.bfloat16),
            pltpu.VMEM((HEAD, BLOCKS * BLOCK), jnp.bfloat16),
            pltpu.VMEM((BLOCKS * BLOCK, 2 * HEAD), jnp.float32),
            pltpu.VMEM((LINKS * BLOCK, 2 * HEAD), jnp.bfloat16),
            pltpu.VMEM((HEAD, LINKS * BLOCK), jnp.bfloat16),
        ],
        compiler_params=pltpu.CompilerParams(vmem_limit_bytes=32 * MIB),
        cost_estimate=pl.CostEstimate(
            flops=4_000_000_000, bytes_accessed=8 * MIB, transcendentals=2_500_000
        ),
    )(links, place, rows, other, seg_cols, seg_rows)


PARTS = tuple((shift, first) for shift in (0, -1, 1, 2) for first in (0, NX // 2))


def weight_kernel(place_ref, grads_ref, *refs):
    out_ref = refs[-1]
    x, y, core = place_ref[0], place_ref[3], place_ref[2]
    total = None
    for p, (shift, first) in enumerate(PARTS):
        for s in range(NX // 2):
            source = (lax.rem(x - first - s + NX, NX) * NY + lax.rem(y + shift + NY, NY)) * NC
            grads = jnp.concatenate([grads_ref[source + core], grads_ref[source + 1 - core]], axis=0)
            inputs = jnp.concatenate([refs[p][s], refs[len(PARTS) + p][s]], axis=0)
            part = dot(grads.T, inputs)
            total = part if total is None else total + part
    out_ref[...] = total.T.astype(jnp.bfloat16)


def weight_grads_part(place, grads, own, other):
    vmem = pl.BlockSpec(memory_space=pltpu.VMEM)
    return pl.pallas_call(
        weight_kernel,
        out_shape=jax.ShapeDtypeStruct((own[0].shape[-1], HEAD), jnp.bfloat16),
        in_specs=[pl.BlockSpec(memory_space=pltpu.SMEM)] + [vmem] * (1 + 2 * len(PARTS)),
        out_specs=vmem,
        compiler_params=pltpu.CompilerParams(vmem_limit_bytes=16 * MIB),
        cost_estimate=pl.CostEstimate(
            flops=1_100_000_000, bytes_accessed=9 * MIB, transcendentals=0
        ),
    )(place, grads, *placed(own, pltpu.VMEM), *placed(other, pltpu.VMEM))


def pack_kernel(queries_ref, grads_ref, keys_ref, values_ref, out_ref, sem):
    copies = []
    for i in range(NZ):
        heads = pl.ds(2 * HEAD * i, 2 * HEAD)
        shared = pl.ds(HEAD * (i * KV_HEADS // NZ), HEAD)
        for ref, source, first, size in (
            (queries_ref, heads, 0, 2), (grads_ref, heads, 2, 2), (keys_ref, shared, 4, 1), (values_ref, shared, 5, 1)
        ):
            target = out_ref.at[i, :, pl.ds(first * HEAD, size * HEAD)]
            copies.append(pltpu.make_async_copy(ref.at[:, source], target, sem.at[len(copies)]))
    for copy in copies:
        copy.start()
    for copy in copies:
        copy.wait()


def packed(queries, grads, keys, values):
    return pl.pallas_call(
        pack_kernel,
        out_shape=jax.ShapeDtypeStruct((NZ, BLOCK, 6 * HEAD), jnp.bfloat16),
        in_specs=[pl.BlockSpec(memory_space=pltpu.HBM)] * 4,
        out_specs=pl.BlockSpec(memory_space=pltpu.VMEM),
        scratch_shapes=[pltpu.SemaphoreType.DMA((4 * NZ,))],
        compiler_params=pltpu.CompilerParams(vmem_limit_bytes=16 * MIB),
        cost_estimate=pl.CostEstimate(flops=0, bytes_accessed=3 * MIB, transcendentals=0),
    )(*placed((queries, grads, keys, values), pltpu.HBM))


def pair_kernel(partials_ref, keys_ref, values_ref, chunks_ref):
    for g in range(KV_HEADS):
        pair = partials_ref[2 * g].astype(jnp.float32) + partials_ref[2 * g + 1].astype(jnp.float32)
        pair = pair.astype(jnp.bfloat16)
        for kind, ref in enumerate((keys_ref, values_ref)):
            part = pair[:, kind * HEAD : (kind + 1) * HEAD]
            ref[:, g * HEAD : (g + 1) * HEAD] = part
            for x in range(NX):
                chunks_ref[(x * NY + g) * NC + kind] = part


def pair_grads(partials):
    vmem = pl.BlockSpec(memory_space=pltpu.VMEM)
    out = jax.ShapeDtypeStruct((BLOCK, KV_HEADS * HEAD), jnp.bfloat16)
    return pl.pallas_call(
        pair_kernel,
        out_shape=(out, out, jax.ShapeDtypeStruct((NX * NY * NC, BLOCK, HEAD), jnp.bfloat16)),
        in_specs=[vmem],
        out_specs=(vmem, vmem, vmem),
        compiler_params=pltpu.CompilerParams(vmem_limit_bytes=16 * MIB),
        cost_estimate=pl.CostEstimate(flops=0, bytes_accessed=2 * MIB, transcendentals=0),
    )(partials)


def join_kernel(place_ref, *refs):
    out_ref = refs[-1]
    z = place_ref[1]
    for s in range(NZ):
        column = lax.rem(z - s + NZ, NZ) * (2 * HEAD)
        out_ref[:, pl.ds(pl.multiple_of(column, 2 * HEAD), 2 * HEAD)] = refs[s][...]


def joined(place, pieces):
    vmem = pl.BlockSpec(memory_space=pltpu.VMEM)
    return pl.pallas_call(
        join_kernel,
        out_shape=jax.ShapeDtypeStruct((BLOCK, NZ * 2 * HEAD), jnp.bfloat16),
        in_specs=[pl.BlockSpec(memory_space=pltpu.SMEM)] + [vmem] * NZ,
        out_specs=vmem,
        compiler_params=pltpu.CompilerParams(vmem_limit_bytes=16 * MIB),
        cost_estimate=pl.CostEstimate(flops=0, bytes_accessed=MIB, transcendentals=0),
    )(place, *pieces)


def ring(size, shift):
    return [(i, (i + shift) % size) for i in range(size)]


def swap_cores(a):
    return lax.ppermute(a, "c", [(0, 1), (1, 0)])


def local(layer_input, queries, keys, values, output_grads, block_links, segment_ids):
    x, y, z, core = (lax.axis_index(axis) for axis in ("x", "y", "z", "c"))
    place = jnp.stack([x, z, core, y]).astype(jnp.int32)
    bf16 = jnp.bfloat16

    inputs = layer_input[0]
    width = inputs.shape[1] // NX
    pieces = [
        lax.dynamic_slice_in_dim(inputs, lax.rem(x + s, NX) * width, width, axis=1)
        for s in range(NX)
    ]
    pieces, queries = lax.optimization_barrier((pieces, queries))
    pieces = [a if s == 0 else lax.ppermute(a, "x", ring(NX, s)) for s, a in enumerate(pieces)]
    half = NX // 2
    mine = (jnp.stack(pieces[:half]), jnp.stack(pieces[half:]))
    before, after = (
        tuple(lax.ppermute(a, "y", ring(NY, shift)) for a in mine) for shift in (1, -1)
    )

    outgoing = packed(queries[0], output_grads[0], keys[0], values[0])
    rows = lax.all_to_all(outgoing, "z", split_axis=0, concat_axis=0, tiled=True)
    rows, mine, before, after = lax.optimization_barrier((rows, mine, before, after))
    other = swap_cores(rows[..., 4 * HEAD :])

    seg_rows = segment_ids[0].reshape(BLOCKS, BLOCK)
    seg_cols = jnp.broadcast_to(seg_rows[:, :, None], (BLOCKS, BLOCK, BLOCK))
    dq, own, away = attention_grads(
        block_links[0], place, rows, other, seg_cols, seg_rows
    )

    dq, own, away, mine, before, after = lax.optimization_barrier(
        (dq, own, away, mine, before, after)
    )
    far = (
        lax.ppermute(before[0], "y", ring(NY, 1)),
        lax.ppermute(after[1], "y", ring(NY, -1)),
    )
    inputs_own = mine + before + after
    inputs_other = tuple(swap_cores(a) for a in inputs_own)

    pair = (own + swap_cores(away)).astype(bf16)
    pair = lax.all_to_all(pair, "z", split_axis=0, concat_axis=0, tiled=True)
    dq, pair, inputs_other, far = lax.optimization_barrier((dq, pair, inputs_other, far))
    far_other = tuple(swap_cores(a) for a in far)
    key_grads, value_grads, chunks = pair_grads(pair)

    grads = lax.all_to_all(chunks, ("x", "y", "c"), split_axis=0, concat_axis=0, tiled=True)
    early, late = (1, 7, 2, 6), (3, 5, 4)
    dq = [dq[s] for s in range(NZ)]
    for s in early:
        dq[s] = lax.ppermute(dq[s], "z", ring(NZ, s))
    grads, dq, far_other = lax.optimization_barrier((grads, dq, far_other))
    part = weight_grads_part(place, grads, inputs_own + far, inputs_other + far_other)

    part, dq = lax.optimization_barrier((part, dq))
    part = part.reshape(NY * NZ * NC, -1, HEAD)
    part = lax.all_to_all(part, ("y", "z", "c"), split_axis=0, concat_axis=0, tiled=True)
    for s in late:
        dq[s] = lax.ppermute(dq[s], "z", ring(NZ, s))
    part, dq = lax.optimization_barrier((part, dq))
    query_grads = joined(place, dq)
    part = part.reshape(NY, NZ, NC, -1, HEAD).astype(jnp.float32)
    part = jnp.transpose(jnp.sum(part, axis=1), (1, 2, 0, 3))
    part = part.reshape(NC, -1, NY * HEAD)
    return query_grads[None], key_grads[None], value_grads[None], part[0], part[1]


def solution(mesh):
    chips = Mesh(mesh.devices.reshape(NX, NY, NZ, NC), ("x", "y", "z", "c"))
    dp, seq = ("x", "y"), ("z", "c")
    by_position = P(dp, seq, None)
    return jax.shard_map(
        local,
        mesh=chips,
        in_specs=(by_position,) * 5 + (P(dp, None, None), P(dp, None)),
        out_specs=(by_position,) * 3 + (P(dp + seq, None),) * 2,
        check_vma=False,
    )
```

time: 177 us -> 169 us (0.955)
  waiting for transfers between devices: 66.2 us -> 56.6 us
  starting transfers between devices: 62.7 us -> 68.2 us
  local copies, waits for them, and re-layouts: 24 us -> 18.8 us
    all_to_all x1, waiting for transfers between devices: 22 us -> 0.01 us  [local(): lax.all_to_all(outgoing, 'z', split_axis=0, concat_axis=0, tiled=True)]
    ppermute x4, waiting for transfers between devices: 6.66 us -> 18.9 us  [local(): lax.ppermute(a, 'y', ring(NY, shift))]
    all_to_all x1, waiting for transfers between devices: 8.92 us -> 0.01 us  [local(): lax.all_to_all(part, ('y', 'z', 'c'), split_axis=0, concat_axis=0, tiled=...]
    unnamed x50 -> x42, local copies, waits for them, and re-layouts: 19.7 us -> 13.9 us
    ppermute x10, waiting for transfers between devices: 16 us -> 21.8 us  [the longest x7 11.6 us: local(): dq[s] = lax.ppermute(dq[s], 'z', ring(NZ, s))]
    all_to_all x1, starting transfers between devices: 3.49 us -> 6.67 us  [local(): pair = lax.all_to_all(pair, 'z', split_axis=0, concat_axis=0, tiled=True)]
    all_to_all x1, waiting for transfers between devices: 0.01 us -> 2.14 us  [local(): lax.all_to_all(chunks, ('x', 'y', 'c'), split_axis=0, concat_axis=0, tile...]
  transfers between devices with their start and end apart: 30 -> 30, of which waited for: 16 -> 14; matrix products, arithmetic and copies ran while one was open for 2% -> 2% of each run, Pallas kernels for 8% -> 0%
where the time goes in v3:
time: 169 us; the launch traced here: 167 us
  starting transfers between devices  68.2 us (40%)
  waiting for transfers between devices  56.6 us (33%)
  Pallas kernels  21.7 us (13%)
  local copies, waits for them, and re-layouts  18.8 us (11%)
    ppermute x4, waiting for transfers between devices, local(): lax.ppermute(a, 'y', ring(NY, shift))  18.9 us
    ppermute x7, starting transfers between devices, local(): dq[s] = lax.ppermute(dq[s], 'z', ring(NZ, s))  16.1 us
    unnamed x42, local copies, waits for them, and re-layouts  13.9 us
    pallas_call x1, Pallas kernels, attention_grads(): pl.pallas_call(attention_kernel, out_shape=(jax.ShapeDtypeStruct((NZ, BLO...  12.7 us
    ppermute x7, waiting for transfers between devices, local(): dq[s] = lax.ppermute(dq[s], 'z', ring(NZ, s))  11.6 us
    ppermute x3, waiting for transfers between devices, local(): lax.ppermute(a, 'x', ring(NX, s))  10.2 us
    all_to_all x1, starting transfers between devices, local(): lax.all_to_all(outgoing, 'z', split_axis=0, concat_axis=0, tiled=True)  9.03 us
    all_to_all x1, starting transfers between devices, local(): lax.all_to_all(part, ('y', 'z', 'c'), split_axis=0, concat_axis=0, tiled=...  8.94 us
  transfers between devices with their start and end apart: 30, of which 14 were waited for; matrix products, arithmetic and copies ran while one was open for 2% of the time, Pallas kernels for 0%

profile of v3, /device:TPU:1, one launch (start us, length us, event | category | flops | bytes accessed | tf_op | source)
XLA Modules:
  0.0 167.3 jit_solution(16336753391105393133)
XLA Ops:
  0.7 1.3 dynamic-slice_bitcast_fusion
  1.9 2.9 %shard_map.110 = bf16[8,128,768]{2,1,0:T(8,128)(2,1)} custom-call(bf16[128,2048]{1,0:T(8,128)(2,1)} %bitcast.58, bf16[128,2048]{1,0:T(8,128)(2,1)} %bitcast.59, bf16[128,512]{1,0:T(8,128)(2,1)} %bitcast.64, bf16[128,512]{1,0:T(8,128)(2,1)} %bitcast.65), custom_call_target="tpu_custom_call" | custom-call | bytes 3145728 | tf_op jit(solution)/shard_map/pallas_call | solution.py:174
  4.8 9.0 %all-to-all-start = ((bf16[8,128,768]{2,1,0:T(8,128)(2,1)}), bf16[8,128,768]{2,1,0:T(8,128)(2,1)S(1)}, u32[]{:S(2)}, u32[]{:S(2)}) async-start(bf16[8,128,768]{2,1,0:T(8,128)(2,1)} %shard_map.110), calls=%async_computation | async-start | bytes 3145728 | tf_op jit(solution)/shard_map/all_to_all | solution.py:257
  13.8 2.7 %collective-permute-start.1 = (bf16[128,1024]{1,0:T(8,128)(2,1)S(1)}, bf16[128,1024]{1,0:T(8,128)(2,1)S(1)}, u32[]{:S(2)}, u32[]{:S(2)}) collective-permute-start(bf16[128,1024]{1,0:T(8,128)(2,1)S(1)} %get-tuple-element.74), channel_id=1, source_target_pairs={{0,128},{64,192},{128,0},{192,64},{1,129},{65,193},{129,1},{193,65... | collective-permute-start | bytes 786440 | tf_op jit(solution)/shard_map/ppermute | solution.py:249
  18.1 4.1 %collective-permute-done.1 = bf16[128,1024]{1,0:T(8,128)(2,1)S(1)} collective-permute-done((bf16[128,1024]{1,0:T(8,128)(2,1)S(1)}, bf16[128,1024]{1,0:T(8,128)(2,1)S(1)}, u32[]{:S(2)}, u32[]{:S(2)}) %collective-permute-start.1) | collective-permute-done | bytes 262176 | tf_op jit(solution)/shard_map/ppermute | solution.py:249
  22.2 6.1 %collective-permute-done.2 = bf16[128,1024]{1,0:T(8,128)(2,1)S(1)} collective-permute-done((bf16[128,1024]{1,0:T(8,128)(2,1)S(1)}, bf16[128,1024]{1,0:T(8,128)(2,1)S(1)}, u32[]{:S(2)}, u32[]{:S(2)}) %collective-permute-start.2) | collective-permute-done | bytes 262176 | tf_op jit(solution)/shard_map/ppermute | solution.py:249
  28.3 1.4 collective-permute-start.4
  29.7 1.5 collective-permute-start.6
  31.4 2.7 %collective-permute-start.5 = (bf16[2,128,1024]{2,1,0:T(8,128)(2,1)S(1)}, bf16[2,128,1024]{2,1,0:T(8,128)(2,1)}, u32[]{:S(2)}, u32[]{:S(2)}) collective-permute-start(bf16[2,128,1024]{2,1,0:T(8,128)(2,1)S(1)} %pad_maximum_fusion.refs_0_), channel_id=1, source_target_pairs={{0,48},{16,0},{32,16},{48,32},{1,49},{17,1},{33,17},{49,33},{2,50}... | collective-permute-start | bytes 1572872 | tf_op jit(solution)/shard_map/ppermute | solution.py:253
  34.0 7.6 %collective-permute-done.4.refs_3_ = bf16[2,128,1024]{2,1,0:T(8,128)(2,1)S(1)} collective-permute-done((bf16[2,128,1024]{2,1,0:T(8,128)(2,1)S(1)}, bf16[2,128,1024]{2,1,0:T(8,128)(2,1)S(1)}, u32[]{:S(2)}, u32[]{:S(2)}) %collective-permute-start.4) | collective-permute-done | bytes 524320 | tf_op jit(solution)/shard_map/ppermute | solution.py:253
  41.6 11.3 %collective-permute-done.3.refs_2_ = bf16[2,128,1024]{2,1,0:T(8,128)(2,1)} collective-permute-done((bf16[2,128,1024]{2,1,0:T(8,128)(2,1)S(1)}, bf16[2,128,1024]{2,1,0:T(8,128)(2,1)}, u32[]{:S(2)}, u32[]{:S(2)}) %collective-permute-start.3) | collective-permute-done | bytes 524320 | tf_op jit(solution)/shard_map/ppermute | solution.py:253
  53.8 2.4 %collective-permute-start.7 = (bf16[8,128,256]{2,1,0:T(8,128)(2,1)}, bf16[8,128,256]{2,1,0:T(8,128)(2,1)}, u32[]{:S(2)}, u32[]{:S(2)}) collective-permute-start(bf16[8,128,256]{2,1,0:T(8,128)(2,1)} %slice.35), channel_id=1, source_target_pairs={{0,1},{1,0},{2,3},{3,2},{4,5},{5,4},{6,7},{7,6},{8,9},{9,8},{10,11... | collective-permute-start | bytes 1572872 | tf_op jit(solution)/shard_map/ppermute | solution.py:234
  56.4 1.7 %collective-permute-done.7.other_ref = bf16[8,128,256]{2,1,0:T(8,128)(2,1)} collective-permute-done((bf16[8,128,256]{2,1,0:T(8,128)(2,1)}, bf16[8,128,256]{2,1,0:T(8,128)(2,1)}, u32[]{:S(2)}, u32[]{:S(2)}) %collective-permute-start.7) | collective-permute-done | bytes 524320 | tf_op jit(solution)/shard_map/ppermute | solution.py:234
  58.4 12.7 %shard_map.111 = (bf16[8,128,256]{2,1,0:T(8,128)(2,1)S(1)}, f32[8,128,256]{2,1,0:T(8,128)S(1)}, f32[8,128,256]{2,1,0:T(8,128)S(1)}) custom-call(s32[16,8]{1,0:T(8,128)S(1)} %copy.14.links_ref, s32[4]{0:T(128)S(1)} %pad_add_fusion.place_ref, bf16[8,128,768]{2,1,0:T(8,128)(2,1)S(1)} %all-to-all-done.rows_ref, ...), custom_call_target="tpu_custom_call" | custom-call | flops 4000000000 | bytes 8388608 | tf_op jit(solution)/shard_map/pallas_call | solution.py:103
  71.9 1.5 collective-permute-start.8
  73.9 1.8 %collective-permute-done.8 = f32[8,128,256]{2,1,0:T(8,128)S(1)} collective-permute-done((f32[8,128,256]{2,1,0:T(8,128)S(1)}, f32[8,128,256]{2,1,0:T(8,128)S(1)}, u32[]{:S(2)}, u32[]{:S(2)}) %collective-permute-start.8) | collective-permute-done | bytes 1048608 | tf_op jit(solution)/shard_map/ppermute | solution.py:234
  76.6 6.7 %all-to-all-start.1 = ((bf16[8,128,256]{2,1,0:T(8,128)(2,1)}), bf16[8,128,256]{2,1,0:T(8,128)(2,1)S(1)}, u32[]{:S(2)}, u32[]{:S(2)}) async-start(bf16[8,128,256]{2,1,0:T(8,128)(2,1)} %add_convert_fusion), calls=%async_computation.1 | async-start | bytes 1048576 | tf_op jit(solution)/shard_map/all_to_all | solution.py:278
  83.3 1.3 collective-permute-start.15
  84.6 0.9 collective-permute-start.13
  85.6 1.5 collective-permute-start.16
  89.4 8.2 %collective-permute-done.15.refs_6_ = bf16[2,128,1024]{2,1,0:T(8,128)(2,1)S(1)} collective-permute-done((bf16[2,128,1024]{2,1,0:T(8,128)(2,1)}, bf16[2,128,1024]{2,1,0:T(8,128)(2,1)S(1)}, u32[]{:S(2)}, u32[]{:S(2)}) %collective-permute-start.15) | collective-permute-done | bytes 524320 | tf_op jit(solution)/shard_map/ppermute | solution.py:271
  97.6 1.2 collective-permute-done.16.refs_7_
  101.2 1.2 shard_map.112
  102.4 8.1 %all-to-all-start.2 = ((bf16[32,128,128]{2,1,0:T(8,128)(2,1)}), bf16[32,128,128]{2,1,0:T(8,128)(2,1)S(1)}, u32[]{:S(2)}, u32[]{:S(2)}) async-start(bf16[32,128,128]{2,1,0:T(8,128)(2,1)} %get-tuple-element.96), calls=%async_computation.2 | async-start | bytes 2097152 | tf_op jit(solution)/shard_map/all_to_all | solution.py:283
  111.1 1.7 %slice_bitcast_fusion = (bf16[128,256]{1,0:T(8,128)(2,1)S(1)}, bf16[128,256]{1,0:T(8,128)(2,1)S(1)}, bf16[128,256]{1,0:T(8,128)(2,1)S(1)}, bf16[128,256]{1,0:T(8...) fusion(bf16[8,128,256]{2,1,0:T(8,128)(2,1)} %copy-done.18), kind=kLoop, calls=%fused_computation.8 | loop fusion | bytes 1048576 | tf_op jit(solution)/shard_map/squeeze | solution.py:285
  112.9 1.6 collective-permute-start.17
  114.4 2.1 %collective-permute-start.18 = (bf16[128,256]{1,0:T(8,128)(2,1)S(1)}, bf16[128,256]{1,0:T(8,128)(2,1)S(1)}, u32[]{:S(2)}, u32[]{:S(2)}) collective-permute-start(bf16[128,256]{1,0:T(8,128)(2,1)S(1)} %get-tuple-element.146), channel_id=1, source_target_pairs={{0,4},{2,6},{4,8},{6,10},{8,12},{10,14},{12,0},{14,2},{1,5},{3,7},... | collective-permute-start | bytes 196616 | tf_op jit(solution)/shard_map/ppermute | solution.py:287
  116.5 1.5 collective-permute-start.19
  118.0 1.1 collective-permute-start.20
  119.1 1.8 %collective-permute-done.18.refs_2_ = bf16[128,256]{1,0:T(8,128)(2,1)S(1)} collective-permute-done((bf16[128,256]{1,0:T(8,128)(2,1)S(1)}, bf16[128,256]{1,0:T(8,128)(2,1)S(1)}, u32[]{:S(2)}, u32[]{:S(2)}) %collective-permute-start.18) | collective-permute-done | bytes 65568 | tf_op jit(solution)/shard_map/ppermute | solution.py:287
  120.9 2.8 %collective-permute-done.20.refs_7_ = bf16[128,256]{1,0:T(8,128)(2,1)S(1)} collective-permute-done((bf16[128,256]{1,0:T(8,128)(2,1)S(1)}, bf16[128,256]{1,0:T(8,128)(2,1)S(1)}, u32[]{:S(2)}, u32[]{:S(2)}) %collective-permute-start.20) | collective-permute-done | bytes 65568 | tf_op jit(solution)/shard_map/ppermute | solution.py:287
  125.3 2.1 %all-to-all-done.2.grads_ref = bf16[32,128,128]{2,1,0:T(8,128)(2,1)S(1)} async-done(((bf16[32,128,128]{2,1,0:T(8,128)(2,1)}), bf16[32,128,128]{2,1,0:T(8,128)(2,1)S(1)}, u32[]{:S(2)}, u32[]{:S(2)}) %all-to-all-start.2) | async-done | bytes 1048608 | tf_op jit(solution)/shard_map/all_to_all | solution.py:283
  127.4 1.0 copy-done.3
  128.5 1.0 copy-done.5
  129.5 1.0 copy-done.7
  130.6 1.0 copy-done.9
  131.6 1.0 copy-done.11
  132.6 1.0 copy-done.13
  133.7 1.0 copy-done.15
  134.7 1.0 copy-done.17
  135.8 3.6 %shard_map.113 = bf16[1024,128]{1,0:T(8,128)(2,1)} custom-call(s32[4]{0:T(128)S(1)} %pad_add_fusion.place_ref, bf16[32,128,128]{2,1,0:T(8,128)(2,1)S(1)} %all-to-all-done.2.grads_ref, bf16[2,128,1024]{2,1,0:T(8,128)(2,1)S(1)} %pad_maximum_fusion.refs_0_, bf16[2,128,1024]{2,1,0:T(8,128)(2,1)S(1)} %pad_maximum_fusion.1.refs_1_, ...), custom_call_target="tpu_custom_call" | custom-call | flops 1100000000 | bytes 9437184 | tf_op jit(solution)/shard_map/pallas_call | solution.py:145
  139.4 8.9 %all-to-all-start.3 = ((bf16[64,16,128]{2,1,0:T(8,128)(2,1)}), bf16[64,16,128]{2,1,0:T(8,128)(2,1)S(1)}, u32[]{:S(2)}, u32[]{:S(2)}) async-start(bf16[64,16,128]{2,1,0:T(8,128)(2,1)} %bitcast.26), calls=%async_computation.3 | async-start | bytes 524288 | tf_op jit(solution)/shard_map/all_to_all | solution.py:293
  148.3 3.3 %collective-permute-start.23 = (bf16[128,256]{1,0:T(8,128)(2,1)}, bf16[128,256]{1,0:T(8,128)(2,1)S(1)}, u32[]{:S(2)}, u32[]{:S(2)}) collective-permute-start(bf16[128,256]{1,0:T(8,128)(2,1)} %get-tuple-element.121), channel_id=1, source_target_pairs={{0,6},{2,8},{4,10},{6,12},{8,14},{10,0},{12,2},{14,4},{1,7},{3,9},... | collective-permute-start | bytes 196616 | tf_op jit(solution)/shard_map/ppermute | solution.py:295
  151.6 2.4 %collective-permute-start.24 = (bf16[128,256]{1,0:T(8,128)(2,1)}, bf16[128,256]{1,0:T(8,128)(2,1)S(1)}, u32[]{:S(2)}, u32[]{:S(2)}) collective-permute-start(bf16[128,256]{1,0:T(8,128)(2,1)} %get-tuple-element.122), channel_id=1, source_target_pairs={{0,8},{2,10},{4,12},{6,14},{8,0},{10,2},{12,4},{14,6},{1,9},{3,11}... | collective-permute-start | bytes 196616 | tf_op jit(solution)/shard_map/ppermute | solution.py:295
  154.0 4.2 %collective-permute-start.25 = (bf16[128,256]{1,0:T(8,128)(2,1)S(1)}, bf16[128,256]{1,0:T(8,128)(2,1)S(1)}, u32[]{:S(2)}, u32[]{:S(2)}) collective-permute-start(bf16[128,256]{1,0:T(8,128)(2,1)S(1)} %get-tuple-element.123), channel_id=1, source_target_pairs={{0,10},{2,12},{4,14},{6,0},{8,2},{10,4},{12,6},{14,8},{1,11},{3,13... | collective-permute-start | bytes 196616 | tf_op jit(solution)/shard_map/ppermute | solution.py:295
  158.2 3.3 %collective-permute-done.23.refs_3_ = bf16[128,256]{1,0:T(8,128)(2,1)S(1)} collective-permute-done((bf16[128,256]{1,0:T(8,128)(2,1)}, bf16[128,256]{1,0:T(8,128)(2,1)S(1)}, u32[]{:S(2)}, u32[]{:S(2)}) %collective-permute-start.23) | collective-permute-done | bytes 65568 | tf_op jit(solution)/shard_map/ppermute | solution.py:295
  161.5 3.7 %collective-permute-done.24.refs_4_ = bf16[128,256]{1,0:T(8,128)(2,1)S(1)} collective-permute-done((bf16[128,256]{1,0:T(8,128)(2,1)}, bf16[128,256]{1,0:T(8,128)(2,1)S(1)}, u32[]{:S(2)}, u32[]{:S(2)}) %collective-permute-start.24) | collective-permute-done | bytes 65568 | tf_op jit(solution)/shard_map/ppermute | solution.py:295
  165.9 1.4 shard_map.114
  (73 shorter events, 12.9 us)
Async XLA Ops:
  4.8 48.1 %all-to-all-start = ((bf16[8,128,768]{2,1,0:T(8,128)(2,1)}), bf16[8,128,768]{2,1,0:T(8,128)(2,1)S(1)}, u32[]{:S(2)}, u32[]{:S(2)}) async-start(bf16[8,128,768]{2,1,0:T(8,128)(2,1)} %shard_map.110), calls=%async_computation | async-start | bytes 3145728 | tf_op jit(solution)/shard_map/all_to_all | solution.py:257
  13.8 8.4 %collective-permute-start.1 = (bf16[128,1024]{1,0:T(8,128)(2,1)S(1)}, bf16[128,1024]{1,0:T(8,128)(2,1)S(1)}, u32[]{:S(2)}, u32[]{:S(2)}) collective-permute-start(bf16[128,1024]{1,0:T(8,128)(2,1)S(1)} %get-tuple-element.74), channel_id=1, source_target_pairs={{0,128},{64,192},{128,0},{192,64},{1,129},{65,193},{129,1},{193,65... | collective-permute-start | bytes 786440 | tf_op jit(solution)/shard_map/ppermute | solution.py:249
  16.6 11.7 %collective-permute-start.2 = (bf16[128,1024]{1,0:T(8,128)(2,1)S(1)}, bf16[128,1024]{1,0:T(8,128)(2,1)S(1)}, u32[]{:S(2)}, u32[]{:S(2)}) collective-permute-start(bf16[128,1024]{1,0:T(8,128)(2,1)S(1)} %get-tuple-element.75), channel_id=1, source_target_pairs={{0,192},{64,0},{128,64},{192,128},{1,193},{65,1},{129,65},{193,129... | collective-permute-start | bytes 786440 | tf_op jit(solution)/shard_map/ppermute | solution.py:249
  17.4 13.8 %collective-permute-start = (bf16[128,1024]{1,0:T(8,128)(2,1)S(1)}, bf16[128,1024]{1,0:T(8,128)(2,1)S(1)}, u32[]{:S(2)}, u32[]{:S(2)}) collective-permute-start(bf16[128,1024]{1,0:T(8,128)(2,1)S(1)} %get-tuple-element.73), channel_id=1, source_target_pairs={{0,64},{64,128},{128,192},{192,0},{1,65},{65,129},{129,193},{193,1... | collective-permute-start | bytes 786440 | tf_op jit(solution)/shard_map/ppermute | solution.py:249
  28.3 27.9 %copy-start.20 = (s32[1,16,8]{1,2,0:T(8,128)S(1)}, s32[1,16,8]{1,2,0:T(8,128)}, u32[]{:S(2)}) copy-start(s32[1,16,8]{1,2,0:T(8,128)} %param.12) | copy-start | bytes 1540
  28.3 29.8 %copy-start.19 = (s32[1,2048]{1,0:T(1,128)S(1)}, s32[1,2048]{1,0:T(1,128)}, u32[]{:S(2)}) copy-start(s32[1,2048]{1,0:T(1,128)} %param.13) | copy-start | bytes 24580
  28.3 13.3 %collective-permute-start.4 = (bf16[2,128,1024]{2,1,0:T(8,128)(2,1)S(1)}, bf16[2,128,1024]{2,1,0:T(8,128)(2,1)S(1)}, u32[]{:S(2)}, u32[]{:S(2)}) collective-permute-start(bf16[2,128,1024]{2,1,0:T(8,128)(2,1)S(1)} %pad_maximum_fusion.1.refs_1_), channel_id=1, source_target_pairs={{0,16},{16,32},{32,48},{48,0},{1,17},{17,33},{33,49},{49,1},{2,18}... | collective-permute-start | bytes 1572872 | tf_op jit(solution)/shard_map/ppermute | solution.py:253
  29.7 11.9 %collective-permute-start.6 = (bf16[2,128,1024]{2,1,0:T(8,128)(2,1)S(1)}, bf16[2,128,1024]{2,1,0:T(8,128)(2,1)S(1)}, u32[]{:S(2)}, u32[]{:S(2)}) collective-permute-start(bf16[2,128,1024]{2,1,0:T(8,128)(2,1)S(1)} %pad_maximum_fusion.1.refs_1_), channel_id=1, source_target_pairs={{0,48},{16,0},{32,16},{48,32},{1,49},{17,1},{33,17},{49,33},{2,50}... | collective-permute-start | bytes 1572872 | tf_op jit(solution)/shard_map/ppermute | solution.py:253
  31.3 21.7 %collective-permute-start.3 = (bf16[2,128,1024]{2,1,0:T(8,128)(2,1)S(1)}, bf16[2,128,1024]{2,1,0:T(8,128)(2,1)}, u32[]{:S(2)}, u32[]{:S(2)}) collective-permute-start(bf16[2,128,1024]{2,1,0:T(8,128)(2,1)S(1)} %pad_maximum_fusion.refs_0_), channel_id=1, source_target_pairs={{0,16},{16,32},{32,48},{48,0},{1,17},{17,33},{33,49},{49,1},{2,18}... | collective-permute-start | bytes 1572872 | tf_op jit(solution)/shard_map/ppermute | solution.py:253
  31.4 21.6 %collective-permute-start.5 = (bf16[2,128,1024]{2,1,0:T(8,128)(2,1)S(1)}, bf16[2,128,1024]{2,1,0:T(8,128)(2,1)}, u32[]{:S(2)}, u32[]{:S(2)}) collective-permute-start(bf16[2,128,1024]{2,1,0:T(8,128)(2,1)S(1)} %pad_maximum_fusion.refs_0_), channel_id=1, source_target_pairs={{0,48},{16,0},{32,16},{48,32},{1,49},{17,1},{33,17},{49,33},{2,50}... | collective-permute-start | bytes 1572872 | tf_op jit(solution)/shard_map/ppermute | solution.py:253
  41.6 11.3 %copy-start = (bf16[2,128,1024]{2,1,0:T(8,128)(2,1)}, bf16[2,128,1024]{2,1,0:T(8,128)(2,1)S(1)}, u32[]{:S(2)}) copy-start(bf16[2,128,1024]{2,1,0:T(8,128)(2,1)S(1)} %collective-permute-done.6.refs_5_) | copy-start | bytes 1572868
  53.8 4.3 %collective-permute-start.7 = (bf16[8,128,256]{2,1,0:T(8,128)(2,1)}, bf16[8,128,256]{2,1,0:T(8,128)(2,1)}, u32[]{:S(2)}, u32[]{:S(2)}) collective-permute-start(bf16[8,128,256]{2,1,0:T(8,128)(2,1)} %slice.35), channel_id=1, source_target_pairs={{0,1},{1,0},{2,3},{3,2},{4,5},{5,4},{6,7},{7,6},{8,9},{9,8},{10,11... | collective-permute-start | bytes 1572872 | tf_op jit(solution)/shard_map/ppermute | solution.py:234
  71.1 0.8 copy-start.18
  71.9 13.6 %copy-start.1 = (bf16[2,128,1024]{2,1,0:T(8,128)(2,1)S(1)}, bf16[2,128,1024]{2,1,0:T(8,128)(2,1)}, u32[]{:S(2)}) copy-start(bf16[2,128,1024]{2,1,0:T(8,128)(2,1)} %copy-done) | copy-start | bytes 1572868
  71.9 3.8 %collective-permute-start.8 = (f32[8,128,256]{2,1,0:T(8,128)S(1)}, f32[8,128,256]{2,1,0:T(8,128)S(1)}, u32[]{:S(2)}, u32[]{:S(2)}) collective-permute-start(f32[8,128,256]{2,1,0:T(8,128)S(1)} %get-tuple-element.88), channel_id=1, source_target_pairs={{0,1},{1,0},{2,3},{3,2},{4,5},{5,4},{6,7},{7,6},{8,9},{9,8},{10,11... | collective-permute-start | bytes 3145736 | tf_op jit(solution)/shard_map/ppermute | solution.py:234
  73.4 12.1 %collective-permute-start.10 = (bf16[2,128,1024]{2,1,0:T(8,128)(2,1)S(1)}, bf16[2,128,1024]{2,1,0:T(8,128)(2,1)S(1)}, u32[]{:S(2)}, u32[]{:S(2)}) collective-permute-start(bf16[2,128,1024]{2,1,0:T(8,128)(2,1)S(1)} %pad_maximum_fusion.1.refs_1_), channel_id=1, source_target_pairs={{0,1},{1,0},{2,3},{3,2},{4,5},{5,4},{6,7},{7,6},{8,9},{9,8},{10,11... | collective-permute-start | bytes 1572872 | tf_op jit(solution)/shard_map/ppermute | solution.py:234
  73.4 12.2 %collective-permute-start.11 = (bf16[2,128,1024]{2,1,0:T(8,128)(2,1)}, bf16[2,128,1024]{2,1,0:T(8,128)(2,1)}, u32[]{:S(2)}, u32[]{:S(2)}) collective-permute-start(bf16[2,128,1024]{2,1,0:T(8,128)(2,1)} %collective-permute-done.3.refs_2_), channel_id=1, source_target_pairs={{0,1},{1,0},{2,3},{3,2},{4,5},{5,4},{6,7},{7,6},{8,9},{9,8},{10,11... | collective-permute-start | bytes 1572872 | tf_op jit(solution)/shard_map/ppermute | solution.py:234
  73.9 13.2 %collective-permute-start.12 = (bf16[2,128,1024]{2,1,0:T(8,128)(2,1)S(1)}, bf16[2,128,1024]{2,1,0:T(8,128)(2,1)}, u32[]{:S(2)}, u32[]{:S(2)}) collective-permute-start(bf16[2,128,1024]{2,1,0:T(8,128)(2,1)S(1)} %collective-permute-done.4.refs_3_), channel_id=1, source_target_pairs={{0,1},{1,0},{2,3},{3,2},{4,5},{5,4},{6,7},{7,6},{8,9},{9,8},{10,11... | collective-permute-start | bytes 1572872 | tf_op jit(solution)/shard_map/ppermute | solution.py:234
  76.6 24.6 %all-to-all-start.1 = ((bf16[8,128,256]{2,1,0:T(8,128)(2,1)}), bf16[8,128,256]{2,1,0:T(8,128)(2,1)S(1)}, u32[]{:S(2)}, u32[]{:S(2)}) async-start(bf16[8,128,256]{2,1,0:T(8,128)(2,1)} %add_convert_fusion), calls=%async_computation.1 | async-start | bytes 1048576 | tf_op jit(solution)/shard_map/all_to_all | solution.py:278
  83.3 14.3 %collective-permute-start.15 = (bf16[2,128,1024]{2,1,0:T(8,128)(2,1)}, bf16[2,128,1024]{2,1,0:T(8,128)(2,1)S(1)}, u32[]{:S(2)}, u32[]{:S(2)}) collective-permute-start(bf16[2,128,1024]{2,1,0:T(8,128)(2,1)} %collective-permute-done.3.refs_2_), channel_id=1, source_target_pairs={{0,16},{16,32},{32,48},{48,0},{1,17},{17,33},{33,49},{49,1},{2,18}... | collective-permute-start | bytes 1572872 | tf_op jit(solution)/shard_map/ppermute | solution.py:271
  84.6 3.2 %collective-permute-start.13 = (bf16[2,128,1024]{2,1,0:T(8,128)(2,1)}, bf16[2,128,1024]{2,1,0:T(8,128)(2,1)S(1)}, u32[]{:S(2)}, u32[]{:S(2)}) collective-permute-start(bf16[2,128,1024]{2,1,0:T(8,128)(2,1)} %collective-permute-done.5.refs_4_), channel_id=1, source_target_pairs={{0,1},{1,0},{2,3},{3,2},{4,5},{5,4},{6,7},{7,6},{8,9},{9,8},{10,11... | collective-permute-start | bytes 1572872 | tf_op jit(solution)/shard_map/ppermute | solution.py:234
  85.5 16.9 %copy-start.2 = (bf16[2,128,1024]{2,1,0:T(8,128)(2,1)}, bf16[2,128,1024]{2,1,0:T(8,128)(2,1)S(1)}, u32[]{:S(2)}) copy-start(bf16[2,128,1024]{2,1,0:T(8,128)(2,1)S(1)} %collective-permute-done.10.refs_9_) | copy-start | bytes 1572868
  85.5 3.0 %collective-permute-start.14 = (bf16[2,128,1024]{2,1,0:T(8,128)(2,1)S(1)}, bf16[2,128,1024]{2,1,0:T(8,128)(2,1)S(1)}, u32[]{:S(2)}, u32[]{:S(2)}) collective-permute-start(bf16[2,128,1024]{2,1,0:T(8,128)(2,1)S(1)} %copy-done.1), channel_id=1, source_target_pairs={{0,1},{1,0},{2,3},{3,2},{4,5},{5,4},{6,7},{7,6},{8,9},{9,8},{10,11... | collective-permute-start | bytes 1572872 | tf_op jit(solution)/shard_map/ppermute | solution.py:234
  85.6 13.2 %collective-permute-start.16 = (bf16[2,128,1024]{2,1,0:T(8,128)(2,1)S(1)}, bf16[2,128,1024]{2,1,0:T(8,128)(2,1)S(1)}, u32[]{:S(2)}, u32[]{:S(2)}) collective-permute-start(bf16[2,128,1024]{2,1,0:T(8,128)(2,1)S(1)} %copy-done.1), channel_id=1, source_target_pairs={{0,48},{16,0},{32,16},{48,32},{1,49},{17,1},{33,17},{49,33},{2,50}... | collective-permute-start | bytes 1572872 | tf_op jit(solution)/shard_map/ppermute | solution.py:272
  87.1 12.5 %collective-permute-start.9 = (bf16[2,128,1024]{2,1,0:T(8,128)(2,1)S(1)}, bf16[2,128,1024]{2,1,0:T(8,128)(2,1)S(1)}, u32[]{:S(2)}, u32[]{:S(2)}) collective-permute-start(bf16[2,128,1024]{2,1,0:T(8,128)(2,1)S(1)} %pad_maximum_fusion.refs_0_), channel_id=1, source_target_pairs={{0,1},{1,0},{2,3},{3,2},{4,5},{5,4},{6,7},{7,6},{8,9},{9,8},{10,11... | collective-permute-start | bytes 1572872 | tf_op jit(solution)/shard_map/ppermute | solution.py:234
  88.6 0.8 copy-start.8
  97.6 1.2 copy-start.4
  98.8 0.8 copy-start.10
  99.6 0.8 copy-start.12
  102.4 25.0 %all-to-all-start.2 = ((bf16[32,128,128]{2,1,0:T(8,128)(2,1)}), bf16[32,128,128]{2,1,0:T(8,128)(2,1)S(1)}, u32[]{:S(2)}, u32[]{:S(2)}) async-start(bf16[32,128,128]{2,1,0:T(8,128)(2,1)} %get-tuple-element.96), calls=%async_computation.2 | async-start | bytes 2097152 | tf_op jit(solution)/shard_map/all_to_all | solution.py:283
  110.5 13.2 %collective-permute-start.21 = (bf16[2,128,1024]{2,1,0:T(8,128)(2,1)}, bf16[2,128,1024]{2,1,0:T(8,128)(2,1)S(1)}, u32[]{:S(2)}, u32[]{:S(2)}) collective-permute-start(bf16[2,128,1024]{2,1,0:T(8,128)(2,1)} %copy-done.4), channel_id=1, source_target_pairs={{0,1},{1,0},{2,3},{3,2},{4,5},{5,4},{6,7},{7,6},{8,9},{9,8},{10,11... | collective-permute-start | bytes 1572872 | tf_op jit(solution)/shard_map/ppermute | solution.py:234
  110.8 13.7 %collective-permute-start.22 = (bf16[2,128,1024]{2,1,0:T(8,128)(2,1)}, bf16[2,128,1024]{2,1,0:T(8,128)(2,1)S(1)}, u32[]{:S(2)}, u32[]{:S(2)}) collective-permute-start(bf16[2,128,1024]{2,1,0:T(8,128)(2,1)} %copy-done.10), channel_id=1, source_target_pairs={{0,1},{1,0},{2,3},{3,2},{4,5},{5,4},{6,7},{7,6},{8,9},{9,8},{10,11... | collective-permute-start | bytes 1572872 | tf_op jit(solution)/shard_map/ppermute | solution.py:234
  112.9 5.1 %collective-permute-start.17 = (bf16[128,256]{1,0:T(8,128)(2,1)S(1)}, bf16[128,256]{1,0:T(8,128)(2,1)S(1)}, u32[]{:S(2)}, u32[]{:S(2)}) collective-permute-start(bf16[128,256]{1,0:T(8,128)(2,1)S(1)} %get-tuple-element.147), channel_id=1, source_target_pairs={{0,2},{2,4},{4,6},{6,8},{8,10},{10,12},{12,14},{14,0},{1,3},{3,5},... | collective-permute-start | bytes 196616 | tf_op jit(solution)/shard_map/ppermute | solution.py:287
  114.4 6.5 %collective-permute-start.18 = (bf16[128,256]{1,0:T(8,128)(2,1)S(1)}, bf16[128,256]{1,0:T(8,128)(2,1)S(1)}, u32[]{:S(2)}, u32[]{:S(2)}) collective-permute-start(bf16[128,256]{1,0:T(8,128)(2,1)S(1)} %get-tuple-element.146), channel_id=1, source_target_pairs={{0,4},{2,6},{4,8},{6,10},{8,12},{10,14},{12,0},{14,2},{1,5},{3,7},... | collective-permute-start | bytes 196616 | tf_op jit(solution)/shard_map/ppermute | solution.py:287
  116.5 4.4 %collective-permute-start.19 = (bf16[128,256]{1,0:T(8,128)(2,1)S(1)}, bf16[128,256]{1,0:T(8,128)(2,1)S(1)}, u32[]{:S(2)}, u32[]{:S(2)}) collective-permute-start(bf16[128,256]{1,0:T(8,128)(2,1)S(1)} %get-tuple-element.142), channel_id=1, source_target_pairs={{0,12},{2,14},{4,0},{6,2},{8,4},{10,6},{12,8},{14,10},{1,13},{3,15... | collective-permute-start | bytes 196616 | tf_op jit(solution)/shard_map/ppermute | solution.py:287
  118.0 5.7 %collective-permute-start.20 = (bf16[128,256]{1,0:T(8,128)(2,1)S(1)}, bf16[128,256]{1,0:T(8,128)(2,1)S(1)}, u32[]{:S(2)}, u32[]{:S(2)}) collective-permute-start(bf16[128,256]{1,0:T(8,128)(2,1)S(1)} %get-tuple-element.141), channel_id=1, source_target_pairs={{0,14},{2,0},{4,2},{6,4},{8,6},{10,8},{12,10},{14,12},{1,15},{3,1}... | collective-permute-start | bytes 196616 | tf_op jit(solution)/shard_map/ppermute | solution.py:287
  127.4 1.0 copy-start.3
  128.5 1.0 copy-start.5
  129.5 1.0 copy-start.7
  130.6 1.0 copy-start.9
  131.6 1.0 copy-start.11
  132.6 1.0 copy-start.13
  133.7 1.0 copy-start.15
  134.7 1.0 copy-start.17
  139.4 25.8 %all-to-all-start.3 = ((bf16[64,16,128]{2,1,0:T(8,128)(2,1)}), bf16[64,16,128]{2,1,0:T(8,128)(2,1)S(1)}, u32[]{:S(2)}, u32[]{:S(2)}) async-start(bf16[64,16,128]{2,1,0:T(8,128)(2,1)} %bitcast.26), calls=%async_computation.3 | async-start | bytes 524288 | tf_op jit(solution)/shard_map/all_to_all | solution.py:293
  148.3 13.2 %collective-permute-start.23 = (bf16[128,256]{1,0:T(8,128)(2,1)}, bf16[128,256]{1,0:T(8,128)(2,1)S(1)}, u32[]{:S(2)}, u32[]{:S(2)}) collective-permute-start(bf16[128,256]{1,0:T(8,128)(2,1)} %get-tuple-element.121), channel_id=1, source_target_pairs={{0,6},{2,8},{4,10},{6,12},{8,14},{10,0},{12,2},{14,4},{1,7},{3,9},... | collective-permute-start | bytes 196616 | tf_op jit(solution)/shard_map/ppermute | solution.py:295
  151.6 13.6 %collective-permute-start.24 = (bf16[128,256]{1,0:T(8,128)(2,1)}, bf16[128,256]{1,0:T(8,128)(2,1)S(1)}, u32[]{:S(2)}, u32[]{:S(2)}) collective-permute-start(bf16[128,256]{1,0:T(8,128)(2,1)} %get-tuple-element.122), channel_id=1, source_target_pairs={{0,8},{2,10},{4,12},{6,14},{8,0},{10,2},{12,4},{14,6},{1,9},{3,11}... | collective-permute-start | bytes 196616 | tf_op jit(solution)/shard_map/ppermute | solution.py:295
  154.0 11.2 %collective-permute-start.25 = (bf16[128,256]{1,0:T(8,128)(2,1)S(1)}, bf16[128,256]{1,0:T(8,128)(2,1)S(1)}, u32[]{:S(2)}, u32[]{:S(2)}) collective-permute-start(bf16[128,256]{1,0:T(8,128)(2,1)S(1)} %get-tuple-element.123), channel_id=1, source_target_pairs={{0,10},{2,12},{4,14},{6,0},{8,2},{10,4},{12,6},{14,8},{1,11},{3,13... | collective-permute-start | bytes 196616 | tf_op jit(solution)/shard_map/ppermute | solution.py:295
  (3 other events, 2.4 us)

commit v4 on v3

--- a/solution.py
+++ b/solution.py
@@ -29,10 +29,17 @@
     )
 
 
+def dot_nt(a, b):
+    return lax.dot_general(
+        a, b, (((1,), (1,)), ((), ())), preferred_element_type=jnp.float32
+    )
+
+
 def attention_kernel(
-    links_ref, place_ref, rows_ref, other_ref, seg_cols_ref, seg_rows_ref,
-    dq_ref, own_ref, away_ref, pair_ref, keys_t_ref, total_ref, near_ref, near_t_ref,
+    links_ref, place_ref, rows_ref, other_ref, seg_cols_ref, seg_rows_ref, *refs
 ):
+    dq_refs, refs = refs[:NZ], refs[NZ:]
+    own_ref, away_ref, pair_ref, keys_t_ref, total_ref, near_ref, near_t_ref, dq_ref = refs
     z, core = place_ref[1], place_ref[2]
 
     def at(block):
@@ -51,15 +58,14 @@
         rows = rows_ref[i]
         queries = jnp.concatenate([rows[:, :HEAD], rows[:, HEAD : 2 * HEAD]], axis=0)
         grads = jnp.concatenate([rows[:, 2 * HEAD : 3 * HEAD], rows[:, 3 * HEAD : 4 * HEAD]], axis=0)
-        queries_t, grads_t = queries.T, grads.T
         seg = seg_rows_ref[pl.ds(2 * i + core, 1), :]
         allowed = jnp.concatenate([seg_cols_ref[j] == seg for j in key_blocks], axis=0)
-        scores = dot(pairs[:, :HEAD], queries_t) * (SCALE * LOG2E)
+        scores = dot_nt(pairs[:, :HEAD], queries) * (SCALE * LOG2E)
         scores = jnp.where(jnp.concatenate([allowed, allowed], axis=1), scores, MASKED)
         weights = jnp.exp2(scores - jnp.max(scores, axis=0, keepdims=True))
         probs = weights * (1.0 / jnp.sum(weights, axis=0, keepdims=True))
         attention = probs.astype(jnp.bfloat16)
-        prob_grads = dot(pairs[:, HEAD:], grads_t)
+        prob_grads = dot_nt(pairs[:, HEAD:], grads)
         delta = jnp.sum(attention.astype(jnp.float32) * prob_grads, axis=0, keepdims=True)
         score_grads = (probs * (prob_grads - delta)).astype(jnp.bfloat16)
         value_part = dot(attention, grads)
@@ -68,10 +74,10 @@
             here = slice(t * BLOCK, (t + 1) * BLOCK)
             total_ref[at(j), :HEAD] += key_part[here]
             total_ref[at(j), HEAD:] += value_part[here]
-        dq = (dot(keys_t, score_grads) * SCALE).T
+        dq = (dot(keys_t, score_grads) * SCALE).astype(jnp.bfloat16).T
         slot = lax.rem(i - z + NZ, NZ)
-        dq_ref[slot, :, :HEAD] = dq[:BLOCK].astype(jnp.bfloat16)
-        dq_ref[slot, :, HEAD:] = dq[BLOCK:].astype(jnp.bfloat16)
+        dq_ref[slot, :, :HEAD] = dq[:BLOCK]
+        dq_ref[slot, :, HEAD:] = dq[BLOCK:]
 
     def linked(i, carry):
         key_blocks = [links_ref[2 * i + core, t] for t in range(LINKS)]
@@ -95,6 +101,8 @@
         return carry
 
     lax.fori_loop(0, NZ, store, 0)
+    for s, ref in enumerate(dq_refs):
+        ref[...] = dq_ref[s]
 
 
 def attention_grads(links, place, rows, other, seg_cols, seg_rows):
@@ -102,19 +110,20 @@
     smem = pl.BlockSpec(memory_space=pltpu.SMEM)
     return pl.pallas_call(
         attention_kernel,
-        out_shape=(
-            jax.ShapeDtypeStruct((NZ, BLOCK, 2 * HEAD), jnp.bfloat16),
+        out_shape=(jax.ShapeDtypeStruct((BLOCK, 2 * HEAD), jnp.bfloat16),) * NZ
+        + (
             jax.ShapeDtypeStruct((NZ, BLOCK, 2 * HEAD), jnp.float32),
             jax.ShapeDtypeStruct((NZ, BLOCK, 2 * HEAD), jnp.float32),
         ),
         in_specs=[smem, smem, vmem, vmem, vmem, vmem],
-        out_specs=(vmem, vmem, vmem),
+        out_specs=(vmem,) * (NZ + 2),
         scratch_shapes=[
             pltpu.VMEM((BLOCKS * BLOCK, 2 * HEAD), jnp.bfloat16),
             pltpu.VMEM((HEAD, BLOCKS * BLOCK), jnp.bfloat16),
             pltpu.VMEM((BLOCKS * BLOCK, 2 * HEAD), jnp.float32),
             pltpu.VMEM((LINKS * BLOCK, 2 * HEAD), jnp.bfloat16),
             pltpu.VMEM((HEAD, LINKS * BLOCK), jnp.bfloat16),
+            pltpu.VMEM((NZ, BLOCK, 2 * HEAD), jnp.bfloat16),
         ],
         compiler_params=pltpu.CompilerParams(vmem_limit_bytes=32 * MIB),
         cost_estimate=pl.CostEstimate(
@@ -127,31 +136,46 @@
 
 
 def weight_kernel(place_ref, grads_ref, *refs):
-    out_ref = refs[-1]
+    count = len(PARTS)
+    out_ref, held_ref, sems = refs[2 * count :]
+    copies = []
+    for p in range(count):
+        for side in range(NC):
+            target = held_ref.at[p, :, pl.ds(side * BLOCK, BLOCK), :]
+            copies.append(pltpu.make_async_copy(refs[side * count + p], target, sems.at[p, side]))
+    for copy in copies:
+        copy.start()
     x, y, core = place_ref[0], place_ref[3], place_ref[2]
     total = None
     for p, (shift, first) in enumerate(PARTS):
+        copies[2 * p].wait()
+        copies[2 * p + 1].wait()
         for s in range(NX // 2):
             source = (lax.rem(x - first - s + NX, NX) * NY + lax.rem(y + shift + NY, NY)) * NC
             grads = jnp.concatenate([grads_ref[source + core], grads_ref[source + 1 - core]], axis=0)
-            inputs = jnp.concatenate([refs[p][s], refs[len(PARTS) + p][s]], axis=0)
-            part = dot(grads.T, inputs)
+            part = dot(grads.T, held_ref[p, s])
             total = part if total is None else total + part
     out_ref[...] = total.T.astype(jnp.bfloat16)
 
 
 def weight_grads_part(place, grads, own, other):
+    half, rows, width = own[0].shape
     vmem = pl.BlockSpec(memory_space=pltpu.VMEM)
     return pl.pallas_call(
         weight_kernel,
-        out_shape=jax.ShapeDtypeStruct((own[0].shape[-1], HEAD), jnp.bfloat16),
-        in_specs=[pl.BlockSpec(memory_space=pltpu.SMEM)] + [vmem] * (1 + 2 * len(PARTS)),
+        out_shape=jax.ShapeDtypeStruct((width, HEAD), jnp.bfloat16),
+        in_specs=[pl.BlockSpec(memory_space=pltpu.SMEM), vmem]
+        + [pl.BlockSpec(memory_space=pltpu.HBM)] * (2 * len(PARTS)),
         out_specs=vmem,
-        compiler_params=pltpu.CompilerParams(vmem_limit_bytes=16 * MIB),
+        scratch_shapes=[
+            pltpu.VMEM((len(PARTS), half, NC * rows, width), jnp.bfloat16),
+            pltpu.SemaphoreType.DMA((len(PARTS), NC)),
+        ],
+        compiler_params=pltpu.CompilerParams(vmem_limit_bytes=24 * MIB),
         cost_estimate=pl.CostEstimate(
             flops=1_100_000_000, bytes_accessed=9 * MIB, transcendentals=0
         ),
-    )(place, grads, *placed(own, pltpu.VMEM), *placed(other, pltpu.VMEM))
+    )(place, grads, *placed(own, pltpu.HBM), *placed(other, pltpu.HBM))
 
 
 def pack_kernel(queries_ref, grads_ref, keys_ref, values_ref, out_ref, sem):
@@ -255,14 +279,13 @@
 
     outgoing = packed(queries[0], output_grads[0], keys[0], values[0])
     rows = lax.all_to_all(outgoing, "z", split_axis=0, concat_axis=0, tiled=True)
-    rows, mine, before, after = lax.optimization_barrier((rows, mine, before, after))
-    other = swap_cores(rows[..., 4 * HEAD :])
-
     seg_rows = segment_ids[0].reshape(BLOCKS, BLOCK)
     seg_cols = jnp.broadcast_to(seg_rows[:, :, None], (BLOCKS, BLOCK, BLOCK))
-    dq, own, away = attention_grads(
-        block_links[0], place, rows, other, seg_cols, seg_rows
-    )
+    rows, mine, before, after, seg_cols = lax.optimization_barrier(
+        (rows, mine, before, after, seg_cols)
+    )
+    other = swap_cores(rows[..., 4 * HEAD :])
+    *dq, own, away = attention_grads(block_links[0], place, rows, other, seg_cols, seg_rows)
 
     dq, own, away, mine, before, after = lax.optimization_barrier(
         (dq, own, away, mine, before, after)
@@ -276,25 +299,21 @@
 
     pair = (own + swap_cores(away)).astype(bf16)
     pair = lax.all_to_all(pair, "z", split_axis=0, concat_axis=0, tiled=True)
+    for s in (1, 7):
+        dq[s] = lax.ppermute(dq[s], "z", ring(NZ, s))
     dq, pair, inputs_other, far = lax.optimization_barrier((dq, pair, inputs_other, far))
     far_other = tuple(swap_cores(a) for a in far)
     key_grads, value_grads, chunks = pair_grads(pair)
 
     grads = lax.all_to_all(chunks, ("x", "y", "c"), split_axis=0, concat_axis=0, tiled=True)
-    early, late = (1, 7, 2, 6), (3, 5, 4)
-    dq = [dq[s] for s in range(NZ)]
-    for s in early:
+    for s in (4, 3, 5, 2, 6):
         dq[s] = lax.ppermute(dq[s], "z", ring(NZ, s))
     grads, dq, far_other = lax.optimization_barrier((grads, dq, far_other))
     part = weight_grads_part(place, grads, inputs_own + far, inputs_other + far_other)
 
-    part, dq = lax.optimization_barrier((part, dq))
+    query_grads = joined(place, dq)
     part = part.reshape(NY * NZ * NC, -1, HEAD)
     part = lax.all_to_all(part, ("y", "z", "c"), split_axis=0, concat_axis=0, tiled=True)
-    for s in late:
-        dq[s] = lax.ppermute(dq[s], "z", ring(NZ, s))
-    part, dq = lax.optimization_barrier((part, dq))
-    query_grads = joined(place, dq)
     part = part.reshape(NY, NZ, NC, -1, HEAD).astype(jnp.float32)
     part = jnp.transpose(jnp.sum(part, axis=1), (1, 2, 0, 3))
     part = part.reshape(NC, -1, NY * HEAD)

time: 169 us -> 175 us (1.036)
  waiting for transfers between devices: 56.6 us -> 69.9 us
  local copies, waits for them, and re-layouts: 18.8 us -> 6.66 us
  starting transfers between devices: 68.2 us -> 71.8 us
    all_to_all x1, waiting for transfers between devices: 0.01 us -> 10.6 us  [local(): lax.all_to_all(part, ('y', 'z', 'c'), split_axis=0, concat_axis=0, tiled=...]
    unnamed x42 -> x38, local copies, waits for them, and re-layouts: 13.9 us -> 3.5 us
    ppermute x7, waiting for transfers between devices: 11.6 us -> 15.9 us  [local(): dq[s] = lax.ppermute(dq[s], 'z', ring(NZ, s))]
    ppermute x7, starting transfers between devices: 16.1 us -> 18.8 us  [local(): dq[s] = lax.ppermute(dq[s], 'z', ring(NZ, s))]
    all_to_all x1, waiting for transfers between devices: 2.14 us -> 0.01 us  [local(): lax.all_to_all(chunks, ('x', 'y', 'c'), split_axis=0, concat_axis=0, tile...]
    ppermute x1, waiting for transfers between devices: 1.18 us -> 3.28 us  [local(): lax.ppermute(after[1], 'y', ring(NY, -1))]
  transfers between devices with their start and end apart: 30 -> 30, of which waited for: 14 -> 12; matrix products, arithmetic and copies ran while one was open for 2% -> 2% of each run, Pallas kernels for 0% -> 1%
where the time goes in v4:
time: 175 us
  starting transfers between devices  71.8 us (41%)
  waiting for transfers between devices  69.9 us (40%)
  Pallas kernels  22.8 us (13%)
  local copies, waits for them, and re-layouts  6.66 us (4%)
  other arithmetic  2.72 us (2%)
    ppermute x7, starting transfers between devices, local(): dq[s] = lax.ppermute(dq[s], 'z', ring(NZ, s))  18.8 us
    ppermute x4, waiting for transfers between devices, local(): lax.ppermute(a, 'y', ring(NY, shift))  18.5 us
    ppermute x7, waiting for transfers between devices, local(): dq[s] = lax.ppermute(dq[s], 'z', ring(NZ, s))  15.9 us
    pallas_call x1, Pallas kernels, attention_grads(): pl.pallas_call(attention_kernel, out_shape=(jax.ShapeDtypeStruct((BLOCK,...  12.2 us
    all_to_all x1, waiting for transfers between devices, local(): lax.all_to_all(part, ('y', 'z', 'c'), split_axis=0, concat_axis=0, tiled=...  10.6 us
    ppermute x3, waiting for transfers between devices, local(): lax.ppermute(a, 'x', ring(NX, s))  10.2 us
    all_to_all x1, starting transfers between devices, local(): lax.all_to_all(outgoing, 'z', split_axis=0, concat_axis=0, tiled=True)  9.03 us
    all_to_all x1, starting transfers between devices, local(): lax.all_to_all(chunks, ('x', 'y', 'c'), split_axis=0, concat_axis=0, tile...  8.76 us
  transfers between devices with their start and end apart: 30, of which 12 were waited for; matrix products, arithmetic and copies ran while one was open for 2% of the time, Pallas kernels for 1%

profile of v4, /device:TPU:1, one launch (start us, length us, event | category | flops | bytes accessed | tf_op | source)
XLA Modules:
  0.0 174.6 jit_solution(9155692791709689305)
XLA Ops:
  0.7 1.3 dynamic-slice_bitcast_fusion
  1.9 2.9 %shard_map.110 = bf16[8,128,768]{2,1,0:T(8,128)(2,1)} custom-call(bf16[128,2048]{1,0:T(8,128)(2,1)} %bitcast.42, bf16[128,2048]{1,0:T(8,128)(2,1)} %bitcast.43, bf16[128,512]{1,0:T(8,128)(2,1)} %bitcast.48, bf16[128,512]{1,0:T(8,128)(2,1)} %bitcast.49), custom_call_target="tpu_custom_call" | custom-call | bytes 3145728 | tf_op jit(solution)/shard_map/pallas_call | solution.py:198
  4.8 9.0 %all-to-all-start = ((bf16[8,128,768]{2,1,0:T(8,128)(2,1)}), bf16[8,128,768]{2,1,0:T(8,128)(2,1)S(1)}, u32[]{:S(2)}, u32[]{:S(2)}) async-start(bf16[8,128,768]{2,1,0:T(8,128)(2,1)} %shard_map.110), calls=%async_computation | async-start | bytes 3145728 | tf_op jit(solution)/shard_map/all_to_all | solution.py:281
  13.8 2.8 %collective-permute-start.1 = (bf16[128,1024]{1,0:T(8,128)(2,1)S(1)}, bf16[128,1024]{1,0:T(8,128)(2,1)S(1)}, u32[]{:S(2)}, u32[]{:S(2)}) collective-permute-start(bf16[128,1024]{1,0:T(8,128)(2,1)S(1)} %get-tuple-element.78), channel_id=1, source_target_pairs={{0,128},{64,192},{128,0},{192,64},{1,129},{65,193},{129,1},{193,65... | collective-permute-start | bytes 786440 | tf_op jit(solution)/shard_map/ppermute | solution.py:273
  16.7 0.9 collective-permute-start.2
  17.5 0.6 collective-permute-start
  18.1 4.1 %collective-permute-done.1 = bf16[128,1024]{1,0:T(8,128)(2,1)S(1)} collective-permute-done((bf16[128,1024]{1,0:T(8,128)(2,1)S(1)}, bf16[128,1024]{1,0:T(8,128)(2,1)S(1)}, u32[]{:S(2)}, u32[]{:S(2)}) %collective-permute-start.1) | collective-permute-done | bytes 262176 | tf_op jit(solution)/shard_map/ppermute | solution.py:273
  22.3 6.1 %collective-permute-done.2 = bf16[128,1024]{1,0:T(8,128)(2,1)S(1)} collective-permute-done((bf16[128,1024]{1,0:T(8,128)(2,1)S(1)}, bf16[128,1024]{1,0:T(8,128)(2,1)S(1)}, u32[]{:S(2)}, u32[]{:S(2)}) %collective-permute-start.2) | collective-permute-done | bytes 262176 | tf_op jit(solution)/shard_map/ppermute | solution.py:273
  28.3 0.8 pad_maximum_fusion.1.refs_1_
  29.2 1.3 collective-permute-start.4
  30.5 1.4 collective-permute-start.6
  31.9 0.8 pad_maximum_fusion.refs_0_
  32.8 2.7 %collective-permute-start.5 = (bf16[2,128,1024]{2,1,0:T(8,128)(2,1)}, bf16[2,128,1024]{2,1,0:T(8,128)(2,1)}, u32[]{:S(2)}, u32[]{:S(2)}) collective-permute-start(bf16[2,128,1024]{2,1,0:T(8,128)(2,1)} %pad_maximum_fusion.refs_0_), channel_id=1, source_target_pairs={{0,48},{16,0},{32,16},{48,32},{1,49},{17,1},{33,17},{49,33},{2,50}... | collective-permute-start | bytes 1572872 | tf_op jit(solution)/shard_map/ppermute | solution.py:277
  35.4 7.1 %collective-permute-done.4.refs_3_ = bf16[2,128,1024]{2,1,0:T(8,128)(2,1)S(1)} collective-permute-done((bf16[2,128,1024]{2,1,0:T(8,128)(2,1)}, bf16[2,128,1024]{2,1,0:T(8,128)(2,1)S(1)}, u32[]{:S(2)}, u32[]{:S(2)}) %collective-permute-start.4) | collective-permute-done | bytes 524320 | tf_op jit(solution)/shard_map/ppermute | solution.py:277
  42.6 11.3 %collective-permute-done.3.refs_2_ = bf16[2,128,1024]{2,1,0:T(8,128)(2,1)} collective-permute-done((bf16[2,128,1024]{2,1,0:T(8,128)(2,1)}, bf16[2,128,1024]{2,1,0:T(8,128)(2,1)}, u32[]{:S(2)}, u32[]{:S(2)}) %collective-permute-start.3) | collective-permute-done | bytes 524320 | tf_op jit(solution)/shard_map/ppermute | solution.py:277
  54.3 0.8 slice.11
  55.1 2.4 %collective-permute-start.7 = (bf16[8,128,256]{2,1,0:T(8,128)(2,1)}, bf16[8,128,256]{2,1,0:T(8,128)(2,1)S(1)}, u32[]{:S(2)}, u32[]{:S(2)}) collective-permute-start(bf16[8,128,256]{2,1,0:T(8,128)(2,1)} %slice.11), channel_id=1, source_target_pairs={{0,1},{1,0},{2,3},{3,2},{4,5},{5,4},{6,7},{7,6},{8,9},{9,8},{10,11... | collective-permute-start | bytes 1572872 | tf_op jit(solution)/shard_map/ppermute | solution.py:258
  57.7 1.6 collective-permute-done.7.other_ref
  59.3 12.2 %shard_map.111 = (bf16[128,256]{1,0:T(8,128)(2,1)S(1)}, bf16[128,256]{1,0:T(8,128)(2,1)S(1)}, bf16[128,256]{1,0:T(8,128)(2,1)S(1)}, bf16[128,256]{1,0:T(8,128)(2...) custom-call(s32[16,8]{1,0:T(8,128)S(1)} %copy.14.links_ref, ...), custom_call_target="tpu_custom_call" | custom-call | flops 4000000000 | bytes 8388608 | tf_op jit(solution)/shard_map/pallas_call | solution.py:111
  72.1 0.6 copy-done.3
  72.7 0.6 copy-done.5
  73.4 1.6 collective-permute-start.10
  75.6 2.2 %collective-permute-done.10 = f32[8,128,256]{2,1,0:T(8,128)S(1)} collective-permute-done((f32[8,128,256]{2,1,0:T(8,128)S(1)}, f32[8,128,256]{2,1,0:T(8,128)S(1)}, u32[]{:S(2)}, u32[]{:S(2)}) %collective-permute-start.10) | collective-permute-done | bytes 1048608 | tf_op jit(solution)/shard_map/ppermute | solution.py:258
  77.8 0.9 add_convert_fusion
  78.7 6.6 %all-to-all-start.1 = ((bf16[8,128,256]{2,1,0:T(8,128)(2,1)}), bf16[8,128,256]{2,1,0:T(8,128)(2,1)S(1)}, u32[]{:S(2)}, u32[]{:S(2)}) async-start(bf16[8,128,256]{2,1,0:T(8,128)(2,1)} %add_convert_fusion), calls=%async_computation.1 | async-start | bytes 1048576 | tf_op jit(solution)/shard_map/all_to_all | solution.py:301
  85.3 1.5 collective-permute-start.8
  86.8 1.3 collective-permute-start.9
  88.1 10.7 %collective-permute-done.8.refs_1_ = bf16[128,256]{1,0:T(8,128)(2,1)S(1)} collective-permute-done((bf16[128,256]{1,0:T(8,128)(2,1)S(1)}, bf16[128,256]{1,0:T(8,128)(2,1)S(1)}, u32[]{:S(2)}, u32[]{:S(2)}) %collective-permute-start.8) | collective-permute-done | bytes 65568 | tf_op jit(solution)/shard_map/ppermute | solution.py:303
  98.9 1.3 collective-permute-start.17
  100.2 1.9 %collective-permute-start.14 = (bf16[2,128,1024]{2,1,0:T(8,128)(2,1)S(1)}, bf16[2,128,1024]{2,1,0:T(8,128)(2,1)S(1)}, u32[]{:S(2)}, u32[]{:S(2)}) collective-permute-start(bf16[2,128,1024]{2,1,0:T(8,128)(2,1)S(1)} %copy-done.8), channel_id=1, source_target_pairs={{0,1},{1,0},{2,3},{3,2},{4,5},{5,4},{6,7},{7,6},{8,9},{9,8},{10,11... | collective-permute-start | bytes 1572872 | tf_op jit(solution)/shard_map/ppermute | solution.py:258
  102.6 1.8 %collective-permute-start.18 = (bf16[2,128,1024]{2,1,0:T(8,128)(2,1)S(1)}, bf16[2,128,1024]{2,1,0:T(8,128)(2,1)}, u32[]{:S(2)}, u32[]{:S(2)}) collective-permute-start(bf16[2,128,1024]{2,1,0:T(8,128)(2,1)S(1)} %copy-done.10), channel_id=1, source_target_pairs={{0,48},{16,0},{32,16},{48,32},{1,49},{17,1},{33,17},{49,33},{2,50}... | collective-permute-start | bytes 1572872 | tf_op jit(solution)/shard_map/ppermute | solution.py:295
  104.4 0.9 collective-permute-done.15.refs_12_
  105.3 6.8 %collective-permute-done.17.refs_6_ = bf16[2,128,1024]{2,1,0:T(8,128)(2,1)S(1)} collective-permute-done((bf16[2,128,1024]{2,1,0:T(8,128)(2,1)}, bf16[2,128,1024]{2,1,0:T(8,128)(2,1)S(1)}, u32[]{:S(2)}, u32[]{:S(2)}) %collective-permute-start.17) | collective-permute-done | bytes 524320 | tf_op jit(solution)/shard_map/ppermute | solution.py:294
  112.1 0.8 copy-done.12
  112.9 3.3 %collective-permute-done.18.refs_7_ = bf16[2,128,1024]{2,1,0:T(8,128)(2,1)} collective-permute-done((bf16[2,128,1024]{2,1,0:T(8,128)(2,1)S(1)}, bf16[2,128,1024]{2,1,0:T(8,128)(2,1)}, u32[]{:S(2)}, u32[]{:S(2)}) %collective-permute-start.18) | collective-permute-done | bytes 524320 | tf_op jit(solution)/shard_map/ppermute | solution.py:295
  116.2 1.2 shard_map.112
  117.4 8.8 %all-to-all-start.2 = ((bf16[32,128,128]{2,1,0:T(8,128)(2,1)}), bf16[32,128,128]{2,1,0:T(8,128)(2,1)S(1)}, u32[]{:S(2)}, u32[]{:S(2)}) async-start(bf16[32,128,128]{2,1,0:T(8,128)(2,1)} %get-tuple-element.115), calls=%async_computation.2 | async-start | bytes 2097152 | tf_op jit(solution)/shard_map/all_to_all | solution.py:308
  126.7 1.1 collective-permute-start.19
  127.9 4.5 %collective-permute-start.20 = (bf16[128,256]{1,0:T(8,128)(2,1)S(1)}, bf16[128,256]{1,0:T(8,128)(2,1)S(1)}, u32[]{:S(2)}, u32[]{:S(2)}) collective-permute-start(bf16[128,256]{1,0:T(8,128)(2,1)S(1)} %get-tuple-element.119), channel_id=1, source_target_pairs={{0,6},{2,8},{4,10},{6,12},{8,14},{10,0},{12,2},{14,4},{1,7},{3,9},... | collective-permute-start | bytes 196616 | tf_op jit(solution)/shard_map/ppermute | solution.py:310
  132.4 6.0 %collective-permute-start.22 = (bf16[128,256]{1,0:T(8,128)(2,1)S(1)}, bf16[128,256]{1,0:T(8,128)(2,1)S(1)}, u32[]{:S(2)}, u32[]{:S(2)}) collective-permute-start(bf16[128,256]{1,0:T(8,128)(2,1)S(1)} %get-tuple-element.121), channel_id=1, source_target_pairs={{0,10},{2,12},{4,14},{6,0},{8,2},{10,4},{12,6},{14,8},{1,11},{3,13... | collective-permute-start | bytes 196616 | tf_op jit(solution)/shard_map/ppermute | solution.py:310
  138.4 4.3 %collective-permute-start.23 = (bf16[128,256]{1,0:T(8,128)(2,1)S(1)}, bf16[128,256]{1,0:T(8,128)(2,1)S(1)}, u32[]{:S(2)}, u32[]{:S(2)}) collective-permute-start(bf16[128,256]{1,0:T(8,128)(2,1)S(1)} %get-tuple-element.122), channel_id=1, source_target_pairs={{0,12},{2,14},{4,0},{6,2},{8,4},{10,6},{12,8},{14,10},{1,13},{3,15... | collective-permute-start | bytes 196616 | tf_op jit(solution)/shard_map/ppermute | solution.py:310
  142.7 5.1 %collective-permute-done.23.refs_6_ = bf16[128,256]{1,0:T(8,128)(2,1)S(1)} collective-permute-done((bf16[128,256]{1,0:T(8,128)(2,1)S(1)}, bf16[128,256]{1,0:T(8,128)(2,1)S(1)}, u32[]{:S(2)}, u32[]{:S(2)}) %collective-permute-start.23) | collective-permute-done | bytes 65568 | tf_op jit(solution)/shard_map/ppermute | solution.py:310
  147.8 0.8 copy-done.17
  148.6 5.2 %shard_map.114 = bf16[1024,128]{1,0:T(8,128)(2,1)} custom-call(s32[4]{0:T(128)S(1)} %pad_add_fusion.place_ref, bf16[32,128,128]{2,1,0:T(8,128)(2,1)S(1)} %all-to-all-done.2.grads_ref, bf16[2,128,1024]{2,1,0:T(8,128)(2,1)} %pad_maximum_fusion.refs_0_, bf16[2,128,1024]{2,1,0:T(8,128)(2,1)} %pad_maximum_fusion.1.refs_1_, ...), custom_call_target="tpu_custom_call" | custom-call | flops 1100000000 | bytes 9437184 | tf_op jit(solution)/shard_map/pallas_call | solution.py:164
  153.8 8.1 %all-to-all-start.3 = ((bf16[64,16,128]{2,1,0:T(8,128)(2,1)}), bf16[64,16,128]{2,1,0:T(8,128)(2,1)S(1)}, u32[]{:S(2)}, u32[]{:S(2)}) async-start(bf16[64,16,128]{2,1,0:T(8,128)(2,1)} %bitcast.21), calls=%async_computation.3 | async-start | bytes 524288 | tf_op jit(solution)/shard_map/all_to_all | solution.py:316
  161.9 1.4 shard_map.113
  163.3 10.6 %all-to-all-done.3 = bf16[64,16,128]{2,1,0:T(8,128)(2,1)S(1)} async-done(((bf16[64,16,128]{2,1,0:T(8,128)(2,1)}), bf16[64,16,128]{2,1,0:T(8,128)(2,1)S(1)}, u32[]{:S(2)}, u32[]{:S(2)}) %all-to-all-start.3) | async-done | bytes 262176 | tf_op jit(solution)/shard_map/all_to_all | solution.py:316
  174.0 0.6 copy_bitcast_fusion
  (68 shorter events, 3.0 us)
Async XLA Ops:
  4.8 49.1 %all-to-all-start = ((bf16[8,128,768]{2,1,0:T(8,128)(2,1)}), bf16[8,128,768]{2,1,0:T(8,128)(2,1)S(1)}, u32[]{:S(2)}, u32[]{:S(2)}) async-start(bf16[8,128,768]{2,1,0:T(8,128)(2,1)} %shard_map.110), calls=%async_computation | async-start | bytes 3145728 | tf_op jit(solution)/shard_map/all_to_all | solution.py:281
  13.8 40.1 %copy-start = (s32[1,2048]{1,0:T(1,128)S(1)}, s32[1,2048]{1,0:T(1,128)}, u32[]{:S(2)}) copy-start(s32[1,2048]{1,0:T(1,128)} %param.13) | copy-start | bytes 24580
  13.8 8.4 %collective-permute-start.1 = (bf16[128,1024]{1,0:T(8,128)(2,1)S(1)}, bf16[128,1024]{1,0:T(8,128)(2,1)S(1)}, u32[]{:S(2)}, u32[]{:S(2)}) collective-permute-start(bf16[128,1024]{1,0:T(8,128)(2,1)S(1)} %get-tuple-element.78), channel_id=1, source_target_pairs={{0,128},{64,192},{128,0},{192,64},{1,129},{65,193},{129,1},{193,65... | collective-permute-start | bytes 786440 | tf_op jit(solution)/shard_map/ppermute | solution.py:273
  16.7 11.7 %collective-permute-start.2 = (bf16[128,1024]{1,0:T(8,128)(2,1)S(1)}, bf16[128,1024]{1,0:T(8,128)(2,1)S(1)}, u32[]{:S(2)}, u32[]{:S(2)}) collective-permute-start(bf16[128,1024]{1,0:T(8,128)(2,1)S(1)} %get-tuple-element.79), channel_id=1, source_target_pairs={{0,192},{64,0},{128,64},{192,128},{1,193},{65,1},{129,65},{193,129... | collective-permute-start | bytes 786440 | tf_op jit(solution)/shard_map/ppermute | solution.py:273
  17.5 14.4 %collective-permute-start = (bf16[128,1024]{1,0:T(8,128)(2,1)S(1)}, bf16[128,1024]{1,0:T(8,128)(2,1)S(1)}, u32[]{:S(2)}, u32[]{:S(2)}) collective-permute-start(bf16[128,1024]{1,0:T(8,128)(2,1)S(1)} %get-tuple-element.77), channel_id=1, source_target_pairs={{0,64},{64,128},{128,192},{192,0},{1,65},{65,129},{129,193},{193,1... | collective-permute-start | bytes 786440 | tf_op jit(solution)/shard_map/ppermute | solution.py:273
  29.2 13.4 %collective-permute-start.4 = (bf16[2,128,1024]{2,1,0:T(8,128)(2,1)}, bf16[2,128,1024]{2,1,0:T(8,128)(2,1)S(1)}, u32[]{:S(2)}, u32[]{:S(2)}) collective-permute-start(bf16[2,128,1024]{2,1,0:T(8,128)(2,1)} %pad_maximum_fusion.1.refs_1_), channel_id=1, source_target_pairs={{0,16},{16,32},{32,48},{48,0},{1,17},{17,33},{33,49},{49,1},{2,18}... | collective-permute-start | bytes 1572872 | tf_op jit(solution)/shard_map/ppermute | solution.py:277
  30.5 12.1 %collective-permute-start.6 = (bf16[2,128,1024]{2,1,0:T(8,128)(2,1)}, bf16[2,128,1024]{2,1,0:T(8,128)(2,1)S(1)}, u32[]{:S(2)}, u32[]{:S(2)}) collective-permute-start(bf16[2,128,1024]{2,1,0:T(8,128)(2,1)} %pad_maximum_fusion.1.refs_1_), channel_id=1, source_target_pairs={{0,48},{16,0},{32,16},{48,32},{1,49},{17,1},{33,17},{49,33},{2,50}... | collective-permute-start | bytes 1572872 | tf_op jit(solution)/shard_map/ppermute | solution.py:277
  31.9 25.6 %copy-start.18 = (s32[1,16,8]{1,2,0:T(8,128)S(1)}, s32[1,16,8]{1,2,0:T(8,128)}, u32[]{:S(2)}) copy-start(s32[1,16,8]{1,2,0:T(8,128)} %param.12) | copy-start | bytes 1540
  32.8 21.2 %collective-permute-start.3 = (bf16[2,128,1024]{2,1,0:T(8,128)(2,1)}, bf16[2,128,1024]{2,1,0:T(8,128)(2,1)}, u32[]{:S(2)}, u32[]{:S(2)}) collective-permute-start(bf16[2,128,1024]{2,1,0:T(8,128)(2,1)} %pad_maximum_fusion.refs_0_), channel_id=1, source_target_pairs={{0,16},{16,32},{32,48},{48,0},{1,17},{17,33},{33,49},{49,1},{2,18}... | collective-permute-start | bytes 1572872 | tf_op jit(solution)/shard_map/ppermute | solution.py:277
  32.8 21.1 %collective-permute-start.5 = (bf16[2,128,1024]{2,1,0:T(8,128)(2,1)}, bf16[2,128,1024]{2,1,0:T(8,128)(2,1)}, u32[]{:S(2)}, u32[]{:S(2)}) collective-permute-start(bf16[2,128,1024]{2,1,0:T(8,128)(2,1)} %pad_maximum_fusion.refs_0_), channel_id=1, source_target_pairs={{0,48},{16,0},{32,16},{48,32},{1,49},{17,1},{33,17},{49,33},{2,50}... | collective-permute-start | bytes 1572872 | tf_op jit(solution)/shard_map/ppermute | solution.py:277
  42.6 11.4 %copy-start.7 = (bf16[2,128,1024]{2,1,0:T(8,128)(2,1)}, bf16[2,128,1024]{2,1,0:T(8,128)(2,1)S(1)}, u32[]{:S(2)}) copy-start(bf16[2,128,1024]{2,1,0:T(8,128)(2,1)S(1)} %collective-permute-done.4.refs_3_) | copy-start | bytes 1572868
  42.6 11.3 %copy-start.9 = (bf16[2,128,1024]{2,1,0:T(8,128)(2,1)}, bf16[2,128,1024]{2,1,0:T(8,128)(2,1)S(1)}, u32[]{:S(2)}) copy-start(bf16[2,128,1024]{2,1,0:T(8,128)(2,1)S(1)} %collective-permute-done.6.refs_5_) | copy-start | bytes 1572868
  55.1 4.2 %collective-permute-start.7 = (bf16[8,128,256]{2,1,0:T(8,128)(2,1)}, bf16[8,128,256]{2,1,0:T(8,128)(2,1)S(1)}, u32[]{:S(2)}, u32[]{:S(2)}) collective-permute-start(bf16[8,128,256]{2,1,0:T(8,128)(2,1)} %slice.11), channel_id=1, source_target_pairs={{0,1},{1,0},{2,3},{3,2},{4,5},{5,4},{6,7},{7,6},{8,9},{9,8},{10,11... | collective-permute-start | bytes 1572872 | tf_op jit(solution)/shard_map/ppermute | solution.py:258
  72.1 0.6 copy-start.3
  72.7 0.6 copy-start.5
  73.4 11.9 %copy-start.6 = (bf16[128,256]{1,0:T(8,128)(2,1)S(1)}, bf16[128,256]{1,0:T(8,128)(2,1)}, u32[]{:S(2)}) copy-start(bf16[128,256]{1,0:T(8,128)(2,1)} %copy-done.5) | copy-start | bytes 196612
  73.4 13.4 %copy-start.4 = (bf16[128,256]{1,0:T(8,128)(2,1)S(1)}, bf16[128,256]{1,0:T(8,128)(2,1)}, u32[]{:S(2)}) copy-start(bf16[128,256]{1,0:T(8,128)(2,1)} %copy-done.3) | copy-start | bytes 196612
  73.4 26.8 %copy-start.8 = (bf16[2,128,1024]{2,1,0:T(8,128)(2,1)S(1)}, bf16[2,128,1024]{2,1,0:T(8,128)(2,1)}, u32[]{:S(2)}) copy-start(bf16[2,128,1024]{2,1,0:T(8,128)(2,1)} %copy-done.7) | copy-start | bytes 1572868
  73.4 28.8 %copy-start.10 = (bf16[2,128,1024]{2,1,0:T(8,128)(2,1)S(1)}, bf16[2,128,1024]{2,1,0:T(8,128)(2,1)}, u32[]{:S(2)}) copy-start(bf16[2,128,1024]{2,1,0:T(8,128)(2,1)} %copy-done.9) | copy-start | bytes 1572868
  73.4 4.4 %collective-permute-start.10 = (f32[8,128,256]{2,1,0:T(8,128)S(1)}, f32[8,128,256]{2,1,0:T(8,128)S(1)}, u32[]{:S(2)}, u32[]{:S(2)}) collective-permute-start(f32[8,128,256]{2,1,0:T(8,128)S(1)} %get-tuple-element.107), channel_id=1, source_target_pairs={{0,1},{1,0},{2,3},{3,2},{4,5},{5,4},{6,7},{7,6},{8,9},{9,8},{10,11... | collective-permute-start | bytes 3145736 | tf_op jit(solution)/shard_map/ppermute | solution.py:258
  75.0 27.1 %collective-permute-start.11 = (bf16[2,128,1024]{2,1,0:T(8,128)(2,1)}, bf16[2,128,1024]{2,1,0:T(8,128)(2,1)S(1)}, u32[]{:S(2)}, u32[]{:S(2)}) collective-permute-start(bf16[2,128,1024]{2,1,0:T(8,128)(2,1)} %pad_maximum_fusion.refs_0_), channel_id=1, source_target_pairs={{0,1},{1,0},{2,3},{3,2},{4,5},{5,4},{6,7},{7,6},{8,9},{9,8},{10,11... | collective-permute-start | bytes 1572872 | tf_op jit(solution)/shard_map/ppermute | solution.py:258
  75.1 27.1 %collective-permute-start.12 = (bf16[2,128,1024]{2,1,0:T(8,128)(2,1)}, bf16[2,128,1024]{2,1,0:T(8,128)(2,1)}, u32[]{:S(2)}, u32[]{:S(2)}) collective-permute-start(bf16[2,128,1024]{2,1,0:T(8,128)(2,1)} %pad_maximum_fusion.1.refs_1_), channel_id=1, source_target_pairs={{0,1},{1,0},{2,3},{3,2},{4,5},{5,4},{6,7},{7,6},{8,9},{9,8},{10,11... | collective-permute-start | bytes 1572872 | tf_op jit(solution)/shard_map/ppermute | solution.py:258
  75.5 27.1 %collective-permute-start.13 = (bf16[2,128,1024]{2,1,0:T(8,128)(2,1)}, bf16[2,128,1024]{2,1,0:T(8,128)(2,1)}, u32[]{:S(2)}, u32[]{:S(2)}) collective-permute-start(bf16[2,128,1024]{2,1,0:T(8,128)(2,1)} %collective-permute-done.3.refs_2_), channel_id=1, source_target_pairs={{0,1},{1,0},{2,3},{3,2},{4,5},{5,4},{6,7},{7,6},{8,9},{9,8},{10,11... | collective-permute-start | bytes 1572872 | tf_op jit(solution)/shard_map/ppermute | solution.py:258
  78.7 37.5 %all-to-all-start.1 = ((bf16[8,128,256]{2,1,0:T(8,128)(2,1)}), bf16[8,128,256]{2,1,0:T(8,128)(2,1)S(1)}, u32[]{:S(2)}, u32[]{:S(2)}) async-start(bf16[8,128,256]{2,1,0:T(8,128)(2,1)} %add_convert_fusion), calls=%async_computation.1 | async-start | bytes 1048576 | tf_op jit(solution)/shard_map/all_to_all | solution.py:301
  85.3 41.4 %copy-start.2 = (bf16[128,256]{1,0:T(8,128)(2,1)S(1)}, bf16[128,256]{1,0:T(8,128)(2,1)}, u32[]{:S(2)}) copy-start(bf16[128,256]{1,0:T(8,128)(2,1)} %copy-done.1) | copy-start | bytes 196612
  85.3 13.6 %collective-permute-start.8 = (bf16[128,256]{1,0:T(8,128)(2,1)S(1)}, bf16[128,256]{1,0:T(8,128)(2,1)S(1)}, u32[]{:S(2)}, u32[]{:S(2)}) collective-permute-start(bf16[128,256]{1,0:T(8,128)(2,1)S(1)} %copy-done.6), channel_id=1, source_target_pairs={{0,2},{2,4},{4,6},{6,8},{8,10},{10,12},{12,14},{14,0},{1,3},{3,5},... | collective-permute-start | bytes 196616 | tf_op jit(solution)/shard_map/ppermute | solution.py:303
  86.8 13.3 %collective-permute-start.9 = (bf16[128,256]{1,0:T(8,128)(2,1)S(1)}, bf16[128,256]{1,0:T(8,128)(2,1)S(1)}, u32[]{:S(2)}, u32[]{:S(2)}) collective-permute-start(bf16[128,256]{1,0:T(8,128)(2,1)S(1)} %copy-done.4), channel_id=1, source_target_pairs={{0,14},{2,0},{4,2},{6,4},{8,6},{10,8},{12,10},{14,12},{1,15},{3,1}... | collective-permute-start | bytes 196616 | tf_op jit(solution)/shard_map/ppermute | solution.py:303
  98.9 13.2 %collective-permute-start.17 = (bf16[2,128,1024]{2,1,0:T(8,128)(2,1)}, bf16[2,128,1024]{2,1,0:T(8,128)(2,1)S(1)}, u32[]{:S(2)}, u32[]{:S(2)}) collective-permute-start(bf16[2,128,1024]{2,1,0:T(8,128)(2,1)} %collective-permute-done.3.refs_2_), channel_id=1, source_target_pairs={{0,16},{16,32},{32,48},{48,0},{1,17},{17,33},{33,49},{49,1},{2,18}... | collective-permute-start | bytes 1572872 | tf_op jit(solution)/shard_map/ppermute | solution.py:294
  100.2 4.3 %collective-permute-start.14 = (bf16[2,128,1024]{2,1,0:T(8,128)(2,1)S(1)}, bf16[2,128,1024]{2,1,0:T(8,128)(2,1)S(1)}, u32[]{:S(2)}, u32[]{:S(2)}) collective-permute-start(bf16[2,128,1024]{2,1,0:T(8,128)(2,1)S(1)} %copy-done.8), channel_id=1, source_target_pairs={{0,1},{1,0},{2,3},{3,2},{4,5},{5,4},{6,7},{7,6},{8,9},{9,8},{10,11... | collective-permute-start | bytes 1572872 | tf_op jit(solution)/shard_map/ppermute | solution.py:258
  102.1 15.3 %copy-start.11 = (bf16[2,128,1024]{2,1,0:T(8,128)(2,1)}, bf16[2,128,1024]{2,1,0:T(8,128)(2,1)S(1)}, u32[]{:S(2)}) copy-start(bf16[2,128,1024]{2,1,0:T(8,128)(2,1)S(1)} %collective-permute-done.11.refs_8_) | copy-start | bytes 1572868
  102.1 3.2 %collective-permute-start.15 = (bf16[2,128,1024]{2,1,0:T(8,128)(2,1)}, bf16[2,128,1024]{2,1,0:T(8,128)(2,1)S(1)}, u32[]{:S(2)}, u32[]{:S(2)}) collective-permute-start(bf16[2,128,1024]{2,1,0:T(8,128)(2,1)} %collective-permute-done.5.refs_4_), channel_id=1, source_target_pairs={{0,1},{1,0},{2,3},{3,2},{4,5},{5,4},{6,7},{7,6},{8,9},{9,8},{10,11... | collective-permute-start | bytes 1572872 | tf_op jit(solution)/shard_map/ppermute | solution.py:258
  102.2 3.1 %collective-permute-start.16 = (bf16[2,128,1024]{2,1,0:T(8,128)(2,1)S(1)}, bf16[2,128,1024]{2,1,0:T(8,128)(2,1)S(1)}, u32[]{:S(2)}, u32[]{:S(2)}) collective-permute-start(bf16[2,128,1024]{2,1,0:T(8,128)(2,1)S(1)} %copy-done.10), channel_id=1, source_target_pairs={{0,1},{1,0},{2,3},{3,2},{4,5},{5,4},{6,7},{7,6},{8,9},{9,8},{10,11... | collective-permute-start | bytes 1572872 | tf_op jit(solution)/shard_map/ppermute | solution.py:258
  102.6 13.6 %collective-permute-start.18 = (bf16[2,128,1024]{2,1,0:T(8,128)(2,1)S(1)}, bf16[2,128,1024]{2,1,0:T(8,128)(2,1)}, u32[]{:S(2)}, u32[]{:S(2)}) collective-permute-start(bf16[2,128,1024]{2,1,0:T(8,128)(2,1)S(1)} %copy-done.10), channel_id=1, source_target_pairs={{0,48},{16,0},{32,16},{48,32},{1,49},{17,1},{33,17},{49,33},{2,50}... | collective-permute-start | bytes 1572872 | tf_op jit(solution)/shard_map/ppermute | solution.py:295
  104.4 7.7 %copy-start.14 = (bf16[2,128,1024]{2,1,0:T(8,128)(2,1)}, bf16[2,128,1024]{2,1,0:T(8,128)(2,1)S(1)}, u32[]{:S(2)}) copy-start(bf16[2,128,1024]{2,1,0:T(8,128)(2,1)S(1)} %collective-permute-done.14.refs_11_) | copy-start | bytes 1572868
  105.3 6.8 %copy-start.15 = (bf16[2,128,1024]{2,1,0:T(8,128)(2,1)}, bf16[2,128,1024]{2,1,0:T(8,128)(2,1)S(1)}, u32[]{:S(2)}) copy-start(bf16[2,128,1024]{2,1,0:T(8,128)(2,1)S(1)} %collective-permute-done.15.refs_12_) | copy-start | bytes 1572868
  105.3 6.8 %copy-start.16 = (bf16[2,128,1024]{2,1,0:T(8,128)(2,1)}, bf16[2,128,1024]{2,1,0:T(8,128)(2,1)S(1)}, u32[]{:S(2)}) copy-start(bf16[2,128,1024]{2,1,0:T(8,128)(2,1)S(1)} %collective-permute-done.16.refs_13_) | copy-start | bytes 1572868
  112.1 0.8 copy-start.12
  116.2 9.9 %copy-start.13 = (bf16[2,128,1024]{2,1,0:T(8,128)(2,1)S(1)}, bf16[2,128,1024]{2,1,0:T(8,128)(2,1)}, u32[]{:S(2)}) copy-start(bf16[2,128,1024]{2,1,0:T(8,128)(2,1)} %copy-done.12) | copy-start | bytes 1572868
  117.4 30.5 %all-to-all-start.2 = ((bf16[32,128,128]{2,1,0:T(8,128)(2,1)}), bf16[32,128,128]{2,1,0:T(8,128)(2,1)S(1)}, u32[]{:S(2)}, u32[]{:S(2)}) async-start(bf16[32,128,128]{2,1,0:T(8,128)(2,1)} %get-tuple-element.115), calls=%async_computation.2 | async-start | bytes 2097152 | tf_op jit(solution)/shard_map/all_to_all | solution.py:308
  126.1 21.7 %collective-permute-start.24 = (bf16[2,128,1024]{2,1,0:T(8,128)(2,1)S(1)}, bf16[2,128,1024]{2,1,0:T(8,128)(2,1)S(1)}, u32[]{:S(2)}, u32[]{:S(2)}) collective-permute-start(bf16[2,128,1024]{2,1,0:T(8,128)(2,1)S(1)} %copy-done.13), channel_id=1, source_target_pairs={{0,1},{1,0},{2,3},{3,2},{4,5},{5,4},{6,7},{7,6},{8,9},{9,8},{10,11... | collective-permute-start | bytes 1572872 | tf_op jit(solution)/shard_map/ppermute | solution.py:258
  126.5 21.4 %collective-permute-start.25 = (bf16[2,128,1024]{2,1,0:T(8,128)(2,1)}, bf16[2,128,1024]{2,1,0:T(8,128)(2,1)}, u32[]{:S(2)}, u32[]{:S(2)}) collective-permute-start(bf16[2,128,1024]{2,1,0:T(8,128)(2,1)} %collective-permute-done.18.refs_7_), channel_id=1, source_target_pairs={{0,1},{1,0},{2,3},{3,2},{4,5},{5,4},{6,7},{7,6},{8,9},{9,8},{10,11... | collective-permute-start | bytes 1572872 | tf_op jit(solution)/shard_map/ppermute | solution.py:258
  126.7 5.7 %collective-permute-start.19 = (bf16[128,256]{1,0:T(8,128)(2,1)S(1)}, bf16[128,256]{1,0:T(8,128)(2,1)S(1)}, u32[]{:S(2)}, u32[]{:S(2)}) collective-permute-start(bf16[128,256]{1,0:T(8,128)(2,1)S(1)} %copy-done.2), channel_id=1, source_target_pairs={{0,4},{2,6},{4,8},{6,10},{8,12},{10,14},{12,0},{14,2},{1,5},{3,7},... | collective-permute-start | bytes 196616 | tf_op jit(solution)/shard_map/ppermute | solution.py:310
  127.9 10.6 %collective-permute-start.20 = (bf16[128,256]{1,0:T(8,128)(2,1)S(1)}, bf16[128,256]{1,0:T(8,128)(2,1)S(1)}, u32[]{:S(2)}, u32[]{:S(2)}) collective-permute-start(bf16[128,256]{1,0:T(8,128)(2,1)S(1)} %get-tuple-element.119), channel_id=1, source_target_pairs={{0,6},{2,8},{4,10},{6,12},{8,14},{10,0},{12,2},{14,4},{1,7},{3,9},... | collective-permute-start | bytes 196616 | tf_op jit(solution)/shard_map/ppermute | solution.py:310
  132.4 10.3 %collective-permute-start.21 = (bf16[128,256]{1,0:T(8,128)(2,1)S(1)}, bf16[128,256]{1,0:T(8,128)(2,1)S(1)}, u32[]{:S(2)}, u32[]{:S(2)}) collective-permute-start(bf16[128,256]{1,0:T(8,128)(2,1)S(1)} %get-tuple-element.120), channel_id=1, source_target_pairs={{0,8},{2,10},{4,12},{6,14},{8,0},{10,2},{12,4},{14,6},{1,9},{3,11}... | collective-permute-start | bytes 196616 | tf_op jit(solution)/shard_map/ppermute | solution.py:310
  132.4 10.3 %collective-permute-start.22 = (bf16[128,256]{1,0:T(8,128)(2,1)S(1)}, bf16[128,256]{1,0:T(8,128)(2,1)S(1)}, u32[]{:S(2)}, u32[]{:S(2)}) collective-permute-start(bf16[128,256]{1,0:T(8,128)(2,1)S(1)} %get-tuple-element.121), channel_id=1, source_target_pairs={{0,10},{2,12},{4,14},{6,0},{8,2},{10,4},{12,6},{14,8},{1,11},{3,13... | collective-permute-start | bytes 196616 | tf_op jit(solution)/shard_map/ppermute | solution.py:310
  138.4 9.4 %collective-permute-start.23 = (bf16[128,256]{1,0:T(8,128)(2,1)S(1)}, bf16[128,256]{1,0:T(8,128)(2,1)S(1)}, u32[]{:S(2)}, u32[]{:S(2)}) collective-permute-start(bf16[128,256]{1,0:T(8,128)(2,1)S(1)} %get-tuple-element.122), channel_id=1, source_target_pairs={{0,12},{2,14},{4,0},{6,2},{8,4},{10,6},{12,8},{14,10},{1,13},{3,15... | collective-permute-start | bytes 196616 | tf_op jit(solution)/shard_map/ppermute | solution.py:310
  147.8 0.8 copy-start.17
  153.8 20.1 %all-to-all-start.3 = ((bf16[64,16,128]{2,1,0:T(8,128)(2,1)}), bf16[64,16,128]{2,1,0:T(8,128)(2,1)S(1)}, u32[]{:S(2)}, u32[]{:S(2)}) async-start(bf16[64,16,128]{2,1,0:T(8,128)(2,1)} %bitcast.21), calls=%async_computation.3 | async-start | bytes 524288 | tf_op jit(solution)/shard_map/all_to_all | solution.py:316
  (1 other events, 0.6 us)

commit v5 on v4

--- a/solution.py
+++ b/solution.py
@@ -39,7 +39,7 @@
     links_ref, place_ref, rows_ref, other_ref, seg_cols_ref, seg_rows_ref, *refs
 ):
     dq_refs, refs = refs[:NZ], refs[NZ:]
-    own_ref, away_ref, pair_ref, keys_t_ref, total_ref, near_ref, near_t_ref, dq_ref = refs
+    own_ref, away_ref, pair_ref, keys_t_ref, total_ref, near_ref, near_t_ref, dq_ref, sems = refs
     z, core = place_ref[1], place_ref[2]
 
     def at(block):
@@ -94,6 +94,10 @@
 
     lax.fori_loop(1 - core, NZ, linked, 0)
 
+    copies = [pltpu.make_async_copy(dq_ref.at[s], dq_refs[s], sems.at[s]) for s in range(NZ)]
+    for copy in copies:
+        copy.start()
+
     def store(i, carry):
         for ref, block in ((own_ref, 2 * i + core), (away_ref, 2 * i + 1 - core)):
             ref[i, :, :HEAD] = total_ref[at(block), :HEAD] * SCALE
@@ -101,8 +105,8 @@
         return carry
 
     lax.fori_loop(0, NZ, store, 0)
-    for s, ref in enumerate(dq_refs):
-        ref[...] = dq_ref[s]
+    for copy in copies:
+        copy.wait()
 
 
 def attention_grads(links, place, rows, other, seg_cols, seg_rows):
@@ -110,13 +114,13 @@
     smem = pl.BlockSpec(memory_space=pltpu.SMEM)
     return pl.pallas_call(
         attention_kernel,
-        out_shape=(jax.ShapeDtypeStruct((BLOCK, 2 * HEAD), jnp.bfloat16),) * NZ
+        out_shape=(pltpu.HBM((BLOCK, 2 * HEAD), jnp.bfloat16),) * NZ
         + (
             jax.ShapeDtypeStruct((NZ, BLOCK, 2 * HEAD), jnp.float32),
             jax.ShapeDtypeStruct((NZ, BLOCK, 2 * HEAD), jnp.float32),
         ),
         in_specs=[smem, smem, vmem, vmem, vmem, vmem],
-        out_specs=(vmem,) * (NZ + 2),
+        out_specs=(pl.BlockSpec(memory_space=pltpu.HBM),) * NZ + (vmem, vmem),
         scratch_shapes=[
             pltpu.VMEM((BLOCKS * BLOCK, 2 * HEAD), jnp.bfloat16),
             pltpu.VMEM((HEAD, BLOCKS * BLOCK), jnp.bfloat16),
@@ -124,6 +128,7 @@
             pltpu.VMEM((LINKS * BLOCK, 2 * HEAD), jnp.bfloat16),
             pltpu.VMEM((HEAD, LINKS * BLOCK), jnp.bfloat16),
             pltpu.VMEM((NZ, BLOCK, 2 * HEAD), jnp.bfloat16),
+            pltpu.SemaphoreType.DMA((NZ,)),
         ],
         compiler_params=pltpu.CompilerParams(vmem_limit_bytes=32 * MIB),
         cost_estimate=pl.CostEstimate(
@@ -197,9 +202,9 @@
 def packed(queries, grads, keys, values):
     return pl.pallas_call(
         pack_kernel,
-        out_shape=jax.ShapeDtypeStruct((NZ, BLOCK, 6 * HEAD), jnp.bfloat16),
+        out_shape=pltpu.HBM((NZ, BLOCK, 6 * HEAD), jnp.bfloat16),
         in_specs=[pl.BlockSpec(memory_space=pltpu.HBM)] * 4,
-        out_specs=pl.BlockSpec(memory_space=pltpu.VMEM),
+        out_specs=pl.BlockSpec(memory_space=pltpu.HBM),
         scratch_shapes=[pltpu.SemaphoreType.DMA((4 * NZ,))],
         compiler_params=pltpu.CompilerParams(vmem_limit_bytes=16 * MIB),
         cost_estimate=pl.CostEstimate(flops=0, bytes_accessed=3 * MIB, transcendentals=0),
@@ -269,13 +274,10 @@
         lax.dynamic_slice_in_dim(inputs, lax.rem(x + s, NX) * width, width, axis=1)
         for s in range(NX)
     ]
-    pieces, queries = lax.optimization_barrier((pieces, queries))
     pieces = [a if s == 0 else lax.ppermute(a, "x", ring(NX, s)) for s, a in enumerate(pieces)]
     half = NX // 2
     mine = (jnp.stack(pieces[:half]), jnp.stack(pieces[half:]))
-    before, after = (
-        tuple(lax.ppermute(a, "y", ring(NY, shift)) for a in mine) for shift in (1, -1)
-    )
+    before, after = lax.ppermute(mine[0], "y", ring(NY, 1)), lax.ppermute(mine[1], "y", ring(NY, -1))
 
     outgoing = packed(queries[0], output_grads[0], keys[0], values[0])
     rows = lax.all_to_all(outgoing, "z", split_axis=0, concat_axis=0, tiled=True)
@@ -285,6 +287,8 @@
         (rows, mine, before, after, seg_cols)
     )
     other = swap_cores(rows[..., 4 * HEAD :])
+    before = (before, lax.ppermute(mine[1], "y", ring(NY, 1)))
+    after = (lax.ppermute(mine[0], "y", ring(NY, -1)), after)
     *dq, own, away = attention_grads(block_links[0], place, rows, other, seg_cols, seg_rows)
 
     dq, own, away, mine, before, after = lax.optimization_barrier(
@@ -299,14 +303,12 @@
 
     pair = (own + swap_cores(away)).astype(bf16)
     pair = lax.all_to_all(pair, "z", split_axis=0, concat_axis=0, tiled=True)
-    for s in (1, 7):
-        dq[s] = lax.ppermute(dq[s], "z", ring(NZ, s))
     dq, pair, inputs_other, far = lax.optimization_barrier((dq, pair, inputs_other, far))
     far_other = tuple(swap_cores(a) for a in far)
     key_grads, value_grads, chunks = pair_grads(pair)
 
     grads = lax.all_to_all(chunks, ("x", "y", "c"), split_axis=0, concat_axis=0, tiled=True)
-    for s in (4, 3, 5, 2, 6):
+    for s in (1, 7, 2, 6, 3, 5, 4):
         dq[s] = lax.ppermute(dq[s], "z", ring(NZ, s))
     grads, dq, far_other = lax.optimization_barrier((grads, dq, far_other))
     part = weight_grads_part(place, grads, inputs_own + far, inputs_other + far_other)

time: 175 us -> 203 us (1.16)
  Pallas kernels: 22.8 us -> 69.6 us
  waiting for transfers between devices: 69.9 us -> 60.4 us
  starting transfers between devices: 71.8 us -> 64.4 us
  local copies, waits for them, and re-layouts: 6.66 us -> 4.59 us
    pallas_call x2, Pallas kernels: 15.1 us -> 61.9 us  [the longest x1 49 us: packed(): pl.pallas_call(pack_kernel, out_shape=pltpu.HBM((NZ, BLOCK, 6 * HEAD), jn...]
    ppermute x7, waiting for transfers between devices: 15.9 us -> 6.44 us  [local(): dq[s] = lax.ppermute(dq[s], 'z', ring(NZ, s))]
    ppermute x4, waiting for transfers between devices: 18.5 us -> 12.3 us  [the longest x1 9.13 us: local(): lax.ppermute(mine[1], 'y', ring(NY, -1))]
    all_to_all x1, waiting for transfers between devices: 0.01 us -> 6.12 us  [local(): lax.all_to_all(outgoing, 'z', split_axis=0, concat_axis=0, tiled=True)]
    ppermute x1, waiting for transfers between devices: 6.77 us -> 10.3 us  [local(): lax.ppermute(before[0], 'y', ring(NY, 1))]
    ppermute x1, waiting for transfers between devices: 3.28 us -> 0.01 us  [local(): lax.ppermute(after[1], 'y', ring(NY, -1))]
    all_to_all x1, starting transfers between devices: 6.55 us -> 3.49 us  [local(): pair = lax.all_to_all(pair, 'z', split_axis=0, concat_axis=0, tiled=True)]
    ppermute x7, starting transfers between devices: 18.8 us -> 15.8 us  [local(): dq[s] = lax.ppermute(dq[s], 'z', ring(NZ, s))]
  transfers between devices with their start and end apart: 30 -> 30, of which waited for: 12 -> 14; matrix products, arithmetic and copies ran while one was open for 2% -> 1% of each run, Pallas kernels for 1% -> 7%
where the time goes in v5:
time: 203 us
  Pallas kernels  69.6 us (34%)
  starting transfers between devices  64.4 us (32%)
  waiting for transfers between devices  60.4 us (30%)
  local copies, waits for them, and re-layouts  4.59 us (2%)
  other arithmetic  2.69 us (1%)
    pallas_call x1, Pallas kernels, packed(): pl.pallas_call(pack_kernel, out_shape=pltpu.HBM((NZ, BLOCK, 6 * HEAD), jn...  49 us
    ppermute x7, starting transfers between devices, local(): dq[s] = lax.ppermute(dq[s], 'z', ring(NZ, s))  15.8 us
    pallas_call x1, Pallas kernels, attention_grads(): pl.pallas_call(attention_kernel, out_shape=(pltpu.HBM((BLOCK, 2 * HEAD),...  12.8 us
    all_to_all x1, waiting for transfers between devices, local(): lax.all_to_all(part, ('y', 'z', 'c'), split_axis=0, concat_axis=0, tiled=...  10.6 us
    ppermute x1, waiting for transfers between devices, local(): lax.ppermute(before[0], 'y', ring(NY, 1))  10.3 us
    ppermute x3, waiting for transfers between devices, local(): lax.ppermute(a, 'x', ring(NX, s))  10.2 us
    all_to_all x1, starting transfers between devices, local(): lax.all_to_all(part, ('y', 'z', 'c'), split_axis=0, concat_axis=0, tiled=...  9.93 us
    all_to_all x1, starting transfers between devices, local(): lax.all_to_all(outgoing, 'z', split_axis=0, concat_axis=0, tiled=True)  9.16 us
  transfers between devices with their start and end apart: 30, of which 14 were waited for; matrix products, arithmetic and copies ran while one was open for 1% of the time, Pallas kernels for 7%

profile of v5, /device:TPU:1, one launch (start us, length us, event | category | flops | bytes accessed | tf_op | source)
XLA Modules:
  0.0 202.7 jit_solution(16428608755314954068)
XLA Ops:
  0.6 49.0 %shard_map.110 = bf16[8,128,768]{2,1,0:T(8,128)(2,1)} custom-call(bf16[128,2048]{1,0:T(8,128)(2,1)} %bitcast.38, bf16[128,2048]{1,0:T(8,128)(2,1)} %bitcast.39, bf16[128,512]{1,0:T(8,128)(2,1)} %bitcast.44, bf16[128,512]{1,0:T(8,128)(2,1)} %bitcast.45), custom_call_target="tpu_custom_call" | custom-call | bytes 3145728 | tf_op jit(solution)/shard_map/pallas_call | solution.py:203
  49.7 9.2 %all-to-all-start = ((bf16[8,128,768]{2,1,0:T(8,128)(2,1)}), bf16[8,128,768]{2,1,0:T(8,128)(2,1)S(1)}, u32[]{:S(2)}, u32[]{:S(2)}) async-start(bf16[8,128,768]{2,1,0:T(8,128)(2,1)} %shard_map.110), calls=%async_computation | async-start | bytes 3145728 | tf_op jit(solution)/shard_map/all_to_all | solution.py:283
  59.0 2.8 %collective-permute-start.1 = (bf16[128,1024]{1,0:T(8,128)(2,1)S(1)}, bf16[128,1024]{1,0:T(8,128)(2,1)S(1)}, u32[]{:S(2)}, u32[]{:S(2)}) collective-permute-start(bf16[128,1024]{1,0:T(8,128)(2,1)S(1)} %get-tuple-element.131), channel_id=1, source_target_pairs={{0,128},{64,192},{128,0},{192,64},{1,129},{65,193},{129,1},{193,65... | collective-permute-start | bytes 786440 | tf_op jit(solution)/shard_map/ppermute | solution.py:277
  61.8 0.9 collective-permute-start.2
  62.7 0.6 collective-permute-start
  63.3 4.1 %collective-permute-done.1 = bf16[128,1024]{1,0:T(8,128)(2,1)S(1)} collective-permute-done((bf16[128,1024]{1,0:T(8,128)(2,1)S(1)}, bf16[128,1024]{1,0:T(8,128)(2,1)S(1)}, u32[]{:S(2)}, u32[]{:S(2)}) %collective-permute-start.1) | collective-permute-done | bytes 262176 | tf_op jit(solution)/shard_map/ppermute | solution.py:277
  67.4 6.1 %collective-permute-done.2 = bf16[128,1024]{1,0:T(8,128)(2,1)S(1)} collective-permute-done((bf16[128,1024]{1,0:T(8,128)(2,1)S(1)}, bf16[128,1024]{1,0:T(8,128)(2,1)S(1)}, u32[]{:S(2)}, u32[]{:S(2)}) %collective-permute-start.2) | collective-permute-done | bytes 262176 | tf_op jit(solution)/shard_map/ppermute | solution.py:277
  73.5 0.8 pad_maximum_fusion.1.refs_1_
  74.3 2.7 %collective-permute-start.4 = (bf16[2,128,1024]{2,1,0:T(8,128)(2,1)}, bf16[2,128,1024]{2,1,0:T(8,128)(2,1)S(1)}, u32[]{:S(2)}, u32[]{:S(2)}) collective-permute-start(bf16[2,128,1024]{2,1,0:T(8,128)(2,1)} %pad_maximum_fusion.1.refs_1_), channel_id=1, source_target_pairs={{0,48},{16,0},{32,16},{48,32},{1,49},{17,1},{33,17},{49,33},{2,50}... | collective-permute-start | bytes 1572872 | tf_op jit(solution)/shard_map/ppermute | solution.py:280
  77.0 0.8 pad_maximum_fusion.refs_0_
  77.9 9.1 %collective-permute-done.4.refs_5_ = bf16[2,128,1024]{2,1,0:T(8,128)(2,1)S(1)} collective-permute-done((bf16[2,128,1024]{2,1,0:T(8,128)(2,1)}, bf16[2,128,1024]{2,1,0:T(8,128)(2,1)S(1)}, u32[]{:S(2)}, u32[]{:S(2)}) %collective-permute-start.4) | collective-permute-done | bytes 524320 | tf_op jit(solution)/shard_map/ppermute | solution.py:280
  87.0 0.8 copy-done.3
  87.8 3.2 %collective-permute-done.3.refs_2_ = bf16[2,128,1024]{2,1,0:T(8,128)(2,1)} collective-permute-done((bf16[2,128,1024]{2,1,0:T(8,128)(2,1)}, bf16[2,128,1024]{2,1,0:T(8,128)(2,1)}, u32[]{:S(2)}, u32[]{:S(2)}) %collective-permute-start.3) | collective-permute-done | bytes 524320 | tf_op jit(solution)/shard_map/ppermute | solution.py:280
  91.0 6.1 %all-to-all-done.rows_ref = bf16[8,128,768]{2,1,0:T(8,128)(2,1)S(1)} async-done(((bf16[8,128,768]{2,1,0:T(8,128)(2,1)}), bf16[8,128,768]{2,1,0:T(8,128)(2,1)S(1)}, u32[]{:S(2)}, u32[]{:S(2)}) %all-to-all-start) | async-done | bytes 1572896 | tf_op jit(solution)/shard_map/all_to_all | solution.py:283
  97.4 0.8 slice.11
  98.3 2.7 %collective-permute-start.5 = (bf16[8,128,256]{2,1,0:T(8,128)(2,1)}, bf16[8,128,256]{2,1,0:T(8,128)(2,1)S(1)}, u32[]{:S(2)}, u32[]{:S(2)}) collective-permute-start(bf16[8,128,256]{2,1,0:T(8,128)(2,1)} %slice.11), channel_id=1, source_target_pairs={{0,1},{1,0},{2,3},{3,2},{4,5},{5,4},{6,7},{7,6},{8,9},{9,8},{10,11... | collective-permute-start | bytes 1572872 | tf_op jit(solution)/shard_map/ppermute | solution.py:263
  100.9 1.3 collective-permute-start.6
  102.2 1.4 collective-permute-start.7
  103.8 12.8 %shard_map.111 = (bf16[128,256]{1,0:T(8,128)(2,1)}, bf16[128,256]{1,0:T(8,128)(2,1)}, bf16[128,256]{1,0:T(8,128)(2,1)}, bf16[128,256]{1,0:T(8,128)(2,1)}, bf16[1...) custom-call(s32[16,8]{1,0:T(8,128)S(1)} %copy.14.links_ref, ...), custom_call_target="tpu_custom_call" | custom-call | flops 4000000000 | bytes 8388608 | tf_op jit(solution)/shard_map/pallas_call | solution.py:115
  116.7 1.8 collective-permute-start.8
  118.6 0.4 collective-permute-start.11
  119.1 2.2 %collective-permute-done.8 = f32[8,128,256]{2,1,0:T(8,128)S(1)} collective-permute-done((f32[8,128,256]{2,1,0:T(8,128)S(1)}, f32[8,128,256]{2,1,0:T(8,128)S(1)}, u32[]{:S(2)}, u32[]{:S(2)}) %collective-permute-start.8) | collective-permute-done | bytes 1048608 | tf_op jit(solution)/shard_map/ppermute | solution.py:263
  121.3 0.9 add_convert_fusion
  122.2 3.5 %all-to-all-start.1 = ((bf16[8,128,256]{2,1,0:T(8,128)(2,1)}), bf16[8,128,256]{2,1,0:T(8,128)(2,1)S(1)}, u32[]{:S(2)}, u32[]{:S(2)}) async-start(bf16[8,128,256]{2,1,0:T(8,128)(2,1)} %add_convert_fusion), calls=%async_computation.1 | async-start | bytes 1048576 | tf_op jit(solution)/shard_map/all_to_all | solution.py:305
  125.9 0.7 collective-permute-start.13
  126.7 2.7 %collective-permute-start.16 = (bf16[2,128,1024]{2,1,0:T(8,128)(2,1)S(1)}, bf16[2,128,1024]{2,1,0:T(8,128)(2,1)S(1)}, u32[]{:S(2)}, u32[]{:S(2)}) collective-permute-start(bf16[2,128,1024]{2,1,0:T(8,128)(2,1)S(1)} %copy-done.4), channel_id=1, source_target_pairs={{0,48},{16,0},{32,16},{48,32},{1,49},{17,1},{33,17},{49,33},{2,50}... | collective-permute-start | bytes 1572872 | tf_op jit(solution)/shard_map/ppermute | solution.py:299
  129.3 0.7 collective-permute-start.9
  130.1 10.3 %collective-permute-done.15.refs_6_ = bf16[2,128,1024]{2,1,0:T(8,128)(2,1)S(1)} collective-permute-done((bf16[2,128,1024]{2,1,0:T(8,128)(2,1)}, bf16[2,128,1024]{2,1,0:T(8,128)(2,1)S(1)}, u32[]{:S(2)}, u32[]{:S(2)}) %collective-permute-start.15) | collective-permute-done | bytes 524320 | tf_op jit(solution)/shard_map/ppermute | solution.py:298
  140.4 0.8 copy-done.12
  141.4 2.2 %all-to-all-done.1.partials_ref = bf16[8,128,256]{2,1,0:T(8,128)(2,1)S(1)} async-done(((bf16[8,128,256]{2,1,0:T(8,128)(2,1)}), bf16[8,128,256]{2,1,0:T(8,128)(2,1)S(1)}, u32[]{:S(2)}, u32[]{:S(2)}) %all-to-all-start.1) | async-done | bytes 524320 | tf_op jit(solution)/shard_map/all_to_all | solution.py:305
  143.6 1.2 shard_map.112
  144.8 6.4 %all-to-all-start.2 = ((bf16[32,128,128]{2,1,0:T(8,128)(2,1)}), bf16[32,128,128]{2,1,0:T(8,128)(2,1)S(1)}, u32[]{:S(2)}, u32[]{:S(2)}) async-start(bf16[32,128,128]{2,1,0:T(8,128)(2,1)} %get-tuple-element.101), calls=%async_computation.2 | async-start | bytes 2097152 | tf_op jit(solution)/shard_map/all_to_all | solution.py:310
  151.8 1.6 collective-permute-start.17
  153.3 2.1 %collective-permute-start.18 = (bf16[128,256]{1,0:T(8,128)(2,1)S(1)}, bf16[128,256]{1,0:T(8,128)(2,1)S(1)}, u32[]{:S(2)}, u32[]{:S(2)}) collective-permute-start(bf16[128,256]{1,0:T(8,128)(2,1)S(1)} %copy-done.20), channel_id=1, source_target_pairs={{0,4},{2,6},{4,8},{6,10},{8,12},{10,14},{12,0},{14,2},{1,5},{3,7},... | collective-permute-start | bytes 196616 | tf_op jit(solution)/shard_map/ppermute | solution.py:312
  155.4 2.4 %collective-permute-start.19 = (bf16[128,256]{1,0:T(8,128)(2,1)S(1)}, bf16[128,256]{1,0:T(8,128)(2,1)S(1)}, u32[]{:S(2)}, u32[]{:S(2)}) collective-permute-start(bf16[128,256]{1,0:T(8,128)(2,1)S(1)} %copy-done.19), channel_id=1, source_target_pairs={{0,6},{2,8},{4,10},{6,12},{8,14},{10,0},{12,2},{14,4},{1,7},{3,9},... | collective-permute-start | bytes 196616 | tf_op jit(solution)/shard_map/ppermute | solution.py:312
  157.8 4.3 %collective-permute-start.20 = (bf16[128,256]{1,0:T(8,128)(2,1)S(1)}, bf16[128,256]{1,0:T(8,128)(2,1)S(1)}, u32[]{:S(2)}, u32[]{:S(2)}) collective-permute-start(bf16[128,256]{1,0:T(8,128)(2,1)S(1)} %copy-done.18), channel_id=1, source_target_pairs={{0,8},{2,10},{4,12},{6,14},{8,0},{10,2},{12,4},{14,6},{1,9},{3,11}... | collective-permute-start | bytes 196616 | tf_op jit(solution)/shard_map/ppermute | solution.py:312
  162.1 2.8 %collective-permute-start.21 = (bf16[128,256]{1,0:T(8,128)(2,1)S(1)}, bf16[128,256]{1,0:T(8,128)(2,1)S(1)}, u32[]{:S(2)}, u32[]{:S(2)}) collective-permute-start(bf16[128,256]{1,0:T(8,128)(2,1)S(1)} %copy-done.17), channel_id=1, source_target_pairs={{0,10},{2,12},{4,14},{6,0},{8,2},{10,4},{12,6},{14,8},{1,11},{3,13... | collective-permute-start | bytes 196616 | tf_op jit(solution)/shard_map/ppermute | solution.py:312
  165.1 1.5 collective-permute-start.22
  166.6 0.6 collective-permute-done.20.refs_4_
  167.2 1.0 collective-permute-start.23
  168.5 2.9 %collective-permute-done.22.refs_6_ = bf16[128,256]{1,0:T(8,128)(2,1)S(1)} collective-permute-done((bf16[128,256]{1,0:T(8,128)(2,1)S(1)}, bf16[128,256]{1,0:T(8,128)(2,1)S(1)}, u32[]{:S(2)}, u32[]{:S(2)}) %collective-permute-start.22) | collective-permute-done | bytes 65568 | tf_op jit(solution)/shard_map/ppermute | solution.py:312
  171.4 2.6 %collective-permute-done.23.refs_7_ = bf16[128,256]{1,0:T(8,128)(2,1)S(1)} collective-permute-done((bf16[128,256]{1,0:T(8,128)(2,1)S(1)}, bf16[128,256]{1,0:T(8,128)(2,1)S(1)}, u32[]{:S(2)}, u32[]{:S(2)}) %collective-permute-start.23) | collective-permute-done | bytes 65568 | tf_op jit(solution)/shard_map/ppermute | solution.py:312
  174.0 0.8 copy-done.13
  174.8 5.2 %shard_map.114 = bf16[1024,128]{1,0:T(8,128)(2,1)} custom-call(s32[4]{0:T(128)S(1)} %pad_add_fusion.place_ref, bf16[32,128,128]{2,1,0:T(8,128)(2,1)S(1)} %all-to-all-done.2.grads_ref, bf16[2,128,1024]{2,1,0:T(8,128)(2,1)} %pad_maximum_fusion.refs_0_, bf16[2,128,1024]{2,1,0:T(8,128)(2,1)} %pad_maximum_fusion.1.refs_1_, ...), custom_call_target="tpu_custom_call" | custom-call | flops 1100000000 | bytes 9437184 | tf_op jit(solution)/shard_map/pallas_call | solution.py:169
  180.0 9.9 %all-to-all-start.3 = ((bf16[64,16,128]{2,1,0:T(8,128)(2,1)}), bf16[64,16,128]{2,1,0:T(8,128)(2,1)S(1)}, u32[]{:S(2)}, u32[]{:S(2)}) async-start(bf16[64,16,128]{2,1,0:T(8,128)(2,1)} %bitcast.19), calls=%async_computation.3 | async-start | bytes 524288 | tf_op jit(solution)/shard_map/all_to_all | solution.py:318
  189.9 1.4 shard_map.113
  191.4 10.6 %all-to-all-done.3 = bf16[64,16,128]{2,1,0:T(8,128)(2,1)S(1)} async-done(((bf16[64,16,128]{2,1,0:T(8,128)(2,1)}), bf16[64,16,128]{2,1,0:T(8,128)(2,1)S(1)}, u32[]{:S(2)}, u32[]{:S(2)}) %all-to-all-start.3) | async-done | bytes 262176 | tf_op jit(solution)/shard_map/all_to_all | solution.py:318
  202.0 0.6 copy_bitcast_fusion
  (72 shorter events, 2.4 us)
Async XLA Ops:
  49.7 9.2 %copy-start.2 = (bf16[1,128,4096]{2,1,0:T(8,128)(2,1)S(1)}, bf16[1,128,4096]{2,1,0:T(8,128)(2,1)}, u32[]{:S(2)}) copy-start(bf16[1,128,4096]{2,1,0:T(8,128)(2,1)} %param.7) | copy-start | bytes 3145732
  49.7 47.4 %all-to-all-start = ((bf16[8,128,768]{2,1,0:T(8,128)(2,1)}), bf16[8,128,768]{2,1,0:T(8,128)(2,1)S(1)}, u32[]{:S(2)}, u32[]{:S(2)}) async-start(bf16[8,128,768]{2,1,0:T(8,128)(2,1)} %shard_map.110), calls=%async_computation | async-start | bytes 3145728 | tf_op jit(solution)/shard_map/all_to_all | solution.py:283
  59.0 38.2 %copy-start.1 = (s32[1,2048]{1,0:T(1,128)S(1)}, s32[1,2048]{1,0:T(1,128)}, u32[]{:S(2)}) copy-start(s32[1,2048]{1,0:T(1,128)} %param.13) | copy-start | bytes 24580
  59.0 8.4 %collective-permute-start.1 = (bf16[128,1024]{1,0:T(8,128)(2,1)S(1)}, bf16[128,1024]{1,0:T(8,128)(2,1)S(1)}, u32[]{:S(2)}, u32[]{:S(2)}) collective-permute-start(bf16[128,1024]{1,0:T(8,128)(2,1)S(1)} %get-tuple-element.131), channel_id=1, source_target_pairs={{0,128},{64,192},{128,0},{192,64},{1,129},{65,193},{129,1},{193,65... | collective-permute-start | bytes 786440 | tf_op jit(solution)/shard_map/ppermute | solution.py:277
  61.8 11.7 %collective-permute-start.2 = (bf16[128,1024]{1,0:T(8,128)(2,1)S(1)}, bf16[128,1024]{1,0:T(8,128)(2,1)S(1)}, u32[]{:S(2)}, u32[]{:S(2)}) collective-permute-start(bf16[128,1024]{1,0:T(8,128)(2,1)S(1)} %get-tuple-element.134), channel_id=1, source_target_pairs={{0,192},{64,0},{128,64},{192,128},{1,193},{65,1},{129,65},{193,129... | collective-permute-start | bytes 786440 | tf_op jit(solution)/shard_map/ppermute | solution.py:277
  62.7 14.4 %collective-permute-start = (bf16[128,1024]{1,0:T(8,128)(2,1)S(1)}, bf16[128,1024]{1,0:T(8,128)(2,1)S(1)}, u32[]{:S(2)}, u32[]{:S(2)}) collective-permute-start(bf16[128,1024]{1,0:T(8,128)(2,1)S(1)} %get-tuple-element.132), channel_id=1, source_target_pairs={{0,64},{64,128},{128,192},{192,0},{1,65},{65,129},{129,193},{193,1... | collective-permute-start | bytes 786440 | tf_op jit(solution)/shard_map/ppermute | solution.py:277
  74.3 12.7 %collective-permute-start.4 = (bf16[2,128,1024]{2,1,0:T(8,128)(2,1)}, bf16[2,128,1024]{2,1,0:T(8,128)(2,1)S(1)}, u32[]{:S(2)}, u32[]{:S(2)}) collective-permute-start(bf16[2,128,1024]{2,1,0:T(8,128)(2,1)} %pad_maximum_fusion.1.refs_1_), channel_id=1, source_target_pairs={{0,48},{16,0},{32,16},{48,32},{1,49},{17,1},{33,17},{49,33},{2,50}... | collective-permute-start | bytes 1572872 | tf_op jit(solution)/shard_map/ppermute | solution.py:280
  77.0 26.6 %copy-start.14 = (s32[1,16,8]{1,2,0:T(8,128)S(1)}, s32[1,16,8]{1,2,0:T(8,128)}, u32[]{:S(2)}) copy-start(s32[1,16,8]{1,2,0:T(8,128)} %param.12) | copy-start | bytes 1540
  77.9 13.1 %collective-permute-start.3 = (bf16[2,128,1024]{2,1,0:T(8,128)(2,1)}, bf16[2,128,1024]{2,1,0:T(8,128)(2,1)}, u32[]{:S(2)}, u32[]{:S(2)}) collective-permute-start(bf16[2,128,1024]{2,1,0:T(8,128)(2,1)} %pad_maximum_fusion.refs_0_), channel_id=1, source_target_pairs={{0,16},{16,32},{32,48},{48,0},{1,17},{17,33},{33,49},{49,1},{2,18}... | collective-permute-start | bytes 1572872 | tf_op jit(solution)/shard_map/ppermute | solution.py:280
  98.3 5.5 %collective-permute-start.5 = (bf16[8,128,256]{2,1,0:T(8,128)(2,1)}, bf16[8,128,256]{2,1,0:T(8,128)(2,1)S(1)}, u32[]{:S(2)}, u32[]{:S(2)}) collective-permute-start(bf16[8,128,256]{2,1,0:T(8,128)(2,1)} %slice.11), channel_id=1, source_target_pairs={{0,1},{1,0},{2,3},{3,2},{4,5},{5,4},{6,7},{7,6},{8,9},{9,8},{10,11... | collective-permute-start | bytes 1572872 | tf_op jit(solution)/shard_map/ppermute | solution.py:263
  100.9 15.7 %collective-permute-start.6 = (bf16[2,128,1024]{2,1,0:T(8,128)(2,1)}, bf16[2,128,1024]{2,1,0:T(8,128)(2,1)}, u32[]{:S(2)}, u32[]{:S(2)}) collective-permute-start(bf16[2,128,1024]{2,1,0:T(8,128)(2,1)} %pad_maximum_fusion.1.refs_1_), channel_id=1, source_target_pairs={{0,16},{16,32},{32,48},{48,0},{1,17},{17,33},{33,49},{49,1},{2,18}... | collective-permute-start | bytes 1572872 | tf_op jit(solution)/shard_map/ppermute | solution.py:290
  102.2 14.5 %collective-permute-start.7 = (bf16[2,128,1024]{2,1,0:T(8,128)(2,1)}, bf16[2,128,1024]{2,1,0:T(8,128)(2,1)}, u32[]{:S(2)}, u32[]{:S(2)}) collective-permute-start(bf16[2,128,1024]{2,1,0:T(8,128)(2,1)} %pad_maximum_fusion.refs_0_), channel_id=1, source_target_pairs={{0,48},{16,0},{32,16},{48,32},{1,49},{17,1},{33,17},{49,33},{2,50}... | collective-permute-start | bytes 1572872 | tf_op jit(solution)/shard_map/ppermute | solution.py:291
  116.7 9.9 %copy-start.4 = (bf16[2,128,1024]{2,1,0:T(8,128)(2,1)S(1)}, bf16[2,128,1024]{2,1,0:T(8,128)(2,1)}, u32[]{:S(2)}) copy-start(bf16[2,128,1024]{2,1,0:T(8,128)(2,1)} %copy-done.3) | copy-start | bytes 1572868
  116.7 4.6 %collective-permute-start.8 = (f32[8,128,256]{2,1,0:T(8,128)S(1)}, f32[8,128,256]{2,1,0:T(8,128)S(1)}, u32[]{:S(2)}, u32[]{:S(2)}) collective-permute-start(f32[8,128,256]{2,1,0:T(8,128)S(1)} %get-tuple-element.93), channel_id=1, source_target_pairs={{0,1},{1,0},{2,3},{3,2},{4,5},{5,4},{6,7},{7,6},{8,9},{9,8},{10,11... | collective-permute-start | bytes 3145736 | tf_op jit(solution)/shard_map/ppermute | solution.py:263
  118.5 8.1 %collective-permute-start.10 = (bf16[2,128,1024]{2,1,0:T(8,128)(2,1)}, bf16[2,128,1024]{2,1,0:T(8,128)(2,1)S(1)}, u32[]{:S(2)}, u32[]{:S(2)}) collective-permute-start(bf16[2,128,1024]{2,1,0:T(8,128)(2,1)} %pad_maximum_fusion.1.refs_1_), channel_id=1, source_target_pairs={{0,1},{1,0},{2,3},{3,2},{4,5},{5,4},{6,7},{7,6},{8,9},{9,8},{10,11... | collective-permute-start | bytes 1572872 | tf_op jit(solution)/shard_map/ppermute | solution.py:263
  118.6 8.1 %collective-permute-start.11 = (bf16[2,128,1024]{2,1,0:T(8,128)(2,1)}, bf16[2,128,1024]{2,1,0:T(8,128)(2,1)S(1)}, u32[]{:S(2)}, u32[]{:S(2)}) collective-permute-start(bf16[2,128,1024]{2,1,0:T(8,128)(2,1)} %collective-permute-done.3.refs_2_), channel_id=1, source_target_pairs={{0,1},{1,0},{2,3},{3,2},{4,5},{5,4},{6,7},{7,6},{8,9},{9,8},{10,11... | collective-permute-start | bytes 1572872 | tf_op jit(solution)/shard_map/ppermute | solution.py:263
  119.0 10.3 %collective-permute-start.12 = (bf16[2,128,1024]{2,1,0:T(8,128)(2,1)}, bf16[2,128,1024]{2,1,0:T(8,128)(2,1)S(1)}, u32[]{:S(2)}, u32[]{:S(2)}) collective-permute-start(bf16[2,128,1024]{2,1,0:T(8,128)(2,1)} %collective-permute-done.6.refs_3_), channel_id=1, source_target_pairs={{0,1},{1,0},{2,3},{3,2},{4,5},{5,4},{6,7},{7,6},{8,9},{9,8},{10,11... | collective-permute-start | bytes 1572872 | tf_op jit(solution)/shard_map/ppermute | solution.py:263
  122.2 21.4 %all-to-all-start.1 = ((bf16[8,128,256]{2,1,0:T(8,128)(2,1)}), bf16[8,128,256]{2,1,0:T(8,128)(2,1)S(1)}, u32[]{:S(2)}, u32[]{:S(2)}) async-start(bf16[8,128,256]{2,1,0:T(8,128)(2,1)} %add_convert_fusion), calls=%async_computation.1 | async-start | bytes 1048576 | tf_op jit(solution)/shard_map/all_to_all | solution.py:305
  125.7 27.6 %copy-start.20 = (bf16[128,256]{1,0:T(8,128)(2,1)S(1)}, bf16[128,256]{1,0:T(8,128)(2,1)}, u32[]{:S(2)}) copy-start(bf16[128,256]{1,0:T(8,128)(2,1)} %get-tuple-element.104) | copy-start | bytes 196612
  125.7 29.7 %copy-start.19 = (bf16[128,256]{1,0:T(8,128)(2,1)S(1)}, bf16[128,256]{1,0:T(8,128)(2,1)}, u32[]{:S(2)}) copy-start(bf16[128,256]{1,0:T(8,128)(2,1)} %get-tuple-element.105) | copy-start | bytes 196612
  125.7 32.1 %copy-start.18 = (bf16[128,256]{1,0:T(8,128)(2,1)S(1)}, bf16[128,256]{1,0:T(8,128)(2,1)}, u32[]{:S(2)}) copy-start(bf16[128,256]{1,0:T(8,128)(2,1)} %get-tuple-element.106) | copy-start | bytes 196612
  125.7 36.4 %copy-start.17 = (bf16[128,256]{1,0:T(8,128)(2,1)S(1)}, bf16[128,256]{1,0:T(8,128)(2,1)}, u32[]{:S(2)}) copy-start(bf16[128,256]{1,0:T(8,128)(2,1)} %get-tuple-element.107) | copy-start | bytes 196612
  125.7 39.4 %copy-start.16 = (bf16[128,256]{1,0:T(8,128)(2,1)S(1)}, bf16[128,256]{1,0:T(8,128)(2,1)}, u32[]{:S(2)}) copy-start(bf16[128,256]{1,0:T(8,128)(2,1)} %get-tuple-element.108) | copy-start | bytes 196612
  125.7 41.5 %copy-start.15 = (bf16[128,256]{1,0:T(8,128)(2,1)S(1)}, bf16[128,256]{1,0:T(8,128)(2,1)}, u32[]{:S(2)}) copy-start(bf16[128,256]{1,0:T(8,128)(2,1)} %get-tuple-element.109) | copy-start | bytes 196612
  125.7 14.6 %collective-permute-start.15 = (bf16[2,128,1024]{2,1,0:T(8,128)(2,1)}, bf16[2,128,1024]{2,1,0:T(8,128)(2,1)S(1)}, u32[]{:S(2)}, u32[]{:S(2)}) collective-permute-start(bf16[2,128,1024]{2,1,0:T(8,128)(2,1)} %collective-permute-done.3.refs_2_), channel_id=1, source_target_pairs={{0,16},{16,32},{32,48},{48,0},{1,17},{17,33},{33,49},{49,1},{2,18}... | collective-permute-start | bytes 1572872 | tf_op jit(solution)/shard_map/ppermute | solution.py:298
  125.9 4.1 %collective-permute-start.13 = (bf16[2,128,1024]{2,1,0:T(8,128)(2,1)}, bf16[2,128,1024]{2,1,0:T(8,128)(2,1)S(1)}, u32[]{:S(2)}, u32[]{:S(2)}) collective-permute-start(bf16[2,128,1024]{2,1,0:T(8,128)(2,1)} %collective-permute-done.7.refs_4_), channel_id=1, source_target_pairs={{0,1},{1,0},{2,3},{3,2},{4,5},{5,4},{6,7},{7,6},{8,9},{9,8},{10,11... | collective-permute-start | bytes 1572872 | tf_op jit(solution)/shard_map/ppermute | solution.py:263
  126.6 48.2 %copy-start.5 = (bf16[2,128,1024]{2,1,0:T(8,128)(2,1)}, bf16[2,128,1024]{2,1,0:T(8,128)(2,1)S(1)}, u32[]{:S(2)}) copy-start(bf16[2,128,1024]{2,1,0:T(8,128)(2,1)S(1)} %collective-permute-done.10.refs_9_) | copy-start | bytes 1572868
  126.6 3.5 %collective-permute-start.14 = (bf16[2,128,1024]{2,1,0:T(8,128)(2,1)S(1)}, bf16[2,128,1024]{2,1,0:T(8,128)(2,1)S(1)}, u32[]{:S(2)}, u32[]{:S(2)}) collective-permute-start(bf16[2,128,1024]{2,1,0:T(8,128)(2,1)S(1)} %copy-done.4), channel_id=1, source_target_pairs={{0,1},{1,0},{2,3},{3,2},{4,5},{5,4},{6,7},{7,6},{8,9},{9,8},{10,11... | collective-permute-start | bytes 1572872 | tf_op jit(solution)/shard_map/ppermute | solution.py:263
  126.7 48.1 %copy-start.6 = (bf16[2,128,1024]{2,1,0:T(8,128)(2,1)}, bf16[2,128,1024]{2,1,0:T(8,128)(2,1)S(1)}, u32[]{:S(2)}) copy-start(bf16[2,128,1024]{2,1,0:T(8,128)(2,1)S(1)} %collective-permute-done.11.refs_10_) | copy-start | bytes 1572868
  126.7 13.7 %collective-permute-start.16 = (bf16[2,128,1024]{2,1,0:T(8,128)(2,1)S(1)}, bf16[2,128,1024]{2,1,0:T(8,128)(2,1)S(1)}, u32[]{:S(2)}, u32[]{:S(2)}) collective-permute-start(bf16[2,128,1024]{2,1,0:T(8,128)(2,1)S(1)} %copy-done.4), channel_id=1, source_target_pairs={{0,48},{16,0},{32,16},{48,32},{1,49},{17,1},{33,17},{49,33},{2,50}... | collective-permute-start | bytes 1572872 | tf_op jit(solution)/shard_map/ppermute | solution.py:299
  129.3 11.0 %copy-start.7 = (bf16[2,128,1024]{2,1,0:T(8,128)(2,1)}, bf16[2,128,1024]{2,1,0:T(8,128)(2,1)S(1)}, u32[]{:S(2)}) copy-start(bf16[2,128,1024]{2,1,0:T(8,128)(2,1)S(1)} %collective-permute-done.12.refs_11_) | copy-start | bytes 1572868
  129.3 11.9 %collective-permute-start.9 = (bf16[2,128,1024]{2,1,0:T(8,128)(2,1)}, bf16[2,128,1024]{2,1,0:T(8,128)(2,1)}, u32[]{:S(2)}, u32[]{:S(2)}) collective-permute-start(bf16[2,128,1024]{2,1,0:T(8,128)(2,1)} %pad_maximum_fusion.refs_0_), channel_id=1, source_target_pairs={{0,1},{1,0},{2,3},{3,2},{4,5},{5,4},{6,7},{7,6},{8,9},{9,8},{10,11... | collective-permute-start | bytes 1572872 | tf_op jit(solution)/shard_map/ppermute | solution.py:263
  130.0 10.3 %copy-start.10 = (bf16[2,128,1024]{2,1,0:T(8,128)(2,1)}, bf16[2,128,1024]{2,1,0:T(8,128)(2,1)S(1)}, u32[]{:S(2)}) copy-start(bf16[2,128,1024]{2,1,0:T(8,128)(2,1)S(1)} %collective-permute-done.13.refs_12_) | copy-start | bytes 1572868
  130.0 10.3 %copy-start.11 = (bf16[2,128,1024]{2,1,0:T(8,128)(2,1)}, bf16[2,128,1024]{2,1,0:T(8,128)(2,1)S(1)}, u32[]{:S(2)}) copy-start(bf16[2,128,1024]{2,1,0:T(8,128)(2,1)S(1)} %collective-permute-done.14.refs_13_) | copy-start | bytes 1572868
  140.4 1.0 copy-start.8
  143.6 7.5 %copy-start.9 = (bf16[2,128,1024]{2,1,0:T(8,128)(2,1)S(1)}, bf16[2,128,1024]{2,1,0:T(8,128)(2,1)}, u32[]{:S(2)}) copy-start(bf16[2,128,1024]{2,1,0:T(8,128)(2,1)} %copy-done.8) | copy-start | bytes 1572868
  144.8 30.0 %all-to-all-start.2 = ((bf16[32,128,128]{2,1,0:T(8,128)(2,1)}), bf16[32,128,128]{2,1,0:T(8,128)(2,1)S(1)}, u32[]{:S(2)}, u32[]{:S(2)}) async-start(bf16[32,128,128]{2,1,0:T(8,128)(2,1)} %get-tuple-element.101), calls=%async_computation.2 | async-start | bytes 2097152 | tf_op jit(solution)/shard_map/all_to_all | solution.py:310
  151.1 38.8 %copy-start = (bf16[128,256]{1,0:T(8,128)(2,1)S(1)}, bf16[128,256]{1,0:T(8,128)(2,1)}, u32[]{:S(2)}) copy-start(bf16[128,256]{1,0:T(8,128)(2,1)} %get-tuple-element.112.refs_0_) | copy-start | bytes 196612
  151.2 22.8 %collective-permute-start.24 = (bf16[2,128,1024]{2,1,0:T(8,128)(2,1)S(1)}, bf16[2,128,1024]{2,1,0:T(8,128)(2,1)S(1)}, u32[]{:S(2)}, u32[]{:S(2)}) collective-permute-start(bf16[2,128,1024]{2,1,0:T(8,128)(2,1)S(1)} %copy-done.9), channel_id=1, source_target_pairs={{0,1},{1,0},{2,3},{3,2},{4,5},{5,4},{6,7},{7,6},{8,9},{9,8},{10,11... | collective-permute-start | bytes 1572872 | tf_op jit(solution)/shard_map/ppermute | solution.py:263
  151.5 23.3 %collective-permute-start.25 = (bf16[2,128,1024]{2,1,0:T(8,128)(2,1)}, bf16[2,128,1024]{2,1,0:T(8,128)(2,1)}, u32[]{:S(2)}, u32[]{:S(2)}) collective-permute-start(bf16[2,128,1024]{2,1,0:T(8,128)(2,1)} %copy-done.12), channel_id=1, source_target_pairs={{0,1},{1,0},{2,3},{3,2},{4,5},{5,4},{6,7},{7,6},{8,9},{9,8},{10,11... | collective-permute-start | bytes 1572872 | tf_op jit(solution)/shard_map/ppermute | solution.py:263
  151.8 6.1 %collective-permute-start.17 = (bf16[128,256]{1,0:T(8,128)(2,1)}, bf16[128,256]{1,0:T(8,128)(2,1)S(1)}, u32[]{:S(2)}, u32[]{:S(2)}) collective-permute-start(bf16[128,256]{1,0:T(8,128)(2,1)} %get-tuple-element.103), channel_id=1, source_target_pairs={{0,2},{2,4},{4,6},{6,8},{8,10},{10,12},{12,14},{14,0},{1,3},{3,5},... | collective-permute-start | bytes 196616 | tf_op jit(solution)/shard_map/ppermute | solution.py:312
  153.3 8.8 %collective-permute-start.18 = (bf16[128,256]{1,0:T(8,128)(2,1)S(1)}, bf16[128,256]{1,0:T(8,128)(2,1)S(1)}, u32[]{:S(2)}, u32[]{:S(2)}) collective-permute-start(bf16[128,256]{1,0:T(8,128)(2,1)S(1)} %copy-done.20), channel_id=1, source_target_pairs={{0,4},{2,6},{4,8},{6,10},{8,12},{10,14},{12,0},{14,2},{1,5},{3,7},... | collective-permute-start | bytes 196616 | tf_op jit(solution)/shard_map/ppermute | solution.py:312
  155.4 9.7 %collective-permute-start.19 = (bf16[128,256]{1,0:T(8,128)(2,1)S(1)}, bf16[128,256]{1,0:T(8,128)(2,1)S(1)}, u32[]{:S(2)}, u32[]{:S(2)}) collective-permute-start(bf16[128,256]{1,0:T(8,128)(2,1)S(1)} %copy-done.19), channel_id=1, source_target_pairs={{0,6},{2,8},{4,10},{6,12},{8,14},{10,0},{12,2},{14,4},{1,7},{3,9},... | collective-permute-start | bytes 196616 | tf_op jit(solution)/shard_map/ppermute | solution.py:312
  157.8 9.4 %collective-permute-start.20 = (bf16[128,256]{1,0:T(8,128)(2,1)S(1)}, bf16[128,256]{1,0:T(8,128)(2,1)S(1)}, u32[]{:S(2)}, u32[]{:S(2)}) collective-permute-start(bf16[128,256]{1,0:T(8,128)(2,1)S(1)} %copy-done.18), channel_id=1, source_target_pairs={{0,8},{2,10},{4,12},{6,14},{8,0},{10,2},{12,4},{14,6},{1,9},{3,11}... | collective-permute-start | bytes 196616 | tf_op jit(solution)/shard_map/ppermute | solution.py:312
  162.1 6.4 %collective-permute-start.21 = (bf16[128,256]{1,0:T(8,128)(2,1)S(1)}, bf16[128,256]{1,0:T(8,128)(2,1)S(1)}, u32[]{:S(2)}, u32[]{:S(2)}) collective-permute-start(bf16[128,256]{1,0:T(8,128)(2,1)S(1)} %copy-done.17), channel_id=1, source_target_pairs={{0,10},{2,12},{4,14},{6,0},{8,2},{10,4},{12,6},{14,8},{1,11},{3,13... | collective-permute-start | bytes 196616 | tf_op jit(solution)/shard_map/ppermute | solution.py:312
  165.1 6.3 %collective-permute-start.22 = (bf16[128,256]{1,0:T(8,128)(2,1)S(1)}, bf16[128,256]{1,0:T(8,128)(2,1)S(1)}, u32[]{:S(2)}, u32[]{:S(2)}) collective-permute-start(bf16[128,256]{1,0:T(8,128)(2,1)S(1)} %copy-done.16), channel_id=1, source_target_pairs={{0,12},{2,14},{4,0},{6,2},{8,4},{10,6},{12,8},{14,10},{1,13},{3,15... | collective-permute-start | bytes 196616 | tf_op jit(solution)/shard_map/ppermute | solution.py:312
  167.2 6.8 %collective-permute-start.23 = (bf16[128,256]{1,0:T(8,128)(2,1)S(1)}, bf16[128,256]{1,0:T(8,128)(2,1)S(1)}, u32[]{:S(2)}, u32[]{:S(2)}) collective-permute-start(bf16[128,256]{1,0:T(8,128)(2,1)S(1)} %copy-done.15), channel_id=1, source_target_pairs={{0,14},{2,0},{4,2},{6,4},{8,6},{10,8},{12,10},{14,12},{1,15},{3,1}... | collective-permute-start | bytes 196616 | tf_op jit(solution)/shard_map/ppermute | solution.py:312
  180.0 21.9 %all-to-all-start.3 = ((bf16[64,16,128]{2,1,0:T(8,128)(2,1)}), bf16[64,16,128]{2,1,0:T(8,128)(2,1)S(1)}, u32[]{:S(2)}, u32[]{:S(2)}) async-start(bf16[64,16,128]{2,1,0:T(8,128)(2,1)} %bitcast.19), calls=%async_computation.3 | async-start | bytes 524288 | tf_op jit(solution)/shard_map/all_to_all | solution.py:318
  (3 other events, 2.4 us)

commit v6 on v5

--- a/solution.py
+++ b/solution.py
@@ -13,6 +13,7 @@
 BLOCKS = NZ * NC
 LINKS = 8
 KV_HEADS = 4
+SIDE = NZ // 2 - 1
 MIB = 1 << 20
 SCALE = 1.0 / math.sqrt(HEAD)
 LOG2E = math.log2(math.e)
@@ -38,7 +39,7 @@
 def attention_kernel(
     links_ref, place_ref, rows_ref, other_ref, seg_cols_ref, seg_rows_ref, *refs
 ):
-    dq_refs, refs = refs[:NZ], refs[NZ:]
+    (keep_ref, across_ref, *ship_refs, give_ref), refs = refs[: SIDE + 3], refs[SIDE + 3 :]
     own_ref, away_ref, pair_ref, keys_t_ref, total_ref, near_ref, near_t_ref, dq_ref, sems = refs
     z, core = place_ref[1], place_ref[2]
 
@@ -94,7 +95,15 @@
 
     lax.fori_loop(1 - core, NZ, linked, 0)
 
-    copies = [pltpu.make_async_copy(dq_ref.at[s], dq_refs[s], sems.at[s]) for s in range(NZ)]
+    moves = [(0, keep_ref), (NZ // 2, across_ref)]
+    for k, ref in enumerate(ship_refs):
+        up, down = k + 1, NZ - 1 - k
+        moves.append((up + core * (down - up), ref))
+        moves.append((down + core * (up - down), give_ref.at[k]))
+    copies = [
+        pltpu.make_async_copy(dq_ref.at[slot], ref, sems.at[n])
+        for n, (slot, ref) in enumerate(moves)
+    ]
     for copy in copies:
         copy.start()
 
@@ -114,13 +123,14 @@
     smem = pl.BlockSpec(memory_space=pltpu.SMEM)
     return pl.pallas_call(
         attention_kernel,
-        out_shape=(pltpu.HBM((BLOCK, 2 * HEAD), jnp.bfloat16),) * NZ
+        out_shape=(pltpu.HBM((BLOCK, 2 * HEAD), jnp.bfloat16),) * (SIDE + 2)
+        + (pltpu.HBM((SIDE, BLOCK, 2 * HEAD), jnp.bfloat16),)
         + (
             jax.ShapeDtypeStruct((NZ, BLOCK, 2 * HEAD), jnp.float32),
             jax.ShapeDtypeStruct((NZ, BLOCK, 2 * HEAD), jnp.float32),
         ),
         in_specs=[smem, smem, vmem, vmem, vmem, vmem],
-        out_specs=(pl.BlockSpec(memory_space=pltpu.HBM),) * NZ + (vmem, vmem),
+        out_specs=(pl.BlockSpec(memory_space=pltpu.HBM),) * (SIDE + 3) + (vmem, vmem),
         scratch_shapes=[
             pltpu.VMEM((BLOCKS * BLOCK, 2 * HEAD), jnp.bfloat16),
             pltpu.VMEM((HEAD, BLOCKS * BLOCK), jnp.bfloat16),
@@ -140,6 +150,9 @@
 PARTS = tuple((shift, first) for shift in (0, -1, 1, 2) for first in (0, NX // 2))
 
 
+AHEAD = 2
+
+
 def weight_kernel(place_ref, grads_ref, *refs):
     count = len(PARTS)
     out_ref, held_ref, sems = refs[2 * count :]
@@ -148,11 +161,13 @@
         for side in range(NC):
             target = held_ref.at[p, :, pl.ds(side * BLOCK, BLOCK), :]
             copies.append(pltpu.make_async_copy(refs[side * count + p], target, sems.at[p, side]))
-    for copy in copies:
+    for copy in copies[: 2 * AHEAD]:
         copy.start()
     x, y, core = place_ref[0], place_ref[3], place_ref[2]
     total = None
     for p, (shift, first) in enumerate(PARTS):
+        for copy in copies[2 * (p + AHEAD) : 2 * (p + AHEAD + 1)]:
+            copy.start()
         copies[2 * p].wait()
         copies[2 * p + 1].wait()
         for s in range(NX // 2):
@@ -202,9 +217,9 @@
 def packed(queries, grads, keys, values):
     return pl.pallas_call(
         pack_kernel,
-        out_shape=pltpu.HBM((NZ, BLOCK, 6 * HEAD), jnp.bfloat16),
+        out_shape=jax.ShapeDtypeStruct((NZ, BLOCK, 6 * HEAD), jnp.bfloat16),
         in_specs=[pl.BlockSpec(memory_space=pltpu.HBM)] * 4,
-        out_specs=pl.BlockSpec(memory_space=pltpu.HBM),
+        out_specs=pl.BlockSpec(memory_space=pltpu.VMEM),
         scratch_shapes=[pltpu.SemaphoreType.DMA((4 * NZ,))],
         compiler_params=pltpu.CompilerParams(vmem_limit_bytes=16 * MIB),
         cost_estimate=pl.CostEstimate(flops=0, bytes_accessed=3 * MIB, transcendentals=0),
@@ -235,24 +250,31 @@
     )(partials)
 
 
-def join_kernel(place_ref, *refs):
-    out_ref = refs[-1]
-    z = place_ref[1]
-    for s in range(NZ):
-        column = lax.rem(z - s + NZ, NZ) * (2 * HEAD)
-        out_ref[:, pl.ds(pl.multiple_of(column, 2 * HEAD), 2 * HEAD)] = refs[s][...]
-
-
-def joined(place, pieces):
+def join_kernel(place_ref, keep_ref, across_ref, *refs):
+    direct_refs, swapped_ref, out_ref = refs[:SIDE], refs[SIDE], refs[SIDE + 1]
+    z, side = place_ref[1], 1 - 2 * place_ref[2]
+
+    def put(source, value):
+        column = lax.rem(source + NZ, NZ) * (2 * HEAD)
+        out_ref[:, pl.ds(pl.multiple_of(column, 2 * HEAD), 2 * HEAD)] = value
+
+    put(z, keep_ref[...])
+    put(z + NZ // 2, across_ref[...])
+    for k in range(SIDE):
+        put(z - side * (k + 1), direct_refs[k][0])
+        put(z + side * (k + 1), swapped_ref[k])
+
+
+def joined(place, keep, across, direct, swapped):
     vmem = pl.BlockSpec(memory_space=pltpu.VMEM)
     return pl.pallas_call(
         join_kernel,
         out_shape=jax.ShapeDtypeStruct((BLOCK, NZ * 2 * HEAD), jnp.bfloat16),
-        in_specs=[pl.BlockSpec(memory_space=pltpu.SMEM)] + [vmem] * NZ,
+        in_specs=[pl.BlockSpec(memory_space=pltpu.SMEM)] + [vmem] * (SIDE + 3),
         out_specs=vmem,
         compiler_params=pltpu.CompilerParams(vmem_limit_bytes=16 * MIB),
         cost_estimate=pl.CostEstimate(flops=0, bytes_accessed=MIB, transcendentals=0),
-    )(place, *pieces)
+    )(place, keep, across, *direct, swapped)
 
 
 def ring(size, shift):
@@ -289,10 +311,11 @@
     other = swap_cores(rows[..., 4 * HEAD :])
     before = (before, lax.ppermute(mine[1], "y", ring(NY, 1)))
     after = (lax.ppermute(mine[0], "y", ring(NY, -1)), after)
-    *dq, own, away = attention_grads(block_links[0], place, rows, other, seg_cols, seg_rows)
-
-    dq, own, away, mine, before, after = lax.optimization_barrier(
-        (dq, own, away, mine, before, after)
+    keep, across, *ship, give, own, away = attention_grads(
+        block_links[0], place, rows, other, seg_cols, seg_rows
+    )
+    keep, across, ship, give, own, away, mine, before, after = lax.optimization_barrier(
+        (keep, across, ship, give, own, away, mine, before, after)
     )
     far = (
         lax.ppermute(before[0], "y", ring(NY, 1)),
@@ -303,17 +326,26 @@
 
     pair = (own + swap_cores(away)).astype(bf16)
     pair = lax.all_to_all(pair, "z", split_axis=0, concat_axis=0, tiled=True)
-    dq, pair, inputs_other, far = lax.optimization_barrier((dq, pair, inputs_other, far))
+    given = swap_cores(give)
+    across, ship, given, pair, inputs_other, far = lax.optimization_barrier(
+        (across, ship, given, pair, inputs_other, far)
+    )
     far_other = tuple(swap_cores(a) for a in far)
     key_grads, value_grads, chunks = pair_grads(pair)
 
     grads = lax.all_to_all(chunks, ("x", "y", "c"), split_axis=0, concat_axis=0, tiled=True)
-    for s in (1, 7, 2, 6, 3, 5, 4):
-        dq[s] = lax.ppermute(dq[s], "z", ring(NZ, s))
-    grads, dq, far_other = lax.optimization_barrier((grads, dq, far_other))
+    direct = []
+    for k in range(SIDE):
+        hops = [((i, 0), ((i + k + 1) % NZ, 0)) for i in range(NZ)]
+        hops += [((i, 1), ((i - k - 1) % NZ, 1)) for i in range(NZ)]
+        hops = [tuple(a * NC + b for a, b in hop) for hop in hops]
+        direct.append(lax.ppermute(jnp.stack([ship[k], given[k]]), ("z", "c"), hops))
+    across = lax.ppermute(across, "z", ring(NZ, NZ // 2))
+    grads, direct, across, far_other = lax.optimization_barrier((grads, direct, across, far_other))
     part = weight_grads_part(place, grads, inputs_own + far, inputs_other + far_other)
 
-    query_grads = joined(place, dq)
+    swapped = swap_cores(jnp.stack([a[1] for a in direct]))
+    query_grads = joined(place, keep, across, direct, swapped)
     part = part.reshape(NY * NZ * NC, -1, HEAD)
     part = lax.all_to_all(part, ("y", "z", "c"), split_axis=0, concat_axis=0, tiled=True)
     part = part.reshape(NY, NZ, NC, -1, HEAD).astype(jnp.float32)

time: 203 us -> 160 us (0.79)
  Pallas kernels: 69.6 us -> 24.5 us
  waiting for transfers between devices: 60.4 us -> 68.3 us
  starting transfers between devices: 64.4 us -> 58.7 us
    pallas_call x1, Pallas kernels: 49 us -> 2.87 us  [packed(): pl.pallas_call(pack_kernel, out_shape=jax.ShapeDtypeStruct((NZ, BLOCK, 6...]
    ppermute x7 -> x4, starting transfers between devices: 15.8 us -> 8.09 us  [the longest x3 5.67 us: local(): lax.ppermute(jnp.stack([ship[k], given[k]]), ('z', 'c'), hops)]
    ppermute x7 -> x4, waiting for transfers between devices: 6.44 us -> 12.1 us  [the longest x1 8.24 us: local(): across = lax.ppermute(across, 'z', ring(NZ, NZ // 2))]
    ppermute x10 -> x12, waiting for transfers between devices: 2.19 us -> 5.21 us  [swap_cores(): return lax.ppermute(a, 'c', [(0, 1), (1, 0)])]
    all_to_all x1, starting transfers between devices: 9.93 us -> 12.4 us  [local(): lax.all_to_all(part, ('y', 'z', 'c'), split_axis=0, concat_axis=0, tiled=...]
    ppermute x10 -> x12, starting transfers between devices: 7.08 us -> 7.63 us  [swap_cores(): return lax.ppermute(a, 'c', [(0, 1), (1, 0)])]
  transfers between devices with their start and end apart: 30 -> 29, of which waited for: 14 -> 15; matrix products, arithmetic and copies ran while one was open for 1% -> 2% of each run, Pallas kernels for 7% -> 9%
where the time goes in v6:
time: 160 us; the launch traced here: 159 us
  waiting for transfers between devices  68.3 us (43%)
  starting transfers between devices  58.7 us (37%)
  Pallas kernels  24.5 us (15%)
  other arithmetic  3.65 us (2%)
  local copies, waits for them, and re-layouts  2.86 us (2%)
    pallas_call x1, Pallas kernels, attention_grads(): pl.pallas_call(attention_kernel, out_shape=(pltpu.HBM((BLOCK, 2 * HEAD),...  12.8 us
    all_to_all x1, starting transfers between devices, local(): lax.all_to_all(part, ('y', 'z', 'c'), split_axis=0, concat_axis=0, tiled=...  12.4 us
    ppermute x1, waiting for transfers between devices, local(): lax.ppermute(before[0], 'y', ring(NY, 1))  10.2 us
    ppermute x3, waiting for transfers between devices, local(): lax.ppermute(a, 'x', ring(NX, s))  10.2 us
    all_to_all x1, starting transfers between devices, local(): lax.all_to_all(outgoing, 'z', split_axis=0, concat_axis=0, tiled=True)  9.16 us
    ppermute x1, waiting for transfers between devices, local(): lax.ppermute(mine[1], 'y', ring(NY, -1))  9.12 us
    all_to_all x1, waiting for transfers between devices, local(): lax.all_to_all(part, ('y', 'z', 'c'), split_axis=0, concat_axis=0, tiled=...  8.9 us
    ppermute x1, waiting for transfers between devices, local(): across = lax.ppermute(across, 'z', ring(NZ, NZ // 2))  8.24 us
  transfers between devices with their start and end apart: 29, of which 15 were waited for; matrix products, arithmetic and copies ran while one was open for 2% of the time, Pallas kernels for 9%

profile of v6, /device:TPU:1, one launch (start us, length us, event | category | flops | bytes accessed | tf_op | source)
XLA Modules:
  0.0 159.0 jit_solution(6898788546284264809)
XLA Ops:
  0.6 2.9 %shard_map.110 = bf16[8,128,768]{2,1,0:T(8,128)(2,1)} custom-call(bf16[128,2048]{1,0:T(8,128)(2,1)} %bitcast.41, bf16[128,2048]{1,0:T(8,128)(2,1)} %bitcast.42, bf16[128,512]{1,0:T(8,128)(2,1)} %bitcast.47, bf16[128,512]{1,0:T(8,128)(2,1)} %bitcast.48), custom_call_target="tpu_custom_call" | custom-call | bytes 3145728 | tf_op jit(solution)/shard_map/pallas_call | solution.py:218
  3.5 9.2 %all-to-all-start = ((bf16[8,128,768]{2,1,0:T(8,128)(2,1)}), bf16[8,128,768]{2,1,0:T(8,128)(2,1)S(1)}, u32[]{:S(2)}, u32[]{:S(2)}) async-start(bf16[8,128,768]{2,1,0:T(8,128)(2,1)} %shard_map.110), calls=%async_computation | async-start | bytes 3145728 | tf_op jit(solution)/shard_map/all_to_all | solution.py:305
  12.8 2.8 %collective-permute-start.1 = (bf16[128,1024]{1,0:T(8,128)(2,1)S(1)}, bf16[128,1024]{1,0:T(8,128)(2,1)S(1)}, u32[]{:S(2)}, u32[]{:S(2)}) collective-permute-start(bf16[128,1024]{1,0:T(8,128)(2,1)S(1)} %get-tuple-element.109), channel_id=1, source_target_pairs={{0,128},{64,192},{128,0},{192,64},{1,129},{65,193},{129,1},{193,65... | collective-permute-start | bytes 786440 | tf_op jit(solution)/shard_map/ppermute | solution.py:299
  15.6 0.9 collective-permute-start.2
  16.5 0.6 collective-permute-start
  17.1 4.1 %collective-permute-done.1 = bf16[128,1024]{1,0:T(8,128)(2,1)S(1)} collective-permute-done((bf16[128,1024]{1,0:T(8,128)(2,1)S(1)}, bf16[128,1024]{1,0:T(8,128)(2,1)S(1)}, u32[]{:S(2)}, u32[]{:S(2)}) %collective-permute-start.1) | collective-permute-done | bytes 262176 | tf_op jit(solution)/shard_map/ppermute | solution.py:299
  21.2 6.1 %collective-permute-done.2 = bf16[128,1024]{1,0:T(8,128)(2,1)S(1)} collective-permute-done((bf16[128,1024]{1,0:T(8,128)(2,1)S(1)}, bf16[128,1024]{1,0:T(8,128)(2,1)S(1)}, u32[]{:S(2)}, u32[]{:S(2)}) %collective-permute-start.2) | collective-permute-done | bytes 262176 | tf_op jit(solution)/shard_map/ppermute | solution.py:299
  27.3 0.8 pad_maximum_fusion.1.refs_1_
  28.1 2.7 %collective-permute-start.4 = (bf16[2,128,1024]{2,1,0:T(8,128)(2,1)}, bf16[2,128,1024]{2,1,0:T(8,128)(2,1)S(1)}, u32[]{:S(2)}, u32[]{:S(2)}) collective-permute-start(bf16[2,128,1024]{2,1,0:T(8,128)(2,1)} %pad_maximum_fusion.1.refs_1_), channel_id=1, source_target_pairs={{0,48},{16,0},{32,16},{48,32},{1,49},{17,1},{33,17},{49,33},{2,50}... | collective-permute-start | bytes 1572872 | tf_op jit(solution)/shard_map/ppermute | solution.py:302
  30.9 0.8 pad_maximum_fusion.refs_0_
  31.7 9.1 %collective-permute-done.4.refs_5_ = bf16[2,128,1024]{2,1,0:T(8,128)(2,1)S(1)} collective-permute-done((bf16[2,128,1024]{2,1,0:T(8,128)(2,1)}, bf16[2,128,1024]{2,1,0:T(8,128)(2,1)S(1)}, u32[]{:S(2)}, u32[]{:S(2)}) %collective-permute-start.4) | collective-permute-done | bytes 524320 | tf_op jit(solution)/shard_map/ppermute | solution.py:302
  40.9 4.0 %collective-permute-done.3.refs_2_ = bf16[2,128,1024]{2,1,0:T(8,128)(2,1)} collective-permute-done((bf16[2,128,1024]{2,1,0:T(8,128)(2,1)}, bf16[2,128,1024]{2,1,0:T(8,128)(2,1)}, u32[]{:S(2)}, u32[]{:S(2)}) %collective-permute-start.3) | collective-permute-done | bytes 524320 | tf_op jit(solution)/shard_map/ppermute | solution.py:302
  44.8 6.1 %all-to-all-done.rows_ref = bf16[8,128,768]{2,1,0:T(8,128)(2,1)S(1)} async-done(((bf16[8,128,768]{2,1,0:T(8,128)(2,1)}), bf16[8,128,768]{2,1,0:T(8,128)(2,1)S(1)}, u32[]{:S(2)}, u32[]{:S(2)}) %all-to-all-start) | async-done | bytes 1572896 | tf_op jit(solution)/shard_map/all_to_all | solution.py:305
  51.3 0.8 slice.29
  52.1 2.7 %collective-permute-start.5 = (bf16[8,128,256]{2,1,0:T(8,128)(2,1)}, bf16[8,128,256]{2,1,0:T(8,128)(2,1)S(1)}, u32[]{:S(2)}, u32[]{:S(2)}) collective-permute-start(bf16[8,128,256]{2,1,0:T(8,128)(2,1)} %slice.29), channel_id=1, source_target_pairs={{0,1},{1,0},{2,3},{3,2},{4,5},{5,4},{6,7},{7,6},{8,9},{9,8},{10,11... | collective-permute-start | bytes 1572872 | tf_op jit(solution)/shard_map/ppermute | solution.py:285
  54.8 1.3 collective-permute-start.6
  56.1 1.4 collective-permute-start.7
  57.7 12.8 %shard_map.111 = (bf16[128,256]{1,0:T(8,128)(2,1)}, bf16[128,256]{1,0:T(8,128)(2,1)}, bf16[128,256]{1,0:T(8,128)(2,1)}, bf16[128,256]{1,0:T(8,128)(2,1)}, bf16[1...) custom-call(s32[16,8]{1,0:T(8,128)S(1)} %copy.14.links_ref, ...), custom_call_target="tpu_custom_call" | custom-call | flops 4000000000 | bytes 8388608 | tf_op jit(solution)/shard_map/pallas_call | solution.py:124
  70.5 1.8 %collective-permute-start.9 = (f32[8,128,256]{2,1,0:T(8,128)S(1)}, f32[8,128,256]{2,1,0:T(8,128)S(1)}, u32[]{:S(2)}, u32[]{:S(2)}) collective-permute-start(f32[8,128,256]{2,1,0:T(8,128)S(1)} %get-tuple-element.78), channel_id=1, source_target_pairs={{0,1},{1,0},{2,3},{3,2},{4,5},{5,4},{6,7},{7,6},{8,9},{9,8},{10,11... | collective-permute-start | bytes 3145736 | tf_op jit(solution)/shard_map/ppermute | solution.py:285
  72.4 0.4 collective-permute-start.11
  73.0 2.2 %collective-permute-done.9 = f32[8,128,256]{2,1,0:T(8,128)S(1)} collective-permute-done((f32[8,128,256]{2,1,0:T(8,128)S(1)}, f32[8,128,256]{2,1,0:T(8,128)S(1)}, u32[]{:S(2)}, u32[]{:S(2)}) %collective-permute-start.9) | collective-permute-done | bytes 1048608 | tf_op jit(solution)/shard_map/ppermute | solution.py:285
  75.1 0.9 add_convert_fusion
  76.1 3.5 %all-to-all-start.1 = ((bf16[8,128,256]{2,1,0:T(8,128)(2,1)}), bf16[8,128,256]{2,1,0:T(8,128)(2,1)S(1)}, u32[]{:S(2)}, u32[]{:S(2)}) async-start(bf16[8,128,256]{2,1,0:T(8,128)(2,1)} %add_convert_fusion), calls=%async_computation.1 | async-start | bytes 1048576 | tf_op jit(solution)/shard_map/all_to_all | solution.py:328
  79.6 0.5 collective-permute-start.8
  80.1 1.0 collective-permute-done.8
  81.1 0.4 collective-permute-start.13
  81.6 0.5 collective-permute-start.15
  82.1 1.7 %collective-permute-start.17 = (bf16[2,128,1024]{2,1,0:T(8,128)(2,1)S(1)}, bf16[2,128,1024]{2,1,0:T(8,128)(2,1)}, u32[]{:S(2)}, u32[]{:S(2)}) collective-permute-start(bf16[2,128,1024]{2,1,0:T(8,128)(2,1)S(1)} %copy-done.4), channel_id=1, source_target_pairs={{0,48},{16,0},{32,16},{48,32},{1,49},{17,1},{33,17},{49,33},{2,50}... | collective-permute-start | bytes 1572872 | tf_op jit(solution)/shard_map/ppermute | solution.py:322
  83.8 0.9 collective-permute-done.14.refs_12_
  84.8 10.2 %collective-permute-done.16.refs_6_ = bf16[2,128,1024]{2,1,0:T(8,128)(2,1)} collective-permute-done((bf16[2,128,1024]{2,1,0:T(8,128)(2,1)}, bf16[2,128,1024]{2,1,0:T(8,128)(2,1)}, u32[]{:S(2)}, u32[]{:S(2)}) %collective-permute-start.16) | collective-permute-done | bytes 524320 | tf_op jit(solution)/shard_map/ppermute | solution.py:321
  95.0 0.6 collective-permute-done.17.refs_7_
  95.6 1.9 %all-to-all-done.1.partials_ref = bf16[8,128,256]{2,1,0:T(8,128)(2,1)S(1)} async-done(((bf16[8,128,256]{2,1,0:T(8,128)(2,1)}), bf16[8,128,256]{2,1,0:T(8,128)(2,1)S(1)}, u32[]{:S(2)}, u32[]{:S(2)}) %all-to-all-start.1) | async-done | bytes 524320 | tf_op jit(solution)/shard_map/all_to_all | solution.py:328
  97.5 1.2 shard_map.112
  98.7 6.4 %all-to-all-start.2 = ((bf16[32,128,128]{2,1,0:T(8,128)(2,1)}), bf16[32,128,128]{2,1,0:T(8,128)(2,1)S(1)}, u32[]{:S(2)}, u32[]{:S(2)}) async-start(bf16[32,128,128]{2,1,0:T(8,128)(2,1)} %get-tuple-element.86), calls=%async_computation.2 | async-start | bytes 2097152 | tf_op jit(solution)/shard_map/all_to_all | solution.py:336
  105.7 0.9 pad_maximum_fusion.5
  106.6 4.4 %collective-permute-start.20 = (bf16[2,128,256]{2,1,0:T(8,128)(2,1)S(1)}, bf16[2,128,256]{2,1,0:T(8,128)(2,1)S(1)}, u32[]{:S(2)}, u32[]{:S(2)}) collective-permute-start(bf16[2,128,256]{2,1,0:T(8,128)(2,1)S(1)} %pad_maximum_fusion.5), channel_id=1, source_target_pairs={{0,6},{2,8},{4,10},{6,12},{8,14},{10,0},{12,2},{14,4},{1,11},{3,13... | collective-permute-start | bytes 393224 | tf_op jit(solution)/shard_map/ppermute | solution.py:342
  111.1 1.2 collective-permute-start.19
  112.3 2.4 %collective-permute-start.21 = (bf16[128,256]{1,0:T(8,128)(2,1)}, bf16[128,256]{1,0:T(8,128)(2,1)S(1)}, u32[]{:S(2)}, u32[]{:S(2)}) collective-permute-start(bf16[128,256]{1,0:T(8,128)(2,1)} %get-tuple-element.91), channel_id=1, source_target_pairs={{0,8},{2,10},{4,12},{6,14},{8,0},{10,2},{12,4},{14,6},{1,9},{3,11}... | collective-permute-start | bytes 196616 | tf_op jit(solution)/shard_map/ppermute | solution.py:343
  114.7 8.2 %collective-permute-done.21.across_ref = bf16[128,256]{1,0:T(8,128)(2,1)S(1)} collective-permute-done((bf16[128,256]{1,0:T(8,128)(2,1)}, bf16[128,256]{1,0:T(8,128)(2,1)S(1)}, u32[]{:S(2)}, u32[]{:S(2)}) %collective-permute-start.21) | collective-permute-done | bytes 65568 | tf_op jit(solution)/shard_map/ppermute | solution.py:343
  123.0 3.8 %collective-permute-done.18.refs_0_ = bf16[2,128,256]{2,1,0:T(8,128)(2,1)S(1)} collective-permute-done((bf16[2,128,256]{2,1,0:T(8,128)(2,1)S(1)}, bf16[2,128,256]{2,1,0:T(8,128)(2,1)S(1)}, u32[]{:S(2)}, u32[]{:S(2)}) %collective-permute-start.18) | collective-permute-done | bytes 131104 | tf_op jit(solution)/shard_map/ppermute | solution.py:342
  126.8 0.8 copy-done.11
  127.6 6.2 %shard_map.114 = bf16[1024,128]{1,0:T(8,128)(2,1)} custom-call(s32[4]{0:T(128)S(1)} %pad_add_fusion.place_ref, bf16[32,128,128]{2,1,0:T(8,128)(2,1)S(1)} %all-to-all-done.2.grads_ref, bf16[2,128,1024]{2,1,0:T(8,128)(2,1)} %pad_maximum_fusion.refs_0_, bf16[2,128,1024]{2,1,0:T(8,128)(2,1)} %pad_maximum_fusion.1.refs_1_, ...), custom_call_target="tpu_custom_call" | custom-call | flops 1100000000 | bytes 9437184 | tf_op jit(solution)/shard_map/pallas_call | solution.py:184
  133.8 12.4 %all-to-all-start.3 = ((bf16[64,16,128]{2,1,0:T(8,128)(2,1)}), bf16[64,16,128]{2,1,0:T(8,128)(2,1)S(1)}, u32[]{:S(2)}, u32[]{:S(2)}) async-start(bf16[64,16,128]{2,1,0:T(8,128)(2,1)} %bitcast.22), calls=%async_computation.3 | async-start | bytes 524288 | tf_op jit(solution)/shard_map/all_to_all | solution.py:350
  146.3 0.5 collective-permute-start.24
  146.9 1.1 collective-permute-done.24.refs_3_
  147.9 1.4 shard_map.113
  149.3 8.9 %all-to-all-done.3 = bf16[64,16,128]{2,1,0:T(8,128)(2,1)S(1)} async-done(((bf16[64,16,128]{2,1,0:T(8,128)(2,1)}), bf16[64,16,128]{2,1,0:T(8,128)(2,1)S(1)}, u32[]{:S(2)}, u32[]{:S(2)}) %all-to-all-start.3) | async-done | bytes 262176 | tf_op jit(solution)/shard_map/all_to_all | solution.py:350
  158.3 0.6 copy_bitcast_fusion
  (68 shorter events, 1.8 us)
Async XLA Ops:
  3.5 9.2 %copy-start.2 = (bf16[1,128,4096]{2,1,0:T(8,128)(2,1)S(1)}, bf16[1,128,4096]{2,1,0:T(8,128)(2,1)}, u32[]{:S(2)}) copy-start(bf16[1,128,4096]{2,1,0:T(8,128)(2,1)} %param.7) | copy-start | bytes 3145732
  3.5 47.4 %all-to-all-start = ((bf16[8,128,768]{2,1,0:T(8,128)(2,1)}), bf16[8,128,768]{2,1,0:T(8,128)(2,1)S(1)}, u32[]{:S(2)}, u32[]{:S(2)}) async-start(bf16[8,128,768]{2,1,0:T(8,128)(2,1)} %shard_map.110), calls=%async_computation | async-start | bytes 3145728 | tf_op jit(solution)/shard_map/all_to_all | solution.py:305
  12.8 38.2 %copy-start.1 = (s32[1,2048]{1,0:T(1,128)S(1)}, s32[1,2048]{1,0:T(1,128)}, u32[]{:S(2)}) copy-start(s32[1,2048]{1,0:T(1,128)} %param.13) | copy-start | bytes 24580
  12.8 8.4 %collective-permute-start.1 = (bf16[128,1024]{1,0:T(8,128)(2,1)S(1)}, bf16[128,1024]{1,0:T(8,128)(2,1)S(1)}, u32[]{:S(2)}, u32[]{:S(2)}) collective-permute-start(bf16[128,1024]{1,0:T(8,128)(2,1)S(1)} %get-tuple-element.109), channel_id=1, source_target_pairs={{0,128},{64,192},{128,0},{192,64},{1,129},{65,193},{129,1},{193,65... | collective-permute-start | bytes 786440 | tf_op jit(solution)/shard_map/ppermute | solution.py:299
  15.6 11.7 %collective-permute-start.2 = (bf16[128,1024]{1,0:T(8,128)(2,1)S(1)}, bf16[128,1024]{1,0:T(8,128)(2,1)S(1)}, u32[]{:S(2)}, u32[]{:S(2)}) collective-permute-start(bf16[128,1024]{1,0:T(8,128)(2,1)S(1)} %get-tuple-element.112), channel_id=1, source_target_pairs={{0,192},{64,0},{128,64},{192,128},{1,193},{65,1},{129,65},{193,129... | collective-permute-start | bytes 786440 | tf_op jit(solution)/shard_map/ppermute | solution.py:299
  16.5 14.4 %collective-permute-start = (bf16[128,1024]{1,0:T(8,128)(2,1)S(1)}, bf16[128,1024]{1,0:T(8,128)(2,1)S(1)}, u32[]{:S(2)}, u32[]{:S(2)}) collective-permute-start(bf16[128,1024]{1,0:T(8,128)(2,1)S(1)} %get-tuple-element.110), channel_id=1, source_target_pairs={{0,64},{64,128},{128,192},{192,0},{1,65},{65,129},{129,193},{193,1... | collective-permute-start | bytes 786440 | tf_op jit(solution)/shard_map/ppermute | solution.py:299
  28.1 12.7 %collective-permute-start.4 = (bf16[2,128,1024]{2,1,0:T(8,128)(2,1)}, bf16[2,128,1024]{2,1,0:T(8,128)(2,1)S(1)}, u32[]{:S(2)}, u32[]{:S(2)}) collective-permute-start(bf16[2,128,1024]{2,1,0:T(8,128)(2,1)} %pad_maximum_fusion.1.refs_1_), channel_id=1, source_target_pairs={{0,48},{16,0},{32,16},{48,32},{1,49},{17,1},{33,17},{49,33},{2,50}... | collective-permute-start | bytes 1572872 | tf_op jit(solution)/shard_map/ppermute | solution.py:302
  30.9 26.6 %copy-start.14 = (s32[1,16,8]{1,2,0:T(8,128)S(1)}, s32[1,16,8]{1,2,0:T(8,128)}, u32[]{:S(2)}) copy-start(s32[1,16,8]{1,2,0:T(8,128)} %param.12) | copy-start | bytes 1540
  31.7 13.1 %collective-permute-start.3 = (bf16[2,128,1024]{2,1,0:T(8,128)(2,1)}, bf16[2,128,1024]{2,1,0:T(8,128)(2,1)}, u32[]{:S(2)}, u32[]{:S(2)}) collective-permute-start(bf16[2,128,1024]{2,1,0:T(8,128)(2,1)} %pad_maximum_fusion.refs_0_), channel_id=1, source_target_pairs={{0,16},{16,32},{32,48},{48,0},{1,17},{17,33},{33,49},{49,1},{2,18}... | collective-permute-start | bytes 1572872 | tf_op jit(solution)/shard_map/ppermute | solution.py:302
  40.9 10.1 %copy-start.3 = (bf16[2,128,1024]{2,1,0:T(8,128)(2,1)}, bf16[2,128,1024]{2,1,0:T(8,128)(2,1)S(1)}, u32[]{:S(2)}) copy-start(bf16[2,128,1024]{2,1,0:T(8,128)(2,1)S(1)} %collective-permute-done.4.refs_5_) | copy-start | bytes 1572868
  52.1 5.5 %collective-permute-start.5 = (bf16[8,128,256]{2,1,0:T(8,128)(2,1)}, bf16[8,128,256]{2,1,0:T(8,128)(2,1)S(1)}, u32[]{:S(2)}, u32[]{:S(2)}) collective-permute-start(bf16[8,128,256]{2,1,0:T(8,128)(2,1)} %slice.29), channel_id=1, source_target_pairs={{0,1},{1,0},{2,3},{3,2},{4,5},{5,4},{6,7},{7,6},{8,9},{9,8},{10,11... | collective-permute-start | bytes 1572872 | tf_op jit(solution)/shard_map/ppermute | solution.py:285
  54.8 15.7 %collective-permute-start.6 = (bf16[2,128,1024]{2,1,0:T(8,128)(2,1)}, bf16[2,128,1024]{2,1,0:T(8,128)(2,1)}, u32[]{:S(2)}, u32[]{:S(2)}) collective-permute-start(bf16[2,128,1024]{2,1,0:T(8,128)(2,1)} %pad_maximum_fusion.1.refs_1_), channel_id=1, source_target_pairs={{0,16},{16,32},{32,48},{48,0},{1,17},{17,33},{33,49},{49,1},{2,18}... | collective-permute-start | bytes 1572872 | tf_op jit(solution)/shard_map/ppermute | solution.py:312
  56.1 14.4 %collective-permute-start.7 = (bf16[2,128,1024]{2,1,0:T(8,128)(2,1)}, bf16[2,128,1024]{2,1,0:T(8,128)(2,1)}, u32[]{:S(2)}, u32[]{:S(2)}) collective-permute-start(bf16[2,128,1024]{2,1,0:T(8,128)(2,1)} %pad_maximum_fusion.refs_0_), channel_id=1, source_target_pairs={{0,48},{16,0},{32,16},{48,32},{1,49},{17,1},{33,17},{49,33},{2,50}... | collective-permute-start | bytes 1572872 | tf_op jit(solution)/shard_map/ppermute | solution.py:313
  70.5 9.1 %copy-start.15 = (bf16[3,128,256]{2,1,0:T(8,128)(2,1)S(1)}, bf16[3,128,256]{2,1,0:T(8,128)(2,1)}, u32[]{:S(2)}) copy-start(bf16[3,128,256]{2,1,0:T(8,128)(2,1)} %get-tuple-element.76) | copy-start | bytes 589828
  70.5 11.1 %copy-start.4 = (bf16[2,128,1024]{2,1,0:T(8,128)(2,1)S(1)}, bf16[2,128,1024]{2,1,0:T(8,128)(2,1)}, u32[]{:S(2)}) copy-start(bf16[2,128,1024]{2,1,0:T(8,128)(2,1)} %copy-done.3) | copy-start | bytes 1572868
  70.5 4.6 %collective-permute-start.9 = (f32[8,128,256]{2,1,0:T(8,128)S(1)}, f32[8,128,256]{2,1,0:T(8,128)S(1)}, u32[]{:S(2)}, u32[]{:S(2)}) collective-permute-start(f32[8,128,256]{2,1,0:T(8,128)S(1)} %get-tuple-element.78), channel_id=1, source_target_pairs={{0,1},{1,0},{2,3},{3,2},{4,5},{5,4},{6,7},{7,6},{8,9},{9,8},{10,11... | collective-permute-start | bytes 3145736 | tf_op jit(solution)/shard_map/ppermute | solution.py:285
  72.3 9.2 %collective-permute-start.10 = (bf16[2,128,1024]{2,1,0:T(8,128)(2,1)}, bf16[2,128,1024]{2,1,0:T(8,128)(2,1)S(1)}, u32[]{:S(2)}, u32[]{:S(2)}) collective-permute-start(bf16[2,128,1024]{2,1,0:T(8,128)(2,1)} %pad_maximum_fusion.refs_0_), channel_id=1, source_target_pairs={{0,1},{1,0},{2,3},{3,2},{4,5},{5,4},{6,7},{7,6},{8,9},{9,8},{10,11... | collective-permute-start | bytes 1572872 | tf_op jit(solution)/shard_map/ppermute | solution.py:285
  72.4 9.2 %collective-permute-start.11 = (bf16[2,128,1024]{2,1,0:T(8,128)(2,1)}, bf16[2,128,1024]{2,1,0:T(8,128)(2,1)S(1)}, u32[]{:S(2)}, u32[]{:S(2)}) collective-permute-start(bf16[2,128,1024]{2,1,0:T(8,128)(2,1)} %pad_maximum_fusion.1.refs_1_), channel_id=1, source_target_pairs={{0,1},{1,0},{2,3},{3,2},{4,5},{5,4},{6,7},{7,6},{8,9},{9,8},{10,11... | collective-permute-start | bytes 1572872 | tf_op jit(solution)/shard_map/ppermute | solution.py:285
  72.9 9.2 %collective-permute-start.12 = (bf16[2,128,1024]{2,1,0:T(8,128)(2,1)}, bf16[2,128,1024]{2,1,0:T(8,128)(2,1)S(1)}, u32[]{:S(2)}, u32[]{:S(2)}) collective-permute-start(bf16[2,128,1024]{2,1,0:T(8,128)(2,1)} %collective-permute-done.3.refs_2_), channel_id=1, source_target_pairs={{0,1},{1,0},{2,3},{3,2},{4,5},{5,4},{6,7},{7,6},{8,9},{9,8},{10,11... | collective-permute-start | bytes 1572872 | tf_op jit(solution)/shard_map/ppermute | solution.py:285
  76.1 21.4 %all-to-all-start.1 = ((bf16[8,128,256]{2,1,0:T(8,128)(2,1)}), bf16[8,128,256]{2,1,0:T(8,128)(2,1)S(1)}, u32[]{:S(2)}, u32[]{:S(2)}) async-start(bf16[8,128,256]{2,1,0:T(8,128)(2,1)} %add_convert_fusion), calls=%async_computation.1 | async-start | bytes 1048576 | tf_op jit(solution)/shard_map/all_to_all | solution.py:328
  79.6 31.5 %copy-start.13 = (bf16[128,256]{1,0:T(8,128)(2,1)S(1)}, bf16[128,256]{1,0:T(8,128)(2,1)}, u32[]{:S(2)}) copy-start(bf16[128,256]{1,0:T(8,128)(2,1)} %get-tuple-element.89) | copy-start | bytes 196612
  79.6 1.5 collective-permute-start.8
  80.1 14.9 %collective-permute-start.16 = (bf16[2,128,1024]{2,1,0:T(8,128)(2,1)}, bf16[2,128,1024]{2,1,0:T(8,128)(2,1)}, u32[]{:S(2)}, u32[]{:S(2)}) collective-permute-start(bf16[2,128,1024]{2,1,0:T(8,128)(2,1)} %collective-permute-done.3.refs_2_), channel_id=1, source_target_pairs={{0,16},{16,32},{32,48},{48,0},{1,17},{17,33},{33,49},{49,1},{2,18}... | collective-permute-start | bytes 1572872 | tf_op jit(solution)/shard_map/ppermute | solution.py:321
  81.1 2.7 %collective-permute-start.13 = (bf16[2,128,1024]{2,1,0:T(8,128)(2,1)}, bf16[2,128,1024]{2,1,0:T(8,128)(2,1)S(1)}, u32[]{:S(2)}, u32[]{:S(2)}) collective-permute-start(bf16[2,128,1024]{2,1,0:T(8,128)(2,1)} %collective-permute-done.6.refs_3_), channel_id=1, source_target_pairs={{0,1},{1,0},{2,3},{3,2},{4,5},{5,4},{6,7},{7,6},{8,9},{9,8},{10,11... | collective-permute-start | bytes 1572872 | tf_op jit(solution)/shard_map/ppermute | solution.py:285
  81.5 25.1 %copy-start.5 = (bf16[2,128,1024]{2,1,0:T(8,128)(2,1)}, bf16[2,128,1024]{2,1,0:T(8,128)(2,1)S(1)}, u32[]{:S(2)}) copy-start(bf16[2,128,1024]{2,1,0:T(8,128)(2,1)S(1)} %collective-permute-done.10.refs_8_) | copy-start | bytes 1572868
  81.5 3.2 %collective-permute-start.14 = (bf16[2,128,1024]{2,1,0:T(8,128)(2,1)}, bf16[2,128,1024]{2,1,0:T(8,128)(2,1)S(1)}, u32[]{:S(2)}, u32[]{:S(2)}) collective-permute-start(bf16[2,128,1024]{2,1,0:T(8,128)(2,1)} %collective-permute-done.7.refs_4_), channel_id=1, source_target_pairs={{0,1},{1,0},{2,3},{3,2},{4,5},{5,4},{6,7},{7,6},{8,9},{9,8},{10,11... | collective-permute-start | bytes 1572872 | tf_op jit(solution)/shard_map/ppermute | solution.py:285
  81.6 25.0 %copy-start.6 = (bf16[2,128,1024]{2,1,0:T(8,128)(2,1)}, bf16[2,128,1024]{2,1,0:T(8,128)(2,1)S(1)}, u32[]{:S(2)}) copy-start(bf16[2,128,1024]{2,1,0:T(8,128)(2,1)S(1)} %collective-permute-done.11.refs_9_) | copy-start | bytes 1572868
  81.6 3.1 %collective-permute-start.15 = (bf16[2,128,1024]{2,1,0:T(8,128)(2,1)S(1)}, bf16[2,128,1024]{2,1,0:T(8,128)(2,1)S(1)}, u32[]{:S(2)}, u32[]{:S(2)}) collective-permute-start(bf16[2,128,1024]{2,1,0:T(8,128)(2,1)S(1)} %copy-done.4), channel_id=1, source_target_pairs={{0,1},{1,0},{2,3},{3,2},{4,5},{5,4},{6,7},{7,6},{8,9},{9,8},{10,11... | collective-permute-start | bytes 1572872 | tf_op jit(solution)/shard_map/ppermute | solution.py:285
  82.1 16.6 %copy-start.7 = (bf16[2,128,1024]{2,1,0:T(8,128)(2,1)}, bf16[2,128,1024]{2,1,0:T(8,128)(2,1)S(1)}, u32[]{:S(2)}) copy-start(bf16[2,128,1024]{2,1,0:T(8,128)(2,1)S(1)} %collective-permute-done.12.refs_10_) | copy-start | bytes 1572868
  82.1 13.5 %collective-permute-start.17 = (bf16[2,128,1024]{2,1,0:T(8,128)(2,1)S(1)}, bf16[2,128,1024]{2,1,0:T(8,128)(2,1)}, u32[]{:S(2)}, u32[]{:S(2)}) collective-permute-start(bf16[2,128,1024]{2,1,0:T(8,128)(2,1)S(1)} %copy-done.4), channel_id=1, source_target_pairs={{0,48},{16,0},{32,16},{48,32},{1,49},{17,1},{33,17},{49,33},{2,50}... | collective-permute-start | bytes 1572872 | tf_op jit(solution)/shard_map/ppermute | solution.py:322
  83.8 21.9 %copy-start.8 = (bf16[2,128,1024]{2,1,0:T(8,128)(2,1)}, bf16[2,128,1024]{2,1,0:T(8,128)(2,1)S(1)}, u32[]{:S(2)}) copy-start(bf16[2,128,1024]{2,1,0:T(8,128)(2,1)S(1)} %collective-permute-done.13.refs_11_) | copy-start | bytes 1572868
  84.7 10.2 %copy-start.9 = (bf16[2,128,1024]{2,1,0:T(8,128)(2,1)}, bf16[2,128,1024]{2,1,0:T(8,128)(2,1)S(1)}, u32[]{:S(2)}) copy-start(bf16[2,128,1024]{2,1,0:T(8,128)(2,1)S(1)} %collective-permute-done.14.refs_12_) | copy-start | bytes 1572868
  84.8 10.2 %copy-start.10 = (bf16[2,128,1024]{2,1,0:T(8,128)(2,1)}, bf16[2,128,1024]{2,1,0:T(8,128)(2,1)S(1)}, u32[]{:S(2)}) copy-start(bf16[2,128,1024]{2,1,0:T(8,128)(2,1)S(1)} %collective-permute-done.15.refs_13_) | copy-start | bytes 1572868
  98.7 16.1 %copy-start.12 = (bf16[128,256]{1,0:T(8,128)(2,1)S(1)}, bf16[128,256]{1,0:T(8,128)(2,1)}, u32[]{:S(2)}) copy-start(bf16[128,256]{1,0:T(8,128)(2,1)} %get-tuple-element.87) | copy-start | bytes 196612
  98.7 28.2 %all-to-all-start.2 = ((bf16[32,128,128]{2,1,0:T(8,128)(2,1)}), bf16[32,128,128]{2,1,0:T(8,128)(2,1)S(1)}, u32[]{:S(2)}, u32[]{:S(2)}) async-start(bf16[32,128,128]{2,1,0:T(8,128)(2,1)} %get-tuple-element.86), calls=%async_computation.2 | async-start | bytes 2097152 | tf_op jit(solution)/shard_map/all_to_all | solution.py:336
  105.1 21.7 %collective-permute-start.22 = (bf16[2,128,1024]{2,1,0:T(8,128)(2,1)}, bf16[2,128,1024]{2,1,0:T(8,128)(2,1)S(1)}, u32[]{:S(2)}, u32[]{:S(2)}) collective-permute-start(bf16[2,128,1024]{2,1,0:T(8,128)(2,1)} %collective-permute-done.16.refs_6_), channel_id=1, source_target_pairs={{0,1},{1,0},{2,3},{3,2},{4,5},{5,4},{6,7},{7,6},{8,9},{9,8},{10,11... | collective-permute-start | bytes 1572872 | tf_op jit(solution)/shard_map/ppermute | solution.py:285
  105.4 21.4 %collective-permute-start.23 = (bf16[2,128,1024]{2,1,0:T(8,128)(2,1)}, bf16[2,128,1024]{2,1,0:T(8,128)(2,1)}, u32[]{:S(2)}, u32[]{:S(2)}) collective-permute-start(bf16[2,128,1024]{2,1,0:T(8,128)(2,1)} %collective-permute-done.17.refs_7_), channel_id=1, source_target_pairs={{0,1},{1,0},{2,3},{3,2},{4,5},{5,4},{6,7},{7,6},{8,9},{9,8},{10,11... | collective-permute-start | bytes 1572872 | tf_op jit(solution)/shard_map/ppermute | solution.py:285
  106.6 16.4 %collective-permute-start.20 = (bf16[2,128,256]{2,1,0:T(8,128)(2,1)S(1)}, bf16[2,128,256]{2,1,0:T(8,128)(2,1)S(1)}, u32[]{:S(2)}, u32[]{:S(2)}) collective-permute-start(bf16[2,128,256]{2,1,0:T(8,128)(2,1)S(1)} %pad_maximum_fusion.5), channel_id=1, source_target_pairs={{0,6},{2,8},{4,10},{6,12},{8,14},{10,0},{12,2},{14,4},{1,11},{3,13... | collective-permute-start | bytes 393224 | tf_op jit(solution)/shard_map/ppermute | solution.py:342
  111.1 11.9 %collective-permute-start.19 = (bf16[2,128,256]{2,1,0:T(8,128)(2,1)S(1)}, bf16[2,128,256]{2,1,0:T(8,128)(2,1)S(1)}, u32[]{:S(2)}, u32[]{:S(2)}) collective-permute-start(bf16[2,128,256]{2,1,0:T(8,128)(2,1)S(1)} %pad_maximum_fusion.4), channel_id=1, source_target_pairs={{0,4},{2,6},{4,8},{6,10},{8,12},{10,14},{12,0},{14,2},{1,13},{3,15... | collective-permute-start | bytes 393224 | tf_op jit(solution)/shard_map/ppermute | solution.py:342
  112.3 10.7 %collective-permute-start.21 = (bf16[128,256]{1,0:T(8,128)(2,1)}, bf16[128,256]{1,0:T(8,128)(2,1)S(1)}, u32[]{:S(2)}, u32[]{:S(2)}) collective-permute-start(bf16[128,256]{1,0:T(8,128)(2,1)} %get-tuple-element.91), channel_id=1, source_target_pairs={{0,8},{2,10},{4,12},{6,14},{8,0},{10,2},{12,4},{14,6},{1,9},{3,11}... | collective-permute-start | bytes 196616 | tf_op jit(solution)/shard_map/ppermute | solution.py:343
  114.7 33.2 %copy-start = (bf16[128,256]{1,0:T(8,128)(2,1)S(1)}, bf16[128,256]{1,0:T(8,128)(2,1)}, u32[]{:S(2)}) copy-start(bf16[128,256]{1,0:T(8,128)(2,1)} %get-tuple-element.71.keep_ref) | copy-start | bytes 196612
  123.0 3.8 %collective-permute-start.18 = (bf16[2,128,256]{2,1,0:T(8,128)(2,1)S(1)}, bf16[2,128,256]{2,1,0:T(8,128)(2,1)S(1)}, u32[]{:S(2)}, u32[]{:S(2)}) collective-permute-start(bf16[2,128,256]{2,1,0:T(8,128)(2,1)S(1)} %pad_maximum_fusion.3), channel_id=1, source_target_pairs={{0,2},{2,4},{4,6},{6,8},{8,10},{10,12},{12,14},{14,0},{1,15},{3,1}... | collective-permute-start | bytes 393224 | tf_op jit(solution)/shard_map/ppermute | solution.py:342
  126.8 0.8 copy-start.11
  133.8 24.4 %all-to-all-start.3 = ((bf16[64,16,128]{2,1,0:T(8,128)(2,1)}), bf16[64,16,128]{2,1,0:T(8,128)(2,1)S(1)}, u32[]{:S(2)}, u32[]{:S(2)}) async-start(bf16[64,16,128]{2,1,0:T(8,128)(2,1)} %bitcast.22), calls=%async_computation.3 | async-start | bytes 524288 | tf_op jit(solution)/shard_map/all_to_all | solution.py:350
  146.3 1.6 %collective-permute-start.24 = (bf16[3,128,256]{2,1,0:T(8,128)(2,1)S(1)}, bf16[3,128,256]{2,1,0:T(8,128)(2,1)S(1)}, u32[]{:S(2)}, u32[]{:S(2)}) collective-permute-start(bf16[3,128,256]{2,1,0:T(8,128)(2,1)S(1)} %pad_maximum_fusion.2), channel_id=1, source_target_pairs={{0,1},{1,0},{2,3},{3,2},{4,5},{5,4},{6,7},{7,6},{8,9},{9,8},{10,11... | collective-permute-start | bytes 589832 | tf_op jit(solution)/shard_map/ppermute | solution.py:285

commit v7 on v6

--- a/solution.py
+++ b/solution.py
@@ -150,9 +150,6 @@
 PARTS = tuple((shift, first) for shift in (0, -1, 1, 2) for first in (0, NX // 2))
 
 
-AHEAD = 2
-
-
 def weight_kernel(place_ref, grads_ref, *refs):
     count = len(PARTS)
     out_ref, held_ref, sems = refs[2 * count :]
@@ -161,13 +158,11 @@
         for side in range(NC):
             target = held_ref.at[p, :, pl.ds(side * BLOCK, BLOCK), :]
             copies.append(pltpu.make_async_copy(refs[side * count + p], target, sems.at[p, side]))
-    for copy in copies[: 2 * AHEAD]:
+    for copy in copies:
         copy.start()
     x, y, core = place_ref[0], place_ref[3], place_ref[2]
     total = None
     for p, (shift, first) in enumerate(PARTS):
-        for copy in copies[2 * (p + AHEAD) : 2 * (p + AHEAD + 1)]:
-            copy.start()
         copies[2 * p].wait()
         copies[2 * p + 1].wait()
         for s in range(NX // 2):
@@ -299,7 +294,9 @@
     pieces = [a if s == 0 else lax.ppermute(a, "x", ring(NX, s)) for s, a in enumerate(pieces)]
     half = NX // 2
     mine = (jnp.stack(pieces[:half]), jnp.stack(pieces[half:]))
-    before, after = lax.ppermute(mine[0], "y", ring(NY, 1)), lax.ppermute(mine[1], "y", ring(NY, -1))
+    before, after = (
+        tuple(lax.ppermute(a, "y", ring(NY, shift)) for a in mine) for shift in (1, -1)
+    )
 
     outgoing = packed(queries[0], output_grads[0], keys[0], values[0])
     rows = lax.all_to_all(outgoing, "z", split_axis=0, concat_axis=0, tiled=True)
@@ -309,28 +306,25 @@
         (rows, mine, before, after, seg_cols)
     )
     other = swap_cores(rows[..., 4 * HEAD :])
-    before = (before, lax.ppermute(mine[1], "y", ring(NY, 1)))
-    after = (lax.ppermute(mine[0], "y", ring(NY, -1)), after)
-    keep, across, *ship, give, own, away = attention_grads(
-        block_links[0], place, rows, other, seg_cols, seg_rows
-    )
-    keep, across, ship, give, own, away, mine, before, after = lax.optimization_barrier(
-        (keep, across, ship, give, own, away, mine, before, after)
-    )
     far = (
         lax.ppermute(before[0], "y", ring(NY, 1)),
         lax.ppermute(after[1], "y", ring(NY, -1)),
     )
-    inputs_own = mine + before + after
+    keep, across, *ship, give, own, away = attention_grads(
+        block_links[0], place, rows, other, seg_cols, seg_rows
+    )
+    inputs_own = mine + before + after + far
+    keep, across, ship, give, own, away, inputs_own = lax.optimization_barrier(
+        (keep, across, ship, give, own, away, inputs_own)
+    )
     inputs_other = tuple(swap_cores(a) for a in inputs_own)
 
     pair = (own + swap_cores(away)).astype(bf16)
     pair = lax.all_to_all(pair, "z", split_axis=0, concat_axis=0, tiled=True)
     given = swap_cores(give)
-    across, ship, given, pair, inputs_other, far = lax.optimization_barrier(
-        (across, ship, given, pair, inputs_other, far)
-    )
-    far_other = tuple(swap_cores(a) for a in far)
+    across, ship, given, pair, inputs_other = lax.optimization_barrier(
+        (across, ship, given, pair, inputs_other)
+    )
     key_grads, value_grads, chunks = pair_grads(pair)
 
     grads = lax.all_to_all(chunks, ("x", "y", "c"), split_axis=0, concat_axis=0, tiled=True)
@@ -341,8 +335,8 @@
         hops = [tuple(a * NC + b for a, b in hop) for hop in hops]
         direct.append(lax.ppermute(jnp.stack([ship[k], given[k]]), ("z", "c"), hops))
     across = lax.ppermute(across, "z", ring(NZ, NZ // 2))
-    grads, direct, across, far_other = lax.optimization_barrier((grads, direct, across, far_other))
-    part = weight_grads_part(place, grads, inputs_own + far, inputs_other + far_other)
+    grads, direct, across = lax.optimization_barrier((grads, direct, across))
+    part = weight_grads_part(place, grads, inputs_own, inputs_other)
 
     swapped = swap_cores(jnp.stack([a[1] for a in direct]))
     query_grads = joined(place, keep, across, direct, swapped)

time: 160 us -> 150 us (0.938)
  starting transfers between devices: 58.7 us -> 53.2 us
  waiting for transfers between devices: 68.3 us -> 66.4 us
    ppermute x1, waiting for transfers between devices: 10.2 us -> 0.01 us  [local(): lax.ppermute(before[0], 'y', ring(NY, 1))]
    all_to_all x1, waiting for transfers between devices: 1.9 us -> 10.6 us  [local(): pair = lax.all_to_all(pair, 'z', split_axis=0, concat_axis=0, tiled=True)]
    ppermute x4, waiting for transfers between devices: 13.1 us -> 19.9 us  [local(): lax.ppermute(a, 'y', ring(NY, shift))]
    all_to_all x1, waiting for transfers between devices: 6.11 us -> 0.01 us  [local(): lax.all_to_all(outgoing, 'z', split_axis=0, concat_axis=0, tiled=True)]
    all_to_all x1, starting transfers between devices: 12.4 us -> 6.61 us  [local(): lax.all_to_all(part, ('y', 'z', 'c'), split_axis=0, concat_axis=0, tiled=...]
    all_to_all x1, waiting for transfers between devices: 0.01 us -> 3.8 us  [local(): lax.all_to_all(chunks, ('x', 'y', 'c'), split_axis=0, concat_axis=0, tile...]
    ppermute x1, waiting for transfers between devices: 8.24 us -> 4.77 us  [local(): across = lax.ppermute(across, 'z', ring(NZ, NZ // 2))]
    all_to_all x1, starting transfers between devices: 3.49 us -> 6.35 us  [local(): pair = lax.all_to_all(pair, 'z', split_axis=0, concat_axis=0, tiled=True)]
  transfers between devices with their start and end apart: 29 -> 29, of which waited for: 15 -> 16; matrix products, arithmetic and copies ran while one was open for 2% -> 2% of each run, Pallas kernels for 9% -> 10%
where the time goes in v7:
time: 150 us
  waiting for transfers between devices  66.4 us (44%)
  starting transfers between devices  53.2 us (35%)
  Pallas kernels  23.4 us (16%)
  local copies, waits for them, and re-layouts  2.99 us (2%)
  other arithmetic  2.79 us (2%)
    ppermute x4, waiting for transfers between devices, local(): lax.ppermute(a, 'y', ring(NY, shift))  19.9 us
    pallas_call x1, Pallas kernels, attention_grads(): pl.pallas_call(attention_kernel, out_shape=(pltpu.HBM((BLOCK, 2 * HEAD),...  12.8 us
    all_to_all x1, waiting for transfers between devices, local(): pair = lax.all_to_all(pair, 'z', split_axis=0, concat_axis=0, tiled=True)  10.6 us
    all_to_all x1, starting transfers between devices, local(): lax.all_to_all(outgoing, 'z', split_axis=0, concat_axis=0, tiled=True)  9.16 us
    all_to_all x1, waiting for transfers between devices, local(): lax.all_to_all(part, ('y', 'z', 'c'), split_axis=0, concat_axis=0, tiled=...  8.9 us
    ppermute x3, waiting for transfers between devices, local(): lax.ppermute(a, 'x', ring(NX, s))  8.33 us
    ppermute x12, starting transfers between devices, swap_cores(): return lax.ppermute(a, 'c', [(0, 1), (1, 0)])  8.08 us
    ppermute x12, waiting for transfers between devices, swap_cores(): return lax.ppermute(a, 'c', [(0, 1), (1, 0)])  7.75 us
  transfers between devices with their start and end apart: 29, of which 16 were waited for; matrix products, arithmetic and copies ran while one was open for 2% of the time, Pallas kernels for 10%

profile of v7, /device:TPU:1, one launch (start us, length us, event | category | flops | bytes accessed | tf_op | source)
XLA Modules:
  0.0 149.8 jit_solution(236976734138908082)
XLA Ops:
  0.6 2.9 %shard_map.110 = bf16[8,128,768]{2,1,0:T(8,128)(2,1)} custom-call(bf16[128,2048]{1,0:T(8,128)(2,1)} %bitcast.41, bf16[128,2048]{1,0:T(8,128)(2,1)} %bitcast.42, bf16[128,512]{1,0:T(8,128)(2,1)} %bitcast.47, bf16[128,512]{1,0:T(8,128)(2,1)} %bitcast.48), custom_call_target="tpu_custom_call" | custom-call | bytes 3145728 | tf_op jit(solution)/shard_map/pallas_call | solution.py:213
  3.5 9.2 %all-to-all-start = ((bf16[8,128,768]{2,1,0:T(8,128)(2,1)}), bf16[8,128,768]{2,1,0:T(8,128)(2,1)S(1)}, u32[]{:S(2)}, u32[]{:S(2)}) async-start(bf16[8,128,768]{2,1,0:T(8,128)(2,1)} %shard_map.110), calls=%async_computation | async-start | bytes 3145728 | tf_op jit(solution)/shard_map/all_to_all | solution.py:302
  12.8 1.3 collective-permute-start
  14.1 1.5 collective-permute-start.2
  15.5 1.5 %collective-permute-start.1 = (bf16[128,1024]{1,0:T(8,128)(2,1)S(1)}, bf16[128,1024]{1,0:T(8,128)(2,1)S(1)}, u32[]{:S(2)}, u32[]{:S(2)}) collective-permute-start(bf16[128,1024]{1,0:T(8,128)(2,1)S(1)} %get-tuple-element.113), channel_id=1, source_target_pairs={{0,128},{64,192},{128,0},{192,64},{1,129},{65,193},{129,1},{193,65... | collective-permute-start | bytes 786440 | tf_op jit(solution)/shard_map/ppermute | solution.py:294
  17.1 3.9 %collective-permute-done = bf16[128,1024]{1,0:T(8,128)(2,1)S(1)} collective-permute-done((bf16[128,1024]{1,0:T(8,128)(2,1)S(1)}, bf16[128,1024]{1,0:T(8,128)(2,1)S(1)}, u32[]{:S(2)}, u32[]{:S(2)}) %collective-permute-start) | collective-permute-done | bytes 262176 | tf_op jit(solution)/shard_map/ppermute | solution.py:294
  20.9 0.8 pad_maximum_fusion.refs_0_
  21.8 1.3 collective-permute-start.3
  23.1 4.5 %collective-permute-done.1 = bf16[128,1024]{1,0:T(8,128)(2,1)S(1)} collective-permute-done((bf16[128,1024]{1,0:T(8,128)(2,1)S(1)}, bf16[128,1024]{1,0:T(8,128)(2,1)S(1)}, u32[]{:S(2)}, u32[]{:S(2)}) %collective-permute-start.1) | collective-permute-done | bytes 262176 | tf_op jit(solution)/shard_map/ppermute | solution.py:294
  27.5 0.8 pad_maximum_fusion.1.refs_1_
  28.4 1.3 collective-permute-start.4
  29.7 1.4 collective-permute-start.5
  31.1 1.5 collective-permute-start.6
  32.6 1.9 %collective-permute-done.3.refs_2_ = bf16[2,128,1024]{2,1,0:T(8,128)(2,1)} collective-permute-done((bf16[2,128,1024]{2,1,0:T(8,128)(2,1)}, bf16[2,128,1024]{2,1,0:T(8,128)(2,1)}, u32[]{:S(2)}, u32[]{:S(2)}) %collective-permute-start.3) | collective-permute-done | bytes 524320 | tf_op jit(solution)/shard_map/ppermute | solution.py:298
  34.5 11.1 %collective-permute-done.4.refs_3_ = bf16[2,128,1024]{2,1,0:T(8,128)(2,1)S(1)} collective-permute-done((bf16[2,128,1024]{2,1,0:T(8,128)(2,1)}, bf16[2,128,1024]{2,1,0:T(8,128)(2,1)S(1)}, u32[]{:S(2)}, u32[]{:S(2)}) %collective-permute-start.4) | collective-permute-done | bytes 524320 | tf_op jit(solution)/shard_map/ppermute | solution.py:298
  45.6 6.9 %collective-permute-done.6.refs_5_ = bf16[2,128,1024]{2,1,0:T(8,128)(2,1)} collective-permute-done((bf16[2,128,1024]{2,1,0:T(8,128)(2,1)}, bf16[2,128,1024]{2,1,0:T(8,128)(2,1)}, u32[]{:S(2)}, u32[]{:S(2)}) %collective-permute-start.6) | collective-permute-done | bytes 524320 | tf_op jit(solution)/shard_map/ppermute | solution.py:298
  52.8 0.8 slice.29
  53.7 3.1 %collective-permute-start.7 = (bf16[8,128,256]{2,1,0:T(8,128)(2,1)}, bf16[8,128,256]{2,1,0:T(8,128)(2,1)S(1)}, u32[]{:S(2)}, u32[]{:S(2)}) collective-permute-start(bf16[8,128,256]{2,1,0:T(8,128)(2,1)} %slice.29), channel_id=1, source_target_pairs={{0,1},{1,0},{2,3},{3,2},{4,5},{5,4},{6,7},{7,6},{8,9},{9,8},{10,11... | collective-permute-start | bytes 1572872 | tf_op jit(solution)/shard_map/ppermute | solution.py:280
  56.8 1.3 collective-permute-start.8
  58.0 1.4 collective-permute-start.9
  59.6 12.8 %shard_map.111 = (bf16[128,256]{1,0:T(8,128)(2,1)}, bf16[128,256]{1,0:T(8,128)(2,1)}, bf16[128,256]{1,0:T(8,128)(2,1)}, bf16[128,256]{1,0:T(8,128)(2,1)}, bf16[1...) custom-call(s32[16,8]{1,0:T(8,128)S(1)} %copy.14.links_ref, ...), custom_call_target="tpu_custom_call" | custom-call | flops 4000000000 | bytes 8388608 | tf_op jit(solution)/shard_map/pallas_call | solution.py:124
  72.5 2.0 %collective-permute-start.11 = (f32[8,128,256]{2,1,0:T(8,128)S(1)}, f32[8,128,256]{2,1,0:T(8,128)S(1)}, u32[]{:S(2)}, u32[]{:S(2)}) collective-permute-start(f32[8,128,256]{2,1,0:T(8,128)S(1)} %get-tuple-element.82), channel_id=1, source_target_pairs={{0,1},{1,0},{2,3},{3,2},{4,5},{5,4},{6,7},{7,6},{8,9},{9,8},{10,11... | collective-permute-start | bytes 3145736 | tf_op jit(solution)/shard_map/ppermute | solution.py:280
  74.6 0.4 collective-permute-start.13
  75.1 2.2 %collective-permute-done.11 = f32[8,128,256]{2,1,0:T(8,128)S(1)} collective-permute-done((f32[8,128,256]{2,1,0:T(8,128)S(1)}, f32[8,128,256]{2,1,0:T(8,128)S(1)}, u32[]{:S(2)}, u32[]{:S(2)}) %collective-permute-start.11) | collective-permute-done | bytes 1048608 | tf_op jit(solution)/shard_map/ppermute | solution.py:280
  77.2 0.9 add_convert_fusion
  78.2 6.3 %all-to-all-start.1 = ((bf16[8,128,256]{2,1,0:T(8,128)(2,1)}), bf16[8,128,256]{2,1,0:T(8,128)(2,1)S(1)}, u32[]{:S(2)}, u32[]{:S(2)}) async-start(bf16[8,128,256]{2,1,0:T(8,128)(2,1)} %add_convert_fusion), calls=%async_computation.1 | async-start | bytes 1048576 | tf_op jit(solution)/shard_map/all_to_all | solution.py:323
  84.6 0.7 collective-permute-start.10
  85.4 1.2 collective-permute-done.10
  87.6 0.9 collective-permute-done.16.refs_12_
  88.5 1.7 %collective-permute-done.17.refs_13_ = bf16[2,128,1024]{2,1,0:T(8,128)(2,1)S(1)} collective-permute-done((bf16[2,128,1024]{2,1,0:T(8,128)(2,1)}, bf16[2,128,1024]{2,1,0:T(8,128)(2,1)S(1)}, u32[]{:S(2)}, u32[]{:S(2)}) %collective-permute-start.17) | collective-permute-done | bytes 524320 | tf_op jit(solution)/shard_map/ppermute | solution.py:280
  90.2 0.7 collective-permute-done.18.refs_14_
  91.1 0.8 copy-done.13
  91.8 10.6 %all-to-all-done.1.partials_ref = bf16[8,128,256]{2,1,0:T(8,128)(2,1)S(1)} async-done(((bf16[8,128,256]{2,1,0:T(8,128)(2,1)}), bf16[8,128,256]{2,1,0:T(8,128)(2,1)S(1)}, u32[]{:S(2)}, u32[]{:S(2)}) %all-to-all-start.1) | async-done | bytes 524320 | tf_op jit(solution)/shard_map/all_to_all | solution.py:323
  102.5 1.2 shard_map.112
  103.7 4.7 %all-to-all-start.2 = ((bf16[32,128,128]{2,1,0:T(8,128)(2,1)}), bf16[32,128,128]{2,1,0:T(8,128)(2,1)S(1)}, u32[]{:S(2)}, u32[]{:S(2)}) async-start(bf16[32,128,128]{2,1,0:T(8,128)(2,1)} %get-tuple-element.92), calls=%async_computation.2 | async-start | bytes 2097152 | tf_op jit(solution)/shard_map/all_to_all | solution.py:330
  108.5 0.6 collective-permute-start.21
  109.2 2.7 %collective-permute-start.22 = (bf16[2,128,256]{2,1,0:T(8,128)(2,1)S(1)}, bf16[2,128,256]{2,1,0:T(8,128)(2,1)S(1)}, u32[]{:S(2)}, u32[]{:S(2)}) collective-permute-start(bf16[2,128,256]{2,1,0:T(8,128)(2,1)S(1)} %pad_maximum_fusion.5), channel_id=1, source_target_pairs={{0,6},{2,8},{4,10},{6,12},{8,14},{10,0},{12,2},{14,4},{1,11},{3,13... | collective-permute-start | bytes 393224 | tf_op jit(solution)/shard_map/ppermute | solution.py:336
  111.8 2.6 %collective-permute-start.23 = (bf16[128,256]{1,0:T(8,128)(2,1)S(1)}, bf16[128,256]{1,0:T(8,128)(2,1)S(1)}, u32[]{:S(2)}, u32[]{:S(2)}) collective-permute-start(bf16[128,256]{1,0:T(8,128)(2,1)S(1)} %copy-done.18), channel_id=1, source_target_pairs={{0,8},{2,10},{4,12},{6,14},{8,0},{10,2},{12,4},{14,6},{1,9},{3,11}... | collective-permute-start | bytes 196616 | tf_op jit(solution)/shard_map/ppermute | solution.py:337
  114.4 4.8 %collective-permute-done.23.across_ref = bf16[128,256]{1,0:T(8,128)(2,1)S(1)} collective-permute-done((bf16[128,256]{1,0:T(8,128)(2,1)S(1)}, bf16[128,256]{1,0:T(8,128)(2,1)S(1)}, u32[]{:S(2)}, u32[]{:S(2)}) %collective-permute-start.23) | collective-permute-done | bytes 65568 | tf_op jit(solution)/shard_map/ppermute | solution.py:337
  119.2 2.2 %collective-permute-done.22.refs_2_ = bf16[2,128,256]{2,1,0:T(8,128)(2,1)S(1)} collective-permute-done((bf16[2,128,256]{2,1,0:T(8,128)(2,1)S(1)}, bf16[2,128,256]{2,1,0:T(8,128)(2,1)S(1)}, u32[]{:S(2)}, u32[]{:S(2)}) %collective-permute-start.22) | collective-permute-done | bytes 131104 | tf_op jit(solution)/shard_map/ppermute | solution.py:336
  121.4 3.8 %all-to-all-done.2.grads_ref = bf16[32,128,128]{2,1,0:T(8,128)(2,1)S(1)} async-done(((bf16[32,128,128]{2,1,0:T(8,128)(2,1)}), bf16[32,128,128]{2,1,0:T(8,128)(2,1)S(1)}, u32[]{:S(2)}, u32[]{:S(2)}) %all-to-all-start.2) | async-done | bytes 1048608 | tf_op jit(solution)/shard_map/all_to_all | solution.py:330
  125.2 5.2 %shard_map.114 = bf16[1024,128]{1,0:T(8,128)(2,1)} custom-call(s32[4]{0:T(128)S(1)} %pad_add_fusion.place_ref, bf16[32,128,128]{2,1,0:T(8,128)(2,1)S(1)} %all-to-all-done.2.grads_ref, bf16[2,128,1024]{2,1,0:T(8,128)(2,1)} %pad_maximum_fusion.refs_0_, bf16[2,128,1024]{2,1,0:T(8,128)(2,1)} %pad_maximum_fusion.1.refs_1_, ...), custom_call_target="tpu_custom_call" | custom-call | flops 1100000000 | bytes 9437184 | tf_op jit(solution)/shard_map/pallas_call | solution.py:179
  130.4 6.6 %all-to-all-start.3 = ((bf16[64,16,128]{2,1,0:T(8,128)(2,1)}), bf16[64,16,128]{2,1,0:T(8,128)(2,1)S(1)}, u32[]{:S(2)}, u32[]{:S(2)}) async-start(bf16[64,16,128]{2,1,0:T(8,128)(2,1)} %bitcast.22), calls=%async_computation.3 | async-start | bytes 524288 | tf_op jit(solution)/shard_map/all_to_all | solution.py:344
  137.1 0.5 collective-permute-start.24
  137.6 1.1 collective-permute-done.24.refs_3_
  138.7 1.4 shard_map.113
  140.1 8.9 %all-to-all-done.3 = bf16[64,16,128]{2,1,0:T(8,128)(2,1)S(1)} async-done(((bf16[64,16,128]{2,1,0:T(8,128)(2,1)}), bf16[64,16,128]{2,1,0:T(8,128)(2,1)S(1)}, u32[]{:S(2)}, u32[]{:S(2)}) %all-to-all-start.3) | async-done | bytes 262176 | tf_op jit(solution)/shard_map/all_to_all | solution.py:344
  149.1 0.6 copy_bitcast_fusion
  (74 shorter events, 2.4 us)
Async XLA Ops:
  3.5 9.2 %copy-start.2 = (bf16[1,128,4096]{2,1,0:T(8,128)(2,1)S(1)}, bf16[1,128,4096]{2,1,0:T(8,128)(2,1)}, u32[]{:S(2)}) copy-start(bf16[1,128,4096]{2,1,0:T(8,128)(2,1)} %param.7) | copy-start | bytes 3145732
  3.5 49.0 %all-to-all-start = ((bf16[8,128,768]{2,1,0:T(8,128)(2,1)}), bf16[8,128,768]{2,1,0:T(8,128)(2,1)S(1)}, u32[]{:S(2)}, u32[]{:S(2)}) async-start(bf16[8,128,768]{2,1,0:T(8,128)(2,1)} %shard_map.110), calls=%async_computation | async-start | bytes 3145728 | tf_op jit(solution)/shard_map/all_to_all | solution.py:302
  12.8 39.7 %copy-start.1 = (s32[1,2048]{1,0:T(1,128)S(1)}, s32[1,2048]{1,0:T(1,128)}, u32[]{:S(2)}) copy-start(s32[1,2048]{1,0:T(1,128)} %param.13) | copy-start | bytes 24580
  12.8 8.1 %collective-permute-start = (bf16[128,1024]{1,0:T(8,128)(2,1)S(1)}, bf16[128,1024]{1,0:T(8,128)(2,1)S(1)}, u32[]{:S(2)}, u32[]{:S(2)}) collective-permute-start(bf16[128,1024]{1,0:T(8,128)(2,1)S(1)} %get-tuple-element.114), channel_id=1, source_target_pairs={{0,64},{64,128},{128,192},{192,0},{1,65},{65,129},{129,193},{193,1... | collective-permute-start | bytes 786440 | tf_op jit(solution)/shard_map/ppermute | solution.py:294
  14.1 9.0 %collective-permute-start.2 = (bf16[128,1024]{1,0:T(8,128)(2,1)S(1)}, bf16[128,1024]{1,0:T(8,128)(2,1)S(1)}, u32[]{:S(2)}, u32[]{:S(2)}) collective-permute-start(bf16[128,1024]{1,0:T(8,128)(2,1)S(1)} %get-tuple-element.116), channel_id=1, source_target_pairs={{0,192},{64,0},{128,64},{192,128},{1,193},{65,1},{129,65},{193,129... | collective-permute-start | bytes 786440 | tf_op jit(solution)/shard_map/ppermute | solution.py:294
  15.5 12.0 %collective-permute-start.1 = (bf16[128,1024]{1,0:T(8,128)(2,1)S(1)}, bf16[128,1024]{1,0:T(8,128)(2,1)S(1)}, u32[]{:S(2)}, u32[]{:S(2)}) collective-permute-start(bf16[128,1024]{1,0:T(8,128)(2,1)S(1)} %get-tuple-element.113), channel_id=1, source_target_pairs={{0,128},{64,192},{128,0},{192,64},{1,129},{65,193},{129,1},{193,65... | collective-permute-start | bytes 786440 | tf_op jit(solution)/shard_map/ppermute | solution.py:294
  21.8 12.7 %collective-permute-start.3 = (bf16[2,128,1024]{2,1,0:T(8,128)(2,1)}, bf16[2,128,1024]{2,1,0:T(8,128)(2,1)}, u32[]{:S(2)}, u32[]{:S(2)}) collective-permute-start(bf16[2,128,1024]{2,1,0:T(8,128)(2,1)} %pad_maximum_fusion.refs_0_), channel_id=1, source_target_pairs={{0,16},{16,32},{32,48},{48,0},{1,17},{17,33},{33,49},{49,1},{2,18}... | collective-permute-start | bytes 1572872 | tf_op jit(solution)/shard_map/ppermute | solution.py:298
  27.5 31.9 %copy-start.17 = (s32[1,16,8]{1,2,0:T(8,128)S(1)}, s32[1,16,8]{1,2,0:T(8,128)}, u32[]{:S(2)}) copy-start(s32[1,16,8]{1,2,0:T(8,128)} %param.12) | copy-start | bytes 1540
  28.4 17.2 %collective-permute-start.4 = (bf16[2,128,1024]{2,1,0:T(8,128)(2,1)}, bf16[2,128,1024]{2,1,0:T(8,128)(2,1)S(1)}, u32[]{:S(2)}, u32[]{:S(2)}) collective-permute-start(bf16[2,128,1024]{2,1,0:T(8,128)(2,1)} %pad_maximum_fusion.1.refs_1_), channel_id=1, source_target_pairs={{0,16},{16,32},{32,48},{48,0},{1,17},{17,33},{33,49},{49,1},{2,18}... | collective-permute-start | bytes 1572872 | tf_op jit(solution)/shard_map/ppermute | solution.py:298
  29.7 16.0 %collective-permute-start.5 = (bf16[2,128,1024]{2,1,0:T(8,128)(2,1)}, bf16[2,128,1024]{2,1,0:T(8,128)(2,1)S(1)}, u32[]{:S(2)}, u32[]{:S(2)}) collective-permute-start(bf16[2,128,1024]{2,1,0:T(8,128)(2,1)} %pad_maximum_fusion.refs_0_), channel_id=1, source_target_pairs={{0,48},{16,0},{32,16},{48,32},{1,49},{17,1},{33,17},{49,33},{2,50}... | collective-permute-start | bytes 1572872 | tf_op jit(solution)/shard_map/ppermute | solution.py:298
  31.1 21.4 %collective-permute-start.6 = (bf16[2,128,1024]{2,1,0:T(8,128)(2,1)}, bf16[2,128,1024]{2,1,0:T(8,128)(2,1)}, u32[]{:S(2)}, u32[]{:S(2)}) collective-permute-start(bf16[2,128,1024]{2,1,0:T(8,128)(2,1)} %pad_maximum_fusion.1.refs_1_), channel_id=1, source_target_pairs={{0,48},{16,0},{32,16},{48,32},{1,49},{17,1},{33,17},{49,33},{2,50}... | collective-permute-start | bytes 1572872 | tf_op jit(solution)/shard_map/ppermute | solution.py:298
  45.6 6.9 %copy-start.3 = (bf16[2,128,1024]{2,1,0:T(8,128)(2,1)}, bf16[2,128,1024]{2,1,0:T(8,128)(2,1)S(1)}, u32[]{:S(2)}) copy-start(bf16[2,128,1024]{2,1,0:T(8,128)(2,1)S(1)} %collective-permute-done.4.refs_3_) | copy-start | bytes 1572868
  45.6 6.9 %copy-start.5 = (bf16[2,128,1024]{2,1,0:T(8,128)(2,1)}, bf16[2,128,1024]{2,1,0:T(8,128)(2,1)S(1)}, u32[]{:S(2)}) copy-start(bf16[2,128,1024]{2,1,0:T(8,128)(2,1)S(1)} %collective-permute-done.5.refs_4_) | copy-start | bytes 1572868
  53.7 5.9 %collective-permute-start.7 = (bf16[8,128,256]{2,1,0:T(8,128)(2,1)}, bf16[8,128,256]{2,1,0:T(8,128)(2,1)S(1)}, u32[]{:S(2)}, u32[]{:S(2)}) collective-permute-start(bf16[8,128,256]{2,1,0:T(8,128)(2,1)} %slice.29), channel_id=1, source_target_pairs={{0,1},{1,0},{2,3},{3,2},{4,5},{5,4},{6,7},{7,6},{8,9},{9,8},{10,11... | collective-permute-start | bytes 1572872 | tf_op jit(solution)/shard_map/ppermute | solution.py:280
  56.8 15.7 %collective-permute-start.8 = (bf16[2,128,1024]{2,1,0:T(8,128)(2,1)}, bf16[2,128,1024]{2,1,0:T(8,128)(2,1)}, u32[]{:S(2)}, u32[]{:S(2)}) collective-permute-start(bf16[2,128,1024]{2,1,0:T(8,128)(2,1)} %collective-permute-done.3.refs_2_), channel_id=1, source_target_pairs={{0,16},{16,32},{32,48},{48,0},{1,17},{17,33},{33,49},{49,1},{2,18}... | collective-permute-start | bytes 1572872 | tf_op jit(solution)/shard_map/ppermute | solution.py:310
  58.0 14.4 %collective-permute-start.9 = (bf16[2,128,1024]{2,1,0:T(8,128)(2,1)}, bf16[2,128,1024]{2,1,0:T(8,128)(2,1)}, u32[]{:S(2)}, u32[]{:S(2)}) collective-permute-start(bf16[2,128,1024]{2,1,0:T(8,128)(2,1)} %collective-permute-done.6.refs_5_), channel_id=1, source_target_pairs={{0,48},{16,0},{32,16},{48,32},{1,49},{17,1},{33,17},{49,33},{2,50}... | collective-permute-start | bytes 1572872 | tf_op jit(solution)/shard_map/ppermute | solution.py:311
  72.5 12.8 %copy-start.4 = (bf16[2,128,1024]{2,1,0:T(8,128)(2,1)S(1)}, bf16[2,128,1024]{2,1,0:T(8,128)(2,1)}, u32[]{:S(2)}) copy-start(bf16[2,128,1024]{2,1,0:T(8,128)(2,1)} %copy-done.3) | copy-start | bytes 1572868
  72.5 14.1 %copy-start.6 = (bf16[2,128,1024]{2,1,0:T(8,128)(2,1)S(1)}, bf16[2,128,1024]{2,1,0:T(8,128)(2,1)}, u32[]{:S(2)}) copy-start(bf16[2,128,1024]{2,1,0:T(8,128)(2,1)} %copy-done.5) | copy-start | bytes 1572868
  72.5 4.8 %collective-permute-start.11 = (f32[8,128,256]{2,1,0:T(8,128)S(1)}, f32[8,128,256]{2,1,0:T(8,128)S(1)}, u32[]{:S(2)}, u32[]{:S(2)}) collective-permute-start(f32[8,128,256]{2,1,0:T(8,128)S(1)} %get-tuple-element.82), channel_id=1, source_target_pairs={{0,1},{1,0},{2,3},{3,2},{4,5},{5,4},{6,7},{7,6},{8,9},{9,8},{10,11... | collective-permute-start | bytes 3145736 | tf_op jit(solution)/shard_map/ppermute | solution.py:280
  74.5 12.5 %collective-permute-start.12 = (bf16[2,128,1024]{2,1,0:T(8,128)(2,1)}, bf16[2,128,1024]{2,1,0:T(8,128)(2,1)S(1)}, u32[]{:S(2)}, u32[]{:S(2)}) collective-permute-start(bf16[2,128,1024]{2,1,0:T(8,128)(2,1)} %pad_maximum_fusion.refs_0_), channel_id=1, source_target_pairs={{0,1},{1,0},{2,3},{3,2},{4,5},{5,4},{6,7},{7,6},{8,9},{9,8},{10,11... | collective-permute-start | bytes 1572872 | tf_op jit(solution)/shard_map/ppermute | solution.py:280
  74.6 12.5 %collective-permute-start.13 = (bf16[2,128,1024]{2,1,0:T(8,128)(2,1)}, bf16[2,128,1024]{2,1,0:T(8,128)(2,1)S(1)}, u32[]{:S(2)}, u32[]{:S(2)}) collective-permute-start(bf16[2,128,1024]{2,1,0:T(8,128)(2,1)} %pad_maximum_fusion.1.refs_1_), channel_id=1, source_target_pairs={{0,1},{1,0},{2,3},{3,2},{4,5},{5,4},{6,7},{7,6},{8,9},{9,8},{10,11... | collective-permute-start | bytes 1572872 | tf_op jit(solution)/shard_map/ppermute | solution.py:280
  75.0 12.5 %collective-permute-start.14 = (bf16[2,128,1024]{2,1,0:T(8,128)(2,1)}, bf16[2,128,1024]{2,1,0:T(8,128)(2,1)S(1)}, u32[]{:S(2)}, u32[]{:S(2)}) collective-permute-start(bf16[2,128,1024]{2,1,0:T(8,128)(2,1)} %collective-permute-done.3.refs_2_), channel_id=1, source_target_pairs={{0,1},{1,0},{2,3},{3,2},{4,5},{5,4},{6,7},{7,6},{8,9},{9,8},{10,11... | collective-permute-start | bytes 1572872 | tf_op jit(solution)/shard_map/ppermute | solution.py:280
  78.2 24.3 %all-to-all-start.1 = ((bf16[8,128,256]{2,1,0:T(8,128)(2,1)}), bf16[8,128,256]{2,1,0:T(8,128)(2,1)S(1)}, u32[]{:S(2)}, u32[]{:S(2)}) async-start(bf16[8,128,256]{2,1,0:T(8,128)(2,1)} %add_convert_fusion), calls=%async_computation.1 | async-start | bytes 1048576 | tf_op jit(solution)/shard_map/all_to_all | solution.py:323
  84.5 23.8 %copy-start.16 = (bf16[128,256]{1,0:T(8,128)(2,1)S(1)}, bf16[128,256]{1,0:T(8,128)(2,1)}, u32[]{:S(2)}) copy-start(bf16[128,256]{1,0:T(8,128)(2,1)} %get-tuple-element.93) | copy-start | bytes 196612
  84.5 23.9 %copy-start.15 = (bf16[128,256]{1,0:T(8,128)(2,1)S(1)}, bf16[128,256]{1,0:T(8,128)(2,1)}, u32[]{:S(2)}) copy-start(bf16[128,256]{1,0:T(8,128)(2,1)} %get-tuple-element.95) | copy-start | bytes 196612
  84.6 2.0 %collective-permute-start.10 = (bf16[3,128,256]{2,1,0:T(8,128)(2,1)}, bf16[3,128,256]{2,1,0:T(8,128)(2,1)S(1)}, u32[]{:S(2)}, u32[]{:S(2)}) collective-permute-start(bf16[3,128,256]{2,1,0:T(8,128)(2,1)} %get-tuple-element.80), channel_id=1, source_target_pairs={{0,1},{1,0},{2,3},{3,2},{4,5},{5,4},{6,7},{7,6},{8,9},{9,8},{10,11... | collective-permute-start | bytes 589832 | tf_op jit(solution)/shard_map/ppermute | solution.py:280
  85.3 2.3 %collective-permute-start.15 = (bf16[2,128,1024]{2,1,0:T(8,128)(2,1)S(1)}, bf16[2,128,1024]{2,1,0:T(8,128)(2,1)S(1)}, u32[]{:S(2)}, u32[]{:S(2)}) collective-permute-start(bf16[2,128,1024]{2,1,0:T(8,128)(2,1)S(1)} %copy-done.4), channel_id=1, source_target_pairs={{0,1},{1,0},{2,3},{3,2},{4,5},{5,4},{6,7},{7,6},{8,9},{9,8},{10,11... | collective-permute-start | bytes 1572872 | tf_op jit(solution)/shard_map/ppermute | solution.py:280
  86.6 1.9 %collective-permute-start.16 = (bf16[2,128,1024]{2,1,0:T(8,128)(2,1)S(1)}, bf16[2,128,1024]{2,1,0:T(8,128)(2,1)S(1)}, u32[]{:S(2)}, u32[]{:S(2)}) collective-permute-start(bf16[2,128,1024]{2,1,0:T(8,128)(2,1)S(1)} %copy-done.6), channel_id=1, source_target_pairs={{0,1},{1,0},{2,3},{3,2},{4,5},{5,4},{6,7},{7,6},{8,9},{9,8},{10,11... | collective-permute-start | bytes 1572872 | tf_op jit(solution)/shard_map/ppermute | solution.py:280
  87.0 21.4 %copy-start.7 = (bf16[2,128,1024]{2,1,0:T(8,128)(2,1)}, bf16[2,128,1024]{2,1,0:T(8,128)(2,1)S(1)}, u32[]{:S(2)}) copy-start(bf16[2,128,1024]{2,1,0:T(8,128)(2,1)S(1)} %collective-permute-done.12.refs_8_) | copy-start | bytes 1572868
  87.0 3.2 %collective-permute-start.17 = (bf16[2,128,1024]{2,1,0:T(8,128)(2,1)}, bf16[2,128,1024]{2,1,0:T(8,128)(2,1)S(1)}, u32[]{:S(2)}, u32[]{:S(2)}) collective-permute-start(bf16[2,128,1024]{2,1,0:T(8,128)(2,1)} %collective-permute-done.6.refs_5_), channel_id=1, source_target_pairs={{0,1},{1,0},{2,3},{3,2},{4,5},{5,4},{6,7},{7,6},{8,9},{9,8},{10,11... | collective-permute-start | bytes 1572872 | tf_op jit(solution)/shard_map/ppermute | solution.py:280
  87.1 16.6 %copy-start.8 = (bf16[2,128,1024]{2,1,0:T(8,128)(2,1)}, bf16[2,128,1024]{2,1,0:T(8,128)(2,1)S(1)}, u32[]{:S(2)}) copy-start(bf16[2,128,1024]{2,1,0:T(8,128)(2,1)S(1)} %collective-permute-done.13.refs_9_) | copy-start | bytes 1572868
  87.1 3.8 %collective-permute-start.18 = (bf16[2,128,1024]{2,1,0:T(8,128)(2,1)}, bf16[2,128,1024]{2,1,0:T(8,128)(2,1)S(1)}, u32[]{:S(2)}, u32[]{:S(2)}) collective-permute-start(bf16[2,128,1024]{2,1,0:T(8,128)(2,1)} %collective-permute-done.8.refs_6_), channel_id=1, source_target_pairs={{0,1},{1,0},{2,3},{3,2},{4,5},{5,4},{6,7},{7,6},{8,9},{9,8},{10,11... | collective-permute-start | bytes 1572872 | tf_op jit(solution)/shard_map/ppermute | solution.py:280
  87.5 20.9 %copy-start.9 = (bf16[2,128,1024]{2,1,0:T(8,128)(2,1)}, bf16[2,128,1024]{2,1,0:T(8,128)(2,1)S(1)}, u32[]{:S(2)}) copy-start(bf16[2,128,1024]{2,1,0:T(8,128)(2,1)S(1)} %collective-permute-done.14.refs_10_) | copy-start | bytes 1572868
  87.5 4.4 %collective-permute-start.19 = (bf16[2,128,1024]{2,1,0:T(8,128)(2,1)}, bf16[2,128,1024]{2,1,0:T(8,128)(2,1)}, u32[]{:S(2)}, u32[]{:S(2)}) collective-permute-start(bf16[2,128,1024]{2,1,0:T(8,128)(2,1)} %collective-permute-done.9.refs_7_), channel_id=1, source_target_pairs={{0,1},{1,0},{2,3},{3,2},{4,5},{5,4},{6,7},{7,6},{8,9},{9,8},{10,11... | collective-permute-start | bytes 1572872 | tf_op jit(solution)/shard_map/ppermute | solution.py:280
  87.6 3.3 %copy-start.10 = (bf16[2,128,1024]{2,1,0:T(8,128)(2,1)}, bf16[2,128,1024]{2,1,0:T(8,128)(2,1)S(1)}, u32[]{:S(2)}) copy-start(bf16[2,128,1024]{2,1,0:T(8,128)(2,1)S(1)} %collective-permute-done.15.refs_11_) | copy-start | bytes 1572868
  88.5 2.5 %copy-start.11 = (bf16[2,128,1024]{2,1,0:T(8,128)(2,1)}, bf16[2,128,1024]{2,1,0:T(8,128)(2,1)S(1)}, u32[]{:S(2)}) copy-start(bf16[2,128,1024]{2,1,0:T(8,128)(2,1)S(1)} %collective-permute-done.16.refs_12_) | copy-start | bytes 1572868
  90.2 0.9 copy-start.12
  91.0 0.8 copy-start.13
  103.6 5.5 %copy-start.14 = (bf16[128,256]{1,0:T(8,128)(2,1)S(1)}, bf16[128,256]{1,0:T(8,128)(2,1)}, u32[]{:S(2)}) copy-start(bf16[128,256]{1,0:T(8,128)(2,1)} %get-tuple-element.96) | copy-start | bytes 196612
  103.7 8.2 %copy-start.18 = (bf16[128,256]{1,0:T(8,128)(2,1)S(1)}, bf16[128,256]{1,0:T(8,128)(2,1)}, u32[]{:S(2)}) copy-start(bf16[128,256]{1,0:T(8,128)(2,1)} %get-tuple-element.97) | copy-start | bytes 196612
  103.7 21.6 %all-to-all-start.2 = ((bf16[32,128,128]{2,1,0:T(8,128)(2,1)}), bf16[32,128,128]{2,1,0:T(8,128)(2,1)S(1)}, u32[]{:S(2)}, u32[]{:S(2)}) async-start(bf16[32,128,128]{2,1,0:T(8,128)(2,1)} %get-tuple-element.92), calls=%async_computation.2 | async-start | bytes 2097152 | tf_op jit(solution)/shard_map/all_to_all | solution.py:330
  108.4 10.8 %collective-permute-start.20 = (bf16[2,128,256]{2,1,0:T(8,128)(2,1)S(1)}, bf16[2,128,256]{2,1,0:T(8,128)(2,1)S(1)}, u32[]{:S(2)}, u32[]{:S(2)}) collective-permute-start(bf16[2,128,256]{2,1,0:T(8,128)(2,1)S(1)} %pad_maximum_fusion.3), channel_id=1, source_target_pairs={{0,2},{2,4},{4,6},{6,8},{8,10},{10,12},{12,14},{14,0},{1,15},{3,1}... | collective-permute-start | bytes 393224 | tf_op jit(solution)/shard_map/ppermute | solution.py:336
  108.5 10.7 %collective-permute-start.21 = (bf16[2,128,256]{2,1,0:T(8,128)(2,1)S(1)}, bf16[2,128,256]{2,1,0:T(8,128)(2,1)S(1)}, u32[]{:S(2)}, u32[]{:S(2)}) collective-permute-start(bf16[2,128,256]{2,1,0:T(8,128)(2,1)S(1)} %pad_maximum_fusion.4), channel_id=1, source_target_pairs={{0,4},{2,6},{4,8},{6,10},{8,12},{10,14},{12,0},{14,2},{1,13},{3,15... | collective-permute-start | bytes 393224 | tf_op jit(solution)/shard_map/ppermute | solution.py:336
  109.2 29.6 %copy-start = (bf16[128,256]{1,0:T(8,128)(2,1)S(1)}, bf16[128,256]{1,0:T(8,128)(2,1)}, u32[]{:S(2)}) copy-start(bf16[128,256]{1,0:T(8,128)(2,1)} %get-tuple-element.75.keep_ref) | copy-start | bytes 196612
  109.2 12.3 %collective-permute-start.22 = (bf16[2,128,256]{2,1,0:T(8,128)(2,1)S(1)}, bf16[2,128,256]{2,1,0:T(8,128)(2,1)S(1)}, u32[]{:S(2)}, u32[]{:S(2)}) collective-permute-start(bf16[2,128,256]{2,1,0:T(8,128)(2,1)S(1)} %pad_maximum_fusion.5), channel_id=1, source_target_pairs={{0,6},{2,8},{4,10},{6,12},{8,14},{10,0},{12,2},{14,4},{1,11},{3,13... | collective-permute-start | bytes 393224 | tf_op jit(solution)/shard_map/ppermute | solution.py:336
  111.8 7.3 %collective-permute-start.23 = (bf16[128,256]{1,0:T(8,128)(2,1)S(1)}, bf16[128,256]{1,0:T(8,128)(2,1)S(1)}, u32[]{:S(2)}, u32[]{:S(2)}) collective-permute-start(bf16[128,256]{1,0:T(8,128)(2,1)S(1)} %copy-done.18), channel_id=1, source_target_pairs={{0,8},{2,10},{4,12},{6,14},{8,0},{10,2},{12,4},{14,6},{1,9},{3,11}... | collective-permute-start | bytes 196616 | tf_op jit(solution)/shard_map/ppermute | solution.py:337
  130.4 18.6 %all-to-all-start.3 = ((bf16[64,16,128]{2,1,0:T(8,128)(2,1)}), bf16[64,16,128]{2,1,0:T(8,128)(2,1)S(1)}, u32[]{:S(2)}, u32[]{:S(2)}) async-start(bf16[64,16,128]{2,1,0:T(8,128)(2,1)} %bitcast.22), calls=%async_computation.3 | async-start | bytes 524288 | tf_op jit(solution)/shard_map/all_to_all | solution.py:344
  137.1 1.6 %collective-permute-start.24 = (bf16[3,128,256]{2,1,0:T(8,128)(2,1)S(1)}, bf16[3,128,256]{2,1,0:T(8,128)(2,1)S(1)}, u32[]{:S(2)}, u32[]{:S(2)}) collective-permute-start(bf16[3,128,256]{2,1,0:T(8,128)(2,1)S(1)} %pad_maximum_fusion.2), channel_id=1, source_target_pairs={{0,1},{1,0},{2,3},{3,2},{4,5},{5,4},{6,7},{7,6},{8,9},{9,8},{10,11... | collective-permute-start | bytes 589832 | tf_op jit(solution)/shard_map/ppermute | solution.py:280

commit v8 on v7

--- a/solution.py
+++ b/solution.py
@@ -152,45 +152,42 @@
 
 def weight_kernel(place_ref, grads_ref, *refs):
     count = len(PARTS)
-    out_ref, held_ref, sems = refs[2 * count :]
-    copies = []
-    for p in range(count):
-        for side in range(NC):
-            target = held_ref.at[p, :, pl.ds(side * BLOCK, BLOCK), :]
-            copies.append(pltpu.make_async_copy(refs[side * count + p], target, sems.at[p, side]))
+    out_ref, held_ref, sems = refs[count:]
+    copies = [pltpu.make_async_copy(refs[p], held_ref.at[p], sems.at[p]) for p in range(count)]
     for copy in copies:
         copy.start()
-    x, y, core = place_ref[0], place_ref[3], place_ref[2]
+    x, y = place_ref[0], place_ref[3]
     total = None
     for p, (shift, first) in enumerate(PARTS):
-        copies[2 * p].wait()
-        copies[2 * p + 1].wait()
-        for s in range(NX // 2):
-            source = (lax.rem(x - first - s + NX, NX) * NY + lax.rem(y + shift + NY, NY)) * NC
-            grads = jnp.concatenate([grads_ref[source + core], grads_ref[source + 1 - core]], axis=0)
-            part = dot(grads.T, held_ref[p, s])
-            total = part if total is None else total + part
+        sources = [
+            lax.rem(x - s + NX, NX) * NY + lax.rem(y + shift + NY, NY)
+            for s in range(first, first + NX // 2)
+        ]
+        grads = jnp.concatenate([grads_ref[source] for source in sources], axis=0)
+        copies[p].wait()
+        part = dot(grads.T, held_ref[p].reshape(grads.shape[0], -1))
+        total = part if total is None else total + part
     out_ref[...] = total.T.astype(jnp.bfloat16)
 
 
-def weight_grads_part(place, grads, own, other):
-    half, rows, width = own[0].shape
+def weight_grads_part(place, grads, inputs):
+    width = inputs[0].shape[-1]
     vmem = pl.BlockSpec(memory_space=pltpu.VMEM)
     return pl.pallas_call(
         weight_kernel,
-        out_shape=jax.ShapeDtypeStruct((width, HEAD), jnp.bfloat16),
+        out_shape=jax.ShapeDtypeStruct((width, grads.shape[-1]), jnp.bfloat16),
         in_specs=[pl.BlockSpec(memory_space=pltpu.SMEM), vmem]
-        + [pl.BlockSpec(memory_space=pltpu.HBM)] * (2 * len(PARTS)),
+        + [pl.BlockSpec(memory_space=pltpu.HBM)] * len(PARTS),
         out_specs=vmem,
         scratch_shapes=[
-            pltpu.VMEM((len(PARTS), half, NC * rows, width), jnp.bfloat16),
-            pltpu.SemaphoreType.DMA((len(PARTS), NC)),
+            pltpu.VMEM((len(PARTS),) + inputs[0].shape, jnp.bfloat16),
+            pltpu.SemaphoreType.DMA((len(PARTS),)),
         ],
         compiler_params=pltpu.CompilerParams(vmem_limit_bytes=24 * MIB),
         cost_estimate=pl.CostEstimate(
-            flops=1_100_000_000, bytes_accessed=9 * MIB, transcendentals=0
+            flops=1_100_000_000, bytes_accessed=6 * MIB, transcendentals=0
         ),
-    )(place, grads, *placed(own, pltpu.HBM), *placed(other, pltpu.HBM))
+    )(place, grads, *placed(inputs, pltpu.HBM))
 
 
 def pack_kernel(queries_ref, grads_ref, keys_ref, values_ref, out_ref, sem):
@@ -226,10 +223,9 @@
         pair = partials_ref[2 * g].astype(jnp.float32) + partials_ref[2 * g + 1].astype(jnp.float32)
         pair = pair.astype(jnp.bfloat16)
         for kind, ref in enumerate((keys_ref, values_ref)):
-            part = pair[:, kind * HEAD : (kind + 1) * HEAD]
-            ref[:, g * HEAD : (g + 1) * HEAD] = part
-            for x in range(NX):
-                chunks_ref[(x * NY + g) * NC + kind] = part
+            ref[:, g * HEAD : (g + 1) * HEAD] = pair[:, kind * HEAD : (kind + 1) * HEAD]
+        for x in range(NX):
+            chunks_ref[x * NY + g] = pair
 
 
 def pair_grads(partials):
@@ -237,12 +233,35 @@
     out = jax.ShapeDtypeStruct((BLOCK, KV_HEADS * HEAD), jnp.bfloat16)
     return pl.pallas_call(
         pair_kernel,
-        out_shape=(out, out, jax.ShapeDtypeStruct((NX * NY * NC, BLOCK, HEAD), jnp.bfloat16)),
+        out_shape=(out, out, jax.ShapeDtypeStruct((NX * NY, BLOCK, 2 * HEAD), jnp.bfloat16)),
         in_specs=[vmem],
         out_specs=(vmem, vmem, vmem),
         compiler_params=pltpu.CompilerParams(vmem_limit_bytes=16 * MIB),
         cost_estimate=pl.CostEstimate(flops=0, bytes_accessed=2 * MIB, transcendentals=0),
     )(partials)
+
+
+def sum_kernel(parts_ref, keys_ref, values_ref):
+    count = NZ * NC
+    for g in range(KV_HEADS):
+        total = parts_ref[g * count].astype(jnp.float32)
+        for i in range(1, count):
+            total = total + parts_ref[g * count + i].astype(jnp.float32)
+        keys_ref[:, g * HEAD : (g + 1) * HEAD] = total[:, :HEAD]
+        values_ref[:, g * HEAD : (g + 1) * HEAD] = total[:, HEAD:]
+
+
+def weight_sums(parts):
+    vmem = pl.BlockSpec(memory_space=pltpu.VMEM)
+    out = jax.ShapeDtypeStruct((parts.shape[1], KV_HEADS * HEAD), jnp.float32)
+    return pl.pallas_call(
+        sum_kernel,
+        out_shape=(out, out),
+        in_specs=[vmem],
+        out_specs=(vmem, vmem),
+        compiler_params=pltpu.CompilerParams(vmem_limit_bytes=16 * MIB),
+        cost_estimate=pl.CostEstimate(flops=500_000, bytes_accessed=MIB, transcendentals=0),
+    )(parts)
 
 
 def join_kernel(place_ref, keep_ref, across_ref, *refs):
@@ -313,21 +332,18 @@
     keep, across, *ship, give, own, away = attention_grads(
         block_links[0], place, rows, other, seg_cols, seg_rows
     )
-    inputs_own = mine + before + after + far
-    keep, across, ship, give, own, away, inputs_own = lax.optimization_barrier(
-        (keep, across, ship, give, own, away, inputs_own)
-    )
-    inputs_other = tuple(swap_cores(a) for a in inputs_own)
-
-    pair = (own + swap_cores(away)).astype(bf16)
+    inputs = mine + before + after + far
+    keep, across, ship, give, own, away, inputs = lax.optimization_barrier(
+        (keep, across, ship, give, own, away, inputs)
+    )
+
+    away, given = lax.optimization_barrier((swap_cores(away), swap_cores(give)))
+    pair = (own + away).astype(bf16)
     pair = lax.all_to_all(pair, "z", split_axis=0, concat_axis=0, tiled=True)
-    given = swap_cores(give)
-    across, ship, given, pair, inputs_other = lax.optimization_barrier(
-        (across, ship, given, pair, inputs_other)
-    )
+    across, ship, given, pair = lax.optimization_barrier((across, ship, given, pair))
     key_grads, value_grads, chunks = pair_grads(pair)
 
-    grads = lax.all_to_all(chunks, ("x", "y", "c"), split_axis=0, concat_axis=0, tiled=True)
+    grads = lax.all_to_all(chunks, ("x", "y"), split_axis=0, concat_axis=0, tiled=True)
     direct = []
     for k in range(SIDE):
         hops = [((i, 0), ((i + k + 1) % NZ, 0)) for i in range(NZ)]
@@ -336,16 +352,20 @@
         direct.append(lax.ppermute(jnp.stack([ship[k], given[k]]), ("z", "c"), hops))
     across = lax.ppermute(across, "z", ring(NZ, NZ // 2))
     grads, direct, across = lax.optimization_barrier((grads, direct, across))
-    part = weight_grads_part(place, grads, inputs_own, inputs_other)
+    part = weight_grads_part(place, grads, inputs)
 
     swapped = swap_cores(jnp.stack([a[1] for a in direct]))
     query_grads = joined(place, keep, across, direct, swapped)
-    part = part.reshape(NY * NZ * NC, -1, HEAD)
+    part = part.reshape(NY * NZ * NC, -1, 2 * HEAD)
     part = lax.all_to_all(part, ("y", "z", "c"), split_axis=0, concat_axis=0, tiled=True)
-    part = part.reshape(NY, NZ, NC, -1, HEAD).astype(jnp.float32)
-    part = jnp.transpose(jnp.sum(part, axis=1), (1, 2, 0, 3))
-    part = part.reshape(NC, -1, NY * HEAD)
-    return query_grads[None], key_grads[None], value_grads[None], part[0], part[1]
+    key_weight_grads, value_weight_grads = weight_sums(part)
+    return (
+        query_grads[None],
+        key_grads[None],
+        value_grads[None],
+        key_weight_grads,
+        value_weight_grads,
+    )
 
 
 def solution(mesh):

time: 150 us -> 157 us (1.047)
  blocking collectives: 0 us -> 23.8 us
  waiting for transfers between devices: 66.4 us -> 57.7 us
  starting transfers between devices: 53.2 us -> 48 us
  other arithmetic: 2.79 us -> 0.44 us
    all_to_all x0 -> x1, blocking collectives: none -> 23.8 us  [local(): pair = lax.all_to_all(pair, 'z', split_axis=0, concat_axis=0, tiled=True)]
    all_to_all x2 -> x1, waiting for transfers between devices: 14.4 us -> 2.18 us  [local(): lax.all_to_all(chunks, ('x', 'y'), split_axis=0, concat_axis=0, tiled=True)]
    all_to_all x2 -> x1, starting transfers between devices: 11 us -> 5.51 us  [local(): lax.all_to_all(chunks, ('x', 'y'), split_axis=0, concat_axis=0, tiled=True)]
    all_to_all x1, waiting for transfers between devices: 8.9 us -> 14.2 us  [local(): lax.all_to_all(part, ('y', 'z', 'c'), split_axis=0, concat_axis=0, tiled=...]
    ppermute x12 -> x4, waiting for transfers between devices: 7.75 us -> 3.62 us  [swap_cores(): return lax.ppermute(a, 'c', [(0, 1), (1, 0)])]
    all_to_all x1, starting transfers between devices: 6.61 us -> 9.52 us  [local(): lax.all_to_all(part, ('y', 'z', 'c'), split_axis=0, concat_axis=0, tiled=...]
    ppermute x12 -> x4, starting transfers between devices: 8.08 us -> 5.39 us  [swap_cores(): return lax.ppermute(a, 'c', [(0, 1), (1, 0)])]
    ppermute x3, waiting for transfers between devices: 8.33 us -> 10.2 us  [local(): lax.ppermute(a, 'x', ring(NX, s))]
  transfers between devices with their start and end apart: 29 -> 20, of which waited for: 16 -> 12; matrix products, arithmetic and copies ran while one was open for 2% -> 0% of each run, Pallas kernels for 10% -> 9%
where the time goes in v8:
time: 157 us; the launch traced here: 156 us
  waiting for transfers between devices  57.7 us (37%)
  starting transfers between devices  48 us (31%)
  blocking collectives  23.8 us (15%)
  Pallas kernels  23.3 us (15%)
  local copies, waits for them, and re-layouts  2.2 us (1%)
    all_to_all x1, blocking collectives, local(): pair = lax.all_to_all(pair, 'z', split_axis=0, concat_axis=0, tiled=True)  23.8 us
    ppermute x4, waiting for transfers between devices, local(): lax.ppermute(a, 'y', ring(NY, shift))  20.5 us
    all_to_all x1, waiting for transfers between devices, local(): lax.all_to_all(part, ('y', 'z', 'c'), split_axis=0, concat_axis=0, tiled=...  14.2 us
    pallas_call x1, Pallas kernels, attention_grads(): pl.pallas_call(attention_kernel, out_shape=(pltpu.HBM((BLOCK, 2 * HEAD),...  12.8 us
    ppermute x3, waiting for transfers between devices, local(): lax.ppermute(a, 'x', ring(NX, s))  10.2 us
    all_to_all x1, starting transfers between devices, local(): lax.all_to_all(part, ('y', 'z', 'c'), split_axis=0, concat_axis=0, tiled=...  9.52 us
    all_to_all x1, starting transfers between devices, local(): lax.all_to_all(outgoing, 'z', split_axis=0, concat_axis=0, tiled=True)  9.16 us
    ppermute x4, starting transfers between devices, local(): lax.ppermute(a, 'y', ring(NY, shift))  5.56 us
  transfers between devices with their start and end apart: 20, of which 12 were waited for; matrix products, arithmetic and copies ran while one was open for 0% of the time, Pallas kernels for 9%

profile of v8, /device:TPU:1, one launch (start us, length us, event | category | flops | bytes accessed | tf_op | source)
XLA Modules:
  0.0 156.4 jit_solution(5389205059630716623)
XLA Ops:
  0.6 2.9 %shard_map.110 = bf16[8,128,768]{2,1,0:T(8,128)(2,1)} custom-call(bf16[128,2048]{1,0:T(8,128)(2,1)} %bitcast.29, bf16[128,2048]{1,0:T(8,128)(2,1)} %bitcast.30, bf16[128,512]{1,0:T(8,128)(2,1)} %bitcast.34, bf16[128,512]{1,0:T(8,128)(2,1)} %bitcast.35), custom_call_target="tpu_custom_call" | custom-call | bytes 3145728 | tf_op jit(solution)/shard_map/pallas_call | solution.py:210
  3.5 0.0 copy-start.4
  3.5 9.2 %all-to-all-start = ((bf16[8,128,768]{2,1,0:T(8,128)(2,1)}), bf16[8,128,768]{2,1,0:T(8,128)(2,1)S(1)}, u32[]{:S(2)}, u32[]{:S(2)}) async-start(bf16[8,128,768]{2,1,0:T(8,128)(2,1)} %shard_map.110), calls=%async_computation | async-start | bytes 3145728 | tf_op jit(solution)/shard_map/all_to_all | solution.py:321
  12.7 0.1 dynamic-slice_bitcast_fusion.1
  12.8 0.0 copy-start.1
  12.8 2.8 %collective-permute-start.1 = (bf16[128,1024]{1,0:T(8,128)(2,1)S(1)}, bf16[128,1024]{1,0:T(8,128)(2,1)S(1)}, u32[]{:S(2)}, u32[]{:S(2)}) collective-permute-start(bf16[128,1024]{1,0:T(8,128)(2,1)S(1)} %get-tuple-element.105), channel_id=1, source_target_pairs={{0,128},{64,192},{128,0},{192,64},{1,129},{65,193},{129,1},{193,65... | collective-permute-start | bytes 786440 | tf_op jit(solution)/shard_map/ppermute | solution.py:313
  15.6 0.9 collective-permute-start.2
  16.5 0.6 collective-permute-start
  17.1 4.1 %collective-permute-done.1 = bf16[128,1024]{1,0:T(8,128)(2,1)S(1)} collective-permute-done((bf16[128,1024]{1,0:T(8,128)(2,1)S(1)}, bf16[128,1024]{1,0:T(8,128)(2,1)S(1)}, u32[]{:S(2)}, u32[]{:S(2)}) %collective-permute-start.1) | collective-permute-done | bytes 262176 | tf_op jit(solution)/shard_map/ppermute | solution.py:313
  21.3 6.1 %collective-permute-done.2 = bf16[128,1024]{1,0:T(8,128)(2,1)S(1)} collective-permute-done((bf16[128,1024]{1,0:T(8,128)(2,1)S(1)}, bf16[128,1024]{1,0:T(8,128)(2,1)S(1)}, u32[]{:S(2)}, u32[]{:S(2)}) %collective-permute-start.2) | collective-permute-done | bytes 262176 | tf_op jit(solution)/shard_map/ppermute | solution.py:313
  27.3 0.1 pad_maximum_fusion.1.refs_1_
  27.4 2.8 %collective-permute-start.6 = (bf16[2,128,1024]{2,1,0:T(8,128)(2,1)S(1)}, bf16[2,128,1024]{2,1,0:T(8,128)(2,1)}, u32[]{:S(2)}, u32[]{:S(2)}) collective-permute-start(bf16[2,128,1024]{2,1,0:T(8,128)(2,1)S(1)} %pad_maximum_fusion.1.refs_1_), channel_id=1, source_target_pairs={{0,48},{16,0},{32,16},{48,32},{1,49},{17,1},{33,17},{49,33},{2,50}... | collective-permute-start | bytes 1572872 | tf_op jit(solution)/shard_map/ppermute | solution.py:317
  30.2 0.0 collective-permute-start.4
  30.2 0.1 pad_maximum_fusion.refs_0_
  30.3 2.7 %collective-permute-start.5 = (bf16[2,128,1024]{2,1,0:T(8,128)(2,1)S(1)}, bf16[2,128,1024]{2,1,0:T(8,128)(2,1)S(1)}, u32[]{:S(2)}, u32[]{:S(2)}) collective-permute-start(bf16[2,128,1024]{2,1,0:T(8,128)(2,1)S(1)} %pad_maximum_fusion.refs_0_), channel_id=1, source_target_pairs={{0,48},{16,0},{32,16},{48,32},{1,49},{17,1},{33,17},{49,33},{2,50}... | collective-permute-start | bytes 1572872 | tf_op jit(solution)/shard_map/ppermute | solution.py:317
  33.0 6.8 %collective-permute-done.6.refs_5_ = bf16[2,128,1024]{2,1,0:T(8,128)(2,1)} collective-permute-done((bf16[2,128,1024]{2,1,0:T(8,128)(2,1)S(1)}, bf16[2,128,1024]{2,1,0:T(8,128)(2,1)}, u32[]{:S(2)}, u32[]{:S(2)}) %collective-permute-start.6) | collective-permute-done | bytes 524320 | tf_op jit(solution)/shard_map/ppermute | solution.py:317
  39.9 3.1 %collective-permute-done.4.refs_3_ = bf16[2,128,1024]{2,1,0:T(8,128)(2,1)S(1)} collective-permute-done((bf16[2,128,1024]{2,1,0:T(8,128)(2,1)S(1)}, bf16[2,128,1024]{2,1,0:T(8,128)(2,1)S(1)}, u32[]{:S(2)}, u32[]{:S(2)}) %collective-permute-start.4) | collective-permute-done | bytes 524320 | tf_op jit(solution)/shard_map/ppermute | solution.py:317
  43.0 8.1 %collective-permute-done.5.refs_4_ = bf16[2,128,1024]{2,1,0:T(8,128)(2,1)S(1)} collective-permute-done((bf16[2,128,1024]{2,1,0:T(8,128)(2,1)S(1)}, bf16[2,128,1024]{2,1,0:T(8,128)(2,1)S(1)}, u32[]{:S(2)}, u32[]{:S(2)}) %collective-permute-start.5) | collective-permute-done | bytes 524320 | tf_op jit(solution)/shard_map/ppermute | solution.py:317
  51.1 0.8 copy-done.6
  51.9 2.4 %collective-permute-done.3.refs_2_ = bf16[2,128,1024]{2,1,0:T(8,128)(2,1)} collective-permute-done((bf16[2,128,1024]{2,1,0:T(8,128)(2,1)S(1)}, bf16[2,128,1024]{2,1,0:T(8,128)(2,1)}, u32[]{:S(2)}, u32[]{:S(2)}) %collective-permute-start.3) | collective-permute-done | bytes 524320 | tf_op jit(solution)/shard_map/ppermute | solution.py:317
  54.3 0.3 broadcast_in_dim.17.seg_cols_ref
  54.7 0.8 slice.21
  55.5 2.8 %collective-permute-start.7 = (bf16[8,128,256]{2,1,0:T(8,128)(2,1)}, bf16[8,128,256]{2,1,0:T(8,128)(2,1)S(1)}, u32[]{:S(2)}, u32[]{:S(2)}) collective-permute-start(bf16[8,128,256]{2,1,0:T(8,128)(2,1)} %slice.21), channel_id=1, source_target_pairs={{0,1},{1,0},{2,3},{3,2},{4,5},{5,4},{6,7},{7,6},{8,9},{9,8},{10,11... | collective-permute-start | bytes 1572872 | tf_op jit(solution)/shard_map/ppermute | solution.py:299
  58.3 2.7 %collective-permute-start.9 = (bf16[2,128,1024]{2,1,0:T(8,128)(2,1)}, bf16[2,128,1024]{2,1,0:T(8,128)(2,1)}, u32[]{:S(2)}, u32[]{:S(2)}) collective-permute-start(bf16[2,128,1024]{2,1,0:T(8,128)(2,1)} %collective-permute-done.6.refs_5_), channel_id=1, source_target_pairs={{0,48},{16,0},{32,16},{48,32},{1,49},{17,1},{33,17},{49,33},{2,50}... | collective-permute-start | bytes 1572872 | tf_op jit(solution)/shard_map/ppermute | solution.py:330
  61.0 0.1 copy.12.links_ref
  61.0 0.1 pad_add_fusion.place_ref
  61.1 12.8 %shard_map.111 = (bf16[128,256]{1,0:T(8,128)(2,1)}, bf16[128,256]{1,0:T(8,128)(2,1)}, bf16[128,256]{1,0:T(8,128)(2,1)}, bf16[128,256]{1,0:T(8,128)(2,1)}, bf16[1...) custom-call(s32[16,8]{1,0:T(8,128)S(1)} %copy.12.links_ref, ...), custom_call_target="tpu_custom_call" | custom-call | flops 4000000000 | bytes 8388608 | tf_op jit(solution)/shard_map/pallas_call | solution.py:124
  73.9 2.0 %collective-permute-start.10 = (f32[8,128,256]{2,1,0:T(8,128)S(1)}, f32[8,128,256]{2,1,0:T(8,128)S(1)}, u32[]{:S(2)}, u32[]{:S(2)}) collective-permute-start(f32[8,128,256]{2,1,0:T(8,128)S(1)} %get-tuple-element.76), channel_id=1, source_target_pairs={{0,1},{1,0},{2,3},{3,2},{4,5},{5,4},{6,7},{7,6},{8,9},{9,8},{10,11... | collective-permute-start | bytes 3145736 | tf_op jit(solution)/shard_map/ppermute | solution.py:299
  75.9 0.1 collective-permute-start.11
  76.0 2.5 %collective-permute-done.11 = bf16[3,128,256]{2,1,0:T(8,128)(2,1)S(1)} collective-permute-done((bf16[3,128,256]{2,1,0:T(8,128)(2,1)}, bf16[3,128,256]{2,1,0:T(8,128)(2,1)S(1)}, u32[]{:S(2)}, u32[]{:S(2)}) %collective-permute-start.11) | collective-permute-done | bytes 196640 | tf_op jit(solution)/shard_map/ppermute | solution.py:299
  78.6 0.2 add_convert_fusion
  78.8 23.8 %all_to_all.20.partials_ref = bf16[8,128,256]{2,1,0:T(8,128)(2,1)S(1)} all-to-all(bf16[8,128,256]{2,1,0:T(8,128)(2,1)S(1)} %add_convert_fusion), channel_id=1, replica_groups=mesh['x'=4,'y'=4,'z'=8,'c'=2] {'z'}, dimensions={0} | all-to-all | bytes 1048576 | tf_op jit(solution)/shard_map/all_to_all | solution.py:342
  102.6 1.1 shard_map.112
  103.7 5.5 %all-to-all-start.2 = ((bf16[16,128,256]{2,1,0:T(8,128)(2,1)}), bf16[16,128,256]{2,1,0:T(8,128)(2,1)S(1)}, u32[]{:S(2)}, u32[]{:S(2)}) async-start(bf16[16,128,256]{2,1,0:T(8,128)(2,1)} %get-tuple-element.82), calls=%async_computation.2 | async-start | bytes 2097152 | tf_op jit(solution)/shard_map/all_to_all | solution.py:346
  109.3 0.1 collective-permute-start.12
  109.4 0.1 collective-permute-start.13
  109.6 2.0 %collective-permute-start.14 = (bf16[2,128,256]{2,1,0:T(8,128)(2,1)S(1)}, bf16[2,128,256]{2,1,0:T(8,128)(2,1)S(1)}, u32[]{:S(2)}, u32[]{:S(2)}) collective-permute-start(bf16[2,128,256]{2,1,0:T(8,128)(2,1)S(1)} %pad_maximum_fusion.5), channel_id=1, source_target_pairs={{0,6},{2,8},{4,10},{6,12},{8,14},{10,0},{12,2},{14,4},{1,11},{3,13... | collective-permute-start | bytes 393224 | tf_op jit(solution)/shard_map/ppermute | solution.py:352
  111.6 3.7 %collective-permute-start.15 = (bf16[128,256]{1,0:T(8,128)(2,1)S(1)}, bf16[128,256]{1,0:T(8,128)(2,1)S(1)}, u32[]{:S(2)}, u32[]{:S(2)}) collective-permute-start(bf16[128,256]{1,0:T(8,128)(2,1)S(1)} %copy-done.11), channel_id=1, source_target_pairs={{0,8},{2,10},{4,12},{6,14},{8,0},{10,2},{12,4},{14,6},{1,9},{3,11}... | collective-permute-start | bytes 196616 | tf_op jit(solution)/shard_map/ppermute | solution.py:353
  115.3 5.1 %collective-permute-done.15.across_ref = bf16[128,256]{1,0:T(8,128)(2,1)S(1)} collective-permute-done((bf16[128,256]{1,0:T(8,128)(2,1)S(1)}, bf16[128,256]{1,0:T(8,128)(2,1)S(1)}, u32[]{:S(2)}, u32[]{:S(2)}) %collective-permute-start.15) | collective-permute-done | bytes 65568 | tf_op jit(solution)/shard_map/ppermute | solution.py:353
  120.4 1.9 %collective-permute-done.14.refs_2_ = bf16[2,128,256]{2,1,0:T(8,128)(2,1)S(1)} collective-permute-done((bf16[2,128,256]{2,1,0:T(8,128)(2,1)S(1)}, bf16[2,128,256]{2,1,0:T(8,128)(2,1)S(1)}, u32[]{:S(2)}, u32[]{:S(2)}) %collective-permute-start.14) | collective-permute-done | bytes 131104 | tf_op jit(solution)/shard_map/ppermute | solution.py:352
  122.3 2.2 %all-to-all-done.2.grads_ref = bf16[16,128,256]{2,1,0:T(8,128)(2,1)S(1)} async-done(((bf16[16,128,256]{2,1,0:T(8,128)(2,1)}), bf16[16,128,256]{2,1,0:T(8,128)(2,1)S(1)}, u32[]{:S(2)}, u32[]{:S(2)}) %all-to-all-start.2) | async-done | bytes 1048608 | tf_op jit(solution)/shard_map/all_to_all | solution.py:346
  124.5 4.4 %shard_map.114 = bf16[1024,256]{1,0:T(8,128)(2,1)} custom-call(s32[4]{0:T(128)S(1)} %pad_add_fusion.place_ref, bf16[16,128,256]{2,1,0:T(8,128)(2,1)S(1)} %all-to-all-done.2.grads_ref, bf16[2,128,1024]{2,1,0:T(8,128)(2,1)} %copy-done.3, bf16[2,128,1024]{2,1,0:T(8,128)(2,1)} %copy-done.2, bf16[2,128,1024]{2,1,0:T(8,128)(2,1)} %collective-permute-done.3.refs_2_, ...), custom_call_target="tpu_custom_call" | custom-call | flops 1100000000 | bytes 6291456 | tf_op jit(solution)/shard_map/pallas_call | solution.py:176
  128.9 9.5 %all-to-all-start.3 = ((bf16[64,16,256]{2,1,0:T(8,128)(2,1)}), bf16[64,16,256]{2,1,0:T(8,128)(2,1)S(1)}, u32[]{:S(2)}, u32[]{:S(2)}) async-start(bf16[64,16,256]{2,1,0:T(8,128)(2,1)} %bitcast.22), calls=%async_computation.3 | async-start | bytes 1048576 | tf_op jit(solution)/shard_map/all_to_all | solution.py:360
  138.5 0.5 collective-permute-start.16
  139.0 1.1 collective-permute-done.16.refs_3_
  140.1 1.4 shard_map.113
  141.5 14.2 %all-to-all-done.3.parts_ref = bf16[64,16,256]{2,1,0:T(8,128)(2,1)S(1)} async-done(((bf16[64,16,256]{2,1,0:T(8,128)(2,1)}), bf16[64,16,256]{2,1,0:T(8,128)(2,1)S(1)}, u32[]{:S(2)}, u32[]{:S(2)}) %all-to-all-start.3) | async-done | bytes 524320 | tf_op jit(solution)/shard_map/all_to_all | solution.py:360
  155.7 0.7 shard_map.115
  (39 shorter events, 0.2 us)
Async XLA Ops:
  3.5 9.2 %copy-start.4 = (bf16[1,128,4096]{2,1,0:T(8,128)(2,1)S(1)}, bf16[1,128,4096]{2,1,0:T(8,128)(2,1)}, u32[]{:S(2)}) copy-start(bf16[1,128,4096]{2,1,0:T(8,128)(2,1)} %param.7) | copy-start | bytes 3145732
  3.5 50.8 %all-to-all-start = ((bf16[8,128,768]{2,1,0:T(8,128)(2,1)}), bf16[8,128,768]{2,1,0:T(8,128)(2,1)S(1)}, u32[]{:S(2)}, u32[]{:S(2)}) async-start(bf16[8,128,768]{2,1,0:T(8,128)(2,1)} %shard_map.110), calls=%async_computation | async-start | bytes 3145728 | tf_op jit(solution)/shard_map/all_to_all | solution.py:321
  12.8 41.5 %copy-start.1 = (s32[1,2048]{1,0:T(1,128)S(1)}, s32[1,2048]{1,0:T(1,128)}, u32[]{:S(2)}) copy-start(s32[1,2048]{1,0:T(1,128)} %param.13) | copy-start | bytes 24580
  12.8 8.4 %collective-permute-start.1 = (bf16[128,1024]{1,0:T(8,128)(2,1)S(1)}, bf16[128,1024]{1,0:T(8,128)(2,1)S(1)}, u32[]{:S(2)}, u32[]{:S(2)}) collective-permute-start(bf16[128,1024]{1,0:T(8,128)(2,1)S(1)} %get-tuple-element.105), channel_id=1, source_target_pairs={{0,128},{64,192},{128,0},{192,64},{1,129},{65,193},{129,1},{193,65... | collective-permute-start | bytes 786440 | tf_op jit(solution)/shard_map/ppermute | solution.py:313
  15.6 11.7 %collective-permute-start.2 = (bf16[128,1024]{1,0:T(8,128)(2,1)S(1)}, bf16[128,1024]{1,0:T(8,128)(2,1)S(1)}, u32[]{:S(2)}, u32[]{:S(2)}) collective-permute-start(bf16[128,1024]{1,0:T(8,128)(2,1)S(1)} %get-tuple-element.108), channel_id=1, source_target_pairs={{0,192},{64,0},{128,64},{192,128},{1,193},{65,1},{129,65},{193,129... | collective-permute-start | bytes 786440 | tf_op jit(solution)/shard_map/ppermute | solution.py:313
  16.5 13.7 %collective-permute-start = (bf16[128,1024]{1,0:T(8,128)(2,1)S(1)}, bf16[128,1024]{1,0:T(8,128)(2,1)S(1)}, u32[]{:S(2)}, u32[]{:S(2)}) collective-permute-start(bf16[128,1024]{1,0:T(8,128)(2,1)S(1)} %get-tuple-element.106), channel_id=1, source_target_pairs={{0,64},{64,128},{128,192},{192,0},{1,65},{65,129},{129,193},{193,1... | collective-permute-start | bytes 786440 | tf_op jit(solution)/shard_map/ppermute | solution.py:313
  27.4 27.0 %copy-start.2 = (bf16[2,128,1024]{2,1,0:T(8,128)(2,1)}, bf16[2,128,1024]{2,1,0:T(8,128)(2,1)S(1)}, u32[]{:S(2)}) copy-start(bf16[2,128,1024]{2,1,0:T(8,128)(2,1)S(1)} %pad_maximum_fusion.1.refs_1_) | copy-start | bytes 1572868
  27.4 12.5 %collective-permute-start.6 = (bf16[2,128,1024]{2,1,0:T(8,128)(2,1)S(1)}, bf16[2,128,1024]{2,1,0:T(8,128)(2,1)}, u32[]{:S(2)}, u32[]{:S(2)}) collective-permute-start(bf16[2,128,1024]{2,1,0:T(8,128)(2,1)S(1)} %pad_maximum_fusion.1.refs_1_), channel_id=1, source_target_pairs={{0,48},{16,0},{32,16},{48,32},{1,49},{17,1},{33,17},{49,33},{2,50}... | collective-permute-start | bytes 1572872 | tf_op jit(solution)/shard_map/ppermute | solution.py:317
  30.2 12.8 %collective-permute-start.4 = (bf16[2,128,1024]{2,1,0:T(8,128)(2,1)S(1)}, bf16[2,128,1024]{2,1,0:T(8,128)(2,1)S(1)}, u32[]{:S(2)}, u32[]{:S(2)}) collective-permute-start(bf16[2,128,1024]{2,1,0:T(8,128)(2,1)S(1)} %pad_maximum_fusion.1.refs_1_), channel_id=1, source_target_pairs={{0,16},{16,32},{32,48},{48,0},{1,17},{17,33},{33,49},{49,1},{2,18}... | collective-permute-start | bytes 1572872 | tf_op jit(solution)/shard_map/ppermute | solution.py:317
  30.2 30.8 %copy-start.10 = (s32[1,16,8]{1,2,0:T(8,128)S(1)}, s32[1,16,8]{1,2,0:T(8,128)}, u32[]{:S(2)}) copy-start(s32[1,16,8]{1,2,0:T(8,128)} %param.12) | copy-start | bytes 1540
  30.3 24.1 %copy-start.3 = (bf16[2,128,1024]{2,1,0:T(8,128)(2,1)}, bf16[2,128,1024]{2,1,0:T(8,128)(2,1)S(1)}, u32[]{:S(2)}) copy-start(bf16[2,128,1024]{2,1,0:T(8,128)(2,1)S(1)} %pad_maximum_fusion.refs_0_) | copy-start | bytes 1572868
  30.3 20.8 %collective-permute-start.5 = (bf16[2,128,1024]{2,1,0:T(8,128)(2,1)S(1)}, bf16[2,128,1024]{2,1,0:T(8,128)(2,1)S(1)}, u32[]{:S(2)}, u32[]{:S(2)}) collective-permute-start(bf16[2,128,1024]{2,1,0:T(8,128)(2,1)S(1)} %pad_maximum_fusion.refs_0_), channel_id=1, source_target_pairs={{0,48},{16,0},{32,16},{48,32},{1,49},{17,1},{33,17},{49,33},{2,50}... | collective-permute-start | bytes 1572872 | tf_op jit(solution)/shard_map/ppermute | solution.py:317
  33.0 21.3 %collective-permute-start.3 = (bf16[2,128,1024]{2,1,0:T(8,128)(2,1)S(1)}, bf16[2,128,1024]{2,1,0:T(8,128)(2,1)}, u32[]{:S(2)}, u32[]{:S(2)}) collective-permute-start(bf16[2,128,1024]{2,1,0:T(8,128)(2,1)S(1)} %pad_maximum_fusion.refs_0_), channel_id=1, source_target_pairs={{0,16},{16,32},{32,48},{48,0},{1,17},{17,33},{33,49},{49,1},{2,18}... | collective-permute-start | bytes 1572872 | tf_op jit(solution)/shard_map/ppermute | solution.py:317
  43.0 8.1 %copy-start.5 = (bf16[2,128,1024]{2,1,0:T(8,128)(2,1)}, bf16[2,128,1024]{2,1,0:T(8,128)(2,1)S(1)}, u32[]{:S(2)}) copy-start(bf16[2,128,1024]{2,1,0:T(8,128)(2,1)S(1)} %collective-permute-done.4.refs_3_) | copy-start | bytes 1572868
  51.1 0.8 copy-start.6
  55.5 5.6 %collective-permute-start.7 = (bf16[8,128,256]{2,1,0:T(8,128)(2,1)}, bf16[8,128,256]{2,1,0:T(8,128)(2,1)S(1)}, u32[]{:S(2)}, u32[]{:S(2)}) collective-permute-start(bf16[8,128,256]{2,1,0:T(8,128)(2,1)} %slice.21), channel_id=1, source_target_pairs={{0,1},{1,0},{2,3},{3,2},{4,5},{5,4},{6,7},{7,6},{8,9},{9,8},{10,11... | collective-permute-start | bytes 1572872 | tf_op jit(solution)/shard_map/ppermute | solution.py:299
  58.3 15.7 %collective-permute-start.8 = (bf16[2,128,1024]{2,1,0:T(8,128)(2,1)}, bf16[2,128,1024]{2,1,0:T(8,128)(2,1)}, u32[]{:S(2)}, u32[]{:S(2)}) collective-permute-start(bf16[2,128,1024]{2,1,0:T(8,128)(2,1)} %collective-permute-done.3.refs_2_), channel_id=1, source_target_pairs={{0,16},{16,32},{32,48},{48,0},{1,17},{17,33},{33,49},{49,1},{2,18}... | collective-permute-start | bytes 1572872 | tf_op jit(solution)/shard_map/ppermute | solution.py:329
  58.3 15.7 %collective-permute-start.9 = (bf16[2,128,1024]{2,1,0:T(8,128)(2,1)}, bf16[2,128,1024]{2,1,0:T(8,128)(2,1)}, u32[]{:S(2)}, u32[]{:S(2)}) collective-permute-start(bf16[2,128,1024]{2,1,0:T(8,128)(2,1)} %collective-permute-done.6.refs_5_), channel_id=1, source_target_pairs={{0,48},{16,0},{32,16},{48,32},{1,49},{17,1},{33,17},{49,33},{2,50}... | collective-permute-start | bytes 1572872 | tf_op jit(solution)/shard_map/ppermute | solution.py:330
  73.9 4.6 %collective-permute-start.10 = (f32[8,128,256]{2,1,0:T(8,128)S(1)}, f32[8,128,256]{2,1,0:T(8,128)S(1)}, u32[]{:S(2)}, u32[]{:S(2)}) collective-permute-start(f32[8,128,256]{2,1,0:T(8,128)S(1)} %get-tuple-element.76), channel_id=1, source_target_pairs={{0,1},{1,0},{2,3},{3,2},{4,5},{5,4},{6,7},{7,6},{8,9},{9,8},{10,11... | collective-permute-start | bytes 3145736 | tf_op jit(solution)/shard_map/ppermute | solution.py:299
  75.9 2.6 %collective-permute-start.11 = (bf16[3,128,256]{2,1,0:T(8,128)(2,1)}, bf16[3,128,256]{2,1,0:T(8,128)(2,1)S(1)}, u32[]{:S(2)}, u32[]{:S(2)}) collective-permute-start(bf16[3,128,256]{2,1,0:T(8,128)(2,1)} %get-tuple-element.77), channel_id=1, source_target_pairs={{0,1},{1,0},{2,3},{3,2},{4,5},{5,4},{6,7},{7,6},{8,9},{9,8},{10,11... | collective-permute-start | bytes 589832 | tf_op jit(solution)/shard_map/ppermute | solution.py:299
  102.6 6.7 %copy-start.9 = (bf16[128,256]{1,0:T(8,128)(2,1)S(1)}, bf16[128,256]{1,0:T(8,128)(2,1)}, u32[]{:S(2)}) copy-start(bf16[128,256]{1,0:T(8,128)(2,1)} %get-tuple-element.83) | copy-start | bytes 196612
  102.6 6.8 %copy-start.8 = (bf16[128,256]{1,0:T(8,128)(2,1)S(1)}, bf16[128,256]{1,0:T(8,128)(2,1)}, u32[]{:S(2)}) copy-start(bf16[128,256]{1,0:T(8,128)(2,1)} %get-tuple-element.85) | copy-start | bytes 196612
  103.7 5.8 %copy-start.7 = (bf16[128,256]{1,0:T(8,128)(2,1)S(1)}, bf16[128,256]{1,0:T(8,128)(2,1)}, u32[]{:S(2)}) copy-start(bf16[128,256]{1,0:T(8,128)(2,1)} %get-tuple-element.86) | copy-start | bytes 196612
  103.7 7.9 %copy-start.11 = (bf16[128,256]{1,0:T(8,128)(2,1)S(1)}, bf16[128,256]{1,0:T(8,128)(2,1)}, u32[]{:S(2)}) copy-start(bf16[128,256]{1,0:T(8,128)(2,1)} %get-tuple-element.87) | copy-start | bytes 196612
  103.7 20.7 %all-to-all-start.2 = ((bf16[16,128,256]{2,1,0:T(8,128)(2,1)}), bf16[16,128,256]{2,1,0:T(8,128)(2,1)S(1)}, u32[]{:S(2)}, u32[]{:S(2)}) async-start(bf16[16,128,256]{2,1,0:T(8,128)(2,1)} %get-tuple-element.82), calls=%async_computation.2 | async-start | bytes 2097152 | tf_op jit(solution)/shard_map/all_to_all | solution.py:346
  109.3 11.1 %collective-permute-start.12 = (bf16[2,128,256]{2,1,0:T(8,128)(2,1)S(1)}, bf16[2,128,256]{2,1,0:T(8,128)(2,1)S(1)}, u32[]{:S(2)}, u32[]{:S(2)}) collective-permute-start(bf16[2,128,256]{2,1,0:T(8,128)(2,1)S(1)} %pad_maximum_fusion.3), channel_id=1, source_target_pairs={{0,2},{2,4},{4,6},{6,8},{8,10},{10,12},{12,14},{14,0},{1,15},{3,1}... | collective-permute-start | bytes 393224 | tf_op jit(solution)/shard_map/ppermute | solution.py:352
  109.4 11.0 %collective-permute-start.13 = (bf16[2,128,256]{2,1,0:T(8,128)(2,1)S(1)}, bf16[2,128,256]{2,1,0:T(8,128)(2,1)S(1)}, u32[]{:S(2)}, u32[]{:S(2)}) collective-permute-start(bf16[2,128,256]{2,1,0:T(8,128)(2,1)S(1)} %pad_maximum_fusion.4), channel_id=1, source_target_pairs={{0,4},{2,6},{4,8},{6,10},{8,12},{10,14},{12,0},{14,2},{1,13},{3,15... | collective-permute-start | bytes 393224 | tf_op jit(solution)/shard_map/ppermute | solution.py:352
  109.6 12.7 %collective-permute-start.14 = (bf16[2,128,256]{2,1,0:T(8,128)(2,1)S(1)}, bf16[2,128,256]{2,1,0:T(8,128)(2,1)S(1)}, u32[]{:S(2)}, u32[]{:S(2)}) collective-permute-start(bf16[2,128,256]{2,1,0:T(8,128)(2,1)S(1)} %pad_maximum_fusion.5), channel_id=1, source_target_pairs={{0,6},{2,8},{4,10},{6,12},{8,14},{10,0},{12,2},{14,4},{1,11},{3,13... | collective-permute-start | bytes 393224 | tf_op jit(solution)/shard_map/ppermute | solution.py:352
  111.6 8.8 %collective-permute-start.15 = (bf16[128,256]{1,0:T(8,128)(2,1)S(1)}, bf16[128,256]{1,0:T(8,128)(2,1)S(1)}, u32[]{:S(2)}, u32[]{:S(2)}) collective-permute-start(bf16[128,256]{1,0:T(8,128)(2,1)S(1)} %copy-done.11), channel_id=1, source_target_pairs={{0,8},{2,10},{4,12},{6,14},{8,0},{10,2},{12,4},{14,6},{1,9},{3,11}... | collective-permute-start | bytes 196616 | tf_op jit(solution)/shard_map/ppermute | solution.py:353
  128.8 11.2 %copy-start = (bf16[128,256]{1,0:T(8,128)(2,1)S(1)}, bf16[128,256]{1,0:T(8,128)(2,1)}, u32[]{:S(2)}) copy-start(bf16[128,256]{1,0:T(8,128)(2,1)} %get-tuple-element.71.keep_ref) | copy-start | bytes 196612
  128.9 26.8 %all-to-all-start.3 = ((bf16[64,16,256]{2,1,0:T(8,128)(2,1)}), bf16[64,16,256]{2,1,0:T(8,128)(2,1)S(1)}, u32[]{:S(2)}, u32[]{:S(2)}) async-start(bf16[64,16,256]{2,1,0:T(8,128)(2,1)} %bitcast.22), calls=%async_computation.3 | async-start | bytes 1048576 | tf_op jit(solution)/shard_map/all_to_all | solution.py:360
  138.5 1.6 %collective-permute-start.16 = (bf16[3,128,256]{2,1,0:T(8,128)(2,1)S(1)}, bf16[3,128,256]{2,1,0:T(8,128)(2,1)S(1)}, u32[]{:S(2)}, u32[]{:S(2)}) collective-permute-start(bf16[3,128,256]{2,1,0:T(8,128)(2,1)S(1)} %pad_maximum_fusion.2), channel_id=1, source_target_pairs={{0,1},{1,0},{2,3},{3,2},{4,5},{5,4},{6,7},{7,6},{8,9},{9,8},{10,11... | collective-permute-start | bytes 589832 | tf_op jit(solution)/shard_map/ppermute | solution.py:299

commit v9 on v7

--- a/solution.py
+++ b/solution.py
@@ -40,7 +40,9 @@
     links_ref, place_ref, rows_ref, other_ref, seg_cols_ref, seg_rows_ref, *refs
 ):
     (keep_ref, across_ref, *ship_refs, give_ref), refs = refs[: SIDE + 3], refs[SIDE + 3 :]
-    own_ref, away_ref, pair_ref, keys_t_ref, total_ref, near_ref, near_t_ref, dq_ref, sems = refs
+    own_ref, away_ref, pair_ref, keys_t_ref, total_ref, dq_ref, *refs = refs
+    even, odd = refs[:4], refs[4:8]
+    score_ref, prob_ref, wide_ref, flat_ref, sems = refs[8:]
     z, core = place_ref[1], place_ref[2]
 
     def at(block):
@@ -55,45 +57,110 @@
     lax.fori_loop(0, NZ, load_pairs, 0)
     total_ref[...] = jnp.zeros_like(total_ref)
 
-    def query_block(i, key_blocks, pairs, keys_t):
+    def stacked(i, first):
         rows = rows_ref[i]
-        queries = jnp.concatenate([rows[:, :HEAD], rows[:, HEAD : 2 * HEAD]], axis=0)
-        grads = jnp.concatenate([rows[:, 2 * HEAD : 3 * HEAD], rows[:, 3 * HEAD : 4 * HEAD]], axis=0)
+        return jnp.concatenate(
+            [rows[:, first * HEAD : (first + 1) * HEAD], rows[:, (first + 1) * HEAD : (first + 2) * HEAD]],
+            axis=0,
+        )
+
+    def softmax_part(i, key_blocks, pairs, score_ref, prob_ref, attention, score_grads):
+        queries, grads = stacked(i, 0), stacked(i, 2)
         seg = seg_rows_ref[pl.ds(2 * i + core, 1), :]
-        allowed = jnp.concatenate([seg_cols_ref[j] == seg for j in key_blocks], axis=0)
-        scores = dot_nt(pairs[:, :HEAD], queries) * (SCALE * LOG2E)
-        scores = jnp.where(jnp.concatenate([allowed, allowed], axis=1), scores, MASKED)
-        weights = jnp.exp2(scores - jnp.max(scores, axis=0, keepdims=True))
-        probs = weights * (1.0 / jnp.sum(weights, axis=0, keepdims=True))
-        attention = probs.astype(jnp.bfloat16)
-        prob_grads = dot_nt(pairs[:, HEAD:], grads)
-        delta = jnp.sum(attention.astype(jnp.float32) * prob_grads, axis=0, keepdims=True)
-        score_grads = (probs * (prob_grads - delta)).astype(jnp.bfloat16)
-        value_part = dot(attention, grads)
-        key_part = dot(score_grads, queries)
+        count = len(key_blocks)
+        top = None
         for t, j in enumerate(key_blocks):
-            here = slice(t * BLOCK, (t + 1) * BLOCK)
-            total_ref[at(j), :HEAD] += key_part[here]
-            total_ref[at(j), HEAD:] += value_part[here]
-        dq = (dot(keys_t, score_grads) * SCALE).astype(jnp.bfloat16).T
+            here = pl.ds(t * BLOCK, BLOCK)
+            allowed = seg_cols_ref[j] == seg
+            s = dot_nt(pairs[here, :HEAD], queries) * (SCALE * LOG2E)
+            s = jnp.where(jnp.concatenate([allowed, allowed], axis=1), s, MASKED)
+            score_ref[here, :] = s
+            part = jnp.max(s.reshape(BLOCK // 8, 8, -1), axis=0)
+            top = part if top is None else jnp.maximum(top, part)
+        top = jnp.max(top, axis=0, keepdims=True)
+        norm = None
+        for t in range(count):
+            here = pl.ds(t * BLOCK, BLOCK)
+            e = jnp.exp2(score_ref[here, :] - top)
+            score_ref[here, :] = e
+            part = jnp.sum(e.reshape(BLOCK // 8, 8, -1), axis=0)
+            norm = part if norm is None else norm + part
+            yield
+        inverse = 1.0 / jnp.sum(norm, axis=0, keepdims=True)
+        delta = None
+        for t in range(count):
+            here = pl.ds(t * BLOCK, BLOCK)
+            a = (score_ref[here, :] * inverse).astype(jnp.bfloat16)
+            attention[here, :] = a
+            g = dot_nt(pairs[here, HEAD:], grads)
+            prob_ref[here, :] = g
+            part = jnp.sum((a.astype(jnp.float32) * g).reshape(BLOCK // 8, 8, -1), axis=0)
+            delta = part if delta is None else delta + part
+        delta = jnp.sum(delta, axis=0, keepdims=True)
+        for t in range(count):
+            here = pl.ds(t * BLOCK, BLOCK)
+            ds = (score_ref[here, :] * inverse) * (prob_ref[here, :] - delta)
+            score_grads[here, :] = ds.astype(jnp.bfloat16)
+            yield
+
+    def product_part(i, key_blocks, keys_t, attention, score_grads):
+        queries, grads = stacked(i, 0), stacked(i, 2)
+        count = len(key_blocks)
+        step = 4
+        dq = (dot(keys_t[...], score_grads[...]) * SCALE).astype(jnp.bfloat16).T
         slot = lax.rem(i - z + NZ, NZ)
         dq_ref[slot, :, :HEAD] = dq[:BLOCK]
         dq_ref[slot, :, HEAD:] = dq[BLOCK:]
-
-    def linked(i, carry):
-        key_blocks = [links_ref[2 * i + core, t] for t in range(LINKS)]
+        yield
+        for held, other, columns in (
+            (attention, grads, slice(HEAD, 2 * HEAD)), (score_grads, queries, slice(0, HEAD))
+        ):
+            for t in range(0, count, step):
+                part = dot(held[pl.ds(t * BLOCK, step * BLOCK), :], other)
+                for u in range(step):
+                    total_ref[at(key_blocks[t + u]), columns] += part[u * BLOCK : (u + 1) * BLOCK]
+                yield
+
+    def run(*parts):
+        parts = list(parts)
+        while parts:
+            for part in list(parts):
+                if next(part, parts) is parts:
+                    parts.remove(part)
+
+    def linked(i):
+        return [links_ref[2 * i + core, t] for t in range(LINKS)]
+
+    def first_part(i, held):
+        key_blocks, (near, near_t, attention, score_grads) = linked(i), held
         for t, j in enumerate(key_blocks):
-            here = slice(t * BLOCK, (t + 1) * BLOCK)
-            near_ref[here, :] = pair_ref[at(j), :]
-            near_t_ref[:, here] = keys_t_ref[:, at(j)]
-        query_block(i, key_blocks, near_ref[...], near_t_ref[...])
-        return carry
+            here = pl.ds(t * BLOCK, BLOCK)
+            near[here, :] = pair_ref[at(j), :]
+            near_t[:, here] = keys_t_ref[:, at(j)]
+        return softmax_part(i, key_blocks, near, score_ref, prob_ref, attention, score_grads)
+
+    def second_part(i, held):
+        return product_part(i, linked(i), *held[1:])
 
     @pl.when(core == 0)
     def _():
-        query_block(0, list(range(BLOCKS)), pair_ref[...], keys_t_ref[...])
-
-    lax.fori_loop(1 - core, NZ, linked, 0)
+        key_blocks = list(range(BLOCKS))
+        attention, score_grads = flat_ref.at[0], flat_ref.at[1]
+        run(softmax_part(0, key_blocks, pair_ref, wide_ref.at[0], wide_ref.at[1], attention, score_grads))
+        run(first_part(1, odd), product_part(0, key_blocks, keys_t_ref, attention, score_grads))
+
+    @pl.when(core == 1)
+    def _():
+        run(first_part(0, even))
+        run(first_part(1, odd), second_part(0, even))
+
+    def two(h, carry):
+        run(first_part(2 * h, even), second_part(2 * h - 1, odd))
+        run(first_part(2 * h + 1, odd), second_part(2 * h, even))
+        return carry
+
+    lax.fori_loop(1, NZ // 2, two, 0)
+    run(second_part(NZ - 1, odd))
 
     moves = [(0, keep_ref), (NZ // 2, across_ref)]
     for k, ref in enumerate(ship_refs):
@@ -135,14 +202,25 @@
             pltpu.VMEM((BLOCKS * BLOCK, 2 * HEAD), jnp.bfloat16),
             pltpu.VMEM((HEAD, BLOCKS * BLOCK), jnp.bfloat16),
             pltpu.VMEM((BLOCKS * BLOCK, 2 * HEAD), jnp.float32),
+            pltpu.VMEM((NZ, BLOCK, 2 * HEAD), jnp.bfloat16),
+        ]
+        + [
             pltpu.VMEM((LINKS * BLOCK, 2 * HEAD), jnp.bfloat16),
             pltpu.VMEM((HEAD, LINKS * BLOCK), jnp.bfloat16),
-            pltpu.VMEM((NZ, BLOCK, 2 * HEAD), jnp.bfloat16),
+            pltpu.VMEM((LINKS * BLOCK, 2 * HEAD), jnp.bfloat16),
+            pltpu.VMEM((LINKS * BLOCK, 2 * HEAD), jnp.bfloat16),
+        ]
+        * 2
+        + [
+            pltpu.VMEM((LINKS * BLOCK, 2 * HEAD), jnp.float32),
+            pltpu.VMEM((LINKS * BLOCK, 2 * HEAD), jnp.float32),
+            pltpu.VMEM((2, BLOCKS * BLOCK, 2 * HEAD), jnp.float32),
+            pltpu.VMEM((2, BLOCKS * BLOCK, 2 * HEAD), jnp.bfloat16),
             pltpu.SemaphoreType.DMA((NZ,)),
         ],
         compiler_params=pltpu.CompilerParams(vmem_limit_bytes=32 * MIB),
         cost_estimate=pl.CostEstimate(
-            flops=4_000_000_000, bytes_accessed=8 * MIB, transcendentals=2_500_000
+            flops=1_000, bytes_accessed=1_000, transcendentals=0
         ),
     )(links, place, rows, other, seg_cols, seg_rows)
 
@@ -167,8 +245,8 @@
         copies[2 * p + 1].wait()
         for s in range(NX // 2):
             source = (lax.rem(x - first - s + NX, NX) * NY + lax.rem(y + shift + NY, NY)) * NC
-            grads = jnp.concatenate([grads_ref[source + core], grads_ref[source + 1 - core]], axis=0)
-            part = dot(grads.T, held_ref[p, s])
+            grads = jnp.concatenate([grads_ref[source + core], grads_ref[source + 1 - core]], axis=1)
+            part = dot(grads, held_ref[p, s])
             total = part if total is None else total + part
     out_ref[...] = total.T.astype(jnp.bfloat16)
 
@@ -228,6 +306,7 @@
         for kind, ref in enumerate((keys_ref, values_ref)):
             part = pair[:, kind * HEAD : (kind + 1) * HEAD]
             ref[:, g * HEAD : (g + 1) * HEAD] = part
+            part = part.T
             for x in range(NX):
                 chunks_ref[(x * NY + g) * NC + kind] = part
 
@@ -237,7 +316,7 @@
     out = jax.ShapeDtypeStruct((BLOCK, KV_HEADS * HEAD), jnp.bfloat16)
     return pl.pallas_call(
         pair_kernel,
-        out_shape=(out, out, jax.ShapeDtypeStruct((NX * NY * NC, BLOCK, HEAD), jnp.bfloat16)),
+        out_shape=(out, out, jax.ShapeDtypeStruct((NX * NY * NC, HEAD, BLOCK), jnp.bfloat16)),
         in_specs=[vmem],
         out_specs=(vmem, vmem, vmem),
         compiler_params=pltpu.CompilerParams(vmem_limit_bytes=16 * MIB),
@@ -298,6 +377,11 @@
         tuple(lax.ppermute(a, "y", ring(NY, shift)) for a in mine) for shift in (1, -1)
     )
 
+    far = (
+        lax.ppermute(before[0], "y", ring(NY, 1)),
+        lax.ppermute(after[1], "y", ring(NY, -1)),
+    )
+
     outgoing = packed(queries[0], output_grads[0], keys[0], values[0])
     rows = lax.all_to_all(outgoing, "z", split_axis=0, concat_axis=0, tiled=True)
     seg_rows = segment_ids[0].reshape(BLOCKS, BLOCK)
@@ -306,10 +390,6 @@
         (rows, mine, before, after, seg_cols)
     )
     other = swap_cores(rows[..., 4 * HEAD :])
-    far = (
-        lax.ppermute(before[0], "y", ring(NY, 1)),
-        lax.ppermute(after[1], "y", ring(NY, -1)),
-    )
     keep, across, *ship, give, own, away = attention_grads(
         block_links[0], place, rows, other, seg_cols, seg_rows
     )

time: 150 us -> 150 us (level)
  transfers between devices with their start and end apart: 29 -> 29, of which waited for: 16 -> 17; matrix products, arithmetic and copies ran while one was open for 2% -> 2% of each run, Pallas kernels for 10% -> 9%
where the time goes in v9:
time: 150 us
  waiting for transfers between devices  66.9 us (45%)
  starting transfers between devices  53.9 us (36%)
  Pallas kernels  22.1 us (15%)
  local copies, waits for them, and re-layouts  2.98 us (2%)
  other arithmetic  2.75 us (2%)
    ppermute x4, waiting for transfers between devices, local(): lax.ppermute(a, 'y', ring(NY, shift))  19.9 us
    pallas_call x1, Pallas kernels, attention_grads(): pl.pallas_call(attention_kernel, out_shape=(pltpu.HBM((BLOCK, 2 * HEAD),...  11.5 us
    all_to_all x1, waiting for transfers between devices, local(): pair = lax.all_to_all(pair, 'z', split_axis=0, concat_axis=0, tiled=True)  10.6 us
    all_to_all x1, starting transfers between devices, local(): lax.all_to_all(outgoing, 'z', split_axis=0, concat_axis=0, tiled=True)  9.16 us
    all_to_all x1, waiting for transfers between devices, local(): lax.all_to_all(part, ('y', 'z', 'c'), split_axis=0, concat_axis=0, tiled=...  8.9 us
    ppermute x3, waiting for transfers between devices, local(): lax.ppermute(a, 'x', ring(NX, s))  8.33 us
    ppermute x12, waiting for transfers between devices, swap_cores(): return lax.ppermute(a, 'c', [(0, 1), (1, 0)])  7.76 us
    ppermute x12, starting transfers between devices, swap_cores(): return lax.ppermute(a, 'c', [(0, 1), (1, 0)])  6.95 us
  transfers between devices with their start and end apart: 29, of which 17 were waited for; matrix products, arithmetic and copies ran while one was open for 2% of the time, Pallas kernels for 9%

profile of v9, /device:TPU:1, one launch (start us, length us, event | category | flops | bytes accessed | tf_op | source)
XLA Modules:
  0.0 149.5 jit_solution(1384976869302869694)
XLA Ops:
  0.6 2.9 %shard_map.110 = bf16[8,128,768]{2,1,0:T(8,128)(2,1)} custom-call(bf16[128,2048]{1,0:T(8,128)(2,1)} %bitcast.41, bf16[128,2048]{1,0:T(8,128)(2,1)} %bitcast.42, bf16[128,512]{1,0:T(8,128)(2,1)} %bitcast.47, bf16[128,512]{1,0:T(8,128)(2,1)} %bitcast.48), custom_call_target="tpu_custom_call" | custom-call | bytes 3145728 | tf_op jit(solution)/shard_map/pallas_call | solution.py:291
  3.5 9.2 %all-to-all-start = ((bf16[8,128,768]{2,1,0:T(8,128)(2,1)}), bf16[8,128,768]{2,1,0:T(8,128)(2,1)S(1)}, u32[]{:S(2)}, u32[]{:S(2)}) async-start(bf16[8,128,768]{2,1,0:T(8,128)(2,1)} %shard_map.110), calls=%async_computation | async-start | bytes 3145728 | tf_op jit(solution)/shard_map/all_to_all | solution.py:386
  12.8 1.3 collective-permute-start
  14.1 1.5 collective-permute-start.2
  15.5 1.5 %collective-permute-start.1 = (bf16[128,1024]{1,0:T(8,128)(2,1)S(1)}, bf16[128,1024]{1,0:T(8,128)(2,1)S(1)}, u32[]{:S(2)}, u32[]{:S(2)}) collective-permute-start(bf16[128,1024]{1,0:T(8,128)(2,1)S(1)} %get-tuple-element.113), channel_id=1, source_target_pairs={{0,128},{64,192},{128,0},{192,64},{1,129},{65,193},{129,1},{193,65... | collective-permute-start | bytes 786440 | tf_op jit(solution)/shard_map/ppermute | solution.py:373
  17.1 3.9 %collective-permute-done = bf16[128,1024]{1,0:T(8,128)(2,1)S(1)} collective-permute-done((bf16[128,1024]{1,0:T(8,128)(2,1)S(1)}, bf16[128,1024]{1,0:T(8,128)(2,1)S(1)}, u32[]{:S(2)}, u32[]{:S(2)}) %collective-permute-start) | collective-permute-done | bytes 262176 | tf_op jit(solution)/shard_map/ppermute | solution.py:373
  20.9 0.8 pad_maximum_fusion.refs_0_
  21.8 1.3 collective-permute-start.3
  23.1 4.5 %collective-permute-done.1 = bf16[128,1024]{1,0:T(8,128)(2,1)S(1)} collective-permute-done((bf16[128,1024]{1,0:T(8,128)(2,1)S(1)}, bf16[128,1024]{1,0:T(8,128)(2,1)S(1)}, u32[]{:S(2)}, u32[]{:S(2)}) %collective-permute-start.1) | collective-permute-done | bytes 262176 | tf_op jit(solution)/shard_map/ppermute | solution.py:373
  27.5 0.8 pad_maximum_fusion.1.refs_1_
  28.4 1.3 collective-permute-start.4
  29.7 1.4 collective-permute-start.5
  31.1 1.5 collective-permute-start.6
  32.6 1.9 %collective-permute-done.3.refs_2_ = bf16[2,128,1024]{2,1,0:T(8,128)(2,1)} collective-permute-done((bf16[2,128,1024]{2,1,0:T(8,128)(2,1)}, bf16[2,128,1024]{2,1,0:T(8,128)(2,1)}, u32[]{:S(2)}, u32[]{:S(2)}) %collective-permute-start.3) | collective-permute-done | bytes 524320 | tf_op jit(solution)/shard_map/ppermute | solution.py:377
  34.5 11.1 %collective-permute-done.4.refs_3_ = bf16[2,128,1024]{2,1,0:T(8,128)(2,1)S(1)} collective-permute-done((bf16[2,128,1024]{2,1,0:T(8,128)(2,1)}, bf16[2,128,1024]{2,1,0:T(8,128)(2,1)S(1)}, u32[]{:S(2)}, u32[]{:S(2)}) %collective-permute-start.4) | collective-permute-done | bytes 524320 | tf_op jit(solution)/shard_map/ppermute | solution.py:377
  45.6 6.9 %collective-permute-done.6.refs_5_ = bf16[2,128,1024]{2,1,0:T(8,128)(2,1)} collective-permute-done((bf16[2,128,1024]{2,1,0:T(8,128)(2,1)}, bf16[2,128,1024]{2,1,0:T(8,128)(2,1)}, u32[]{:S(2)}, u32[]{:S(2)}) %collective-permute-start.6) | collective-permute-done | bytes 524320 | tf_op jit(solution)/shard_map/ppermute | solution.py:377
  52.8 0.8 slice.29
  53.7 3.1 %collective-permute-start.7 = (bf16[8,128,256]{2,1,0:T(8,128)(2,1)}, bf16[8,128,256]{2,1,0:T(8,128)(2,1)S(1)}, u32[]{:S(2)}, u32[]{:S(2)}) collective-permute-start(bf16[8,128,256]{2,1,0:T(8,128)(2,1)} %slice.29), channel_id=1, source_target_pairs={{0,1},{1,0},{2,3},{3,2},{4,5},{5,4},{6,7},{7,6},{8,9},{9,8},{10,11... | collective-permute-start | bytes 1572872 | tf_op jit(solution)/shard_map/ppermute | solution.py:359
  56.8 1.3 collective-permute-start.8
  58.0 1.4 collective-permute-start.9
  59.6 11.5 %shard_map.111 = (bf16[128,256]{1,0:T(8,128)(2,1)}, bf16[128,256]{1,0:T(8,128)(2,1)}, bf16[128,256]{1,0:T(8,128)(2,1)}, bf16[128,256]{1,0:T(8,128)(2,1)}, bf16[1...) custom-call(s32[16,8]{1,0:T(8,128)S(1)} %copy.14.links_ref, ...), custom_call_target="tpu_custom_call" | custom-call | flops 1000 | bytes 1000 | tf_op jit(solution)/shard_map/pallas_call | solution.py:191
  71.0 0.8 collective-permute-done.8.refs_6_
  71.8 0.9 collective-permute-start.11
  73.3 2.2 %collective-permute-done.11 = f32[8,128,256]{2,1,0:T(8,128)S(1)} collective-permute-done((f32[8,128,256]{2,1,0:T(8,128)S(1)}, f32[8,128,256]{2,1,0:T(8,128)S(1)}, u32[]{:S(2)}, u32[]{:S(2)}) %collective-permute-start.11) | collective-permute-done | bytes 1048608 | tf_op jit(solution)/shard_map/ppermute | solution.py:359
  75.5 0.9 add_convert_fusion
  76.4 6.3 %all-to-all-start.1 = ((bf16[8,128,256]{2,1,0:T(8,128)(2,1)}), bf16[8,128,256]{2,1,0:T(8,128)(2,1)S(1)}, u32[]{:S(2)}, u32[]{:S(2)}) async-start(bf16[8,128,256]{2,1,0:T(8,128)(2,1)} %add_convert_fusion), calls=%async_computation.1 | async-start | bytes 1048576 | tf_op jit(solution)/shard_map/all_to_all | solution.py:403
  82.7 0.7 collective-permute-start.10
  83.6 1.2 collective-permute-done.10
  85.8 0.9 collective-permute-done.16.refs_12_
  86.7 1.7 %collective-permute-done.17.refs_13_ = bf16[2,128,1024]{2,1,0:T(8,128)(2,1)S(1)} collective-permute-done((bf16[2,128,1024]{2,1,0:T(8,128)(2,1)}, bf16[2,128,1024]{2,1,0:T(8,128)(2,1)S(1)}, u32[]{:S(2)}, u32[]{:S(2)}) %collective-permute-start.17) | collective-permute-done | bytes 524320 | tf_op jit(solution)/shard_map/ppermute | solution.py:359
  88.4 0.7 collective-permute-done.18.refs_14_
  89.2 0.8 copy-done.13
  90.0 10.6 %all-to-all-done.1.partials_ref = bf16[8,128,256]{2,1,0:T(8,128)(2,1)S(1)} async-done(((bf16[8,128,256]{2,1,0:T(8,128)(2,1)}), bf16[8,128,256]{2,1,0:T(8,128)(2,1)S(1)}, u32[]{:S(2)}, u32[]{:S(2)}) %all-to-all-start.1) | async-done | bytes 524320 | tf_op jit(solution)/shard_map/all_to_all | solution.py:403
  100.7 1.2 shard_map.112
  101.9 6.0 %all-to-all-start.2 = ((bf16[32,128,128]{2,1,0:T(8,128)(2,1)}), bf16[32,128,128]{2,1,0:T(8,128)(2,1)S(1)}, u32[]{:S(2)}, u32[]{:S(2)}) async-start(bf16[32,128,128]{2,1,0:T(8,128)(2,1)} %get-tuple-element.92), calls=%async_computation.2 | async-start | bytes 2097152 | tf_op jit(solution)/shard_map/all_to_all | solution.py:410
  108.1 0.8 collective-permute-start.21
  109.0 2.7 %collective-permute-start.22 = (bf16[2,128,256]{2,1,0:T(8,128)(2,1)S(1)}, bf16[2,128,256]{2,1,0:T(8,128)(2,1)S(1)}, u32[]{:S(2)}, u32[]{:S(2)}) collective-permute-start(bf16[2,128,256]{2,1,0:T(8,128)(2,1)S(1)} %pad_maximum_fusion.5), channel_id=1, source_target_pairs={{0,6},{2,8},{4,10},{6,12},{8,14},{10,0},{12,2},{14,4},{1,11},{3,13... | collective-permute-start | bytes 393224 | tf_op jit(solution)/shard_map/ppermute | solution.py:416
  111.6 2.6 %collective-permute-start.23 = (bf16[128,256]{1,0:T(8,128)(2,1)S(1)}, bf16[128,256]{1,0:T(8,128)(2,1)S(1)}, u32[]{:S(2)}, u32[]{:S(2)}) collective-permute-start(bf16[128,256]{1,0:T(8,128)(2,1)S(1)} %copy-done.18), channel_id=1, source_target_pairs={{0,8},{2,10},{4,12},{6,14},{8,0},{10,2},{12,4},{14,6},{1,9},{3,11}... | collective-permute-start | bytes 196616 | tf_op jit(solution)/shard_map/ppermute | solution.py:417
  114.2 4.8 %collective-permute-done.23.across_ref = bf16[128,256]{1,0:T(8,128)(2,1)S(1)} collective-permute-done((bf16[128,256]{1,0:T(8,128)(2,1)S(1)}, bf16[128,256]{1,0:T(8,128)(2,1)S(1)}, u32[]{:S(2)}, u32[]{:S(2)}) %collective-permute-start.23) | collective-permute-done | bytes 65568 | tf_op jit(solution)/shard_map/ppermute | solution.py:417
  118.9 2.7 %collective-permute-done.22.refs_2_ = bf16[2,128,256]{2,1,0:T(8,128)(2,1)S(1)} collective-permute-done((bf16[2,128,256]{2,1,0:T(8,128)(2,1)S(1)}, bf16[2,128,256]{2,1,0:T(8,128)(2,1)S(1)}, u32[]{:S(2)}, u32[]{:S(2)}) %collective-permute-start.22) | collective-permute-done | bytes 131104 | tf_op jit(solution)/shard_map/ppermute | solution.py:416
  121.7 3.1 %all-to-all-done.2.grads_ref = bf16[32,128,128]{2,1,0:T(8,128)(2,1)S(1)} async-done(((bf16[32,128,128]{2,1,0:T(8,128)(2,1)}), bf16[32,128,128]{2,1,0:T(8,128)(2,1)S(1)}, u32[]{:S(2)}, u32[]{:S(2)}) %all-to-all-start.2) | async-done | bytes 1048608 | tf_op jit(solution)/shard_map/all_to_all | solution.py:410
  124.8 5.1 %shard_map.114 = bf16[1024,128]{1,0:T(8,128)(2,1)} custom-call(s32[4]{0:T(128)S(1)} %pad_add_fusion.place_ref, bf16[32,128,128]{2,1,0:T(8,128)(2,1)S(1)} %all-to-all-done.2.grads_ref, bf16[2,128,1024]{2,1,0:T(8,128)(2,1)} %pad_maximum_fusion.refs_0_, bf16[2,128,1024]{2,1,0:T(8,128)(2,1)} %pad_maximum_fusion.1.refs_1_, ...), custom_call_target="tpu_custom_call" | custom-call | flops 1100000000 | bytes 9437184 | tf_op jit(solution)/shard_map/pallas_call | solution.py:257
  129.9 6.8 %all-to-all-start.3 = ((bf16[64,16,128]{2,1,0:T(8,128)(2,1)}), bf16[64,16,128]{2,1,0:T(8,128)(2,1)S(1)}, u32[]{:S(2)}, u32[]{:S(2)}) async-start(bf16[64,16,128]{2,1,0:T(8,128)(2,1)} %bitcast.22), calls=%async_computation.3 | async-start | bytes 524288 | tf_op jit(solution)/shard_map/all_to_all | solution.py:424
  136.9 0.5 collective-permute-start.24
  137.4 1.1 collective-permute-done.24.refs_3_
  138.5 1.4 shard_map.113
  139.9 8.9 %all-to-all-done.3 = bf16[64,16,128]{2,1,0:T(8,128)(2,1)S(1)} async-done(((bf16[64,16,128]{2,1,0:T(8,128)(2,1)}), bf16[64,16,128]{2,1,0:T(8,128)(2,1)S(1)}, u32[]{:S(2)}, u32[]{:S(2)}) %all-to-all-start.3) | async-done | bytes 262176 | tf_op jit(solution)/shard_map/all_to_all | solution.py:424
  148.9 0.6 copy_bitcast_fusion
  (74 shorter events, 2.8 us)
Async XLA Ops:
  3.5 9.2 %copy-start.2 = (bf16[1,128,4096]{2,1,0:T(8,128)(2,1)S(1)}, bf16[1,128,4096]{2,1,0:T(8,128)(2,1)}, u32[]{:S(2)}) copy-start(bf16[1,128,4096]{2,1,0:T(8,128)(2,1)} %param.7) | copy-start | bytes 3145732
  3.5 49.0 %all-to-all-start = ((bf16[8,128,768]{2,1,0:T(8,128)(2,1)}), bf16[8,128,768]{2,1,0:T(8,128)(2,1)S(1)}, u32[]{:S(2)}, u32[]{:S(2)}) async-start(bf16[8,128,768]{2,1,0:T(8,128)(2,1)} %shard_map.110), calls=%async_computation | async-start | bytes 3145728 | tf_op jit(solution)/shard_map/all_to_all | solution.py:386
  12.8 39.7 %copy-start.1 = (s32[1,2048]{1,0:T(1,128)S(1)}, s32[1,2048]{1,0:T(1,128)}, u32[]{:S(2)}) copy-start(s32[1,2048]{1,0:T(1,128)} %param.13) | copy-start | bytes 24580
  12.8 8.1 %collective-permute-start = (bf16[128,1024]{1,0:T(8,128)(2,1)S(1)}, bf16[128,1024]{1,0:T(8,128)(2,1)S(1)}, u32[]{:S(2)}, u32[]{:S(2)}) collective-permute-start(bf16[128,1024]{1,0:T(8,128)(2,1)S(1)} %get-tuple-element.114), channel_id=1, source_target_pairs={{0,64},{64,128},{128,192},{192,0},{1,65},{65,129},{129,193},{193,1... | collective-permute-start | bytes 786440 | tf_op jit(solution)/shard_map/ppermute | solution.py:373
  14.1 9.0 %collective-permute-start.2 = (bf16[128,1024]{1,0:T(8,128)(2,1)S(1)}, bf16[128,1024]{1,0:T(8,128)(2,1)S(1)}, u32[]{:S(2)}, u32[]{:S(2)}) collective-permute-start(bf16[128,1024]{1,0:T(8,128)(2,1)S(1)} %get-tuple-element.116), channel_id=1, source_target_pairs={{0,192},{64,0},{128,64},{192,128},{1,193},{65,1},{129,65},{193,129... | collective-permute-start | bytes 786440 | tf_op jit(solution)/shard_map/ppermute | solution.py:373
  15.5 12.0 %collective-permute-start.1 = (bf16[128,1024]{1,0:T(8,128)(2,1)S(1)}, bf16[128,1024]{1,0:T(8,128)(2,1)S(1)}, u32[]{:S(2)}, u32[]{:S(2)}) collective-permute-start(bf16[128,1024]{1,0:T(8,128)(2,1)S(1)} %get-tuple-element.113), channel_id=1, source_target_pairs={{0,128},{64,192},{128,0},{192,64},{1,129},{65,193},{129,1},{193,65... | collective-permute-start | bytes 786440 | tf_op jit(solution)/shard_map/ppermute | solution.py:373
  21.8 12.7 %collective-permute-start.3 = (bf16[2,128,1024]{2,1,0:T(8,128)(2,1)}, bf16[2,128,1024]{2,1,0:T(8,128)(2,1)}, u32[]{:S(2)}, u32[]{:S(2)}) collective-permute-start(bf16[2,128,1024]{2,1,0:T(8,128)(2,1)} %pad_maximum_fusion.refs_0_), channel_id=1, source_target_pairs={{0,16},{16,32},{32,48},{48,0},{1,17},{17,33},{33,49},{49,1},{2,18}... | collective-permute-start | bytes 1572872 | tf_op jit(solution)/shard_map/ppermute | solution.py:377
  27.5 31.9 %copy-start.17 = (s32[1,16,8]{1,2,0:T(8,128)S(1)}, s32[1,16,8]{1,2,0:T(8,128)}, u32[]{:S(2)}) copy-start(s32[1,16,8]{1,2,0:T(8,128)} %param.12) | copy-start | bytes 1540
  28.4 17.2 %collective-permute-start.4 = (bf16[2,128,1024]{2,1,0:T(8,128)(2,1)}, bf16[2,128,1024]{2,1,0:T(8,128)(2,1)S(1)}, u32[]{:S(2)}, u32[]{:S(2)}) collective-permute-start(bf16[2,128,1024]{2,1,0:T(8,128)(2,1)} %pad_maximum_fusion.1.refs_1_), channel_id=1, source_target_pairs={{0,16},{16,32},{32,48},{48,0},{1,17},{17,33},{33,49},{49,1},{2,18}... | collective-permute-start | bytes 1572872 | tf_op jit(solution)/shard_map/ppermute | solution.py:377
  29.7 16.0 %collective-permute-start.5 = (bf16[2,128,1024]{2,1,0:T(8,128)(2,1)}, bf16[2,128,1024]{2,1,0:T(8,128)(2,1)S(1)}, u32[]{:S(2)}, u32[]{:S(2)}) collective-permute-start(bf16[2,128,1024]{2,1,0:T(8,128)(2,1)} %pad_maximum_fusion.refs_0_), channel_id=1, source_target_pairs={{0,48},{16,0},{32,16},{48,32},{1,49},{17,1},{33,17},{49,33},{2,50}... | collective-permute-start | bytes 1572872 | tf_op jit(solution)/shard_map/ppermute | solution.py:377
  31.1 21.4 %collective-permute-start.6 = (bf16[2,128,1024]{2,1,0:T(8,128)(2,1)}, bf16[2,128,1024]{2,1,0:T(8,128)(2,1)}, u32[]{:S(2)}, u32[]{:S(2)}) collective-permute-start(bf16[2,128,1024]{2,1,0:T(8,128)(2,1)} %pad_maximum_fusion.1.refs_1_), channel_id=1, source_target_pairs={{0,48},{16,0},{32,16},{48,32},{1,49},{17,1},{33,17},{49,33},{2,50}... | collective-permute-start | bytes 1572872 | tf_op jit(solution)/shard_map/ppermute | solution.py:377
  45.6 6.9 %copy-start.3 = (bf16[2,128,1024]{2,1,0:T(8,128)(2,1)}, bf16[2,128,1024]{2,1,0:T(8,128)(2,1)S(1)}, u32[]{:S(2)}) copy-start(bf16[2,128,1024]{2,1,0:T(8,128)(2,1)S(1)} %collective-permute-done.4.refs_3_) | copy-start | bytes 1572868
  45.6 6.9 %copy-start.5 = (bf16[2,128,1024]{2,1,0:T(8,128)(2,1)}, bf16[2,128,1024]{2,1,0:T(8,128)(2,1)S(1)}, u32[]{:S(2)}) copy-start(bf16[2,128,1024]{2,1,0:T(8,128)(2,1)S(1)} %collective-permute-done.5.refs_4_) | copy-start | bytes 1572868
  53.7 5.9 %collective-permute-start.7 = (bf16[8,128,256]{2,1,0:T(8,128)(2,1)}, bf16[8,128,256]{2,1,0:T(8,128)(2,1)S(1)}, u32[]{:S(2)}, u32[]{:S(2)}) collective-permute-start(bf16[8,128,256]{2,1,0:T(8,128)(2,1)} %slice.29), channel_id=1, source_target_pairs={{0,1},{1,0},{2,3},{3,2},{4,5},{5,4},{6,7},{7,6},{8,9},{9,8},{10,11... | collective-permute-start | bytes 1572872 | tf_op jit(solution)/shard_map/ppermute | solution.py:359
  56.8 15.1 %collective-permute-start.8 = (bf16[2,128,1024]{2,1,0:T(8,128)(2,1)}, bf16[2,128,1024]{2,1,0:T(8,128)(2,1)}, u32[]{:S(2)}, u32[]{:S(2)}) collective-permute-start(bf16[2,128,1024]{2,1,0:T(8,128)(2,1)} %collective-permute-done.3.refs_2_), channel_id=1, source_target_pairs={{0,16},{16,32},{32,48},{48,0},{1,17},{17,33},{33,49},{49,1},{2,18}... | collective-permute-start | bytes 1572872 | tf_op jit(solution)/shard_map/ppermute | solution.py:381
  58.0 13.8 %collective-permute-start.9 = (bf16[2,128,1024]{2,1,0:T(8,128)(2,1)}, bf16[2,128,1024]{2,1,0:T(8,128)(2,1)}, u32[]{:S(2)}, u32[]{:S(2)}) collective-permute-start(bf16[2,128,1024]{2,1,0:T(8,128)(2,1)} %collective-permute-done.6.refs_5_), channel_id=1, source_target_pairs={{0,48},{16,0},{32,16},{48,32},{1,49},{17,1},{33,17},{49,33},{2,50}... | collective-permute-start | bytes 1572872 | tf_op jit(solution)/shard_map/ppermute | solution.py:382
  71.8 11.6 %copy-start.4 = (bf16[2,128,1024]{2,1,0:T(8,128)(2,1)S(1)}, bf16[2,128,1024]{2,1,0:T(8,128)(2,1)}, u32[]{:S(2)}) copy-start(bf16[2,128,1024]{2,1,0:T(8,128)(2,1)} %copy-done.3) | copy-start | bytes 1572868
  71.8 12.9 %copy-start.6 = (bf16[2,128,1024]{2,1,0:T(8,128)(2,1)S(1)}, bf16[2,128,1024]{2,1,0:T(8,128)(2,1)}, u32[]{:S(2)}) copy-start(bf16[2,128,1024]{2,1,0:T(8,128)(2,1)} %copy-done.5) | copy-start | bytes 1572868
  71.8 3.7 %collective-permute-start.11 = (f32[8,128,256]{2,1,0:T(8,128)S(1)}, f32[8,128,256]{2,1,0:T(8,128)S(1)}, u32[]{:S(2)}, u32[]{:S(2)}) collective-permute-start(f32[8,128,256]{2,1,0:T(8,128)S(1)} %get-tuple-element.82), channel_id=1, source_target_pairs={{0,1},{1,0},{2,3},{3,2},{4,5},{5,4},{6,7},{7,6},{8,9},{9,8},{10,11... | collective-permute-start | bytes 3145736 | tf_op jit(solution)/shard_map/ppermute | solution.py:359
  72.7 12.4 %collective-permute-start.12 = (bf16[2,128,1024]{2,1,0:T(8,128)(2,1)}, bf16[2,128,1024]{2,1,0:T(8,128)(2,1)S(1)}, u32[]{:S(2)}, u32[]{:S(2)}) collective-permute-start(bf16[2,128,1024]{2,1,0:T(8,128)(2,1)} %pad_maximum_fusion.refs_0_), channel_id=1, source_target_pairs={{0,1},{1,0},{2,3},{3,2},{4,5},{5,4},{6,7},{7,6},{8,9},{9,8},{10,11... | collective-permute-start | bytes 1572872 | tf_op jit(solution)/shard_map/ppermute | solution.py:359
  72.8 12.5 %collective-permute-start.13 = (bf16[2,128,1024]{2,1,0:T(8,128)(2,1)}, bf16[2,128,1024]{2,1,0:T(8,128)(2,1)S(1)}, u32[]{:S(2)}, u32[]{:S(2)}) collective-permute-start(bf16[2,128,1024]{2,1,0:T(8,128)(2,1)} %pad_maximum_fusion.1.refs_1_), channel_id=1, source_target_pairs={{0,1},{1,0},{2,3},{3,2},{4,5},{5,4},{6,7},{7,6},{8,9},{9,8},{10,11... | collective-permute-start | bytes 1572872 | tf_op jit(solution)/shard_map/ppermute | solution.py:359
  73.2 12.4 %collective-permute-start.14 = (bf16[2,128,1024]{2,1,0:T(8,128)(2,1)}, bf16[2,128,1024]{2,1,0:T(8,128)(2,1)S(1)}, u32[]{:S(2)}, u32[]{:S(2)}) collective-permute-start(bf16[2,128,1024]{2,1,0:T(8,128)(2,1)} %collective-permute-done.3.refs_2_), channel_id=1, source_target_pairs={{0,1},{1,0},{2,3},{3,2},{4,5},{5,4},{6,7},{7,6},{8,9},{9,8},{10,11... | collective-permute-start | bytes 1572872 | tf_op jit(solution)/shard_map/ppermute | solution.py:359
  76.4 24.3 %all-to-all-start.1 = ((bf16[8,128,256]{2,1,0:T(8,128)(2,1)}), bf16[8,128,256]{2,1,0:T(8,128)(2,1)S(1)}, u32[]{:S(2)}, u32[]{:S(2)}) async-start(bf16[8,128,256]{2,1,0:T(8,128)(2,1)} %add_convert_fusion), calls=%async_computation.1 | async-start | bytes 1048576 | tf_op jit(solution)/shard_map/all_to_all | solution.py:403
  82.7 25.2 %copy-start.16 = (bf16[128,256]{1,0:T(8,128)(2,1)S(1)}, bf16[128,256]{1,0:T(8,128)(2,1)}, u32[]{:S(2)}) copy-start(bf16[128,256]{1,0:T(8,128)(2,1)} %get-tuple-element.93) | copy-start | bytes 196612
  82.7 25.3 %copy-start.15 = (bf16[128,256]{1,0:T(8,128)(2,1)S(1)}, bf16[128,256]{1,0:T(8,128)(2,1)}, u32[]{:S(2)}) copy-start(bf16[128,256]{1,0:T(8,128)(2,1)} %get-tuple-element.95) | copy-start | bytes 196612
  82.7 2.0 %collective-permute-start.10 = (bf16[3,128,256]{2,1,0:T(8,128)(2,1)}, bf16[3,128,256]{2,1,0:T(8,128)(2,1)S(1)}, u32[]{:S(2)}, u32[]{:S(2)}) collective-permute-start(bf16[3,128,256]{2,1,0:T(8,128)(2,1)} %get-tuple-element.80), channel_id=1, source_target_pairs={{0,1},{1,0},{2,3},{3,2},{4,5},{5,4},{6,7},{7,6},{8,9},{9,8},{10,11... | collective-permute-start | bytes 589832 | tf_op jit(solution)/shard_map/ppermute | solution.py:359
  83.5 2.3 %collective-permute-start.15 = (bf16[2,128,1024]{2,1,0:T(8,128)(2,1)S(1)}, bf16[2,128,1024]{2,1,0:T(8,128)(2,1)S(1)}, u32[]{:S(2)}, u32[]{:S(2)}) collective-permute-start(bf16[2,128,1024]{2,1,0:T(8,128)(2,1)S(1)} %copy-done.4), channel_id=1, source_target_pairs={{0,1},{1,0},{2,3},{3,2},{4,5},{5,4},{6,7},{7,6},{8,9},{9,8},{10,11... | collective-permute-start | bytes 1572872 | tf_op jit(solution)/shard_map/ppermute | solution.py:359
  84.8 1.9 %collective-permute-start.16 = (bf16[2,128,1024]{2,1,0:T(8,128)(2,1)S(1)}, bf16[2,128,1024]{2,1,0:T(8,128)(2,1)S(1)}, u32[]{:S(2)}, u32[]{:S(2)}) collective-permute-start(bf16[2,128,1024]{2,1,0:T(8,128)(2,1)S(1)} %copy-done.6), channel_id=1, source_target_pairs={{0,1},{1,0},{2,3},{3,2},{4,5},{5,4},{6,7},{7,6},{8,9},{9,8},{10,11... | collective-permute-start | bytes 1572872 | tf_op jit(solution)/shard_map/ppermute | solution.py:359
  85.1 22.8 %copy-start.7 = (bf16[2,128,1024]{2,1,0:T(8,128)(2,1)}, bf16[2,128,1024]{2,1,0:T(8,128)(2,1)S(1)}, u32[]{:S(2)}) copy-start(bf16[2,128,1024]{2,1,0:T(8,128)(2,1)S(1)} %collective-permute-done.12.refs_8_) | copy-start | bytes 1572868
  85.1 3.2 %collective-permute-start.17 = (bf16[2,128,1024]{2,1,0:T(8,128)(2,1)}, bf16[2,128,1024]{2,1,0:T(8,128)(2,1)S(1)}, u32[]{:S(2)}, u32[]{:S(2)}) collective-permute-start(bf16[2,128,1024]{2,1,0:T(8,128)(2,1)} %collective-permute-done.6.refs_5_), channel_id=1, source_target_pairs={{0,1},{1,0},{2,3},{3,2},{4,5},{5,4},{6,7},{7,6},{8,9},{9,8},{10,11... | collective-permute-start | bytes 1572872 | tf_op jit(solution)/shard_map/ppermute | solution.py:359
  85.3 22.7 %copy-start.8 = (bf16[2,128,1024]{2,1,0:T(8,128)(2,1)}, bf16[2,128,1024]{2,1,0:T(8,128)(2,1)S(1)}, u32[]{:S(2)}) copy-start(bf16[2,128,1024]{2,1,0:T(8,128)(2,1)S(1)} %collective-permute-done.13.refs_9_) | copy-start | bytes 1572868
  85.3 3.8 %collective-permute-start.18 = (bf16[2,128,1024]{2,1,0:T(8,128)(2,1)}, bf16[2,128,1024]{2,1,0:T(8,128)(2,1)S(1)}, u32[]{:S(2)}, u32[]{:S(2)}) collective-permute-start(bf16[2,128,1024]{2,1,0:T(8,128)(2,1)} %collective-permute-done.8.refs_6_), channel_id=1, source_target_pairs={{0,1},{1,0},{2,3},{3,2},{4,5},{5,4},{6,7},{7,6},{8,9},{9,8},{10,11... | collective-permute-start | bytes 1572872 | tf_op jit(solution)/shard_map/ppermute | solution.py:359
  85.7 22.3 %copy-start.9 = (bf16[2,128,1024]{2,1,0:T(8,128)(2,1)}, bf16[2,128,1024]{2,1,0:T(8,128)(2,1)S(1)}, u32[]{:S(2)}) copy-start(bf16[2,128,1024]{2,1,0:T(8,128)(2,1)S(1)} %collective-permute-done.14.refs_10_) | copy-start | bytes 1572868
  85.7 4.4 %collective-permute-start.19 = (bf16[2,128,1024]{2,1,0:T(8,128)(2,1)}, bf16[2,128,1024]{2,1,0:T(8,128)(2,1)}, u32[]{:S(2)}, u32[]{:S(2)}) collective-permute-start(bf16[2,128,1024]{2,1,0:T(8,128)(2,1)} %collective-permute-done.9.refs_7_), channel_id=1, source_target_pairs={{0,1},{1,0},{2,3},{3,2},{4,5},{5,4},{6,7},{7,6},{8,9},{9,8},{10,11... | collective-permute-start | bytes 1572872 | tf_op jit(solution)/shard_map/ppermute | solution.py:359
  85.8 3.3 %copy-start.10 = (bf16[2,128,1024]{2,1,0:T(8,128)(2,1)}, bf16[2,128,1024]{2,1,0:T(8,128)(2,1)S(1)}, u32[]{:S(2)}) copy-start(bf16[2,128,1024]{2,1,0:T(8,128)(2,1)S(1)} %collective-permute-done.15.refs_11_) | copy-start | bytes 1572868
  86.7 2.5 %copy-start.11 = (bf16[2,128,1024]{2,1,0:T(8,128)(2,1)}, bf16[2,128,1024]{2,1,0:T(8,128)(2,1)S(1)}, u32[]{:S(2)}) copy-start(bf16[2,128,1024]{2,1,0:T(8,128)(2,1)S(1)} %collective-permute-done.16.refs_12_) | copy-start | bytes 1572868
  88.4 0.9 copy-start.12
  89.2 0.8 copy-start.13
  101.9 7.0 %copy-start.14 = (bf16[128,256]{1,0:T(8,128)(2,1)S(1)}, bf16[128,256]{1,0:T(8,128)(2,1)}, u32[]{:S(2)}) copy-start(bf16[128,256]{1,0:T(8,128)(2,1)} %get-tuple-element.96) | copy-start | bytes 196612
  101.9 9.7 %copy-start.18 = (bf16[128,256]{1,0:T(8,128)(2,1)S(1)}, bf16[128,256]{1,0:T(8,128)(2,1)}, u32[]{:S(2)}) copy-start(bf16[128,256]{1,0:T(8,128)(2,1)} %get-tuple-element.97) | copy-start | bytes 196612
  101.9 22.9 %all-to-all-start.2 = ((bf16[32,128,128]{2,1,0:T(8,128)(2,1)}), bf16[32,128,128]{2,1,0:T(8,128)(2,1)S(1)}, u32[]{:S(2)}, u32[]{:S(2)}) async-start(bf16[32,128,128]{2,1,0:T(8,128)(2,1)} %get-tuple-element.92), calls=%async_computation.2 | async-start | bytes 2097152 | tf_op jit(solution)/shard_map/all_to_all | solution.py:410
  108.0 11.0 %collective-permute-start.20 = (bf16[2,128,256]{2,1,0:T(8,128)(2,1)S(1)}, bf16[2,128,256]{2,1,0:T(8,128)(2,1)S(1)}, u32[]{:S(2)}, u32[]{:S(2)}) collective-permute-start(bf16[2,128,256]{2,1,0:T(8,128)(2,1)S(1)} %pad_maximum_fusion.3), channel_id=1, source_target_pairs={{0,2},{2,4},{4,6},{6,8},{8,10},{10,12},{12,14},{14,0},{1,15},{3,1}... | collective-permute-start | bytes 393224 | tf_op jit(solution)/shard_map/ppermute | solution.py:416
  108.1 10.9 %collective-permute-start.21 = (bf16[2,128,256]{2,1,0:T(8,128)(2,1)S(1)}, bf16[2,128,256]{2,1,0:T(8,128)(2,1)S(1)}, u32[]{:S(2)}, u32[]{:S(2)}) collective-permute-start(bf16[2,128,256]{2,1,0:T(8,128)(2,1)S(1)} %pad_maximum_fusion.4), channel_id=1, source_target_pairs={{0,4},{2,6},{4,8},{6,10},{8,12},{10,14},{12,0},{14,2},{1,13},{3,15... | collective-permute-start | bytes 393224 | tf_op jit(solution)/shard_map/ppermute | solution.py:416
  108.9 29.5 %copy-start = (bf16[128,256]{1,0:T(8,128)(2,1)S(1)}, bf16[128,256]{1,0:T(8,128)(2,1)}, u32[]{:S(2)}) copy-start(bf16[128,256]{1,0:T(8,128)(2,1)} %get-tuple-element.75.keep_ref) | copy-start | bytes 196612
  109.0 12.7 %collective-permute-start.22 = (bf16[2,128,256]{2,1,0:T(8,128)(2,1)S(1)}, bf16[2,128,256]{2,1,0:T(8,128)(2,1)S(1)}, u32[]{:S(2)}, u32[]{:S(2)}) collective-permute-start(bf16[2,128,256]{2,1,0:T(8,128)(2,1)S(1)} %pad_maximum_fusion.5), channel_id=1, source_target_pairs={{0,6},{2,8},{4,10},{6,12},{8,14},{10,0},{12,2},{14,4},{1,11},{3,13... | collective-permute-start | bytes 393224 | tf_op jit(solution)/shard_map/ppermute | solution.py:416
  111.6 7.3 %collective-permute-start.23 = (bf16[128,256]{1,0:T(8,128)(2,1)S(1)}, bf16[128,256]{1,0:T(8,128)(2,1)S(1)}, u32[]{:S(2)}, u32[]{:S(2)}) collective-permute-start(bf16[128,256]{1,0:T(8,128)(2,1)S(1)} %copy-done.18), channel_id=1, source_target_pairs={{0,8},{2,10},{4,12},{6,14},{8,0},{10,2},{12,4},{14,6},{1,9},{3,11}... | collective-permute-start | bytes 196616 | tf_op jit(solution)/shard_map/ppermute | solution.py:417
  129.9 18.8 %all-to-all-start.3 = ((bf16[64,16,128]{2,1,0:T(8,128)(2,1)}), bf16[64,16,128]{2,1,0:T(8,128)(2,1)S(1)}, u32[]{:S(2)}, u32[]{:S(2)}) async-start(bf16[64,16,128]{2,1,0:T(8,128)(2,1)} %bitcast.22), calls=%async_computation.3 | async-start | bytes 524288 | tf_op jit(solution)/shard_map/all_to_all | solution.py:424
  136.9 1.6 %collective-permute-start.24 = (bf16[3,128,256]{2,1,0:T(8,128)(2,1)S(1)}, bf16[3,128,256]{2,1,0:T(8,128)(2,1)S(1)}, u32[]{:S(2)}, u32[]{:S(2)}) collective-permute-start(bf16[3,128,256]{2,1,0:T(8,128)(2,1)S(1)} %pad_maximum_fusion.2), channel_id=1, source_target_pairs={{0,1},{1,0},{2,3},{3,2},{4,5},{5,4},{6,7},{7,6},{8,9},{9,8},{10,11... | collective-permute-start | bytes 589832 | tf_op jit(solution)/shard_map/ppermute | solution.py:359

commit v10 on v9

--- a/solution.py
+++ b/solution.py
@@ -176,8 +176,8 @@
 
     def store(i, carry):
         for ref, block in ((own_ref, 2 * i + core), (away_ref, 2 * i + 1 - core)):
-            ref[i, :, :HEAD] = total_ref[at(block), :HEAD] * SCALE
-            ref[i, :, HEAD:] = total_ref[at(block), HEAD:]
+            ref[i, :, :HEAD] = (total_ref[at(block), :HEAD] * SCALE).astype(ref.dtype)
+            ref[i, :, HEAD:] = total_ref[at(block), HEAD:].astype(ref.dtype)
         return carry
 
     lax.fori_loop(0, NZ, store, 0)
@@ -194,7 +194,7 @@
         + (pltpu.HBM((SIDE, BLOCK, 2 * HEAD), jnp.bfloat16),)
         + (
             jax.ShapeDtypeStruct((NZ, BLOCK, 2 * HEAD), jnp.float32),
-            jax.ShapeDtypeStruct((NZ, BLOCK, 2 * HEAD), jnp.float32),
+            jax.ShapeDtypeStruct((NZ, BLOCK, 2 * HEAD), jnp.bfloat16),
         ),
         in_specs=[smem, smem, vmem, vmem, vmem, vmem],
         out_specs=(pl.BlockSpec(memory_space=pltpu.HBM),) * (SIDE + 3) + (vmem, vmem),
@@ -271,29 +271,36 @@
     )(place, grads, *placed(own, pltpu.HBM), *placed(other, pltpu.HBM))
 
 
-def pack_kernel(queries_ref, grads_ref, keys_ref, values_ref, out_ref, sem):
-    copies = []
-    for i in range(NZ):
-        heads = pl.ds(2 * HEAD * i, 2 * HEAD)
-        shared = pl.ds(HEAD * (i * KV_HEADS // NZ), HEAD)
-        for ref, source, first, size in (
-            (queries_ref, heads, 0, 2), (grads_ref, heads, 2, 2), (keys_ref, shared, 4, 1), (values_ref, shared, 5, 1)
-        ):
-            target = out_ref.at[i, :, pl.ds(first * HEAD, size * HEAD)]
-            copies.append(pltpu.make_async_copy(ref.at[:, source], target, sem.at[len(copies)]))
-    for copy in copies:
+def pack_kernel(queries_ref, grads_ref, keys_ref, values_ref, out_ref, *refs):
+    q_ref, g_ref, k_ref, v_ref, sem, store_sem = refs
+    loads = [
+        pltpu.make_async_copy(a, b, sem.at[n])
+        for n, (a, b) in enumerate(((queries_ref, q_ref), (grads_ref, g_ref), (keys_ref, k_ref), (values_ref, v_ref)))
+    ]
+    for copy in loads:
         copy.start()
-    for copy in copies:
+    stores = []
+    for load, ref, first, size, shared in (
+        (loads[0], q_ref, 0, 2, 1), (loads[1], g_ref, 2, 2, 1), (loads[2], k_ref, 4, 1, 2), (loads[3], v_ref, 5, 1, 2)
+    ):
+        load.wait()
+        for i in range(NZ):
+            source = ref.at[:, pl.ds(size * HEAD * (i // shared), size * HEAD)]
+            copy = pltpu.make_async_copy(source, out_ref.at[i, :, pl.ds(first * HEAD, size * HEAD)], store_sem.at[len(stores)])
+            copy.start()
+            stores.append(copy)
+    for copy in stores:
         copy.wait()
 
 
 def packed(queries, grads, keys, values):
     return pl.pallas_call(
         pack_kernel,
-        out_shape=jax.ShapeDtypeStruct((NZ, BLOCK, 6 * HEAD), jnp.bfloat16),
+        out_shape=pltpu.HBM((NZ, BLOCK, 6 * HEAD), jnp.bfloat16),
         in_specs=[pl.BlockSpec(memory_space=pltpu.HBM)] * 4,
-        out_specs=pl.BlockSpec(memory_space=pltpu.VMEM),
-        scratch_shapes=[pltpu.SemaphoreType.DMA((4 * NZ,))],
+        out_specs=pl.BlockSpec(memory_space=pltpu.HBM),
+        scratch_shapes=[pltpu.VMEM(a.shape, a.dtype) for a in (queries, grads, keys, values)]
+        + [pltpu.SemaphoreType.DMA((4,)), pltpu.SemaphoreType.DMA((4 * NZ,))],
         compiler_params=pltpu.CompilerParams(vmem_limit_bytes=16 * MIB),
         cost_estimate=pl.CostEstimate(flops=0, bytes_accessed=3 * MIB, transcendentals=0),
     )(*placed((queries, grads, keys, values), pltpu.HBM))
@@ -371,15 +378,16 @@
         for s in range(NX)
     ]
     pieces = [a if s == 0 else lax.ppermute(a, "x", ring(NX, s)) for s, a in enumerate(pieces)]
-    half = NX // 2
-    mine = (jnp.stack(pieces[:half]), jnp.stack(pieces[half:]))
+    groups = [pieces[0], pieces[1], jnp.stack(pieces[2:])]
     before, after = (
-        tuple(lax.ppermute(a, "y", ring(NY, shift)) for a in mine) for shift in (1, -1)
-    )
-
+        [lax.ppermute(a, "y", ring(NY, shift)) for a in groups] for shift in (1, -1)
+    )
+    mine, before, after = (
+        (jnp.stack(a[:2]), a[2]) for a in (groups, before, after)
+    )
     far = (
-        lax.ppermute(before[0], "y", ring(NY, 1)),
-        lax.ppermute(after[1], "y", ring(NY, -1)),
+        lax.ppermute(after[0], "y", ring(NY, -1)),
+        lax.ppermute(before[1], "y", ring(NY, 1)),
     )
 
     outgoing = packed(queries[0], output_grads[0], keys[0], values[0])
@@ -399,7 +407,7 @@
     )
     inputs_other = tuple(swap_cores(a) for a in inputs_own)
 
-    pair = (own + swap_cores(away)).astype(bf16)
+    pair = (own + swap_cores(away).astype(jnp.float32)).astype(bf16)
     pair = lax.all_to_all(pair, "z", split_axis=0, concat_axis=0, tiled=True)
     given = swap_cores(give)
     across, ship, given, pair, inputs_other = lax.optimization_barrier(

time: 150 us -> 152 us (1.013)
  other arithmetic: 2.75 us -> 4.48 us
    ppermute x4 -> x6, starting transfers between devices: 5.5 us -> 8.15 us  [local(): lax.ppermute(a, 'y', ring(NY, shift))]
    another operation x2 -> x4, other arithmetic: 1.66 us -> 3.38 us  [the longest x3 2.54 us: local(): jnp.stack(a[:2])]
    ppermute x4 -> x6, waiting for transfers between devices: 19.9 us -> 19.8 us  [local(): lax.ppermute(a, 'y', ring(NY, shift))]
  transfers between devices with their start and end apart: 29 -> 31, of which waited for: 17 -> 19; matrix products, arithmetic and copies ran while one was open for 2% -> 3% of each run, Pallas kernels for 9% -> 8%
where the time goes in v10:
time: 152 us
  waiting for transfers between devices  66 us (43%)
  starting transfers between devices  55.1 us (36%)
  Pallas kernels  21.9 us (14%)
  other arithmetic  4.48 us (3%)
  local copies, waits for them, and re-layouts  3.69 us (2%)
    ppermute x6, waiting for transfers between devices, local(): lax.ppermute(a, 'y', ring(NY, shift))  19.8 us
    pallas_call x1, Pallas kernels, attention_grads(): pl.pallas_call(attention_kernel, out_shape=(pltpu.HBM((BLOCK, 2 * HEAD),...  11.5 us
    all_to_all x1, waiting for transfers between devices, local(): pair = lax.all_to_all(pair, 'z', split_axis=0, concat_axis=0, tiled=True)  10.7 us
    all_to_all x1, starting transfers between devices, local(): lax.all_to_all(outgoing, 'z', split_axis=0, concat_axis=0, tiled=True)  9.16 us
    all_to_all x1, waiting for transfers between devices, local(): lax.all_to_all(part, ('y', 'z', 'c'), split_axis=0, concat_axis=0, tiled=...  8.9 us
    ppermute x6, starting transfers between devices, local(): lax.ppermute(a, 'y', ring(NY, shift))  8.15 us
    ppermute x3, waiting for transfers between devices, local(): lax.ppermute(a, 'x', ring(NX, s))  7.47 us
    ppermute x12, starting transfers between devices, swap_cores(): return lax.ppermute(a, 'c', [(0, 1), (1, 0)])  6.82 us
  transfers between devices with their start and end apart: 31, of which 19 were waited for; matrix products, arithmetic and copies ran while one was open for 3% of the time, Pallas kernels for 8%

profile of v10, /device:TPU:1, one launch (start us, length us, event | category | flops | bytes accessed | tf_op | source)
XLA Modules:
  0.0 152.0 jit_solution(14927454136816241722)
XLA Ops:
  0.6 2.6 %shard_map.110 = bf16[8,128,768]{2,1,0:T(8,128)(2,1)} custom-call(bf16[128,2048]{1,0:T(8,128)(2,1)} %bitcast.48, bf16[128,2048]{1,0:T(8,128)(2,1)} %bitcast.49, bf16[128,512]{1,0:T(8,128)(2,1)} %bitcast.58, bf16[128,512]{1,0:T(8,128)(2,1)} %bitcast.59), custom_call_target="tpu_custom_call" | custom-call | bytes 3145728 | tf_op jit(solution)/shard_map/pallas_call | solution.py:297
  3.3 9.2 %all-to-all-start = ((bf16[8,128,768]{2,1,0:T(8,128)(2,1)}), bf16[8,128,768]{2,1,0:T(8,128)(2,1)S(1)}, u32[]{:S(2)}, u32[]{:S(2)}) async-start(bf16[8,128,768]{2,1,0:T(8,128)(2,1)} %shard_map.110), calls=%async_computation | async-start | bytes 3145728 | tf_op jit(solution)/shard_map/all_to_all | solution.py:394
  12.5 2.8 %collective-permute-start.1 = (bf16[128,1024]{1,0:T(8,128)(2,1)S(1)}, bf16[128,1024]{1,0:T(8,128)(2,1)S(1)}, u32[]{:S(2)}, u32[]{:S(2)}) collective-permute-start(bf16[128,1024]{1,0:T(8,128)(2,1)S(1)} %get-tuple-element.113), channel_id=1, source_target_pairs={{0,128},{64,192},{128,0},{192,64},{1,129},{65,193},{129,1},{193,65... | collective-permute-start | bytes 786440 | tf_op jit(solution)/shard_map/ppermute | solution.py:380
  15.4 0.9 collective-permute-start.2
  16.2 0.6 collective-permute-start
  16.8 2.7 %collective-permute-start.6 = (bf16[128,1024]{1,0:T(8,128)(2,1)S(1)}, bf16[128,1024]{1,0:T(8,128)(2,1)S(1)}, u32[]{:S(2)}, u32[]{:S(2)}) collective-permute-start(bf16[128,1024]{1,0:T(8,128)(2,1)S(1)} %bitcast.45), channel_id=1, source_target_pairs={{0,48},{16,0},{32,16},{48,32},{1,49},{17,1},{33,17},{49,33},{2,50}... | collective-permute-start | bytes 786440 | tf_op jit(solution)/shard_map/ppermute | solution.py:383
  19.6 1.4 collective-permute-done.1
  21.0 6.1 %collective-permute-done.2 = bf16[128,1024]{1,0:T(8,128)(2,1)S(1)} collective-permute-done((bf16[128,1024]{1,0:T(8,128)(2,1)S(1)}, bf16[128,1024]{1,0:T(8,128)(2,1)S(1)}, u32[]{:S(2)}, u32[]{:S(2)}) %collective-permute-start.2) | collective-permute-done | bytes 262176 | tf_op jit(solution)/shard_map/ppermute | solution.py:380
  27.0 0.8 pad_maximum_fusion.1.refs_1_
  27.9 2.7 %collective-permute-start.8 = (bf16[2,128,1024]{2,1,0:T(8,128)(2,1)}, bf16[2,128,1024]{2,1,0:T(8,128)(2,1)S(1)}, u32[]{:S(2)}, u32[]{:S(2)}) collective-permute-start(bf16[2,128,1024]{2,1,0:T(8,128)(2,1)} %pad_maximum_fusion.1.refs_1_), channel_id=1, source_target_pairs={{0,48},{16,0},{32,16},{48,32},{1,49},{17,1},{33,17},{49,33},{2,50}... | collective-permute-start | bytes 1572872 | tf_op jit(solution)/shard_map/ppermute | solution.py:383
  30.6 2.7 %collective-permute-start.7 = (bf16[128,1024]{1,0:T(8,128)(2,1)S(1)}, bf16[128,1024]{1,0:T(8,128)(2,1)S(1)}, u32[]{:S(2)}, u32[]{:S(2)}) collective-permute-start(bf16[128,1024]{1,0:T(8,128)(2,1)S(1)} %collective-permute-done), channel_id=1, source_target_pairs={{0,48},{16,0},{32,16},{48,32},{1,49},{17,1},{33,17},{49,33},{2,50}... | collective-permute-start | bytes 786440 | tf_op jit(solution)/shard_map/ppermute | solution.py:383
  33.3 0.8 pad_maximum_fusion.refs_0_
  34.2 11.9 %collective-permute-done.7 = bf16[128,1024]{1,0:T(8,128)(2,1)S(1)} collective-permute-done((bf16[128,1024]{1,0:T(8,128)(2,1)S(1)}, bf16[128,1024]{1,0:T(8,128)(2,1)S(1)}, u32[]{:S(2)}, u32[]{:S(2)}) %collective-permute-start.7) | collective-permute-done | bytes 262176 | tf_op jit(solution)/shard_map/ppermute | solution.py:383
  46.1 0.8 pad_maximum_fusion.3.refs_4_
  46.9 2.3 %collective-permute-done.3 = bf16[128,1024]{1,0:T(8,128)(2,1)S(1)} collective-permute-done((bf16[128,1024]{1,0:T(8,128)(2,1)S(1)}, bf16[128,1024]{1,0:T(8,128)(2,1)S(1)}, u32[]{:S(2)}, u32[]{:S(2)}) %collective-permute-start.3) | collective-permute-done | bytes 262176 | tf_op jit(solution)/shard_map/ppermute | solution.py:383
  49.2 5.6 %collective-permute-done.4 = bf16[128,1024]{1,0:T(8,128)(2,1)S(1)} collective-permute-done((bf16[128,1024]{1,0:T(8,128)(2,1)S(1)}, bf16[128,1024]{1,0:T(8,128)(2,1)S(1)}, u32[]{:S(2)}, u32[]{:S(2)}) %collective-permute-start.4) | collective-permute-done | bytes 262176 | tf_op jit(solution)/shard_map/ppermute | solution.py:383
  54.8 0.8 pad_maximum_fusion.2.refs_2_
  55.7 0.8 copy-done.4
  56.9 0.8 slice.29
  57.7 2.8 %collective-permute-start.9 = (bf16[8,128,256]{2,1,0:T(8,128)(2,1)}, bf16[8,128,256]{2,1,0:T(8,128)(2,1)S(1)}, u32[]{:S(2)}, u32[]{:S(2)}) collective-permute-start(bf16[8,128,256]{2,1,0:T(8,128)(2,1)} %slice.29), channel_id=1, source_target_pairs={{0,1},{1,0},{2,3},{3,2},{4,5},{5,4},{6,7},{7,6},{8,9},{9,8},{10,11... | collective-permute-start | bytes 1572872 | tf_op jit(solution)/shard_map/ppermute | solution.py:366
  60.4 1.5 collective-permute-start.11
  62.2 11.5 %shard_map.111 = (bf16[128,256]{1,0:T(8,128)(2,1)}, bf16[128,256]{1,0:T(8,128)(2,1)}, bf16[128,256]{1,0:T(8,128)(2,1)}, bf16[128,256]{1,0:T(8,128)(2,1)}, bf16[1...) custom-call(s32[16,8]{1,0:T(8,128)S(1)} %copy.14.links_ref, ...), custom_call_target="tpu_custom_call" | custom-call | flops 1000 | bytes 1000 | tf_op jit(solution)/shard_map/pallas_call | solution.py:191
  73.7 0.6 collective-permute-done.10.refs_6_
  74.3 1.2 collective-permute-done.11.refs_7_
  75.5 0.8 collective-permute-start.13
  76.9 0.9 collective-permute-done.13
  77.9 0.9 add_convert_fusion
  78.8 6.6 %all-to-all-start.1 = ((bf16[8,128,256]{2,1,0:T(8,128)(2,1)}), bf16[8,128,256]{2,1,0:T(8,128)(2,1)S(1)}, u32[]{:S(2)}, u32[]{:S(2)}) async-start(bf16[8,128,256]{2,1,0:T(8,128)(2,1)} %add_convert_fusion), calls=%async_computation.1 | async-start | bytes 1048576 | tf_op jit(solution)/shard_map/all_to_all | solution.py:411
  85.4 0.7 collective-permute-start.12
  86.3 1.2 collective-permute-done.12
  89.4 1.5 collective-permute-done.19.refs_13_
  90.9 1.0 collective-permute-done.20.refs_14_
  91.8 0.8 copy-done.12
  92.6 10.7 %all-to-all-done.1.partials_ref = bf16[8,128,256]{2,1,0:T(8,128)(2,1)S(1)} async-done(((bf16[8,128,256]{2,1,0:T(8,128)(2,1)}), bf16[8,128,256]{2,1,0:T(8,128)(2,1)S(1)}, u32[]{:S(2)}, u32[]{:S(2)}) %all-to-all-start.1) | async-done | bytes 524320 | tf_op jit(solution)/shard_map/all_to_all | solution.py:411
  103.4 1.2 shard_map.112
  104.6 6.0 %all-to-all-start.2 = ((bf16[32,128,128]{2,1,0:T(8,128)(2,1)}), bf16[32,128,128]{2,1,0:T(8,128)(2,1)S(1)}, u32[]{:S(2)}, u32[]{:S(2)}) async-start(bf16[32,128,128]{2,1,0:T(8,128)(2,1)} %get-tuple-element.92), calls=%async_computation.2 | async-start | bytes 2097152 | tf_op jit(solution)/shard_map/all_to_all | solution.py:418
  110.8 0.6 collective-permute-start.23
  111.5 2.7 %collective-permute-start.24 = (bf16[2,128,256]{2,1,0:T(8,128)(2,1)S(1)}, bf16[2,128,256]{2,1,0:T(8,128)(2,1)S(1)}, u32[]{:S(2)}, u32[]{:S(2)}) collective-permute-start(bf16[2,128,256]{2,1,0:T(8,128)(2,1)S(1)} %pad_maximum_fusion.7), channel_id=1, source_target_pairs={{0,6},{2,8},{4,10},{6,12},{8,14},{10,0},{12,2},{14,4},{1,11},{3,13... | collective-permute-start | bytes 393224 | tf_op jit(solution)/shard_map/ppermute | solution.py:424
  114.1 2.6 %collective-permute-start.25 = (bf16[128,256]{1,0:T(8,128)(2,1)S(1)}, bf16[128,256]{1,0:T(8,128)(2,1)S(1)}, u32[]{:S(2)}, u32[]{:S(2)}) collective-permute-start(bf16[128,256]{1,0:T(8,128)(2,1)S(1)} %copy-done.17), channel_id=1, source_target_pairs={{0,8},{2,10},{4,12},{6,14},{8,0},{10,2},{12,4},{14,6},{1,9},{3,11}... | collective-permute-start | bytes 196616 | tf_op jit(solution)/shard_map/ppermute | solution.py:425
  116.7 4.8 %collective-permute-done.25.across_ref = bf16[128,256]{1,0:T(8,128)(2,1)S(1)} collective-permute-done((bf16[128,256]{1,0:T(8,128)(2,1)S(1)}, bf16[128,256]{1,0:T(8,128)(2,1)S(1)}, u32[]{:S(2)}, u32[]{:S(2)}) %collective-permute-start.25) | collective-permute-done | bytes 65568 | tf_op jit(solution)/shard_map/ppermute | solution.py:425
  121.5 2.2 %collective-permute-done.24.refs_2_ = bf16[2,128,256]{2,1,0:T(8,128)(2,1)S(1)} collective-permute-done((bf16[2,128,256]{2,1,0:T(8,128)(2,1)S(1)}, bf16[2,128,256]{2,1,0:T(8,128)(2,1)S(1)}, u32[]{:S(2)}, u32[]{:S(2)}) %collective-permute-start.24) | collective-permute-done | bytes 131104 | tf_op jit(solution)/shard_map/ppermute | solution.py:424
  123.7 3.8 %all-to-all-done.2.grads_ref = bf16[32,128,128]{2,1,0:T(8,128)(2,1)S(1)} async-done(((bf16[32,128,128]{2,1,0:T(8,128)(2,1)}), bf16[32,128,128]{2,1,0:T(8,128)(2,1)S(1)}, u32[]{:S(2)}, u32[]{:S(2)}) %all-to-all-start.2) | async-done | bytes 1048608 | tf_op jit(solution)/shard_map/all_to_all | solution.py:418
  127.5 5.1 %shard_map.114 = bf16[1024,128]{1,0:T(8,128)(2,1)} custom-call(s32[4]{0:T(128)S(1)} %pad_add_fusion.place_ref, bf16[32,128,128]{2,1,0:T(8,128)(2,1)S(1)} %all-to-all-done.2.grads_ref, bf16[2,128,1024]{2,1,0:T(8,128)(2,1)} %pad_maximum_fusion.refs_0_, bf16[2,128,1024]{2,1,0:T(8,128)(2,1)} %pad_maximum_fusion.1.refs_1_, ...), custom_call_target="tpu_custom_call" | custom-call | flops 1100000000 | bytes 9437184 | tf_op jit(solution)/shard_map/pallas_call | solution.py:257
  132.7 6.6 %all-to-all-start.3 = ((bf16[64,16,128]{2,1,0:T(8,128)(2,1)}), bf16[64,16,128]{2,1,0:T(8,128)(2,1)S(1)}, u32[]{:S(2)}, u32[]{:S(2)}) async-start(bf16[64,16,128]{2,1,0:T(8,128)(2,1)} %bitcast.27), calls=%async_computation.3 | async-start | bytes 524288 | tf_op jit(solution)/shard_map/all_to_all | solution.py:432
  139.9 1.1 collective-permute-done.26.refs_3_
  141.0 1.4 shard_map.113
  142.4 8.9 %all-to-all-done.3 = bf16[64,16,128]{2,1,0:T(8,128)(2,1)S(1)} async-done(((bf16[64,16,128]{2,1,0:T(8,128)(2,1)}), bf16[64,16,128]{2,1,0:T(8,128)(2,1)S(1)}, u32[]{:S(2)}, u32[]{:S(2)}) %all-to-all-start.3) | async-done | bytes 262176 | tf_op jit(solution)/shard_map/all_to_all | solution.py:432
  151.4 0.6 copy_bitcast_fusion
  (78 shorter events, 4.2 us)
Async XLA Ops:
  3.2 9.2 %copy-start.3 = (bf16[1,128,4096]{2,1,0:T(8,128)(2,1)S(1)}, bf16[1,128,4096]{2,1,0:T(8,128)(2,1)}, u32[]{:S(2)}) copy-start(bf16[1,128,4096]{2,1,0:T(8,128)(2,1)} %param.7) | copy-start | bytes 3145732
  3.3 53.3 %all-to-all-start = ((bf16[8,128,768]{2,1,0:T(8,128)(2,1)}), bf16[8,128,768]{2,1,0:T(8,128)(2,1)S(1)}, u32[]{:S(2)}, u32[]{:S(2)}) async-start(bf16[8,128,768]{2,1,0:T(8,128)(2,1)} %shard_map.110), calls=%async_computation | async-start | bytes 3145728 | tf_op jit(solution)/shard_map/all_to_all | solution.py:394
  12.5 8.4 %collective-permute-start.1 = (bf16[128,1024]{1,0:T(8,128)(2,1)S(1)}, bf16[128,1024]{1,0:T(8,128)(2,1)S(1)}, u32[]{:S(2)}, u32[]{:S(2)}) collective-permute-start(bf16[128,1024]{1,0:T(8,128)(2,1)S(1)} %get-tuple-element.113), channel_id=1, source_target_pairs={{0,128},{64,192},{128,0},{192,64},{1,129},{65,193},{129,1},{193,65... | collective-permute-start | bytes 786440 | tf_op jit(solution)/shard_map/ppermute | solution.py:380
  15.4 11.7 %collective-permute-start.2 = (bf16[128,1024]{1,0:T(8,128)(2,1)S(1)}, bf16[128,1024]{1,0:T(8,128)(2,1)S(1)}, u32[]{:S(2)}, u32[]{:S(2)}) collective-permute-start(bf16[128,1024]{1,0:T(8,128)(2,1)S(1)} %get-tuple-element.116), channel_id=1, source_target_pairs={{0,192},{64,0},{128,64},{192,128},{1,193},{65,1},{129,65},{193,129... | collective-permute-start | bytes 786440 | tf_op jit(solution)/shard_map/ppermute | solution.py:380
  16.2 14.4 %collective-permute-start = (bf16[128,1024]{1,0:T(8,128)(2,1)S(1)}, bf16[128,1024]{1,0:T(8,128)(2,1)S(1)}, u32[]{:S(2)}, u32[]{:S(2)}) collective-permute-start(bf16[128,1024]{1,0:T(8,128)(2,1)S(1)} %get-tuple-element.114), channel_id=1, source_target_pairs={{0,64},{64,128},{128,192},{192,0},{1,65},{65,129},{129,193},{193,1... | collective-permute-start | bytes 786440 | tf_op jit(solution)/shard_map/ppermute | solution.py:380
  16.8 16.5 %collective-permute-start.6 = (bf16[128,1024]{1,0:T(8,128)(2,1)S(1)}, bf16[128,1024]{1,0:T(8,128)(2,1)S(1)}, u32[]{:S(2)}, u32[]{:S(2)}) collective-permute-start(bf16[128,1024]{1,0:T(8,128)(2,1)S(1)} %bitcast.45), channel_id=1, source_target_pairs={{0,48},{16,0},{32,16},{48,32},{1,49},{17,1},{33,17},{49,33},{2,50}... | collective-permute-start | bytes 786440 | tf_op jit(solution)/shard_map/ppermute | solution.py:383
  27.9 27.8 %collective-permute-start.8 = (bf16[2,128,1024]{2,1,0:T(8,128)(2,1)}, bf16[2,128,1024]{2,1,0:T(8,128)(2,1)S(1)}, u32[]{:S(2)}, u32[]{:S(2)}) collective-permute-start(bf16[2,128,1024]{2,1,0:T(8,128)(2,1)} %pad_maximum_fusion.1.refs_1_), channel_id=1, source_target_pairs={{0,48},{16,0},{32,16},{48,32},{1,49},{17,1},{33,17},{49,33},{2,50}... | collective-permute-start | bytes 1572872 | tf_op jit(solution)/shard_map/ppermute | solution.py:383
  30.6 25.9 %collective-permute-start.5 = (bf16[2,128,1024]{2,1,0:T(8,128)(2,1)}, bf16[2,128,1024]{2,1,0:T(8,128)(2,1)}, u32[]{:S(2)}, u32[]{:S(2)}) collective-permute-start(bf16[2,128,1024]{2,1,0:T(8,128)(2,1)} %pad_maximum_fusion.1.refs_1_), channel_id=1, source_target_pairs={{0,16},{16,32},{32,48},{48,0},{1,17},{17,33},{33,49},{49,1},{2,18}... | collective-permute-start | bytes 1572872 | tf_op jit(solution)/shard_map/ppermute | solution.py:383
  30.6 15.5 %collective-permute-start.7 = (bf16[128,1024]{1,0:T(8,128)(2,1)S(1)}, bf16[128,1024]{1,0:T(8,128)(2,1)S(1)}, u32[]{:S(2)}, u32[]{:S(2)}) collective-permute-start(bf16[128,1024]{1,0:T(8,128)(2,1)S(1)} %collective-permute-done), channel_id=1, source_target_pairs={{0,48},{16,0},{32,16},{48,32},{1,49},{17,1},{33,17},{49,33},{2,50}... | collective-permute-start | bytes 786440 | tf_op jit(solution)/shard_map/ppermute | solution.py:383
  33.3 15.9 %collective-permute-start.3 = (bf16[128,1024]{1,0:T(8,128)(2,1)S(1)}, bf16[128,1024]{1,0:T(8,128)(2,1)S(1)}, u32[]{:S(2)}, u32[]{:S(2)}) collective-permute-start(bf16[128,1024]{1,0:T(8,128)(2,1)S(1)} %bitcast.46), channel_id=1, source_target_pairs={{0,16},{16,32},{32,48},{48,0},{1,17},{17,33},{33,49},{49,1},{2,18}... | collective-permute-start | bytes 786440 | tf_op jit(solution)/shard_map/ppermute | solution.py:383
  33.3 21.5 %collective-permute-start.4 = (bf16[128,1024]{1,0:T(8,128)(2,1)S(1)}, bf16[128,1024]{1,0:T(8,128)(2,1)S(1)}, u32[]{:S(2)}, u32[]{:S(2)}) collective-permute-start(bf16[128,1024]{1,0:T(8,128)(2,1)S(1)} %collective-permute-done), channel_id=1, source_target_pairs={{0,16},{16,32},{32,48},{48,0},{1,17},{17,33},{33,49},{49,1},{2,18}... | collective-permute-start | bytes 786440 | tf_op jit(solution)/shard_map/ppermute | solution.py:383
  33.3 23.2 %copy-start.1 = (s32[1,2048]{1,0:T(1,128)S(1)}, s32[1,2048]{1,0:T(1,128)}, u32[]{:S(2)}) copy-start(s32[1,2048]{1,0:T(1,128)} %param.13) | copy-start | bytes 24580
  54.8 7.1 %copy-start.16 = (s32[1,16,8]{1,2,0:T(8,128)S(1)}, s32[1,16,8]{1,2,0:T(8,128)}, u32[]{:S(2)}) copy-start(s32[1,16,8]{1,2,0:T(8,128)} %param.12) | copy-start | bytes 1540
  55.7 0.8 copy-start.4
  57.7 4.5 %collective-permute-start.9 = (bf16[8,128,256]{2,1,0:T(8,128)(2,1)}, bf16[8,128,256]{2,1,0:T(8,128)(2,1)S(1)}, u32[]{:S(2)}, u32[]{:S(2)}) collective-permute-start(bf16[8,128,256]{2,1,0:T(8,128)(2,1)} %slice.29), channel_id=1, source_target_pairs={{0,1},{1,0},{2,3},{3,2},{4,5},{5,4},{6,7},{7,6},{8,9},{9,8},{10,11... | collective-permute-start | bytes 1572872 | tf_op jit(solution)/shard_map/ppermute | solution.py:366
  60.4 13.9 %collective-permute-start.10 = (bf16[2,128,1024]{2,1,0:T(8,128)(2,1)}, bf16[2,128,1024]{2,1,0:T(8,128)(2,1)}, u32[]{:S(2)}, u32[]{:S(2)}) collective-permute-start(bf16[2,128,1024]{2,1,0:T(8,128)(2,1)} %pad_maximum_fusion.3.refs_4_), channel_id=1, source_target_pairs={{0,48},{16,0},{32,16},{48,32},{1,49},{17,1},{33,17},{49,33},{2,50}... | collective-permute-start | bytes 1572872 | tf_op jit(solution)/shard_map/ppermute | solution.py:389
  60.4 15.1 %collective-permute-start.11 = (bf16[2,128,1024]{2,1,0:T(8,128)(2,1)}, bf16[2,128,1024]{2,1,0:T(8,128)(2,1)}, u32[]{:S(2)}, u32[]{:S(2)}) collective-permute-start(bf16[2,128,1024]{2,1,0:T(8,128)(2,1)} %collective-permute-done.5.refs_3_), channel_id=1, source_target_pairs={{0,16},{16,32},{32,48},{48,0},{1,17},{17,33},{33,49},{49,1},{2,18}... | collective-permute-start | bytes 1572872 | tf_op jit(solution)/shard_map/ppermute | solution.py:390
  75.5 11.9 %copy-start.2 = (bf16[2,128,1024]{2,1,0:T(8,128)(2,1)S(1)}, bf16[2,128,1024]{2,1,0:T(8,128)(2,1)}, u32[]{:S(2)}) copy-start(bf16[2,128,1024]{2,1,0:T(8,128)(2,1)} %pad_maximum_fusion.3.refs_4_) | copy-start | bytes 1572868
  75.5 12.3 %copy-start.5 = (bf16[2,128,1024]{2,1,0:T(8,128)(2,1)S(1)}, bf16[2,128,1024]{2,1,0:T(8,128)(2,1)}, u32[]{:S(2)}) copy-start(bf16[2,128,1024]{2,1,0:T(8,128)(2,1)} %copy-done.4) | copy-start | bytes 1572868
  75.5 2.3 %collective-permute-start.13 = (bf16[8,128,256]{2,1,0:T(8,128)(2,1)S(1)}, bf16[8,128,256]{2,1,0:T(8,128)(2,1)S(1)}, u32[]{:S(2)}, u32[]{:S(2)}) collective-permute-start(bf16[8,128,256]{2,1,0:T(8,128)(2,1)S(1)} %get-tuple-element.82), channel_id=1, source_target_pairs={{0,1},{1,0},{2,3},{3,2},{4,5},{5,4},{6,7},{7,6},{8,9},{9,8},{10,11... | collective-permute-start | bytes 1572872 | tf_op jit(solution)/shard_map/ppermute | solution.py:366
  76.3 11.5 %collective-permute-start.14 = (bf16[2,128,1024]{2,1,0:T(8,128)(2,1)}, bf16[2,128,1024]{2,1,0:T(8,128)(2,1)S(1)}, u32[]{:S(2)}, u32[]{:S(2)}) collective-permute-start(bf16[2,128,1024]{2,1,0:T(8,128)(2,1)} %pad_maximum_fusion.refs_0_), channel_id=1, source_target_pairs={{0,1},{1,0},{2,3},{3,2},{4,5},{5,4},{6,7},{7,6},{8,9},{9,8},{10,11... | collective-permute-start | bytes 1572872 | tf_op jit(solution)/shard_map/ppermute | solution.py:366
  76.4 11.6 %collective-permute-start.15 = (bf16[2,128,1024]{2,1,0:T(8,128)(2,1)}, bf16[2,128,1024]{2,1,0:T(8,128)(2,1)S(1)}, u32[]{:S(2)}, u32[]{:S(2)}) collective-permute-start(bf16[2,128,1024]{2,1,0:T(8,128)(2,1)} %pad_maximum_fusion.1.refs_1_), channel_id=1, source_target_pairs={{0,1},{1,0},{2,3},{3,2},{4,5},{5,4},{6,7},{7,6},{8,9},{9,8},{10,11... | collective-permute-start | bytes 1572872 | tf_op jit(solution)/shard_map/ppermute | solution.py:366
  76.8 11.6 %collective-permute-start.16 = (bf16[2,128,1024]{2,1,0:T(8,128)(2,1)}, bf16[2,128,1024]{2,1,0:T(8,128)(2,1)S(1)}, u32[]{:S(2)}, u32[]{:S(2)}) collective-permute-start(bf16[2,128,1024]{2,1,0:T(8,128)(2,1)} %pad_maximum_fusion.2.refs_2_), channel_id=1, source_target_pairs={{0,1},{1,0},{2,3},{3,2},{4,5},{5,4},{6,7},{7,6},{8,9},{9,8},{10,11... | collective-permute-start | bytes 1572872 | tf_op jit(solution)/shard_map/ppermute | solution.py:366
  78.8 24.6 %all-to-all-start.1 = ((bf16[8,128,256]{2,1,0:T(8,128)(2,1)}), bf16[8,128,256]{2,1,0:T(8,128)(2,1)S(1)}, u32[]{:S(2)}, u32[]{:S(2)}) async-start(bf16[8,128,256]{2,1,0:T(8,128)(2,1)} %add_convert_fusion), calls=%async_computation.1 | async-start | bytes 1048576 | tf_op jit(solution)/shard_map/all_to_all | solution.py:411
  85.4 25.2 %copy-start.15 = (bf16[128,256]{1,0:T(8,128)(2,1)S(1)}, bf16[128,256]{1,0:T(8,128)(2,1)}, u32[]{:S(2)}) copy-start(bf16[128,256]{1,0:T(8,128)(2,1)} %get-tuple-element.93) | copy-start | bytes 196612
  85.4 25.4 %copy-start.14 = (bf16[128,256]{1,0:T(8,128)(2,1)S(1)}, bf16[128,256]{1,0:T(8,128)(2,1)}, u32[]{:S(2)}) copy-start(bf16[128,256]{1,0:T(8,128)(2,1)} %get-tuple-element.95) | copy-start | bytes 196612
  85.4 2.0 %collective-permute-start.12 = (bf16[3,128,256]{2,1,0:T(8,128)(2,1)}, bf16[3,128,256]{2,1,0:T(8,128)(2,1)S(1)}, u32[]{:S(2)}, u32[]{:S(2)}) collective-permute-start(bf16[3,128,256]{2,1,0:T(8,128)(2,1)} %get-tuple-element.80), channel_id=1, source_target_pairs={{0,1},{1,0},{2,3},{3,2},{4,5},{5,4},{6,7},{7,6},{8,9},{9,8},{10,11... | collective-permute-start | bytes 589832 | tf_op jit(solution)/shard_map/ppermute | solution.py:366
  86.2 2.6 %collective-permute-start.17 = (bf16[2,128,1024]{2,1,0:T(8,128)(2,1)}, bf16[2,128,1024]{2,1,0:T(8,128)(2,1)S(1)}, u32[]{:S(2)}, u32[]{:S(2)}) collective-permute-start(bf16[2,128,1024]{2,1,0:T(8,128)(2,1)} %collective-permute-done.5.refs_3_), channel_id=1, source_target_pairs={{0,1},{1,0},{2,3},{3,2},{4,5},{5,4},{6,7},{7,6},{8,9},{9,8},{10,11... | collective-permute-start | bytes 1572872 | tf_op jit(solution)/shard_map/ppermute | solution.py:366
  87.4 1.9 %collective-permute-start.18 = (bf16[2,128,1024]{2,1,0:T(8,128)(2,1)S(1)}, bf16[2,128,1024]{2,1,0:T(8,128)(2,1)S(1)}, u32[]{:S(2)}, u32[]{:S(2)}) collective-permute-start(bf16[2,128,1024]{2,1,0:T(8,128)(2,1)S(1)} %copy-done.2), channel_id=1, source_target_pairs={{0,1},{1,0},{2,3},{3,2},{4,5},{5,4},{6,7},{7,6},{8,9},{9,8},{10,11... | collective-permute-start | bytes 1572872 | tf_op jit(solution)/shard_map/ppermute | solution.py:366
  87.8 22.9 %copy-start.6 = (bf16[2,128,1024]{2,1,0:T(8,128)(2,1)}, bf16[2,128,1024]{2,1,0:T(8,128)(2,1)S(1)}, u32[]{:S(2)}) copy-start(bf16[2,128,1024]{2,1,0:T(8,128)(2,1)S(1)} %collective-permute-done.14.refs_8_) | copy-start | bytes 1572868
  87.8 3.0 %collective-permute-start.19 = (bf16[2,128,1024]{2,1,0:T(8,128)(2,1)S(1)}, bf16[2,128,1024]{2,1,0:T(8,128)(2,1)S(1)}, u32[]{:S(2)}, u32[]{:S(2)}) collective-permute-start(bf16[2,128,1024]{2,1,0:T(8,128)(2,1)S(1)} %copy-done.5), channel_id=1, source_target_pairs={{0,1},{1,0},{2,3},{3,2},{4,5},{5,4},{6,7},{7,6},{8,9},{9,8},{10,11... | collective-permute-start | bytes 1572872 | tf_op jit(solution)/shard_map/ppermute | solution.py:366
  88.1 3.8 %copy-start.7 = (bf16[2,128,1024]{2,1,0:T(8,128)(2,1)}, bf16[2,128,1024]{2,1,0:T(8,128)(2,1)S(1)}, u32[]{:S(2)}) copy-start(bf16[2,128,1024]{2,1,0:T(8,128)(2,1)S(1)} %collective-permute-done.15.refs_9_) | copy-start | bytes 1572868
  88.1 3.8 %collective-permute-start.20 = (bf16[2,128,1024]{2,1,0:T(8,128)(2,1)}, bf16[2,128,1024]{2,1,0:T(8,128)(2,1)S(1)}, u32[]{:S(2)}, u32[]{:S(2)}) collective-permute-start(bf16[2,128,1024]{2,1,0:T(8,128)(2,1)} %collective-permute-done.10.refs_6_), channel_id=1, source_target_pairs={{0,1},{1,0},{2,3},{3,2},{4,5},{5,4},{6,7},{7,6},{8,9},{9,8},{10,11... | collective-permute-start | bytes 1572872 | tf_op jit(solution)/shard_map/ppermute | solution.py:366
  88.4 4.2 %copy-start.8 = (bf16[2,128,1024]{2,1,0:T(8,128)(2,1)}, bf16[2,128,1024]{2,1,0:T(8,128)(2,1)S(1)}, u32[]{:S(2)}) copy-start(bf16[2,128,1024]{2,1,0:T(8,128)(2,1)S(1)} %collective-permute-done.16.refs_10_) | copy-start | bytes 1572868
  88.4 4.2 %collective-permute-start.21 = (bf16[2,128,1024]{2,1,0:T(8,128)(2,1)}, bf16[2,128,1024]{2,1,0:T(8,128)(2,1)}, u32[]{:S(2)}, u32[]{:S(2)}) collective-permute-start(bf16[2,128,1024]{2,1,0:T(8,128)(2,1)} %collective-permute-done.11.refs_7_), channel_id=1, source_target_pairs={{0,1},{1,0},{2,3},{3,2},{4,5},{5,4},{6,7},{7,6},{8,9},{9,8},{10,11... | collective-permute-start | bytes 1572872 | tf_op jit(solution)/shard_map/ppermute | solution.py:366
  88.8 3.1 %copy-start.9 = (bf16[2,128,1024]{2,1,0:T(8,128)(2,1)}, bf16[2,128,1024]{2,1,0:T(8,128)(2,1)S(1)}, u32[]{:S(2)}) copy-start(bf16[2,128,1024]{2,1,0:T(8,128)(2,1)S(1)} %collective-permute-done.17.refs_11_) | copy-start | bytes 1572868
  89.4 2.5 %copy-start.10 = (bf16[2,128,1024]{2,1,0:T(8,128)(2,1)}, bf16[2,128,1024]{2,1,0:T(8,128)(2,1)S(1)}, u32[]{:S(2)}) copy-start(bf16[2,128,1024]{2,1,0:T(8,128)(2,1)S(1)} %collective-permute-done.18.refs_12_) | copy-start | bytes 1572868
  90.9 1.0 copy-start.11
  104.6 6.9 %copy-start.13 = (bf16[128,256]{1,0:T(8,128)(2,1)S(1)}, bf16[128,256]{1,0:T(8,128)(2,1)}, u32[]{:S(2)}) copy-start(bf16[128,256]{1,0:T(8,128)(2,1)} %get-tuple-element.96) | copy-start | bytes 196612
  104.6 9.6 %copy-start.17 = (bf16[128,256]{1,0:T(8,128)(2,1)S(1)}, bf16[128,256]{1,0:T(8,128)(2,1)}, u32[]{:S(2)}) copy-start(bf16[128,256]{1,0:T(8,128)(2,1)} %get-tuple-element.97) | copy-start | bytes 196612
  104.6 23.0 %all-to-all-start.2 = ((bf16[32,128,128]{2,1,0:T(8,128)(2,1)}), bf16[32,128,128]{2,1,0:T(8,128)(2,1)S(1)}, u32[]{:S(2)}, u32[]{:S(2)}) async-start(bf16[32,128,128]{2,1,0:T(8,128)(2,1)} %get-tuple-element.92), calls=%async_computation.2 | async-start | bytes 2097152 | tf_op jit(solution)/shard_map/all_to_all | solution.py:418
  110.7 10.8 %collective-permute-start.22 = (bf16[2,128,256]{2,1,0:T(8,128)(2,1)S(1)}, bf16[2,128,256]{2,1,0:T(8,128)(2,1)S(1)}, u32[]{:S(2)}, u32[]{:S(2)}) collective-permute-start(bf16[2,128,256]{2,1,0:T(8,128)(2,1)S(1)} %pad_maximum_fusion.5), channel_id=1, source_target_pairs={{0,2},{2,4},{4,6},{6,8},{8,10},{10,12},{12,14},{14,0},{1,15},{3,1}... | collective-permute-start | bytes 393224 | tf_op jit(solution)/shard_map/ppermute | solution.py:424
  110.8 10.7 %collective-permute-start.23 = (bf16[2,128,256]{2,1,0:T(8,128)(2,1)S(1)}, bf16[2,128,256]{2,1,0:T(8,128)(2,1)S(1)}, u32[]{:S(2)}, u32[]{:S(2)}) collective-permute-start(bf16[2,128,256]{2,1,0:T(8,128)(2,1)S(1)} %pad_maximum_fusion.6), channel_id=1, source_target_pairs={{0,4},{2,6},{4,8},{6,10},{8,12},{10,14},{12,0},{14,2},{1,13},{3,15... | collective-permute-start | bytes 393224 | tf_op jit(solution)/shard_map/ppermute | solution.py:424
  111.5 29.5 %copy-start = (bf16[128,256]{1,0:T(8,128)(2,1)S(1)}, bf16[128,256]{1,0:T(8,128)(2,1)}, u32[]{:S(2)}) copy-start(bf16[128,256]{1,0:T(8,128)(2,1)} %get-tuple-element.75.keep_ref) | copy-start | bytes 196612
  111.5 12.3 %collective-permute-start.24 = (bf16[2,128,256]{2,1,0:T(8,128)(2,1)S(1)}, bf16[2,128,256]{2,1,0:T(8,128)(2,1)S(1)}, u32[]{:S(2)}, u32[]{:S(2)}) collective-permute-start(bf16[2,128,256]{2,1,0:T(8,128)(2,1)S(1)} %pad_maximum_fusion.7), channel_id=1, source_target_pairs={{0,6},{2,8},{4,10},{6,12},{8,14},{10,0},{12,2},{14,4},{1,11},{3,13... | collective-permute-start | bytes 393224 | tf_op jit(solution)/shard_map/ppermute | solution.py:424
  114.1 7.3 %collective-permute-start.25 = (bf16[128,256]{1,0:T(8,128)(2,1)S(1)}, bf16[128,256]{1,0:T(8,128)(2,1)S(1)}, u32[]{:S(2)}, u32[]{:S(2)}) collective-permute-start(bf16[128,256]{1,0:T(8,128)(2,1)S(1)} %copy-done.17), channel_id=1, source_target_pairs={{0,8},{2,10},{4,12},{6,14},{8,0},{10,2},{12,4},{14,6},{1,9},{3,11}... | collective-permute-start | bytes 196616 | tf_op jit(solution)/shard_map/ppermute | solution.py:425
  132.7 18.6 %all-to-all-start.3 = ((bf16[64,16,128]{2,1,0:T(8,128)(2,1)}), bf16[64,16,128]{2,1,0:T(8,128)(2,1)S(1)}, u32[]{:S(2)}, u32[]{:S(2)}) async-start(bf16[64,16,128]{2,1,0:T(8,128)(2,1)} %bitcast.27), calls=%async_computation.3 | async-start | bytes 524288 | tf_op jit(solution)/shard_map/all_to_all | solution.py:432
  139.4 1.6 %collective-permute-start.26 = (bf16[3,128,256]{2,1,0:T(8,128)(2,1)S(1)}, bf16[3,128,256]{2,1,0:T(8,128)(2,1)S(1)}, u32[]{:S(2)}, u32[]{:S(2)}) collective-permute-start(bf16[3,128,256]{2,1,0:T(8,128)(2,1)S(1)} %pad_maximum_fusion.4), channel_id=1, source_target_pairs={{0,1},{1,0},{2,3},{3,2},{4,5},{5,4},{6,7},{7,6},{8,9},{9,8},{10,11... | collective-permute-start | bytes 589832 | tf_op jit(solution)/shard_map/ppermute | solution.py:366
  (1 other events, 0.8 us)

commit v11 on v10

--- a/solution.py
+++ b/solution.py
@@ -377,17 +377,19 @@
         lax.dynamic_slice_in_dim(inputs, lax.rem(x + s, NX) * width, width, axis=1)
         for s in range(NX)
     ]
-    pieces = [a if s == 0 else lax.ppermute(a, "x", ring(NX, s)) for s, a in enumerate(pieces)]
-    groups = [pieces[0], pieces[1], jnp.stack(pieces[2:])]
-    before, after = (
-        [lax.ppermute(a, "y", ring(NY, shift)) for a in groups] for shift in (1, -1)
-    )
-    mine, before, after = (
-        (jnp.stack(a[:2]), a[2]) for a in (groups, before, after)
+    near = lax.ppermute(pieces[1], "x", ring(NX, 1))
+    near, later = lax.optimization_barrier((near, pieces[2:]))
+    pieces = [pieces[0], near] + [
+        lax.ppermute(a, "x", ring(NX, s)) for s, a in enumerate(later, 2)
+    ]
+    half = NX // 2
+    mine = (jnp.stack(pieces[:half]), jnp.stack(pieces[half:]))
+    before, after = zip(
+        *[[lax.ppermute(a, "y", ring(NY, shift)) for shift in (1, -1)] for a in mine]
     )
     far = (
-        lax.ppermute(after[0], "y", ring(NY, -1)),
-        lax.ppermute(before[1], "y", ring(NY, 1)),
+        lax.ppermute(before[0], "y", ring(NY, 1)),
+        lax.ppermute(after[1], "y", ring(NY, -1)),
     )
 
     outgoing = packed(queries[0], output_grads[0], keys[0], values[0])

time: 152 us -> 149 us (0.980)
  other arithmetic: 4.48 us -> 2.77 us
    ppermute x6 -> x4, waiting for transfers between devices: 19.8 us -> 14 us  [local(): lax.ppermute(a, 'y', ring(NY, shift))]
    ppermute x2 -> x3, waiting for transfers between devices: 1.83 us -> 7.65 us  [the longest x1 6.85 us: local(): near = lax.ppermute(pieces[1], 'x', ring(NX, 1))]
    ppermute x6 -> x4, starting transfers between devices: 8.15 us -> 5.47 us  [local(): lax.ppermute(a, 'y', ring(NY, shift))]
    ppermute x2 -> x3, starting transfers between devices: 1.47 us -> 3.97 us  [the longest x1 1.79 us: local(): lax.ppermute(after[1], 'y', ring(NY, -1))]
    all_to_all x1, starting transfers between devices: 6.04 us -> 8.06 us  [local(): lax.all_to_all(chunks, ('x', 'y', 'c'), split_axis=0, concat_axis=0, tile...]
    ppermute x3 -> x2, starting transfers between devices: 4.3 us -> 2.39 us  [local(): lax.ppermute(a, 'x', ring(NX, s))]
    another operation x4 -> x2, other arithmetic: 3.38 us -> 1.68 us  [local(): mine = (jnp.stack(pieces[:half]), jnp.stack(pieces[half:]))]
    ppermute x3 -> x2, waiting for transfers between devices: 7.47 us -> 7.21 us  [local(): lax.ppermute(a, 'x', ring(NX, s))]
  transfers between devices with their start and end apart: 31 -> 29, of which waited for: 19 -> 18; matrix products, arithmetic and copies ran while one was open for 3% -> 2% of each run, Pallas kernels for 8% -> 9%
where the time goes in v11:
time: 149 us; the launch traced here: 148 us
  waiting for transfers between devices  65.5 us (44%)
  starting transfers between devices  54.5 us (37%)
  Pallas kernels  21.8 us (15%)
  local copies, waits for them, and re-layouts  3 us (2%)
  other arithmetic  2.77 us (2%)
    ppermute x4, waiting for transfers between devices, local(): lax.ppermute(a, 'y', ring(NY, shift))  14 us
    pallas_call x1, Pallas kernels, attention_grads(): pl.pallas_call(attention_kernel, out_shape=(pltpu.HBM((BLOCK, 2 * HEAD),...  11.5 us
    all_to_all x1, waiting for transfers between devices, local(): pair = lax.all_to_all(pair, 'z', split_axis=0, concat_axis=0, tiled=True)  10.6 us
    all_to_all x1, starting transfers between devices, local(): lax.all_to_all(outgoing, 'z', split_axis=0, concat_axis=0, tiled=True)  9.16 us
    all_to_all x1, waiting for transfers between devices, local(): lax.all_to_all(part, ('y', 'z', 'c'), split_axis=0, concat_axis=0, tiled=...  8.9 us
    all_to_all x1, starting transfers between devices, local(): lax.all_to_all(chunks, ('x', 'y', 'c'), split_axis=0, concat_axis=0, tile...  8.06 us
    ppermute x2, waiting for transfers between devices, local(): lax.ppermute(a, 'x', ring(NX, s))  7.21 us
    ppermute x1, waiting for transfers between devices, local(): near = lax.ppermute(pieces[1], 'x', ring(NX, 1))  6.85 us
  transfers between devices with their start and end apart: 29, of which 18 were waited for; matrix products, arithmetic and copies ran while one was open for 2% of the time, Pallas kernels for 9%

profile of v11, /device:TPU:1, one launch (start us, length us, event | category | flops | bytes accessed | tf_op | source)
XLA Modules:
  0.0 148.4 jit_solution(14224119714887265454)
XLA Ops:
  0.6 2.6 %shard_map.110 = bf16[8,128,768]{2,1,0:T(8,128)(2,1)} custom-call(bf16[128,2048]{1,0:T(8,128)(2,1)} %bitcast.41, bf16[128,2048]{1,0:T(8,128)(2,1)} %bitcast.42, bf16[128,512]{1,0:T(8,128)(2,1)} %bitcast.47, bf16[128,512]{1,0:T(8,128)(2,1)} %bitcast.48), custom_call_target="tpu_custom_call" | custom-call | bytes 3145728 | tf_op jit(solution)/shard_map/pallas_call | solution.py:297
  3.3 9.2 %all-to-all-start = ((bf16[8,128,768]{2,1,0:T(8,128)(2,1)}), bf16[8,128,768]{2,1,0:T(8,128)(2,1)S(1)}, u32[]{:S(2)}, u32[]{:S(2)}) async-start(bf16[8,128,768]{2,1,0:T(8,128)(2,1)} %shard_map.110), calls=%async_computation | async-start | bytes 3145728 | tf_op jit(solution)/shard_map/all_to_all | solution.py:396
  12.5 1.3 collective-permute-start
  13.8 6.9 %collective-permute-done = bf16[128,1024]{1,0:T(8,128)(2,1)S(1)} collective-permute-done((bf16[128,1024]{1,0:T(8,128)(2,1)S(1)}, bf16[128,1024]{1,0:T(8,128)(2,1)S(1)}, u32[]{:S(2)}, u32[]{:S(2)}) %collective-permute-start) | collective-permute-done | bytes 262176 | tf_op jit(solution)/shard_map/ppermute | solution.py:380
  20.7 1.5 %collective-permute-start.1 = (bf16[128,1024]{1,0:T(8,128)(2,1)S(1)}, bf16[128,1024]{1,0:T(8,128)(2,1)S(1)}, u32[]{:S(2)}, u32[]{:S(2)}) collective-permute-start(bf16[128,1024]{1,0:T(8,128)(2,1)S(1)} %get-tuple-element.63), channel_id=1, source_target_pairs={{0,128},{64,192},{128,0},{192,64},{1,129},{65,193},{129,1},{193,65... | collective-permute-start | bytes 786440 | tf_op jit(solution)/shard_map/ppermute | solution.py:383
  22.2 0.9 collective-permute-start.2
  23.1 0.8 pad_maximum_fusion.refs_0_
  23.9 2.7 %collective-permute-start.5 = (bf16[2,128,1024]{2,1,0:T(8,128)(2,1)}, bf16[2,128,1024]{2,1,0:T(8,128)(2,1)S(1)}, u32[]{:S(2)}, u32[]{:S(2)}) collective-permute-start(bf16[2,128,1024]{2,1,0:T(8,128)(2,1)} %pad_maximum_fusion.refs_0_), channel_id=1, source_target_pairs={{0,48},{16,0},{32,16},{48,32},{1,49},{17,1},{33,17},{49,33},{2,50}... | collective-permute-start | bytes 1572872 | tf_op jit(solution)/shard_map/ppermute | solution.py:388
  26.7 1.5 collective-permute-done.1
  28.1 5.7 %collective-permute-done.2 = bf16[128,1024]{1,0:T(8,128)(2,1)S(1)} collective-permute-done((bf16[128,1024]{1,0:T(8,128)(2,1)S(1)}, bf16[128,1024]{1,0:T(8,128)(2,1)S(1)}, u32[]{:S(2)}, u32[]{:S(2)}) %collective-permute-start.2) | collective-permute-done | bytes 262176 | tf_op jit(solution)/shard_map/ppermute | solution.py:383
  33.9 0.8 pad_maximum_fusion.1.refs_1_
  34.7 2.7 %collective-permute-start.6 = (bf16[2,128,1024]{2,1,0:T(8,128)(2,1)}, bf16[2,128,1024]{2,1,0:T(8,128)(2,1)}, u32[]{:S(2)}, u32[]{:S(2)}) collective-permute-start(bf16[2,128,1024]{2,1,0:T(8,128)(2,1)} %pad_maximum_fusion.1.refs_1_), channel_id=1, source_target_pairs={{0,48},{16,0},{32,16},{48,32},{1,49},{17,1},{33,17},{49,33},{2,50}... | collective-permute-start | bytes 1572872 | tf_op jit(solution)/shard_map/ppermute | solution.py:388
  37.5 1.4 collective-permute-done.3.refs_2_
  38.9 9.4 %collective-permute-done.6.refs_5_ = bf16[2,128,1024]{2,1,0:T(8,128)(2,1)} collective-permute-done((bf16[2,128,1024]{2,1,0:T(8,128)(2,1)}, bf16[2,128,1024]{2,1,0:T(8,128)(2,1)}, u32[]{:S(2)}, u32[]{:S(2)}) %collective-permute-start.6) | collective-permute-done | bytes 524320 | tf_op jit(solution)/shard_map/ppermute | solution.py:388
  48.3 3.1 %collective-permute-done.4.refs_3_ = bf16[2,128,1024]{2,1,0:T(8,128)(2,1)} collective-permute-done((bf16[2,128,1024]{2,1,0:T(8,128)(2,1)}, bf16[2,128,1024]{2,1,0:T(8,128)(2,1)}, u32[]{:S(2)}, u32[]{:S(2)}) %collective-permute-start.4) | collective-permute-done | bytes 524320 | tf_op jit(solution)/shard_map/ppermute | solution.py:388
  51.7 0.8 slice.29
  52.6 2.3 %collective-permute-start.7 = (bf16[8,128,256]{2,1,0:T(8,128)(2,1)}, bf16[8,128,256]{2,1,0:T(8,128)(2,1)S(1)}, u32[]{:S(2)}, u32[]{:S(2)}) collective-permute-start(bf16[8,128,256]{2,1,0:T(8,128)(2,1)} %slice.29), channel_id=1, source_target_pairs={{0,1},{1,0},{2,3},{3,2},{4,5},{5,4},{6,7},{7,6},{8,9},{9,8},{10,11... | collective-permute-start | bytes 1572872 | tf_op jit(solution)/shard_map/ppermute | solution.py:366
  54.9 0.9 collective-permute-start.8
  55.8 1.8 %collective-permute-start.9 = (bf16[2,128,1024]{2,1,0:T(8,128)(2,1)}, bf16[2,128,1024]{2,1,0:T(8,128)(2,1)}, u32[]{:S(2)}, u32[]{:S(2)}) collective-permute-start(bf16[2,128,1024]{2,1,0:T(8,128)(2,1)} %collective-permute-done.6.refs_5_), channel_id=1, source_target_pairs={{0,48},{16,0},{32,16},{48,32},{1,49},{17,1},{33,17},{49,33},{2,50}... | collective-permute-start | bytes 1572872 | tf_op jit(solution)/shard_map/ppermute | solution.py:392
  57.8 11.5 %shard_map.111 = (bf16[128,256]{1,0:T(8,128)(2,1)}, bf16[128,256]{1,0:T(8,128)(2,1)}, bf16[128,256]{1,0:T(8,128)(2,1)}, bf16[128,256]{1,0:T(8,128)(2,1)}, bf16[1...) custom-call(s32[16,8]{1,0:T(8,128)S(1)} %copy.14.links_ref, ...), custom_call_target="tpu_custom_call" | custom-call | flops 1000 | bytes 1000 | tf_op jit(solution)/shard_map/pallas_call | solution.py:191
  69.2 0.8 collective-permute-done.8.refs_6_
  70.0 0.8 collective-permute-start.11
  70.9 0.4 collective-permute-start.13
  71.4 0.9 collective-permute-done.11
  72.3 0.9 add_convert_fusion
  73.2 6.3 %all-to-all-start.1 = ((bf16[8,128,256]{2,1,0:T(8,128)(2,1)}), bf16[8,128,256]{2,1,0:T(8,128)(2,1)S(1)}, u32[]{:S(2)}, u32[]{:S(2)}) async-start(bf16[8,128,256]{2,1,0:T(8,128)(2,1)} %add_convert_fusion), calls=%async_computation.1 | async-start | bytes 1048576 | tf_op jit(solution)/shard_map/all_to_all | solution.py:413
  79.6 0.7 collective-permute-start.10
  80.4 1.2 collective-permute-done.10
  82.7 0.9 collective-permute-done.16.refs_12_
  83.5 1.7 %collective-permute-done.17.refs_13_ = bf16[2,128,1024]{2,1,0:T(8,128)(2,1)S(1)} collective-permute-done((bf16[2,128,1024]{2,1,0:T(8,128)(2,1)}, bf16[2,128,1024]{2,1,0:T(8,128)(2,1)S(1)}, u32[]{:S(2)}, u32[]{:S(2)}) %collective-permute-start.17) | collective-permute-done | bytes 524320 | tf_op jit(solution)/shard_map/ppermute | solution.py:366
  85.2 0.7 collective-permute-done.18.refs_14_
  86.1 0.8 copy-done.11
  86.9 10.6 %all-to-all-done.1.partials_ref = bf16[8,128,256]{2,1,0:T(8,128)(2,1)S(1)} async-done(((bf16[8,128,256]{2,1,0:T(8,128)(2,1)}), bf16[8,128,256]{2,1,0:T(8,128)(2,1)S(1)}, u32[]{:S(2)}, u32[]{:S(2)}) %all-to-all-start.1) | async-done | bytes 524320 | tf_op jit(solution)/shard_map/all_to_all | solution.py:413
  97.5 1.2 shard_map.112
  98.8 8.1 %all-to-all-start.2 = ((bf16[32,128,128]{2,1,0:T(8,128)(2,1)}), bf16[32,128,128]{2,1,0:T(8,128)(2,1)S(1)}, u32[]{:S(2)}, u32[]{:S(2)}) async-start(bf16[32,128,128]{2,1,0:T(8,128)(2,1)} %get-tuple-element.98), calls=%async_computation.2 | async-start | bytes 2097152 | tf_op jit(solution)/shard_map/all_to_all | solution.py:420
  107.0 0.8 collective-permute-start.21
  107.9 2.7 %collective-permute-start.22 = (bf16[2,128,256]{2,1,0:T(8,128)(2,1)S(1)}, bf16[2,128,256]{2,1,0:T(8,128)(2,1)S(1)}, u32[]{:S(2)}, u32[]{:S(2)}) collective-permute-start(bf16[2,128,256]{2,1,0:T(8,128)(2,1)S(1)} %pad_maximum_fusion.5), channel_id=1, source_target_pairs={{0,6},{2,8},{4,10},{6,12},{8,14},{10,0},{12,2},{14,4},{1,11},{3,13... | collective-permute-start | bytes 393224 | tf_op jit(solution)/shard_map/ppermute | solution.py:426
  110.6 2.6 %collective-permute-start.23 = (bf16[128,256]{1,0:T(8,128)(2,1)S(1)}, bf16[128,256]{1,0:T(8,128)(2,1)S(1)}, u32[]{:S(2)}, u32[]{:S(2)}) collective-permute-start(bf16[128,256]{1,0:T(8,128)(2,1)S(1)} %copy-done.16), channel_id=1, source_target_pairs={{0,8},{2,10},{4,12},{6,14},{8,0},{10,2},{12,4},{14,6},{1,9},{3,11}... | collective-permute-start | bytes 196616 | tf_op jit(solution)/shard_map/ppermute | solution.py:427
  113.1 4.8 %collective-permute-done.23.across_ref = bf16[128,256]{1,0:T(8,128)(2,1)S(1)} collective-permute-done((bf16[128,256]{1,0:T(8,128)(2,1)S(1)}, bf16[128,256]{1,0:T(8,128)(2,1)S(1)}, u32[]{:S(2)}, u32[]{:S(2)}) %collective-permute-start.23) | collective-permute-done | bytes 65568 | tf_op jit(solution)/shard_map/ppermute | solution.py:427
  117.9 2.7 %collective-permute-done.22.refs_2_ = bf16[2,128,256]{2,1,0:T(8,128)(2,1)S(1)} collective-permute-done((bf16[2,128,256]{2,1,0:T(8,128)(2,1)S(1)}, bf16[2,128,256]{2,1,0:T(8,128)(2,1)S(1)}, u32[]{:S(2)}, u32[]{:S(2)}) %collective-permute-start.22) | collective-permute-done | bytes 131104 | tf_op jit(solution)/shard_map/ppermute | solution.py:426
  120.6 3.1 %all-to-all-done.2.grads_ref = bf16[32,128,128]{2,1,0:T(8,128)(2,1)S(1)} async-done(((bf16[32,128,128]{2,1,0:T(8,128)(2,1)}), bf16[32,128,128]{2,1,0:T(8,128)(2,1)S(1)}, u32[]{:S(2)}, u32[]{:S(2)}) %all-to-all-start.2) | async-done | bytes 1048608 | tf_op jit(solution)/shard_map/all_to_all | solution.py:420
  123.7 5.1 %shard_map.114 = bf16[1024,128]{1,0:T(8,128)(2,1)} custom-call(s32[4]{0:T(128)S(1)} %pad_add_fusion.place_ref, bf16[32,128,128]{2,1,0:T(8,128)(2,1)S(1)} %all-to-all-done.2.grads_ref, bf16[2,128,1024]{2,1,0:T(8,128)(2,1)} %pad_maximum_fusion.refs_0_, bf16[2,128,1024]{2,1,0:T(8,128)(2,1)} %pad_maximum_fusion.1.refs_1_, ...), custom_call_target="tpu_custom_call" | custom-call | flops 1100000000 | bytes 9437184 | tf_op jit(solution)/shard_map/pallas_call | solution.py:257
  128.9 6.8 %all-to-all-start.3 = ((bf16[64,16,128]{2,1,0:T(8,128)(2,1)}), bf16[64,16,128]{2,1,0:T(8,128)(2,1)S(1)}, u32[]{:S(2)}, u32[]{:S(2)}) async-start(bf16[64,16,128]{2,1,0:T(8,128)(2,1)} %bitcast.22), calls=%async_computation.3 | async-start | bytes 524288 | tf_op jit(solution)/shard_map/all_to_all | solution.py:434
  135.8 0.5 collective-permute-start.24
  136.3 1.1 collective-permute-done.24.refs_3_
  137.4 1.4 shard_map.113
  138.8 8.9 %all-to-all-done.3 = bf16[64,16,128]{2,1,0:T(8,128)(2,1)S(1)} async-done(((bf16[64,16,128]{2,1,0:T(8,128)(2,1)}), bf16[64,16,128]{2,1,0:T(8,128)(2,1)S(1)}, u32[]{:S(2)}, u32[]{:S(2)}) %all-to-all-start.3) | async-done | bytes 262176 | tf_op jit(solution)/shard_map/all_to_all | solution.py:434
  147.8 0.6 copy_bitcast_fusion
  (70 shorter events, 2.3 us)
Async XLA Ops:
  3.2 9.2 %copy-start.2 = (bf16[1,128,4096]{2,1,0:T(8,128)(2,1)S(1)}, bf16[1,128,4096]{2,1,0:T(8,128)(2,1)}, u32[]{:S(2)}) copy-start(bf16[1,128,4096]{2,1,0:T(8,128)(2,1)} %param.7) | copy-start | bytes 3145732
  3.3 48.2 %all-to-all-start = ((bf16[8,128,768]{2,1,0:T(8,128)(2,1)}), bf16[8,128,768]{2,1,0:T(8,128)(2,1)S(1)}, u32[]{:S(2)}, u32[]{:S(2)}) async-start(bf16[8,128,768]{2,1,0:T(8,128)(2,1)} %shard_map.110), calls=%async_computation | async-start | bytes 3145728 | tf_op jit(solution)/shard_map/all_to_all | solution.py:396
  12.5 38.9 %copy-start.1 = (s32[1,2048]{1,0:T(1,128)S(1)}, s32[1,2048]{1,0:T(1,128)}, u32[]{:S(2)}) copy-start(s32[1,2048]{1,0:T(1,128)} %param.13) | copy-start | bytes 24580
  12.5 8.1 %collective-permute-start = (bf16[128,1024]{1,0:T(8,128)(2,1)S(1)}, bf16[128,1024]{1,0:T(8,128)(2,1)S(1)}, u32[]{:S(2)}, u32[]{:S(2)}) collective-permute-start(bf16[128,1024]{1,0:T(8,128)(2,1)S(1)} %get-tuple-element.120), channel_id=1, source_target_pairs={{0,64},{64,128},{128,192},{192,0},{1,65},{65,129},{129,193},{193,1... | collective-permute-start | bytes 786440 | tf_op jit(solution)/shard_map/ppermute | solution.py:380
  20.7 7.4 %collective-permute-start.1 = (bf16[128,1024]{1,0:T(8,128)(2,1)S(1)}, bf16[128,1024]{1,0:T(8,128)(2,1)S(1)}, u32[]{:S(2)}, u32[]{:S(2)}) collective-permute-start(bf16[128,1024]{1,0:T(8,128)(2,1)S(1)} %get-tuple-element.63), channel_id=1, source_target_pairs={{0,128},{64,192},{128,0},{192,64},{1,129},{65,193},{129,1},{193,65... | collective-permute-start | bytes 786440 | tf_op jit(solution)/shard_map/ppermute | solution.py:383
  22.2 11.6 %collective-permute-start.2 = (bf16[128,1024]{1,0:T(8,128)(2,1)S(1)}, bf16[128,1024]{1,0:T(8,128)(2,1)S(1)}, u32[]{:S(2)}, u32[]{:S(2)}) collective-permute-start(bf16[128,1024]{1,0:T(8,128)(2,1)S(1)} %get-tuple-element.64), channel_id=1, source_target_pairs={{0,192},{64,0},{128,64},{192,128},{1,193},{65,1},{129,65},{193,129... | collective-permute-start | bytes 786440 | tf_op jit(solution)/shard_map/ppermute | solution.py:383
  23.9 13.5 %collective-permute-start.5 = (bf16[2,128,1024]{2,1,0:T(8,128)(2,1)}, bf16[2,128,1024]{2,1,0:T(8,128)(2,1)S(1)}, u32[]{:S(2)}, u32[]{:S(2)}) collective-permute-start(bf16[2,128,1024]{2,1,0:T(8,128)(2,1)} %pad_maximum_fusion.refs_0_), channel_id=1, source_target_pairs={{0,48},{16,0},{32,16},{48,32},{1,49},{17,1},{33,17},{49,33},{2,50}... | collective-permute-start | bytes 1572872 | tf_op jit(solution)/shard_map/ppermute | solution.py:388
  26.6 12.2 %collective-permute-start.3 = (bf16[2,128,1024]{2,1,0:T(8,128)(2,1)}, bf16[2,128,1024]{2,1,0:T(8,128)(2,1)}, u32[]{:S(2)}, u32[]{:S(2)}) collective-permute-start(bf16[2,128,1024]{2,1,0:T(8,128)(2,1)} %pad_maximum_fusion.refs_0_), channel_id=1, source_target_pairs={{0,16},{16,32},{32,48},{48,0},{1,17},{17,33},{33,49},{49,1},{2,18}... | collective-permute-start | bytes 1572872 | tf_op jit(solution)/shard_map/ppermute | solution.py:388
  33.9 23.7 %copy-start.15 = (s32[1,16,8]{1,2,0:T(8,128)S(1)}, s32[1,16,8]{1,2,0:T(8,128)}, u32[]{:S(2)}) copy-start(s32[1,16,8]{1,2,0:T(8,128)} %param.12) | copy-start | bytes 1540
  34.7 13.6 %collective-permute-start.6 = (bf16[2,128,1024]{2,1,0:T(8,128)(2,1)}, bf16[2,128,1024]{2,1,0:T(8,128)(2,1)}, u32[]{:S(2)}, u32[]{:S(2)}) collective-permute-start(bf16[2,128,1024]{2,1,0:T(8,128)(2,1)} %pad_maximum_fusion.1.refs_1_), channel_id=1, source_target_pairs={{0,48},{16,0},{32,16},{48,32},{1,49},{17,1},{33,17},{49,33},{2,50}... | collective-permute-start | bytes 1572872 | tf_op jit(solution)/shard_map/ppermute | solution.py:388
  37.4 14.0 %collective-permute-start.4 = (bf16[2,128,1024]{2,1,0:T(8,128)(2,1)}, bf16[2,128,1024]{2,1,0:T(8,128)(2,1)}, u32[]{:S(2)}, u32[]{:S(2)}) collective-permute-start(bf16[2,128,1024]{2,1,0:T(8,128)(2,1)} %pad_maximum_fusion.1.refs_1_), channel_id=1, source_target_pairs={{0,16},{16,32},{32,48},{48,0},{1,17},{17,33},{33,49},{49,1},{2,18}... | collective-permute-start | bytes 1572872 | tf_op jit(solution)/shard_map/ppermute | solution.py:388
  37.4 10.8 %copy-start.3 = (bf16[2,128,1024]{2,1,0:T(8,128)(2,1)}, bf16[2,128,1024]{2,1,0:T(8,128)(2,1)S(1)}, u32[]{:S(2)}) copy-start(bf16[2,128,1024]{2,1,0:T(8,128)(2,1)S(1)} %collective-permute-done.5.refs_4_) | copy-start | bytes 1572868
  52.6 5.2 %collective-permute-start.7 = (bf16[8,128,256]{2,1,0:T(8,128)(2,1)}, bf16[8,128,256]{2,1,0:T(8,128)(2,1)S(1)}, u32[]{:S(2)}, u32[]{:S(2)}) collective-permute-start(bf16[8,128,256]{2,1,0:T(8,128)(2,1)} %slice.29), channel_id=1, source_target_pairs={{0,1},{1,0},{2,3},{3,2},{4,5},{5,4},{6,7},{7,6},{8,9},{9,8},{10,11... | collective-permute-start | bytes 1572872 | tf_op jit(solution)/shard_map/ppermute | solution.py:366
  54.9 15.1 %collective-permute-start.8 = (bf16[2,128,1024]{2,1,0:T(8,128)(2,1)}, bf16[2,128,1024]{2,1,0:T(8,128)(2,1)}, u32[]{:S(2)}, u32[]{:S(2)}) collective-permute-start(bf16[2,128,1024]{2,1,0:T(8,128)(2,1)} %collective-permute-done.3.refs_2_), channel_id=1, source_target_pairs={{0,16},{16,32},{32,48},{48,0},{1,17},{17,33},{33,49},{49,1},{2,18}... | collective-permute-start | bytes 1572872 | tf_op jit(solution)/shard_map/ppermute | solution.py:391
  55.8 14.2 %collective-permute-start.9 = (bf16[2,128,1024]{2,1,0:T(8,128)(2,1)}, bf16[2,128,1024]{2,1,0:T(8,128)(2,1)}, u32[]{:S(2)}, u32[]{:S(2)}) collective-permute-start(bf16[2,128,1024]{2,1,0:T(8,128)(2,1)} %collective-permute-done.6.refs_5_), channel_id=1, source_target_pairs={{0,48},{16,0},{32,16},{48,32},{1,49},{17,1},{33,17},{49,33},{2,50}... | collective-permute-start | bytes 1572872 | tf_op jit(solution)/shard_map/ppermute | solution.py:392
  70.0 11.6 %copy-start.4 = (bf16[2,128,1024]{2,1,0:T(8,128)(2,1)S(1)}, bf16[2,128,1024]{2,1,0:T(8,128)(2,1)}, u32[]{:S(2)}) copy-start(bf16[2,128,1024]{2,1,0:T(8,128)(2,1)} %copy-done.3) | copy-start | bytes 1572868
  70.0 2.3 %collective-permute-start.11 = (bf16[8,128,256]{2,1,0:T(8,128)(2,1)S(1)}, bf16[8,128,256]{2,1,0:T(8,128)(2,1)S(1)}, u32[]{:S(2)}, u32[]{:S(2)}) collective-permute-start(bf16[8,128,256]{2,1,0:T(8,128)(2,1)S(1)} %get-tuple-element.88), channel_id=1, source_target_pairs={{0,1},{1,0},{2,3},{3,2},{4,5},{5,4},{6,7},{7,6},{8,9},{9,8},{10,11... | collective-permute-start | bytes 1572872 | tf_op jit(solution)/shard_map/ppermute | solution.py:366
  70.8 11.2 %collective-permute-start.12 = (bf16[2,128,1024]{2,1,0:T(8,128)(2,1)}, bf16[2,128,1024]{2,1,0:T(8,128)(2,1)S(1)}, u32[]{:S(2)}, u32[]{:S(2)}) collective-permute-start(bf16[2,128,1024]{2,1,0:T(8,128)(2,1)} %pad_maximum_fusion.refs_0_), channel_id=1, source_target_pairs={{0,1},{1,0},{2,3},{3,2},{4,5},{5,4},{6,7},{7,6},{8,9},{9,8},{10,11... | collective-permute-start | bytes 1572872 | tf_op jit(solution)/shard_map/ppermute | solution.py:366
  70.9 11.3 %collective-permute-start.13 = (bf16[2,128,1024]{2,1,0:T(8,128)(2,1)}, bf16[2,128,1024]{2,1,0:T(8,128)(2,1)S(1)}, u32[]{:S(2)}, u32[]{:S(2)}) collective-permute-start(bf16[2,128,1024]{2,1,0:T(8,128)(2,1)} %pad_maximum_fusion.1.refs_1_), channel_id=1, source_target_pairs={{0,1},{1,0},{2,3},{3,2},{4,5},{5,4},{6,7},{7,6},{8,9},{9,8},{10,11... | collective-permute-start | bytes 1572872 | tf_op jit(solution)/shard_map/ppermute | solution.py:366
  71.3 11.2 %collective-permute-start.14 = (bf16[2,128,1024]{2,1,0:T(8,128)(2,1)}, bf16[2,128,1024]{2,1,0:T(8,128)(2,1)S(1)}, u32[]{:S(2)}, u32[]{:S(2)}) collective-permute-start(bf16[2,128,1024]{2,1,0:T(8,128)(2,1)} %collective-permute-done.3.refs_2_), channel_id=1, source_target_pairs={{0,1},{1,0},{2,3},{3,2},{4,5},{5,4},{6,7},{7,6},{8,9},{9,8},{10,11... | collective-permute-start | bytes 1572872 | tf_op jit(solution)/shard_map/ppermute | solution.py:366
  73.2 24.3 %all-to-all-start.1 = ((bf16[8,128,256]{2,1,0:T(8,128)(2,1)}), bf16[8,128,256]{2,1,0:T(8,128)(2,1)S(1)}, u32[]{:S(2)}, u32[]{:S(2)}) async-start(bf16[8,128,256]{2,1,0:T(8,128)(2,1)} %add_convert_fusion), calls=%async_computation.1 | async-start | bytes 1048576 | tf_op jit(solution)/shard_map/all_to_all | solution.py:413
  79.6 27.3 %copy-start.14 = (bf16[128,256]{1,0:T(8,128)(2,1)S(1)}, bf16[128,256]{1,0:T(8,128)(2,1)}, u32[]{:S(2)}) copy-start(bf16[128,256]{1,0:T(8,128)(2,1)} %get-tuple-element.99) | copy-start | bytes 196612
  79.6 27.4 %copy-start.13 = (bf16[128,256]{1,0:T(8,128)(2,1)S(1)}, bf16[128,256]{1,0:T(8,128)(2,1)}, u32[]{:S(2)}) copy-start(bf16[128,256]{1,0:T(8,128)(2,1)} %get-tuple-element.101) | copy-start | bytes 196612
  79.6 2.0 %collective-permute-start.10 = (bf16[3,128,256]{2,1,0:T(8,128)(2,1)}, bf16[3,128,256]{2,1,0:T(8,128)(2,1)S(1)}, u32[]{:S(2)}, u32[]{:S(2)}) collective-permute-start(bf16[3,128,256]{2,1,0:T(8,128)(2,1)} %get-tuple-element.86), channel_id=1, source_target_pairs={{0,1},{1,0},{2,3},{3,2},{4,5},{5,4},{6,7},{7,6},{8,9},{9,8},{10,11... | collective-permute-start | bytes 589832 | tf_op jit(solution)/shard_map/ppermute | solution.py:366
  80.3 2.3 %collective-permute-start.15 = (bf16[2,128,1024]{2,1,0:T(8,128)(2,1)}, bf16[2,128,1024]{2,1,0:T(8,128)(2,1)S(1)}, u32[]{:S(2)}, u32[]{:S(2)}) collective-permute-start(bf16[2,128,1024]{2,1,0:T(8,128)(2,1)} %collective-permute-done.4.refs_3_), channel_id=1, source_target_pairs={{0,1},{1,0},{2,3},{3,2},{4,5},{5,4},{6,7},{7,6},{8,9},{9,8},{10,11... | collective-permute-start | bytes 1572872 | tf_op jit(solution)/shard_map/ppermute | solution.py:366
  81.6 1.9 %collective-permute-start.16 = (bf16[2,128,1024]{2,1,0:T(8,128)(2,1)S(1)}, bf16[2,128,1024]{2,1,0:T(8,128)(2,1)S(1)}, u32[]{:S(2)}, u32[]{:S(2)}) collective-permute-start(bf16[2,128,1024]{2,1,0:T(8,128)(2,1)S(1)} %copy-done.4), channel_id=1, source_target_pairs={{0,1},{1,0},{2,3},{3,2},{4,5},{5,4},{6,7},{7,6},{8,9},{9,8},{10,11... | collective-permute-start | bytes 1572872 | tf_op jit(solution)/shard_map/ppermute | solution.py:366
  82.0 24.9 %copy-start.5 = (bf16[2,128,1024]{2,1,0:T(8,128)(2,1)}, bf16[2,128,1024]{2,1,0:T(8,128)(2,1)S(1)}, u32[]{:S(2)}) copy-start(bf16[2,128,1024]{2,1,0:T(8,128)(2,1)S(1)} %collective-permute-done.12.refs_8_) | copy-start | bytes 1572868
  82.0 3.2 %collective-permute-start.17 = (bf16[2,128,1024]{2,1,0:T(8,128)(2,1)}, bf16[2,128,1024]{2,1,0:T(8,128)(2,1)S(1)}, u32[]{:S(2)}, u32[]{:S(2)}) collective-permute-start(bf16[2,128,1024]{2,1,0:T(8,128)(2,1)} %collective-permute-done.6.refs_5_), channel_id=1, source_target_pairs={{0,1},{1,0},{2,3},{3,2},{4,5},{5,4},{6,7},{7,6},{8,9},{9,8},{10,11... | collective-permute-start | bytes 1572872 | tf_op jit(solution)/shard_map/ppermute | solution.py:366
  82.1 24.7 %copy-start.6 = (bf16[2,128,1024]{2,1,0:T(8,128)(2,1)}, bf16[2,128,1024]{2,1,0:T(8,128)(2,1)S(1)}, u32[]{:S(2)}) copy-start(bf16[2,128,1024]{2,1,0:T(8,128)(2,1)S(1)} %collective-permute-done.13.refs_9_) | copy-start | bytes 1572868
  82.1 3.8 %collective-permute-start.18 = (bf16[2,128,1024]{2,1,0:T(8,128)(2,1)}, bf16[2,128,1024]{2,1,0:T(8,128)(2,1)S(1)}, u32[]{:S(2)}, u32[]{:S(2)}) collective-permute-start(bf16[2,128,1024]{2,1,0:T(8,128)(2,1)} %collective-permute-done.8.refs_6_), channel_id=1, source_target_pairs={{0,1},{1,0},{2,3},{3,2},{4,5},{5,4},{6,7},{7,6},{8,9},{9,8},{10,11... | collective-permute-start | bytes 1572872 | tf_op jit(solution)/shard_map/ppermute | solution.py:366
  82.5 3.5 %copy-start.7 = (bf16[2,128,1024]{2,1,0:T(8,128)(2,1)}, bf16[2,128,1024]{2,1,0:T(8,128)(2,1)S(1)}, u32[]{:S(2)}) copy-start(bf16[2,128,1024]{2,1,0:T(8,128)(2,1)S(1)} %collective-permute-done.14.refs_10_) | copy-start | bytes 1572868
  82.5 4.4 %collective-permute-start.19 = (bf16[2,128,1024]{2,1,0:T(8,128)(2,1)}, bf16[2,128,1024]{2,1,0:T(8,128)(2,1)}, u32[]{:S(2)}, u32[]{:S(2)}) collective-permute-start(bf16[2,128,1024]{2,1,0:T(8,128)(2,1)} %collective-permute-done.9.refs_7_), channel_id=1, source_target_pairs={{0,1},{1,0},{2,3},{3,2},{4,5},{5,4},{6,7},{7,6},{8,9},{9,8},{10,11... | collective-permute-start | bytes 1572872 | tf_op jit(solution)/shard_map/ppermute | solution.py:366
  82.7 4.3 %copy-start.8 = (bf16[2,128,1024]{2,1,0:T(8,128)(2,1)}, bf16[2,128,1024]{2,1,0:T(8,128)(2,1)S(1)}, u32[]{:S(2)}) copy-start(bf16[2,128,1024]{2,1,0:T(8,128)(2,1)S(1)} %collective-permute-done.15.refs_11_) | copy-start | bytes 1572868
  83.5 2.5 %copy-start.9 = (bf16[2,128,1024]{2,1,0:T(8,128)(2,1)}, bf16[2,128,1024]{2,1,0:T(8,128)(2,1)S(1)}, u32[]{:S(2)}) copy-start(bf16[2,128,1024]{2,1,0:T(8,128)(2,1)S(1)} %collective-permute-done.16.refs_12_) | copy-start | bytes 1572868
  85.2 0.9 copy-start.10
  86.1 0.8 copy-start.11
  98.7 9.1 %copy-start.12 = (bf16[128,256]{1,0:T(8,128)(2,1)S(1)}, bf16[128,256]{1,0:T(8,128)(2,1)}, u32[]{:S(2)}) copy-start(bf16[128,256]{1,0:T(8,128)(2,1)} %get-tuple-element.102) | copy-start | bytes 196612
  98.7 11.8 %copy-start.16 = (bf16[128,256]{1,0:T(8,128)(2,1)S(1)}, bf16[128,256]{1,0:T(8,128)(2,1)}, u32[]{:S(2)}) copy-start(bf16[128,256]{1,0:T(8,128)(2,1)} %get-tuple-element.103) | copy-start | bytes 196612
  98.8 25.0 %all-to-all-start.2 = ((bf16[32,128,128]{2,1,0:T(8,128)(2,1)}), bf16[32,128,128]{2,1,0:T(8,128)(2,1)S(1)}, u32[]{:S(2)}, u32[]{:S(2)}) async-start(bf16[32,128,128]{2,1,0:T(8,128)(2,1)} %get-tuple-element.98), calls=%async_computation.2 | async-start | bytes 2097152 | tf_op jit(solution)/shard_map/all_to_all | solution.py:420
  106.9 11.0 %collective-permute-start.20 = (bf16[2,128,256]{2,1,0:T(8,128)(2,1)S(1)}, bf16[2,128,256]{2,1,0:T(8,128)(2,1)S(1)}, u32[]{:S(2)}, u32[]{:S(2)}) collective-permute-start(bf16[2,128,256]{2,1,0:T(8,128)(2,1)S(1)} %pad_maximum_fusion.3), channel_id=1, source_target_pairs={{0,2},{2,4},{4,6},{6,8},{8,10},{10,12},{12,14},{14,0},{1,15},{3,1}... | collective-permute-start | bytes 393224 | tf_op jit(solution)/shard_map/ppermute | solution.py:426
  107.0 10.9 %collective-permute-start.21 = (bf16[2,128,256]{2,1,0:T(8,128)(2,1)S(1)}, bf16[2,128,256]{2,1,0:T(8,128)(2,1)S(1)}, u32[]{:S(2)}, u32[]{:S(2)}) collective-permute-start(bf16[2,128,256]{2,1,0:T(8,128)(2,1)S(1)} %pad_maximum_fusion.4), channel_id=1, source_target_pairs={{0,4},{2,6},{4,8},{6,10},{8,12},{10,14},{12,0},{14,2},{1,13},{3,15... | collective-permute-start | bytes 393224 | tf_op jit(solution)/shard_map/ppermute | solution.py:426
  107.9 29.5 %copy-start = (bf16[128,256]{1,0:T(8,128)(2,1)S(1)}, bf16[128,256]{1,0:T(8,128)(2,1)}, u32[]{:S(2)}) copy-start(bf16[128,256]{1,0:T(8,128)(2,1)} %get-tuple-element.81.keep_ref) | copy-start | bytes 196612
  107.9 12.7 %collective-permute-start.22 = (bf16[2,128,256]{2,1,0:T(8,128)(2,1)S(1)}, bf16[2,128,256]{2,1,0:T(8,128)(2,1)S(1)}, u32[]{:S(2)}, u32[]{:S(2)}) collective-permute-start(bf16[2,128,256]{2,1,0:T(8,128)(2,1)S(1)} %pad_maximum_fusion.5), channel_id=1, source_target_pairs={{0,6},{2,8},{4,10},{6,12},{8,14},{10,0},{12,2},{14,4},{1,11},{3,13... | collective-permute-start | bytes 393224 | tf_op jit(solution)/shard_map/ppermute | solution.py:426
  110.6 7.3 %collective-permute-start.23 = (bf16[128,256]{1,0:T(8,128)(2,1)S(1)}, bf16[128,256]{1,0:T(8,128)(2,1)S(1)}, u32[]{:S(2)}, u32[]{:S(2)}) collective-permute-start(bf16[128,256]{1,0:T(8,128)(2,1)S(1)} %copy-done.16), channel_id=1, source_target_pairs={{0,8},{2,10},{4,12},{6,14},{8,0},{10,2},{12,4},{14,6},{1,9},{3,11}... | collective-permute-start | bytes 196616 | tf_op jit(solution)/shard_map/ppermute | solution.py:427
  128.9 18.8 %all-to-all-start.3 = ((bf16[64,16,128]{2,1,0:T(8,128)(2,1)}), bf16[64,16,128]{2,1,0:T(8,128)(2,1)S(1)}, u32[]{:S(2)}, u32[]{:S(2)}) async-start(bf16[64,16,128]{2,1,0:T(8,128)(2,1)} %bitcast.22), calls=%async_computation.3 | async-start | bytes 524288 | tf_op jit(solution)/shard_map/all_to_all | solution.py:434
  135.8 1.6 %collective-permute-start.24 = (bf16[3,128,256]{2,1,0:T(8,128)(2,1)S(1)}, bf16[3,128,256]{2,1,0:T(8,128)(2,1)S(1)}, u32[]{:S(2)}, u32[]{:S(2)}) collective-permute-start(bf16[3,128,256]{2,1,0:T(8,128)(2,1)S(1)} %pad_maximum_fusion.2), channel_id=1, source_target_pairs={{0,1},{1,0},{2,3},{3,2},{4,5},{5,4},{6,7},{7,6},{8,9},{9,8},{10,11... | collective-permute-start | bytes 589832 | tf_op jit(solution)/shard_map/ppermute | solution.py:366

commit v12 on v11

--- a/solution.py
+++ b/solution.py
@@ -54,7 +54,7 @@
             keys_t_ref[:, at(block)] = pair[:, :HEAD].T
         return carry
 
-    lax.fori_loop(0, NZ, load_pairs, 0)
+    lax.fori_loop(0, NZ, load_pairs, 0, unroll=True)
     total_ref[...] = jnp.zeros_like(total_ref)
 
     def stacked(i, first):
@@ -180,7 +180,7 @@
             ref[i, :, HEAD:] = total_ref[at(block), HEAD:].astype(ref.dtype)
         return carry
 
-    lax.fori_loop(0, NZ, store, 0)
+    lax.fori_loop(0, NZ, store, 0, unroll=True)
     for copy in copies:
         copy.wait()
 

time: 149 us -> 149 us (level)
  transfers between devices with their start and end apart: 29 -> 29, of which waited for: 18 -> 18; matrix products, arithmetic and copies ran while one was open for 2% -> 2% of each run, Pallas kernels for 9% -> 8%
where the time goes in v12:
time: 149 us; the launch traced here: 148 us
  waiting for transfers between devices  65.7 us (44%)
  starting transfers between devices  54.5 us (37%)
  Pallas kernels  21.5 us (14%)
  local copies, waits for them, and re-layouts  3 us (2%)
  other arithmetic  2.77 us (2%)
    ppermute x4, waiting for transfers between devices, local(): lax.ppermute(a, 'y', ring(NY, shift))  14 us
    pallas_call x1, Pallas kernels, attention_grads(): pl.pallas_call(attention_kernel, out_shape=(pltpu.HBM((BLOCK, 2 * HEAD),...  11.2 us
    all_to_all x1, waiting for transfers between devices, local(): pair = lax.all_to_all(pair, 'z', split_axis=0, concat_axis=0, tiled=True)  10.6 us
    all_to_all x1, starting transfers between devices, local(): lax.all_to_all(outgoing, 'z', split_axis=0, concat_axis=0, tiled=True)  9.16 us
    all_to_all x1, waiting for transfers between devices, local(): lax.all_to_all(part, ('y', 'z', 'c'), split_axis=0, concat_axis=0, tiled=...  8.9 us
    all_to_all x1, starting transfers between devices, local(): lax.all_to_all(chunks, ('x', 'y', 'c'), split_axis=0, concat_axis=0, tile...  8.06 us
    ppermute x2, waiting for transfers between devices, local(): lax.ppermute(a, 'x', ring(NX, s))  7.21 us
    ppermute x1, waiting for transfers between devices, local(): near = lax.ppermute(pieces[1], 'x', ring(NX, 1))  6.85 us
  transfers between devices with their start and end apart: 29, of which 18 were waited for; matrix products, arithmetic and copies ran while one was open for 2% of the time, Pallas kernels for 8%

profile of v12, /device:TPU:1, one launch (start us, length us, event | category | flops | bytes accessed | tf_op | source)
XLA Modules:
  0.0 148.4 jit_solution(3125122762565411810)
XLA Ops:
  0.6 2.6 %shard_map.110 = bf16[8,128,768]{2,1,0:T(8,128)(2,1)} custom-call(bf16[128,2048]{1,0:T(8,128)(2,1)} %bitcast.41, bf16[128,2048]{1,0:T(8,128)(2,1)} %bitcast.42, bf16[128,512]{1,0:T(8,128)(2,1)} %bitcast.47, bf16[128,512]{1,0:T(8,128)(2,1)} %bitcast.48), custom_call_target="tpu_custom_call" | custom-call | bytes 3145728 | tf_op jit(solution)/shard_map/pallas_call | solution.py:297
  3.3 9.2 %all-to-all-start = ((bf16[8,128,768]{2,1,0:T(8,128)(2,1)}), bf16[8,128,768]{2,1,0:T(8,128)(2,1)S(1)}, u32[]{:S(2)}, u32[]{:S(2)}) async-start(bf16[8,128,768]{2,1,0:T(8,128)(2,1)} %shard_map.110), calls=%async_computation | async-start | bytes 3145728 | tf_op jit(solution)/shard_map/all_to_all | solution.py:396
  12.5 1.3 collective-permute-start
  13.8 6.9 %collective-permute-done = bf16[128,1024]{1,0:T(8,128)(2,1)S(1)} collective-permute-done((bf16[128,1024]{1,0:T(8,128)(2,1)S(1)}, bf16[128,1024]{1,0:T(8,128)(2,1)S(1)}, u32[]{:S(2)}, u32[]{:S(2)}) %collective-permute-start) | collective-permute-done | bytes 262176 | tf_op jit(solution)/shard_map/ppermute | solution.py:380
  20.7 1.5 %collective-permute-start.1 = (bf16[128,1024]{1,0:T(8,128)(2,1)S(1)}, bf16[128,1024]{1,0:T(8,128)(2,1)S(1)}, u32[]{:S(2)}, u32[]{:S(2)}) collective-permute-start(bf16[128,1024]{1,0:T(8,128)(2,1)S(1)} %get-tuple-element.63), channel_id=1, source_target_pairs={{0,128},{64,192},{128,0},{192,64},{1,129},{65,193},{129,1},{193,65... | collective-permute-start | bytes 786440 | tf_op jit(solution)/shard_map/ppermute | solution.py:383
  22.2 0.9 collective-permute-start.2
  23.1 0.8 pad_maximum_fusion.refs_0_
  23.9 2.7 %collective-permute-start.5 = (bf16[2,128,1024]{2,1,0:T(8,128)(2,1)}, bf16[2,128,1024]{2,1,0:T(8,128)(2,1)S(1)}, u32[]{:S(2)}, u32[]{:S(2)}) collective-permute-start(bf16[2,128,1024]{2,1,0:T(8,128)(2,1)} %pad_maximum_fusion.refs_0_), channel_id=1, source_target_pairs={{0,48},{16,0},{32,16},{48,32},{1,49},{17,1},{33,17},{49,33},{2,50}... | collective-permute-start | bytes 1572872 | tf_op jit(solution)/shard_map/ppermute | solution.py:388
  26.7 1.5 collective-permute-done.1
  28.1 5.7 %collective-permute-done.2 = bf16[128,1024]{1,0:T(8,128)(2,1)S(1)} collective-permute-done((bf16[128,1024]{1,0:T(8,128)(2,1)S(1)}, bf16[128,1024]{1,0:T(8,128)(2,1)S(1)}, u32[]{:S(2)}, u32[]{:S(2)}) %collective-permute-start.2) | collective-permute-done | bytes 262176 | tf_op jit(solution)/shard_map/ppermute | solution.py:383
  33.9 0.8 pad_maximum_fusion.1.refs_1_
  34.7 2.7 %collective-permute-start.6 = (bf16[2,128,1024]{2,1,0:T(8,128)(2,1)}, bf16[2,128,1024]{2,1,0:T(8,128)(2,1)}, u32[]{:S(2)}, u32[]{:S(2)}) collective-permute-start(bf16[2,128,1024]{2,1,0:T(8,128)(2,1)} %pad_maximum_fusion.1.refs_1_), channel_id=1, source_target_pairs={{0,48},{16,0},{32,16},{48,32},{1,49},{17,1},{33,17},{49,33},{2,50}... | collective-permute-start | bytes 1572872 | tf_op jit(solution)/shard_map/ppermute | solution.py:388
  37.5 1.4 collective-permute-done.3.refs_2_
  38.9 9.4 %collective-permute-done.6.refs_5_ = bf16[2,128,1024]{2,1,0:T(8,128)(2,1)} collective-permute-done((bf16[2,128,1024]{2,1,0:T(8,128)(2,1)}, bf16[2,128,1024]{2,1,0:T(8,128)(2,1)}, u32[]{:S(2)}, u32[]{:S(2)}) %collective-permute-start.6) | collective-permute-done | bytes 524320 | tf_op jit(solution)/shard_map/ppermute | solution.py:388
  48.3 3.1 %collective-permute-done.4.refs_3_ = bf16[2,128,1024]{2,1,0:T(8,128)(2,1)} collective-permute-done((bf16[2,128,1024]{2,1,0:T(8,128)(2,1)}, bf16[2,128,1024]{2,1,0:T(8,128)(2,1)}, u32[]{:S(2)}, u32[]{:S(2)}) %collective-permute-start.4) | collective-permute-done | bytes 524320 | tf_op jit(solution)/shard_map/ppermute | solution.py:388
  51.7 0.8 slice.29
  52.6 2.3 %collective-permute-start.7 = (bf16[8,128,256]{2,1,0:T(8,128)(2,1)}, bf16[8,128,256]{2,1,0:T(8,128)(2,1)S(1)}, u32[]{:S(2)}, u32[]{:S(2)}) collective-permute-start(bf16[8,128,256]{2,1,0:T(8,128)(2,1)} %slice.29), channel_id=1, source_target_pairs={{0,1},{1,0},{2,3},{3,2},{4,5},{5,4},{6,7},{7,6},{8,9},{9,8},{10,11... | collective-permute-start | bytes 1572872 | tf_op jit(solution)/shard_map/ppermute | solution.py:366
  54.9 0.9 collective-permute-start.8
  55.8 1.8 %collective-permute-start.9 = (bf16[2,128,1024]{2,1,0:T(8,128)(2,1)}, bf16[2,128,1024]{2,1,0:T(8,128)(2,1)}, u32[]{:S(2)}, u32[]{:S(2)}) collective-permute-start(bf16[2,128,1024]{2,1,0:T(8,128)(2,1)} %collective-permute-done.6.refs_5_), channel_id=1, source_target_pairs={{0,48},{16,0},{32,16},{48,32},{1,49},{17,1},{33,17},{49,33},{2,50}... | collective-permute-start | bytes 1572872 | tf_op jit(solution)/shard_map/ppermute | solution.py:392
  57.8 11.2 %shard_map.111 = (bf16[128,256]{1,0:T(8,128)(2,1)}, bf16[128,256]{1,0:T(8,128)(2,1)}, bf16[128,256]{1,0:T(8,128)(2,1)}, bf16[128,256]{1,0:T(8,128)(2,1)}, bf16[1...) custom-call(s32[16,8]{1,0:T(8,128)S(1)} %copy.14.links_ref, ...), custom_call_target="tpu_custom_call" | custom-call | flops 1000 | bytes 1000 | tf_op jit(solution)/shard_map/pallas_call | solution.py:191
  68.9 1.1 collective-permute-done.8.refs_6_
  70.0 0.8 collective-permute-start.11
  70.9 0.4 collective-permute-start.13
  71.4 0.9 collective-permute-done.11
  72.3 0.9 add_convert_fusion
  73.2 6.3 %all-to-all-start.1 = ((bf16[8,128,256]{2,1,0:T(8,128)(2,1)}), bf16[8,128,256]{2,1,0:T(8,128)(2,1)S(1)}, u32[]{:S(2)}, u32[]{:S(2)}) async-start(bf16[8,128,256]{2,1,0:T(8,128)(2,1)} %add_convert_fusion), calls=%async_computation.1 | async-start | bytes 1048576 | tf_op jit(solution)/shard_map/all_to_all | solution.py:413
  79.6 0.7 collective-permute-start.10
  80.4 1.2 collective-permute-done.10
  82.7 0.9 collective-permute-done.16.refs_12_
  83.5 1.7 %collective-permute-done.17.refs_13_ = bf16[2,128,1024]{2,1,0:T(8,128)(2,1)S(1)} collective-permute-done((bf16[2,128,1024]{2,1,0:T(8,128)(2,1)}, bf16[2,128,1024]{2,1,0:T(8,128)(2,1)S(1)}, u32[]{:S(2)}, u32[]{:S(2)}) %collective-permute-start.17) | collective-permute-done | bytes 524320 | tf_op jit(solution)/shard_map/ppermute | solution.py:366
  85.2 0.7 collective-permute-done.18.refs_14_
  86.1 0.8 copy-done.11
  86.9 10.6 %all-to-all-done.1.partials_ref = bf16[8,128,256]{2,1,0:T(8,128)(2,1)S(1)} async-done(((bf16[8,128,256]{2,1,0:T(8,128)(2,1)}), bf16[8,128,256]{2,1,0:T(8,128)(2,1)S(1)}, u32[]{:S(2)}, u32[]{:S(2)}) %all-to-all-start.1) | async-done | bytes 524320 | tf_op jit(solution)/shard_map/all_to_all | solution.py:413
  97.5 1.2 shard_map.112
  98.8 8.1 %all-to-all-start.2 = ((bf16[32,128,128]{2,1,0:T(8,128)(2,1)}), bf16[32,128,128]{2,1,0:T(8,128)(2,1)S(1)}, u32[]{:S(2)}, u32[]{:S(2)}) async-start(bf16[32,128,128]{2,1,0:T(8,128)(2,1)} %get-tuple-element.98), calls=%async_computation.2 | async-start | bytes 2097152 | tf_op jit(solution)/shard_map/all_to_all | solution.py:420
  107.0 0.8 collective-permute-start.21
  107.9 2.7 %collective-permute-start.22 = (bf16[2,128,256]{2,1,0:T(8,128)(2,1)S(1)}, bf16[2,128,256]{2,1,0:T(8,128)(2,1)S(1)}, u32[]{:S(2)}, u32[]{:S(2)}) collective-permute-start(bf16[2,128,256]{2,1,0:T(8,128)(2,1)S(1)} %pad_maximum_fusion.5), channel_id=1, source_target_pairs={{0,6},{2,8},{4,10},{6,12},{8,14},{10,0},{12,2},{14,4},{1,11},{3,13... | collective-permute-start | bytes 393224 | tf_op jit(solution)/shard_map/ppermute | solution.py:426
  110.6 2.6 %collective-permute-start.23 = (bf16[128,256]{1,0:T(8,128)(2,1)S(1)}, bf16[128,256]{1,0:T(8,128)(2,1)S(1)}, u32[]{:S(2)}, u32[]{:S(2)}) collective-permute-start(bf16[128,256]{1,0:T(8,128)(2,1)S(1)} %copy-done.16), channel_id=1, source_target_pairs={{0,8},{2,10},{4,12},{6,14},{8,0},{10,2},{12,4},{14,6},{1,9},{3,11}... | collective-permute-start | bytes 196616 | tf_op jit(solution)/shard_map/ppermute | solution.py:427
  113.1 4.8 %collective-permute-done.23.across_ref = bf16[128,256]{1,0:T(8,128)(2,1)S(1)} collective-permute-done((bf16[128,256]{1,0:T(8,128)(2,1)S(1)}, bf16[128,256]{1,0:T(8,128)(2,1)S(1)}, u32[]{:S(2)}, u32[]{:S(2)}) %collective-permute-start.23) | collective-permute-done | bytes 65568 | tf_op jit(solution)/shard_map/ppermute | solution.py:427
  117.9 2.7 %collective-permute-done.22.refs_2_ = bf16[2,128,256]{2,1,0:T(8,128)(2,1)S(1)} collective-permute-done((bf16[2,128,256]{2,1,0:T(8,128)(2,1)S(1)}, bf16[2,128,256]{2,1,0:T(8,128)(2,1)S(1)}, u32[]{:S(2)}, u32[]{:S(2)}) %collective-permute-start.22) | collective-permute-done | bytes 131104 | tf_op jit(solution)/shard_map/ppermute | solution.py:426
  120.6 3.1 %all-to-all-done.2.grads_ref = bf16[32,128,128]{2,1,0:T(8,128)(2,1)S(1)} async-done(((bf16[32,128,128]{2,1,0:T(8,128)(2,1)}), bf16[32,128,128]{2,1,0:T(8,128)(2,1)S(1)}, u32[]{:S(2)}, u32[]{:S(2)}) %all-to-all-start.2) | async-done | bytes 1048608 | tf_op jit(solution)/shard_map/all_to_all | solution.py:420
  123.7 5.1 %shard_map.114 = bf16[1024,128]{1,0:T(8,128)(2,1)} custom-call(s32[4]{0:T(128)S(1)} %pad_add_fusion.place_ref, bf16[32,128,128]{2,1,0:T(8,128)(2,1)S(1)} %all-to-all-done.2.grads_ref, bf16[2,128,1024]{2,1,0:T(8,128)(2,1)} %pad_maximum_fusion.refs_0_, bf16[2,128,1024]{2,1,0:T(8,128)(2,1)} %pad_maximum_fusion.1.refs_1_, ...), custom_call_target="tpu_custom_call" | custom-call | flops 1100000000 | bytes 9437184 | tf_op jit(solution)/shard_map/pallas_call | solution.py:257
  128.9 6.8 %all-to-all-start.3 = ((bf16[64,16,128]{2,1,0:T(8,128)(2,1)}), bf16[64,16,128]{2,1,0:T(8,128)(2,1)S(1)}, u32[]{:S(2)}, u32[]{:S(2)}) async-start(bf16[64,16,128]{2,1,0:T(8,128)(2,1)} %bitcast.22), calls=%async_computation.3 | async-start | bytes 524288 | tf_op jit(solution)/shard_map/all_to_all | solution.py:434
  135.8 0.5 collective-permute-start.24
  136.3 1.1 collective-permute-done.24.refs_3_
  137.4 1.4 shard_map.113
  138.8 8.9 %all-to-all-done.3 = bf16[64,16,128]{2,1,0:T(8,128)(2,1)S(1)} async-done(((bf16[64,16,128]{2,1,0:T(8,128)(2,1)}), bf16[64,16,128]{2,1,0:T(8,128)(2,1)S(1)}, u32[]{:S(2)}, u32[]{:S(2)}) %all-to-all-start.3) | async-done | bytes 262176 | tf_op jit(solution)/shard_map/all_to_all | solution.py:434
  147.8 0.6 copy_bitcast_fusion
  (70 shorter events, 2.3 us)
Async XLA Ops:
  3.2 9.2 %copy-start.2 = (bf16[1,128,4096]{2,1,0:T(8,128)(2,1)S(1)}, bf16[1,128,4096]{2,1,0:T(8,128)(2,1)}, u32[]{:S(2)}) copy-start(bf16[1,128,4096]{2,1,0:T(8,128)(2,1)} %param.7) | copy-start | bytes 3145732
  3.3 48.2 %all-to-all-start = ((bf16[8,128,768]{2,1,0:T(8,128)(2,1)}), bf16[8,128,768]{2,1,0:T(8,128)(2,1)S(1)}, u32[]{:S(2)}, u32[]{:S(2)}) async-start(bf16[8,128,768]{2,1,0:T(8,128)(2,1)} %shard_map.110), calls=%async_computation | async-start | bytes 3145728 | tf_op jit(solution)/shard_map/all_to_all | solution.py:396
  12.5 38.9 %copy-start.1 = (s32[1,2048]{1,0:T(1,128)S(1)}, s32[1,2048]{1,0:T(1,128)}, u32[]{:S(2)}) copy-start(s32[1,2048]{1,0:T(1,128)} %param.13) | copy-start | bytes 24580
  12.5 8.1 %collective-permute-start = (bf16[128,1024]{1,0:T(8,128)(2,1)S(1)}, bf16[128,1024]{1,0:T(8,128)(2,1)S(1)}, u32[]{:S(2)}, u32[]{:S(2)}) collective-permute-start(bf16[128,1024]{1,0:T(8,128)(2,1)S(1)} %get-tuple-element.120), channel_id=1, source_target_pairs={{0,64},{64,128},{128,192},{192,0},{1,65},{65,129},{129,193},{193,1... | collective-permute-start | bytes 786440 | tf_op jit(solution)/shard_map/ppermute | solution.py:380
  20.7 7.4 %collective-permute-start.1 = (bf16[128,1024]{1,0:T(8,128)(2,1)S(1)}, bf16[128,1024]{1,0:T(8,128)(2,1)S(1)}, u32[]{:S(2)}, u32[]{:S(2)}) collective-permute-start(bf16[128,1024]{1,0:T(8,128)(2,1)S(1)} %get-tuple-element.63), channel_id=1, source_target_pairs={{0,128},{64,192},{128,0},{192,64},{1,129},{65,193},{129,1},{193,65... | collective-permute-start | bytes 786440 | tf_op jit(solution)/shard_map/ppermute | solution.py:383
  22.2 11.6 %collective-permute-start.2 = (bf16[128,1024]{1,0:T(8,128)(2,1)S(1)}, bf16[128,1024]{1,0:T(8,128)(2,1)S(1)}, u32[]{:S(2)}, u32[]{:S(2)}) collective-permute-start(bf16[128,1024]{1,0:T(8,128)(2,1)S(1)} %get-tuple-element.64), channel_id=1, source_target_pairs={{0,192},{64,0},{128,64},{192,128},{1,193},{65,1},{129,65},{193,129... | collective-permute-start | bytes 786440 | tf_op jit(solution)/shard_map/ppermute | solution.py:383
  23.9 13.5 %collective-permute-start.5 = (bf16[2,128,1024]{2,1,0:T(8,128)(2,1)}, bf16[2,128,1024]{2,1,0:T(8,128)(2,1)S(1)}, u32[]{:S(2)}, u32[]{:S(2)}) collective-permute-start(bf16[2,128,1024]{2,1,0:T(8,128)(2,1)} %pad_maximum_fusion.refs_0_), channel_id=1, source_target_pairs={{0,48},{16,0},{32,16},{48,32},{1,49},{17,1},{33,17},{49,33},{2,50}... | collective-permute-start | bytes 1572872 | tf_op jit(solution)/shard_map/ppermute | solution.py:388
  26.6 12.2 %collective-permute-start.3 = (bf16[2,128,1024]{2,1,0:T(8,128)(2,1)}, bf16[2,128,1024]{2,1,0:T(8,128)(2,1)}, u32[]{:S(2)}, u32[]{:S(2)}) collective-permute-start(bf16[2,128,1024]{2,1,0:T(8,128)(2,1)} %pad_maximum_fusion.refs_0_), channel_id=1, source_target_pairs={{0,16},{16,32},{32,48},{48,0},{1,17},{17,33},{33,49},{49,1},{2,18}... | collective-permute-start | bytes 1572872 | tf_op jit(solution)/shard_map/ppermute | solution.py:388
  33.9 23.7 %copy-start.15 = (s32[1,16,8]{1,2,0:T(8,128)S(1)}, s32[1,16,8]{1,2,0:T(8,128)}, u32[]{:S(2)}) copy-start(s32[1,16,8]{1,2,0:T(8,128)} %param.12) | copy-start | bytes 1540
  34.7 13.6 %collective-permute-start.6 = (bf16[2,128,1024]{2,1,0:T(8,128)(2,1)}, bf16[2,128,1024]{2,1,0:T(8,128)(2,1)}, u32[]{:S(2)}, u32[]{:S(2)}) collective-permute-start(bf16[2,128,1024]{2,1,0:T(8,128)(2,1)} %pad_maximum_fusion.1.refs_1_), channel_id=1, source_target_pairs={{0,48},{16,0},{32,16},{48,32},{1,49},{17,1},{33,17},{49,33},{2,50}... | collective-permute-start | bytes 1572872 | tf_op jit(solution)/shard_map/ppermute | solution.py:388
  37.4 14.0 %collective-permute-start.4 = (bf16[2,128,1024]{2,1,0:T(8,128)(2,1)}, bf16[2,128,1024]{2,1,0:T(8,128)(2,1)}, u32[]{:S(2)}, u32[]{:S(2)}) collective-permute-start(bf16[2,128,1024]{2,1,0:T(8,128)(2,1)} %pad_maximum_fusion.1.refs_1_), channel_id=1, source_target_pairs={{0,16},{16,32},{32,48},{48,0},{1,17},{17,33},{33,49},{49,1},{2,18}... | collective-permute-start | bytes 1572872 | tf_op jit(solution)/shard_map/ppermute | solution.py:388
  37.4 10.8 %copy-start.3 = (bf16[2,128,1024]{2,1,0:T(8,128)(2,1)}, bf16[2,128,1024]{2,1,0:T(8,128)(2,1)S(1)}, u32[]{:S(2)}) copy-start(bf16[2,128,1024]{2,1,0:T(8,128)(2,1)S(1)} %collective-permute-done.5.refs_4_) | copy-start | bytes 1572868
  52.6 5.2 %collective-permute-start.7 = (bf16[8,128,256]{2,1,0:T(8,128)(2,1)}, bf16[8,128,256]{2,1,0:T(8,128)(2,1)S(1)}, u32[]{:S(2)}, u32[]{:S(2)}) collective-permute-start(bf16[8,128,256]{2,1,0:T(8,128)(2,1)} %slice.29), channel_id=1, source_target_pairs={{0,1},{1,0},{2,3},{3,2},{4,5},{5,4},{6,7},{7,6},{8,9},{9,8},{10,11... | collective-permute-start | bytes 1572872 | tf_op jit(solution)/shard_map/ppermute | solution.py:366
  54.9 15.1 %collective-permute-start.8 = (bf16[2,128,1024]{2,1,0:T(8,128)(2,1)}, bf16[2,128,1024]{2,1,0:T(8,128)(2,1)}, u32[]{:S(2)}, u32[]{:S(2)}) collective-permute-start(bf16[2,128,1024]{2,1,0:T(8,128)(2,1)} %collective-permute-done.3.refs_2_), channel_id=1, source_target_pairs={{0,16},{16,32},{32,48},{48,0},{1,17},{17,33},{33,49},{49,1},{2,18}... | collective-permute-start | bytes 1572872 | tf_op jit(solution)/shard_map/ppermute | solution.py:391
  55.8 14.2 %collective-permute-start.9 = (bf16[2,128,1024]{2,1,0:T(8,128)(2,1)}, bf16[2,128,1024]{2,1,0:T(8,128)(2,1)}, u32[]{:S(2)}, u32[]{:S(2)}) collective-permute-start(bf16[2,128,1024]{2,1,0:T(8,128)(2,1)} %collective-permute-done.6.refs_5_), channel_id=1, source_target_pairs={{0,48},{16,0},{32,16},{48,32},{1,49},{17,1},{33,17},{49,33},{2,50}... | collective-permute-start | bytes 1572872 | tf_op jit(solution)/shard_map/ppermute | solution.py:392
  70.0 11.6 %copy-start.4 = (bf16[2,128,1024]{2,1,0:T(8,128)(2,1)S(1)}, bf16[2,128,1024]{2,1,0:T(8,128)(2,1)}, u32[]{:S(2)}) copy-start(bf16[2,128,1024]{2,1,0:T(8,128)(2,1)} %copy-done.3) | copy-start | bytes 1572868
  70.0 2.3 %collective-permute-start.11 = (bf16[8,128,256]{2,1,0:T(8,128)(2,1)S(1)}, bf16[8,128,256]{2,1,0:T(8,128)(2,1)S(1)}, u32[]{:S(2)}, u32[]{:S(2)}) collective-permute-start(bf16[8,128,256]{2,1,0:T(8,128)(2,1)S(1)} %get-tuple-element.88), channel_id=1, source_target_pairs={{0,1},{1,0},{2,3},{3,2},{4,5},{5,4},{6,7},{7,6},{8,9},{9,8},{10,11... | collective-permute-start | bytes 1572872 | tf_op jit(solution)/shard_map/ppermute | solution.py:366
  70.8 11.2 %collective-permute-start.12 = (bf16[2,128,1024]{2,1,0:T(8,128)(2,1)}, bf16[2,128,1024]{2,1,0:T(8,128)(2,1)S(1)}, u32[]{:S(2)}, u32[]{:S(2)}) collective-permute-start(bf16[2,128,1024]{2,1,0:T(8,128)(2,1)} %pad_maximum_fusion.refs_0_), channel_id=1, source_target_pairs={{0,1},{1,0},{2,3},{3,2},{4,5},{5,4},{6,7},{7,6},{8,9},{9,8},{10,11... | collective-permute-start | bytes 1572872 | tf_op jit(solution)/shard_map/ppermute | solution.py:366
  70.9 11.3 %collective-permute-start.13 = (bf16[2,128,1024]{2,1,0:T(8,128)(2,1)}, bf16[2,128,1024]{2,1,0:T(8,128)(2,1)S(1)}, u32[]{:S(2)}, u32[]{:S(2)}) collective-permute-start(bf16[2,128,1024]{2,1,0:T(8,128)(2,1)} %pad_maximum_fusion.1.refs_1_), channel_id=1, source_target_pairs={{0,1},{1,0},{2,3},{3,2},{4,5},{5,4},{6,7},{7,6},{8,9},{9,8},{10,11... | collective-permute-start | bytes 1572872 | tf_op jit(solution)/shard_map/ppermute | solution.py:366
  71.3 11.2 %collective-permute-start.14 = (bf16[2,128,1024]{2,1,0:T(8,128)(2,1)}, bf16[2,128,1024]{2,1,0:T(8,128)(2,1)S(1)}, u32[]{:S(2)}, u32[]{:S(2)}) collective-permute-start(bf16[2,128,1024]{2,1,0:T(8,128)(2,1)} %collective-permute-done.3.refs_2_), channel_id=1, source_target_pairs={{0,1},{1,0},{2,3},{3,2},{4,5},{5,4},{6,7},{7,6},{8,9},{9,8},{10,11... | collective-permute-start | bytes 1572872 | tf_op jit(solution)/shard_map/ppermute | solution.py:366
  73.2 24.3 %all-to-all-start.1 = ((bf16[8,128,256]{2,1,0:T(8,128)(2,1)}), bf16[8,128,256]{2,1,0:T(8,128)(2,1)S(1)}, u32[]{:S(2)}, u32[]{:S(2)}) async-start(bf16[8,128,256]{2,1,0:T(8,128)(2,1)} %add_convert_fusion), calls=%async_computation.1 | async-start | bytes 1048576 | tf_op jit(solution)/shard_map/all_to_all | solution.py:413
  79.6 27.3 %copy-start.14 = (bf16[128,256]{1,0:T(8,128)(2,1)S(1)}, bf16[128,256]{1,0:T(8,128)(2,1)}, u32[]{:S(2)}) copy-start(bf16[128,256]{1,0:T(8,128)(2,1)} %get-tuple-element.99) | copy-start | bytes 196612
  79.6 27.4 %copy-start.13 = (bf16[128,256]{1,0:T(8,128)(2,1)S(1)}, bf16[128,256]{1,0:T(8,128)(2,1)}, u32[]{:S(2)}) copy-start(bf16[128,256]{1,0:T(8,128)(2,1)} %get-tuple-element.101) | copy-start | bytes 196612
  79.6 2.0 %collective-permute-start.10 = (bf16[3,128,256]{2,1,0:T(8,128)(2,1)}, bf16[3,128,256]{2,1,0:T(8,128)(2,1)S(1)}, u32[]{:S(2)}, u32[]{:S(2)}) collective-permute-start(bf16[3,128,256]{2,1,0:T(8,128)(2,1)} %get-tuple-element.86), channel_id=1, source_target_pairs={{0,1},{1,0},{2,3},{3,2},{4,5},{5,4},{6,7},{7,6},{8,9},{9,8},{10,11... | collective-permute-start | bytes 589832 | tf_op jit(solution)/shard_map/ppermute | solution.py:366
  80.3 2.3 %collective-permute-start.15 = (bf16[2,128,1024]{2,1,0:T(8,128)(2,1)}, bf16[2,128,1024]{2,1,0:T(8,128)(2,1)S(1)}, u32[]{:S(2)}, u32[]{:S(2)}) collective-permute-start(bf16[2,128,1024]{2,1,0:T(8,128)(2,1)} %collective-permute-done.4.refs_3_), channel_id=1, source_target_pairs={{0,1},{1,0},{2,3},{3,2},{4,5},{5,4},{6,7},{7,6},{8,9},{9,8},{10,11... | collective-permute-start | bytes 1572872 | tf_op jit(solution)/shard_map/ppermute | solution.py:366
  81.6 1.9 %collective-permute-start.16 = (bf16[2,128,1024]{2,1,0:T(8,128)(2,1)S(1)}, bf16[2,128,1024]{2,1,0:T(8,128)(2,1)S(1)}, u32[]{:S(2)}, u32[]{:S(2)}) collective-permute-start(bf16[2,128,1024]{2,1,0:T(8,128)(2,1)S(1)} %copy-done.4), channel_id=1, source_target_pairs={{0,1},{1,0},{2,3},{3,2},{4,5},{5,4},{6,7},{7,6},{8,9},{9,8},{10,11... | collective-permute-start | bytes 1572872 | tf_op jit(solution)/shard_map/ppermute | solution.py:366
  82.0 24.9 %copy-start.5 = (bf16[2,128,1024]{2,1,0:T(8,128)(2,1)}, bf16[2,128,1024]{2,1,0:T(8,128)(2,1)S(1)}, u32[]{:S(2)}) copy-start(bf16[2,128,1024]{2,1,0:T(8,128)(2,1)S(1)} %collective-permute-done.12.refs_8_) | copy-start | bytes 1572868
  82.0 3.2 %collective-permute-start.17 = (bf16[2,128,1024]{2,1,0:T(8,128)(2,1)}, bf16[2,128,1024]{2,1,0:T(8,128)(2,1)S(1)}, u32[]{:S(2)}, u32[]{:S(2)}) collective-permute-start(bf16[2,128,1024]{2,1,0:T(8,128)(2,1)} %collective-permute-done.6.refs_5_), channel_id=1, source_target_pairs={{0,1},{1,0},{2,3},{3,2},{4,5},{5,4},{6,7},{7,6},{8,9},{9,8},{10,11... | collective-permute-start | bytes 1572872 | tf_op jit(solution)/shard_map/ppermute | solution.py:366
  82.1 24.7 %copy-start.6 = (bf16[2,128,1024]{2,1,0:T(8,128)(2,1)}, bf16[2,128,1024]{2,1,0:T(8,128)(2,1)S(1)}, u32[]{:S(2)}) copy-start(bf16[2,128,1024]{2,1,0:T(8,128)(2,1)S(1)} %collective-permute-done.13.refs_9_) | copy-start | bytes 1572868
  82.1 3.8 %collective-permute-start.18 = (bf16[2,128,1024]{2,1,0:T(8,128)(2,1)}, bf16[2,128,1024]{2,1,0:T(8,128)(2,1)S(1)}, u32[]{:S(2)}, u32[]{:S(2)}) collective-permute-start(bf16[2,128,1024]{2,1,0:T(8,128)(2,1)} %collective-permute-done.8.refs_6_), channel_id=1, source_target_pairs={{0,1},{1,0},{2,3},{3,2},{4,5},{5,4},{6,7},{7,6},{8,9},{9,8},{10,11... | collective-permute-start | bytes 1572872 | tf_op jit(solution)/shard_map/ppermute | solution.py:366
  82.5 3.5 %copy-start.7 = (bf16[2,128,1024]{2,1,0:T(8,128)(2,1)}, bf16[2,128,1024]{2,1,0:T(8,128)(2,1)S(1)}, u32[]{:S(2)}) copy-start(bf16[2,128,1024]{2,1,0:T(8,128)(2,1)S(1)} %collective-permute-done.14.refs_10_) | copy-start | bytes 1572868
  82.5 4.4 %collective-permute-start.19 = (bf16[2,128,1024]{2,1,0:T(8,128)(2,1)}, bf16[2,128,1024]{2,1,0:T(8,128)(2,1)}, u32[]{:S(2)}, u32[]{:S(2)}) collective-permute-start(bf16[2,128,1024]{2,1,0:T(8,128)(2,1)} %collective-permute-done.9.refs_7_), channel_id=1, source_target_pairs={{0,1},{1,0},{2,3},{3,2},{4,5},{5,4},{6,7},{7,6},{8,9},{9,8},{10,11... | collective-permute-start | bytes 1572872 | tf_op jit(solution)/shard_map/ppermute | solution.py:366
  82.7 4.3 %copy-start.8 = (bf16[2,128,1024]{2,1,0:T(8,128)(2,1)}, bf16[2,128,1024]{2,1,0:T(8,128)(2,1)S(1)}, u32[]{:S(2)}) copy-start(bf16[2,128,1024]{2,1,0:T(8,128)(2,1)S(1)} %collective-permute-done.15.refs_11_) | copy-start | bytes 1572868
  83.5 2.5 %copy-start.9 = (bf16[2,128,1024]{2,1,0:T(8,128)(2,1)}, bf16[2,128,1024]{2,1,0:T(8,128)(2,1)S(1)}, u32[]{:S(2)}) copy-start(bf16[2,128,1024]{2,1,0:T(8,128)(2,1)S(1)} %collective-permute-done.16.refs_12_) | copy-start | bytes 1572868
  85.2 0.9 copy-start.10
  86.1 0.8 copy-start.11
  98.7 9.1 %copy-start.12 = (bf16[128,256]{1,0:T(8,128)(2,1)S(1)}, bf16[128,256]{1,0:T(8,128)(2,1)}, u32[]{:S(2)}) copy-start(bf16[128,256]{1,0:T(8,128)(2,1)} %get-tuple-element.102) | copy-start | bytes 196612
  98.7 11.8 %copy-start.16 = (bf16[128,256]{1,0:T(8,128)(2,1)S(1)}, bf16[128,256]{1,0:T(8,128)(2,1)}, u32[]{:S(2)}) copy-start(bf16[128,256]{1,0:T(8,128)(2,1)} %get-tuple-element.103) | copy-start | bytes 196612
  98.8 25.0 %all-to-all-start.2 = ((bf16[32,128,128]{2,1,0:T(8,128)(2,1)}), bf16[32,128,128]{2,1,0:T(8,128)(2,1)S(1)}, u32[]{:S(2)}, u32[]{:S(2)}) async-start(bf16[32,128,128]{2,1,0:T(8,128)(2,1)} %get-tuple-element.98), calls=%async_computation.2 | async-start | bytes 2097152 | tf_op jit(solution)/shard_map/all_to_all | solution.py:420
  106.9 11.0 %collective-permute-start.20 = (bf16[2,128,256]{2,1,0:T(8,128)(2,1)S(1)}, bf16[2,128,256]{2,1,0:T(8,128)(2,1)S(1)}, u32[]{:S(2)}, u32[]{:S(2)}) collective-permute-start(bf16[2,128,256]{2,1,0:T(8,128)(2,1)S(1)} %pad_maximum_fusion.3), channel_id=1, source_target_pairs={{0,2},{2,4},{4,6},{6,8},{8,10},{10,12},{12,14},{14,0},{1,15},{3,1}... | collective-permute-start | bytes 393224 | tf_op jit(solution)/shard_map/ppermute | solution.py:426
  107.0 10.9 %collective-permute-start.21 = (bf16[2,128,256]{2,1,0:T(8,128)(2,1)S(1)}, bf16[2,128,256]{2,1,0:T(8,128)(2,1)S(1)}, u32[]{:S(2)}, u32[]{:S(2)}) collective-permute-start(bf16[2,128,256]{2,1,0:T(8,128)(2,1)S(1)} %pad_maximum_fusion.4), channel_id=1, source_target_pairs={{0,4},{2,6},{4,8},{6,10},{8,12},{10,14},{12,0},{14,2},{1,13},{3,15... | collective-permute-start | bytes 393224 | tf_op jit(solution)/shard_map/ppermute | solution.py:426
  107.9 29.5 %copy-start = (bf16[128,256]{1,0:T(8,128)(2,1)S(1)}, bf16[128,256]{1,0:T(8,128)(2,1)}, u32[]{:S(2)}) copy-start(bf16[128,256]{1,0:T(8,128)(2,1)} %get-tuple-element.81.keep_ref) | copy-start | bytes 196612
  107.9 12.7 %collective-permute-start.22 = (bf16[2,128,256]{2,1,0:T(8,128)(2,1)S(1)}, bf16[2,128,256]{2,1,0:T(8,128)(2,1)S(1)}, u32[]{:S(2)}, u32[]{:S(2)}) collective-permute-start(bf16[2,128,256]{2,1,0:T(8,128)(2,1)S(1)} %pad_maximum_fusion.5), channel_id=1, source_target_pairs={{0,6},{2,8},{4,10},{6,12},{8,14},{10,0},{12,2},{14,4},{1,11},{3,13... | collective-permute-start | bytes 393224 | tf_op jit(solution)/shard_map/ppermute | solution.py:426
  110.6 7.3 %collective-permute-start.23 = (bf16[128,256]{1,0:T(8,128)(2,1)S(1)}, bf16[128,256]{1,0:T(8,128)(2,1)S(1)}, u32[]{:S(2)}, u32[]{:S(2)}) collective-permute-start(bf16[128,256]{1,0:T(8,128)(2,1)S(1)} %copy-done.16), channel_id=1, source_target_pairs={{0,8},{2,10},{4,12},{6,14},{8,0},{10,2},{12,4},{14,6},{1,9},{3,11}... | collective-permute-start | bytes 196616 | tf_op jit(solution)/shard_map/ppermute | solution.py:427
  128.9 18.8 %all-to-all-start.3 = ((bf16[64,16,128]{2,1,0:T(8,128)(2,1)}), bf16[64,16,128]{2,1,0:T(8,128)(2,1)S(1)}, u32[]{:S(2)}, u32[]{:S(2)}) async-start(bf16[64,16,128]{2,1,0:T(8,128)(2,1)} %bitcast.22), calls=%async_computation.3 | async-start | bytes 524288 | tf_op jit(solution)/shard_map/all_to_all | solution.py:434
  135.8 1.6 %collective-permute-start.24 = (bf16[3,128,256]{2,1,0:T(8,128)(2,1)S(1)}, bf16[3,128,256]{2,1,0:T(8,128)(2,1)S(1)}, u32[]{:S(2)}, u32[]{:S(2)}) collective-permute-start(bf16[3,128,256]{2,1,0:T(8,128)(2,1)S(1)} %pad_maximum_fusion.2), channel_id=1, source_target_pairs={{0,1},{1,0},{2,3},{3,2},{4,5},{5,4},{6,7},{7,6},{8,9},{9,8},{10,11... | collective-permute-start | bytes 589832 | tf_op jit(solution)/shard_map/ppermute | solution.py:366

commit v13 on v11

--- a/solution.py
+++ b/solution.py
@@ -387,10 +387,7 @@
     before, after = zip(
         *[[lax.ppermute(a, "y", ring(NY, shift)) for shift in (1, -1)] for a in mine]
     )
-    far = (
-        lax.ppermute(before[0], "y", ring(NY, 1)),
-        lax.ppermute(after[1], "y", ring(NY, -1)),
-    )
+    far_low = lax.ppermute(before[0], "y", ring(NY, 1))
 
     outgoing = packed(queries[0], output_grads[0], keys[0], values[0])
     rows = lax.all_to_all(outgoing, "z", split_axis=0, concat_axis=0, tiled=True)
@@ -403,10 +400,12 @@
     keep, across, *ship, give, own, away = attention_grads(
         block_links[0], place, rows, other, seg_cols, seg_rows
     )
-    inputs_own = mine + before + after + far
+    inputs_own = mine + before + after + (far_low,)
     keep, across, ship, give, own, away, inputs_own = lax.optimization_barrier(
         (keep, across, ship, give, own, away, inputs_own)
     )
+    far_high = lax.ppermute(inputs_own[5], "y", ring(NY, -1))
+    inputs_own = tuple(inputs_own) + (far_high,)
     inputs_other = tuple(swap_cores(a) for a in inputs_own)
 
     pair = (own + swap_cores(away).astype(jnp.float32)).astype(bf16)

time: 149 us -> 146 us (0.980)
  starting transfers between devices: 54.5 us -> 51.8 us
    all_to_all x1, starting transfers between devices: 8.06 us -> 4.96 us  [local(): lax.all_to_all(chunks, ('x', 'y', 'c'), split_axis=0, concat_axis=0, tile...]
    ppermute x2, waiting for transfers between devices: 0.79 us -> 2.9 us  [the longest x1 1.85 us: local(): far_low = lax.ppermute(before[0], 'y', ring(NY, 1))]
    ppermute x12, waiting for transfers between devices: 6.52 us -> 4.47 us  [swap_cores(): return lax.ppermute(a, 'c', [(0, 1), (1, 0)])]
  transfers between devices with their start and end apart: 29 -> 29, of which waited for: 18 -> 19; matrix products, arithmetic and copies ran while one was open for 2% -> 2% of each run, Pallas kernels for 9% -> 9%
where the time goes in v13:
time: 146 us
  waiting for transfers between devices  64.8 us (44%)
  starting transfers between devices  51.8 us (35%)
  Pallas kernels  21.8 us (15%)
  local copies, waits for them, and re-layouts  3.74 us (3%)
  other arithmetic  2.78 us (2%)
    ppermute x4, waiting for transfers between devices, local(): lax.ppermute(a, 'y', ring(NY, shift))  13.9 us
    pallas_call x1, Pallas kernels, attention_grads(): pl.pallas_call(attention_kernel, out_shape=(pltpu.HBM((BLOCK, 2 * HEAD),...  11.5 us
    all_to_all x1, waiting for transfers between devices, local(): pair = lax.all_to_all(pair, 'z', split_axis=0, concat_axis=0, tiled=True)  9.88 us
    all_to_all x1, starting transfers between devices, local(): lax.all_to_all(outgoing, 'z', split_axis=0, concat_axis=0, tiled=True)  9.16 us
    all_to_all x1, waiting for transfers between devices, local(): lax.all_to_all(part, ('y', 'z', 'c'), split_axis=0, concat_axis=0, tiled=...  8.9 us
    ppermute x12, starting transfers between devices, swap_cores(): return lax.ppermute(a, 'c', [(0, 1), (1, 0)])  7.4 us
    ppermute x2, waiting for transfers between devices, local(): lax.ppermute(a, 'x', ring(NX, s))  7.21 us
    ppermute x1, waiting for transfers between devices, local(): near = lax.ppermute(pieces[1], 'x', ring(NX, 1))  6.85 us
  transfers between devices with their start and end apart: 29, of which 19 were waited for; matrix products, arithmetic and copies ran while one was open for 2% of the time, Pallas kernels for 9%

profile of v13, /device:TPU:1, one launch (start us, length us, event | category | flops | bytes accessed | tf_op | source)
XLA Modules:
  0.0 145.8 jit_solution(10819483606734025552)
XLA Ops:
  0.6 2.6 %shard_map.110 = bf16[8,128,768]{2,1,0:T(8,128)(2,1)} custom-call(bf16[128,2048]{1,0:T(8,128)(2,1)} %bitcast.41, bf16[128,2048]{1,0:T(8,128)(2,1)} %bitcast.42, bf16[128,512]{1,0:T(8,128)(2,1)} %bitcast.47, bf16[128,512]{1,0:T(8,128)(2,1)} %bitcast.48), custom_call_target="tpu_custom_call" | custom-call | bytes 3145728 | tf_op jit(solution)/shard_map/pallas_call | solution.py:297
  3.2 9.2 %all-to-all-start = ((bf16[8,128,768]{2,1,0:T(8,128)(2,1)}), bf16[8,128,768]{2,1,0:T(8,128)(2,1)S(1)}, u32[]{:S(2)}, u32[]{:S(2)}) async-start(bf16[8,128,768]{2,1,0:T(8,128)(2,1)} %shard_map.110), calls=%async_computation | async-start | bytes 3145728 | tf_op jit(solution)/shard_map/all_to_all | solution.py:393
  12.5 1.3 collective-permute-start
  13.8 6.9 %collective-permute-done = bf16[128,1024]{1,0:T(8,128)(2,1)S(1)} collective-permute-done((bf16[128,1024]{1,0:T(8,128)(2,1)S(1)}, bf16[128,1024]{1,0:T(8,128)(2,1)S(1)}, u32[]{:S(2)}, u32[]{:S(2)}) %collective-permute-start) | collective-permute-done | bytes 262176 | tf_op jit(solution)/shard_map/ppermute | solution.py:380
  20.6 1.5 %collective-permute-start.1 = (bf16[128,1024]{1,0:T(8,128)(2,1)S(1)}, bf16[128,1024]{1,0:T(8,128)(2,1)S(1)}, u32[]{:S(2)}, u32[]{:S(2)}) collective-permute-start(bf16[128,1024]{1,0:T(8,128)(2,1)S(1)} %get-tuple-element.62), channel_id=1, source_target_pairs={{0,128},{64,192},{128,0},{192,64},{1,129},{65,193},{129,1},{193,65... | collective-permute-start | bytes 786440 | tf_op jit(solution)/shard_map/ppermute | solution.py:383
  22.2 0.9 collective-permute-start.2
  23.0 0.8 pad_maximum_fusion.refs_0_
  23.9 2.7 %collective-permute-start.5 = (bf16[2,128,1024]{2,1,0:T(8,128)(2,1)}, bf16[2,128,1024]{2,1,0:T(8,128)(2,1)S(1)}, u32[]{:S(2)}, u32[]{:S(2)}) collective-permute-start(bf16[2,128,1024]{2,1,0:T(8,128)(2,1)} %pad_maximum_fusion.refs_0_), channel_id=1, source_target_pairs={{0,48},{16,0},{32,16},{48,32},{1,49},{17,1},{33,17},{49,33},{2,50}... | collective-permute-start | bytes 1572872 | tf_op jit(solution)/shard_map/ppermute | solution.py:388
  26.6 1.5 %collective-permute-done.1 = bf16[128,1024]{1,0:T(8,128)(2,1)S(1)} collective-permute-done((bf16[128,1024]{1,0:T(8,128)(2,1)S(1)}, bf16[128,1024]{1,0:T(8,128)(2,1)S(1)}, u32[]{:S(2)}, u32[]{:S(2)}) %collective-permute-start.1) | collective-permute-done | bytes 262176 | tf_op jit(solution)/shard_map/ppermute | solution.py:383
  28.1 5.7 %collective-permute-done.2 = bf16[128,1024]{1,0:T(8,128)(2,1)S(1)} collective-permute-done((bf16[128,1024]{1,0:T(8,128)(2,1)S(1)}, bf16[128,1024]{1,0:T(8,128)(2,1)S(1)}, u32[]{:S(2)}, u32[]{:S(2)}) %collective-permute-start.2) | collective-permute-done | bytes 262176 | tf_op jit(solution)/shard_map/ppermute | solution.py:383
  33.8 0.8 pad_maximum_fusion.1.refs_1_
  34.7 2.7 %collective-permute-start.6 = (bf16[2,128,1024]{2,1,0:T(8,128)(2,1)}, bf16[2,128,1024]{2,1,0:T(8,128)(2,1)}, u32[]{:S(2)}, u32[]{:S(2)}) collective-permute-start(bf16[2,128,1024]{2,1,0:T(8,128)(2,1)} %pad_maximum_fusion.1.refs_1_), channel_id=1, source_target_pairs={{0,48},{16,0},{32,16},{48,32},{1,49},{17,1},{33,17},{49,33},{2,50}... | collective-permute-start | bytes 1572872 | tf_op jit(solution)/shard_map/ppermute | solution.py:388
  37.4 1.4 collective-permute-done.3.refs_2_
  38.9 9.4 %collective-permute-done.6.refs_5_ = bf16[2,128,1024]{2,1,0:T(8,128)(2,1)} collective-permute-done((bf16[2,128,1024]{2,1,0:T(8,128)(2,1)}, bf16[2,128,1024]{2,1,0:T(8,128)(2,1)}, u32[]{:S(2)}, u32[]{:S(2)}) %collective-permute-start.6) | collective-permute-done | bytes 524320 | tf_op jit(solution)/shard_map/ppermute | solution.py:388
  48.2 3.1 %collective-permute-done.4.refs_3_ = bf16[2,128,1024]{2,1,0:T(8,128)(2,1)} collective-permute-done((bf16[2,128,1024]{2,1,0:T(8,128)(2,1)}, bf16[2,128,1024]{2,1,0:T(8,128)(2,1)}, u32[]{:S(2)}, u32[]{:S(2)}) %collective-permute-start.4) | collective-permute-done | bytes 524320 | tf_op jit(solution)/shard_map/ppermute | solution.py:388
  51.7 0.8 slice.29
  52.5 2.4 %collective-permute-start.7 = (bf16[8,128,256]{2,1,0:T(8,128)(2,1)}, bf16[8,128,256]{2,1,0:T(8,128)(2,1)S(1)}, u32[]{:S(2)}, u32[]{:S(2)}) collective-permute-start(bf16[8,128,256]{2,1,0:T(8,128)(2,1)} %slice.29), channel_id=1, source_target_pairs={{0,1},{1,0},{2,3},{3,2},{4,5},{5,4},{6,7},{7,6},{8,9},{9,8},{10,11... | collective-permute-start | bytes 1572872 | tf_op jit(solution)/shard_map/ppermute | solution.py:366
  54.9 0.9 collective-permute-start.8
  55.9 0.7 collective-permute-done.7.other_ref
  56.6 11.5 %shard_map.111 = (bf16[128,256]{1,0:T(8,128)(2,1)}, bf16[128,256]{1,0:T(8,128)(2,1)}, bf16[128,256]{1,0:T(8,128)(2,1)}, bf16[128,256]{1,0:T(8,128)(2,1)}, bf16[1...) custom-call(s32[16,8]{1,0:T(8,128)S(1)} %copy.14.links_ref, ...), custom_call_target="tpu_custom_call" | custom-call | flops 1000 | bytes 1000 | tf_op jit(solution)/shard_map/pallas_call | solution.py:191
  68.1 1.9 %collective-permute-done.8.refs_6_ = bf16[2,128,1024]{2,1,0:T(8,128)(2,1)} collective-permute-done((bf16[2,128,1024]{2,1,0:T(8,128)(2,1)}, bf16[2,128,1024]{2,1,0:T(8,128)(2,1)}, u32[]{:S(2)}, u32[]{:S(2)}) %collective-permute-start.8) | collective-permute-done | bytes 524320 | tf_op jit(solution)/shard_map/ppermute | solution.py:390
  70.0 0.8 collective-permute-start.10
  71.3 1.2 collective-permute-start.18
  72.4 0.6 collective-permute-done.10
  73.0 0.9 add_convert_fusion
  73.9 6.3 %all-to-all-start.1 = ((bf16[8,128,256]{2,1,0:T(8,128)(2,1)}), bf16[8,128,256]{2,1,0:T(8,128)(2,1)S(1)}, u32[]{:S(2)}, u32[]{:S(2)}) async-start(bf16[8,128,256]{2,1,0:T(8,128)(2,1)} %add_convert_fusion), calls=%async_computation.1 | async-start | bytes 1048576 | tf_op jit(solution)/shard_map/all_to_all | solution.py:412
  80.3 0.7 collective-permute-start.9
  81.0 1.3 collective-permute-done.9
  83.4 1.0 collective-permute-done.18.refs_7_
  84.5 1.4 collective-permute-start.19
  85.9 0.7 collective-permute-done.17.refs_14_
  87.5 0.9 copy-done.9
  88.3 9.9 %all-to-all-done.1.partials_ref = bf16[8,128,256]{2,1,0:T(8,128)(2,1)S(1)} async-done(((bf16[8,128,256]{2,1,0:T(8,128)(2,1)}), bf16[8,128,256]{2,1,0:T(8,128)(2,1)S(1)}, u32[]{:S(2)}, u32[]{:S(2)}) %all-to-all-start.1) | async-done | bytes 524320 | tf_op jit(solution)/shard_map/all_to_all | solution.py:412
  98.2 1.2 shard_map.112
  99.4 5.0 %all-to-all-start.2 = ((bf16[32,128,128]{2,1,0:T(8,128)(2,1)}), bf16[32,128,128]{2,1,0:T(8,128)(2,1)S(1)}, u32[]{:S(2)}, u32[]{:S(2)}) async-start(bf16[32,128,128]{2,1,0:T(8,128)(2,1)} %get-tuple-element.96), calls=%async_computation.2 | async-start | bytes 2097152 | tf_op jit(solution)/shard_map/all_to_all | solution.py:419
  104.6 0.6 collective-permute-start.21
  105.2 2.9 %collective-permute-start.22 = (bf16[2,128,256]{2,1,0:T(8,128)(2,1)S(1)}, bf16[2,128,256]{2,1,0:T(8,128)(2,1)S(1)}, u32[]{:S(2)}, u32[]{:S(2)}) collective-permute-start(bf16[2,128,256]{2,1,0:T(8,128)(2,1)S(1)} %pad_maximum_fusion.5), channel_id=1, source_target_pairs={{0,6},{2,8},{4,10},{6,12},{8,14},{10,0},{12,2},{14,4},{1,11},{3,13... | collective-permute-start | bytes 393224 | tf_op jit(solution)/shard_map/ppermute | solution.py:425
  108.1 2.6 %collective-permute-start.23 = (bf16[128,256]{1,0:T(8,128)(2,1)S(1)}, bf16[128,256]{1,0:T(8,128)(2,1)S(1)}, u32[]{:S(2)}, u32[]{:S(2)}) collective-permute-start(bf16[128,256]{1,0:T(8,128)(2,1)S(1)} %copy-done.17), channel_id=1, source_target_pairs={{0,8},{2,10},{4,12},{6,14},{8,0},{10,2},{12,4},{14,6},{1,9},{3,11}... | collective-permute-start | bytes 196616 | tf_op jit(solution)/shard_map/ppermute | solution.py:426
  110.7 4.8 %collective-permute-done.23.across_ref = bf16[128,256]{1,0:T(8,128)(2,1)S(1)} collective-permute-done((bf16[128,256]{1,0:T(8,128)(2,1)S(1)}, bf16[128,256]{1,0:T(8,128)(2,1)S(1)}, u32[]{:S(2)}, u32[]{:S(2)}) %collective-permute-start.23) | collective-permute-done | bytes 65568 | tf_op jit(solution)/shard_map/ppermute | solution.py:426
  115.4 2.4 %collective-permute-done.22.refs_2_ = bf16[2,128,256]{2,1,0:T(8,128)(2,1)S(1)} collective-permute-done((bf16[2,128,256]{2,1,0:T(8,128)(2,1)S(1)}, bf16[2,128,256]{2,1,0:T(8,128)(2,1)S(1)}, u32[]{:S(2)}, u32[]{:S(2)}) %collective-permute-start.22) | collective-permute-done | bytes 131104 | tf_op jit(solution)/shard_map/ppermute | solution.py:425
  117.9 3.4 %all-to-all-done.2.grads_ref = bf16[32,128,128]{2,1,0:T(8,128)(2,1)S(1)} async-done(((bf16[32,128,128]{2,1,0:T(8,128)(2,1)}), bf16[32,128,128]{2,1,0:T(8,128)(2,1)S(1)}, u32[]{:S(2)}, u32[]{:S(2)}) %all-to-all-start.2) | async-done | bytes 1048608 | tf_op jit(solution)/shard_map/all_to_all | solution.py:419
  121.3 5.1 %shard_map.114 = bf16[1024,128]{1,0:T(8,128)(2,1)} custom-call(s32[4]{0:T(128)S(1)} %pad_add_fusion.place_ref, bf16[32,128,128]{2,1,0:T(8,128)(2,1)S(1)} %all-to-all-done.2.grads_ref, bf16[2,128,1024]{2,1,0:T(8,128)(2,1)} %pad_maximum_fusion.refs_0_, bf16[2,128,1024]{2,1,0:T(8,128)(2,1)} %pad_maximum_fusion.1.refs_1_, ...), custom_call_target="tpu_custom_call" | custom-call | flops 1100000000 | bytes 9437184 | tf_op jit(solution)/shard_map/pallas_call | solution.py:257
  126.4 6.6 %all-to-all-start.3 = ((bf16[64,16,128]{2,1,0:T(8,128)(2,1)}), bf16[64,16,128]{2,1,0:T(8,128)(2,1)S(1)}, u32[]{:S(2)}, u32[]{:S(2)}) async-start(bf16[64,16,128]{2,1,0:T(8,128)(2,1)} %bitcast.22), calls=%async_computation.3 | async-start | bytes 524288 | tf_op jit(solution)/shard_map/all_to_all | solution.py:433
  133.1 0.5 collective-permute-start.24
  133.7 1.1 collective-permute-done.24.refs_3_
  134.8 1.4 shard_map.113
  136.2 8.9 %all-to-all-done.3 = bf16[64,16,128]{2,1,0:T(8,128)(2,1)S(1)} async-done(((bf16[64,16,128]{2,1,0:T(8,128)(2,1)}), bf16[64,16,128]{2,1,0:T(8,128)(2,1)S(1)}, u32[]{:S(2)}, u32[]{:S(2)}) %all-to-all-start.3) | async-done | bytes 262176 | tf_op jit(solution)/shard_map/all_to_all | solution.py:433
  145.2 0.6 copy_bitcast_fusion
  (72 shorter events, 3.4 us)
Async XLA Ops:
  3.2 9.2 %copy-start.2 = (bf16[1,128,4096]{2,1,0:T(8,128)(2,1)S(1)}, bf16[1,128,4096]{2,1,0:T(8,128)(2,1)}, u32[]{:S(2)}) copy-start(bf16[1,128,4096]{2,1,0:T(8,128)(2,1)} %param.7) | copy-start | bytes 3145732
  3.2 48.1 %all-to-all-start = ((bf16[8,128,768]{2,1,0:T(8,128)(2,1)}), bf16[8,128,768]{2,1,0:T(8,128)(2,1)S(1)}, u32[]{:S(2)}, u32[]{:S(2)}) async-start(bf16[8,128,768]{2,1,0:T(8,128)(2,1)} %shard_map.110), calls=%async_computation | async-start | bytes 3145728 | tf_op jit(solution)/shard_map/all_to_all | solution.py:393
  12.5 38.9 %copy-start.1 = (s32[1,2048]{1,0:T(1,128)S(1)}, s32[1,2048]{1,0:T(1,128)}, u32[]{:S(2)}) copy-start(s32[1,2048]{1,0:T(1,128)} %param.13) | copy-start | bytes 24580
  12.5 8.1 %collective-permute-start = (bf16[128,1024]{1,0:T(8,128)(2,1)S(1)}, bf16[128,1024]{1,0:T(8,128)(2,1)S(1)}, u32[]{:S(2)}, u32[]{:S(2)}) collective-permute-start(bf16[128,1024]{1,0:T(8,128)(2,1)S(1)} %get-tuple-element.118), channel_id=1, source_target_pairs={{0,64},{64,128},{128,192},{192,0},{1,65},{65,129},{129,193},{193,1... | collective-permute-start | bytes 786440 | tf_op jit(solution)/shard_map/ppermute | solution.py:380
  20.6 7.4 %collective-permute-start.1 = (bf16[128,1024]{1,0:T(8,128)(2,1)S(1)}, bf16[128,1024]{1,0:T(8,128)(2,1)S(1)}, u32[]{:S(2)}, u32[]{:S(2)}) collective-permute-start(bf16[128,1024]{1,0:T(8,128)(2,1)S(1)} %get-tuple-element.62), channel_id=1, source_target_pairs={{0,128},{64,192},{128,0},{192,64},{1,129},{65,193},{129,1},{193,65... | collective-permute-start | bytes 786440 | tf_op jit(solution)/shard_map/ppermute | solution.py:383
  22.2 11.6 %collective-permute-start.2 = (bf16[128,1024]{1,0:T(8,128)(2,1)S(1)}, bf16[128,1024]{1,0:T(8,128)(2,1)S(1)}, u32[]{:S(2)}, u32[]{:S(2)}) collective-permute-start(bf16[128,1024]{1,0:T(8,128)(2,1)S(1)} %get-tuple-element.63), channel_id=1, source_target_pairs={{0,192},{64,0},{128,64},{192,128},{1,193},{65,1},{129,65},{193,129... | collective-permute-start | bytes 786440 | tf_op jit(solution)/shard_map/ppermute | solution.py:383
  23.9 13.5 %collective-permute-start.5 = (bf16[2,128,1024]{2,1,0:T(8,128)(2,1)}, bf16[2,128,1024]{2,1,0:T(8,128)(2,1)S(1)}, u32[]{:S(2)}, u32[]{:S(2)}) collective-permute-start(bf16[2,128,1024]{2,1,0:T(8,128)(2,1)} %pad_maximum_fusion.refs_0_), channel_id=1, source_target_pairs={{0,48},{16,0},{32,16},{48,32},{1,49},{17,1},{33,17},{49,33},{2,50}... | collective-permute-start | bytes 1572872 | tf_op jit(solution)/shard_map/ppermute | solution.py:388
  26.6 12.2 %collective-permute-start.3 = (bf16[2,128,1024]{2,1,0:T(8,128)(2,1)}, bf16[2,128,1024]{2,1,0:T(8,128)(2,1)}, u32[]{:S(2)}, u32[]{:S(2)}) collective-permute-start(bf16[2,128,1024]{2,1,0:T(8,128)(2,1)} %pad_maximum_fusion.refs_0_), channel_id=1, source_target_pairs={{0,16},{16,32},{32,48},{48,0},{1,17},{17,33},{33,49},{49,1},{2,18}... | collective-permute-start | bytes 1572872 | tf_op jit(solution)/shard_map/ppermute | solution.py:388
  33.8 21.9 %copy-start.16 = (s32[1,16,8]{1,2,0:T(8,128)S(1)}, s32[1,16,8]{1,2,0:T(8,128)}, u32[]{:S(2)}) copy-start(s32[1,16,8]{1,2,0:T(8,128)} %param.12) | copy-start | bytes 1540
  34.7 13.6 %collective-permute-start.6 = (bf16[2,128,1024]{2,1,0:T(8,128)(2,1)}, bf16[2,128,1024]{2,1,0:T(8,128)(2,1)}, u32[]{:S(2)}, u32[]{:S(2)}) collective-permute-start(bf16[2,128,1024]{2,1,0:T(8,128)(2,1)} %pad_maximum_fusion.1.refs_1_), channel_id=1, source_target_pairs={{0,48},{16,0},{32,16},{48,32},{1,49},{17,1},{33,17},{49,33},{2,50}... | collective-permute-start | bytes 1572872 | tf_op jit(solution)/shard_map/ppermute | solution.py:388
  37.4 13.9 %collective-permute-start.4 = (bf16[2,128,1024]{2,1,0:T(8,128)(2,1)}, bf16[2,128,1024]{2,1,0:T(8,128)(2,1)}, u32[]{:S(2)}, u32[]{:S(2)}) collective-permute-start(bf16[2,128,1024]{2,1,0:T(8,128)(2,1)} %pad_maximum_fusion.1.refs_1_), channel_id=1, source_target_pairs={{0,16},{16,32},{32,48},{48,0},{1,17},{17,33},{33,49},{49,1},{2,18}... | collective-permute-start | bytes 1572872 | tf_op jit(solution)/shard_map/ppermute | solution.py:388
  37.4 10.8 %copy-start.3 = (bf16[2,128,1024]{2,1,0:T(8,128)(2,1)}, bf16[2,128,1024]{2,1,0:T(8,128)(2,1)S(1)}, u32[]{:S(2)}) copy-start(bf16[2,128,1024]{2,1,0:T(8,128)(2,1)S(1)} %collective-permute-done.5.refs_4_) | copy-start | bytes 1572868
  52.5 4.1 %collective-permute-start.7 = (bf16[8,128,256]{2,1,0:T(8,128)(2,1)}, bf16[8,128,256]{2,1,0:T(8,128)(2,1)S(1)}, u32[]{:S(2)}, u32[]{:S(2)}) collective-permute-start(bf16[8,128,256]{2,1,0:T(8,128)(2,1)} %slice.29), channel_id=1, source_target_pairs={{0,1},{1,0},{2,3},{3,2},{4,5},{5,4},{6,7},{7,6},{8,9},{9,8},{10,11... | collective-permute-start | bytes 1572872 | tf_op jit(solution)/shard_map/ppermute | solution.py:366
  54.9 15.1 %collective-permute-start.8 = (bf16[2,128,1024]{2,1,0:T(8,128)(2,1)}, bf16[2,128,1024]{2,1,0:T(8,128)(2,1)}, u32[]{:S(2)}, u32[]{:S(2)}) collective-permute-start(bf16[2,128,1024]{2,1,0:T(8,128)(2,1)} %collective-permute-done.3.refs_2_), channel_id=1, source_target_pairs={{0,16},{16,32},{32,48},{48,0},{1,17},{17,33},{33,49},{49,1},{2,18}... | collective-permute-start | bytes 1572872 | tf_op jit(solution)/shard_map/ppermute | solution.py:390
  70.0 12.8 %copy-start.4 = (bf16[2,128,1024]{2,1,0:T(8,128)(2,1)S(1)}, bf16[2,128,1024]{2,1,0:T(8,128)(2,1)}, u32[]{:S(2)}) copy-start(bf16[2,128,1024]{2,1,0:T(8,128)(2,1)} %copy-done.3) | copy-start | bytes 1572868
  70.0 3.0 %collective-permute-start.10 = (bf16[8,128,256]{2,1,0:T(8,128)(2,1)S(1)}, bf16[8,128,256]{2,1,0:T(8,128)(2,1)S(1)}, u32[]{:S(2)}, u32[]{:S(2)}) collective-permute-start(bf16[8,128,256]{2,1,0:T(8,128)(2,1)S(1)} %get-tuple-element.87), channel_id=1, source_target_pairs={{0,1},{1,0},{2,3},{3,2},{4,5},{5,4},{6,7},{7,6},{8,9},{9,8},{10,11... | collective-permute-start | bytes 1572872 | tf_op jit(solution)/shard_map/ppermute | solution.py:366
  70.8 11.9 %collective-permute-start.11 = (bf16[2,128,1024]{2,1,0:T(8,128)(2,1)}, bf16[2,128,1024]{2,1,0:T(8,128)(2,1)S(1)}, u32[]{:S(2)}, u32[]{:S(2)}) collective-permute-start(bf16[2,128,1024]{2,1,0:T(8,128)(2,1)} %pad_maximum_fusion.refs_0_), channel_id=1, source_target_pairs={{0,1},{1,0},{2,3},{3,2},{4,5},{5,4},{6,7},{7,6},{8,9},{9,8},{10,11... | collective-permute-start | bytes 1572872 | tf_op jit(solution)/shard_map/ppermute | solution.py:366
  70.8 12.1 %collective-permute-start.12 = (bf16[2,128,1024]{2,1,0:T(8,128)(2,1)}, bf16[2,128,1024]{2,1,0:T(8,128)(2,1)S(1)}, u32[]{:S(2)}, u32[]{:S(2)}) collective-permute-start(bf16[2,128,1024]{2,1,0:T(8,128)(2,1)} %pad_maximum_fusion.1.refs_1_), channel_id=1, source_target_pairs={{0,1},{1,0},{2,3},{3,2},{4,5},{5,4},{6,7},{7,6},{8,9},{9,8},{10,11... | collective-permute-start | bytes 1572872 | tf_op jit(solution)/shard_map/ppermute | solution.py:366
  71.3 12.0 %collective-permute-start.13 = (bf16[2,128,1024]{2,1,0:T(8,128)(2,1)}, bf16[2,128,1024]{2,1,0:T(8,128)(2,1)S(1)}, u32[]{:S(2)}, u32[]{:S(2)}) collective-permute-start(bf16[2,128,1024]{2,1,0:T(8,128)(2,1)} %collective-permute-done.3.refs_2_), channel_id=1, source_target_pairs={{0,1},{1,0},{2,3},{3,2},{4,5},{5,4},{6,7},{7,6},{8,9},{9,8},{10,11... | collective-permute-start | bytes 1572872 | tf_op jit(solution)/shard_map/ppermute | solution.py:366
  71.3 13.2 %collective-permute-start.18 = (bf16[2,128,1024]{2,1,0:T(8,128)(2,1)}, bf16[2,128,1024]{2,1,0:T(8,128)(2,1)S(1)}, u32[]{:S(2)}, u32[]{:S(2)}) collective-permute-start(bf16[2,128,1024]{2,1,0:T(8,128)(2,1)} %collective-permute-done.6.refs_5_), channel_id=1, source_target_pairs={{0,48},{16,0},{32,16},{48,32},{1,49},{17,1},{33,17},{49,33},{2,50}... | collective-permute-start | bytes 1572872 | tf_op jit(solution)/shard_map/ppermute | solution.py:407
  73.9 24.3 %all-to-all-start.1 = ((bf16[8,128,256]{2,1,0:T(8,128)(2,1)}), bf16[8,128,256]{2,1,0:T(8,128)(2,1)S(1)}, u32[]{:S(2)}, u32[]{:S(2)}) async-start(bf16[8,128,256]{2,1,0:T(8,128)(2,1)} %add_convert_fusion), calls=%async_computation.1 | async-start | bytes 1048576 | tf_op jit(solution)/shard_map/all_to_all | solution.py:412
  80.3 24.2 %copy-start.15 = (bf16[128,256]{1,0:T(8,128)(2,1)S(1)}, bf16[128,256]{1,0:T(8,128)(2,1)}, u32[]{:S(2)}) copy-start(bf16[128,256]{1,0:T(8,128)(2,1)} %get-tuple-element.97) | copy-start | bytes 196612
  80.3 24.3 %copy-start.14 = (bf16[128,256]{1,0:T(8,128)(2,1)S(1)}, bf16[128,256]{1,0:T(8,128)(2,1)}, u32[]{:S(2)}) copy-start(bf16[128,256]{1,0:T(8,128)(2,1)} %get-tuple-element.99) | copy-start | bytes 196612
  80.3 2.0 %collective-permute-start.9 = (bf16[3,128,256]{2,1,0:T(8,128)(2,1)}, bf16[3,128,256]{2,1,0:T(8,128)(2,1)S(1)}, u32[]{:S(2)}, u32[]{:S(2)}) collective-permute-start(bf16[3,128,256]{2,1,0:T(8,128)(2,1)} %get-tuple-element.85), channel_id=1, source_target_pairs={{0,1},{1,0},{2,3},{3,2},{4,5},{5,4},{6,7},{7,6},{8,9},{9,8},{10,11... | collective-permute-start | bytes 589832 | tf_op jit(solution)/shard_map/ppermute | solution.py:366
  82.3 4.4 %collective-permute-start.16 = (bf16[2,128,1024]{2,1,0:T(8,128)(2,1)}, bf16[2,128,1024]{2,1,0:T(8,128)(2,1)S(1)}, u32[]{:S(2)}, u32[]{:S(2)}) collective-permute-start(bf16[2,128,1024]{2,1,0:T(8,128)(2,1)} %collective-permute-done.6.refs_5_), channel_id=1, source_target_pairs={{0,1},{1,0},{2,3},{3,2},{4,5},{5,4},{6,7},{7,6},{8,9},{9,8},{10,11... | collective-permute-start | bytes 1572872 | tf_op jit(solution)/shard_map/ppermute | solution.py:366
  82.7 21.8 %copy-start.5 = (bf16[2,128,1024]{2,1,0:T(8,128)(2,1)}, bf16[2,128,1024]{2,1,0:T(8,128)(2,1)S(1)}, u32[]{:S(2)}) copy-start(bf16[2,128,1024]{2,1,0:T(8,128)(2,1)S(1)} %collective-permute-done.11.refs_8_) | copy-start | bytes 1572868
  82.7 3.2 %collective-permute-start.14 = (bf16[2,128,1024]{2,1,0:T(8,128)(2,1)}, bf16[2,128,1024]{2,1,0:T(8,128)(2,1)S(1)}, u32[]{:S(2)}, u32[]{:S(2)}) collective-permute-start(bf16[2,128,1024]{2,1,0:T(8,128)(2,1)} %collective-permute-done.4.refs_3_), channel_id=1, source_target_pairs={{0,1},{1,0},{2,3},{3,2},{4,5},{5,4},{6,7},{7,6},{8,9},{9,8},{10,11... | collective-permute-start | bytes 1572872 | tf_op jit(solution)/shard_map/ppermute | solution.py:366
  82.8 21.6 %copy-start.6 = (bf16[2,128,1024]{2,1,0:T(8,128)(2,1)}, bf16[2,128,1024]{2,1,0:T(8,128)(2,1)S(1)}, u32[]{:S(2)}) copy-start(bf16[2,128,1024]{2,1,0:T(8,128)(2,1)S(1)} %collective-permute-done.12.refs_9_) | copy-start | bytes 1572868
  82.8 3.1 %collective-permute-start.15 = (bf16[2,128,1024]{2,1,0:T(8,128)(2,1)S(1)}, bf16[2,128,1024]{2,1,0:T(8,128)(2,1)S(1)}, u32[]{:S(2)}, u32[]{:S(2)}) collective-permute-start(bf16[2,128,1024]{2,1,0:T(8,128)(2,1)S(1)} %copy-done.4), channel_id=1, source_target_pairs={{0,1},{1,0},{2,3},{3,2},{4,5},{5,4},{6,7},{7,6},{8,9},{9,8},{10,11... | collective-permute-start | bytes 1572872 | tf_op jit(solution)/shard_map/ppermute | solution.py:366
  83.3 3.4 %copy-start.7 = (bf16[2,128,1024]{2,1,0:T(8,128)(2,1)}, bf16[2,128,1024]{2,1,0:T(8,128)(2,1)S(1)}, u32[]{:S(2)}) copy-start(bf16[2,128,1024]{2,1,0:T(8,128)(2,1)S(1)} %collective-permute-done.13.refs_10_) | copy-start | bytes 1572868
  83.3 3.4 %collective-permute-start.17 = (bf16[2,128,1024]{2,1,0:T(8,128)(2,1)}, bf16[2,128,1024]{2,1,0:T(8,128)(2,1)S(1)}, u32[]{:S(2)}, u32[]{:S(2)}) collective-permute-start(bf16[2,128,1024]{2,1,0:T(8,128)(2,1)} %collective-permute-done.8.refs_6_), channel_id=1, source_target_pairs={{0,1},{1,0},{2,3},{3,2},{4,5},{5,4},{6,7},{7,6},{8,9},{9,8},{10,11... | collective-permute-start | bytes 1572872 | tf_op jit(solution)/shard_map/ppermute | solution.py:366
  84.5 3.9 %copy-start.8 = (bf16[2,128,1024]{2,1,0:T(8,128)(2,1)}, bf16[2,128,1024]{2,1,0:T(8,128)(2,1)S(1)}, u32[]{:S(2)}) copy-start(bf16[2,128,1024]{2,1,0:T(8,128)(2,1)S(1)} %collective-permute-done.18.refs_7_) | copy-start | bytes 1572868
  84.5 3.9 %collective-permute-start.19 = (bf16[2,128,1024]{2,1,0:T(8,128)(2,1)S(1)}, bf16[2,128,1024]{2,1,0:T(8,128)(2,1)}, u32[]{:S(2)}, u32[]{:S(2)}) collective-permute-start(bf16[2,128,1024]{2,1,0:T(8,128)(2,1)S(1)} %collective-permute-done.18.refs_7_), channel_id=1, source_target_pairs={{0,1},{1,0},{2,3},{3,2},{4,5},{5,4},{6,7},{7,6},{8,9},{9,8},{10,11... | collective-permute-start | bytes 1572872 | tf_op jit(solution)/shard_map/ppermute | solution.py:366
  85.9 0.8 copy-start.10
  85.9 1.0 copy-start.11
  86.7 0.8 copy-start.12
  87.5 0.9 copy-start.9
  99.4 5.8 %copy-start.13 = (bf16[128,256]{1,0:T(8,128)(2,1)S(1)}, bf16[128,256]{1,0:T(8,128)(2,1)}, u32[]{:S(2)}) copy-start(bf16[128,256]{1,0:T(8,128)(2,1)} %get-tuple-element.100) | copy-start | bytes 196612
  99.4 8.7 %copy-start.17 = (bf16[128,256]{1,0:T(8,128)(2,1)S(1)}, bf16[128,256]{1,0:T(8,128)(2,1)}, u32[]{:S(2)}) copy-start(bf16[128,256]{1,0:T(8,128)(2,1)} %get-tuple-element.101) | copy-start | bytes 196612
  99.4 21.9 %all-to-all-start.2 = ((bf16[32,128,128]{2,1,0:T(8,128)(2,1)}), bf16[32,128,128]{2,1,0:T(8,128)(2,1)S(1)}, u32[]{:S(2)}, u32[]{:S(2)}) async-start(bf16[32,128,128]{2,1,0:T(8,128)(2,1)} %get-tuple-element.96), calls=%async_computation.2 | async-start | bytes 2097152 | tf_op jit(solution)/shard_map/all_to_all | solution.py:419
  104.5 11.0 %collective-permute-start.20 = (bf16[2,128,256]{2,1,0:T(8,128)(2,1)S(1)}, bf16[2,128,256]{2,1,0:T(8,128)(2,1)S(1)}, u32[]{:S(2)}, u32[]{:S(2)}) collective-permute-start(bf16[2,128,256]{2,1,0:T(8,128)(2,1)S(1)} %pad_maximum_fusion.3), channel_id=1, source_target_pairs={{0,2},{2,4},{4,6},{6,8},{8,10},{10,12},{12,14},{14,0},{1,15},{3,1}... | collective-permute-start | bytes 393224 | tf_op jit(solution)/shard_map/ppermute | solution.py:425
  104.6 10.9 %collective-permute-start.21 = (bf16[2,128,256]{2,1,0:T(8,128)(2,1)S(1)}, bf16[2,128,256]{2,1,0:T(8,128)(2,1)S(1)}, u32[]{:S(2)}, u32[]{:S(2)}) collective-permute-start(bf16[2,128,256]{2,1,0:T(8,128)(2,1)S(1)} %pad_maximum_fusion.4), channel_id=1, source_target_pairs={{0,4},{2,6},{4,8},{6,10},{8,12},{10,14},{12,0},{14,2},{1,13},{3,15... | collective-permute-start | bytes 393224 | tf_op jit(solution)/shard_map/ppermute | solution.py:425
  105.2 29.5 %copy-start = (bf16[128,256]{1,0:T(8,128)(2,1)S(1)}, bf16[128,256]{1,0:T(8,128)(2,1)}, u32[]{:S(2)}) copy-start(bf16[128,256]{1,0:T(8,128)(2,1)} %get-tuple-element.80.keep_ref) | copy-start | bytes 196612
  105.2 12.6 %collective-permute-start.22 = (bf16[2,128,256]{2,1,0:T(8,128)(2,1)S(1)}, bf16[2,128,256]{2,1,0:T(8,128)(2,1)S(1)}, u32[]{:S(2)}, u32[]{:S(2)}) collective-permute-start(bf16[2,128,256]{2,1,0:T(8,128)(2,1)S(1)} %pad_maximum_fusion.5), channel_id=1, source_target_pairs={{0,6},{2,8},{4,10},{6,12},{8,14},{10,0},{12,2},{14,4},{1,11},{3,13... | collective-permute-start | bytes 393224 | tf_op jit(solution)/shard_map/ppermute | solution.py:425
  108.1 7.3 %collective-permute-start.23 = (bf16[128,256]{1,0:T(8,128)(2,1)S(1)}, bf16[128,256]{1,0:T(8,128)(2,1)S(1)}, u32[]{:S(2)}, u32[]{:S(2)}) collective-permute-start(bf16[128,256]{1,0:T(8,128)(2,1)S(1)} %copy-done.17), channel_id=1, source_target_pairs={{0,8},{2,10},{4,12},{6,14},{8,0},{10,2},{12,4},{14,6},{1,9},{3,11}... | collective-permute-start | bytes 196616 | tf_op jit(solution)/shard_map/ppermute | solution.py:426
  126.4 18.6 %all-to-all-start.3 = ((bf16[64,16,128]{2,1,0:T(8,128)(2,1)}), bf16[64,16,128]{2,1,0:T(8,128)(2,1)S(1)}, u32[]{:S(2)}, u32[]{:S(2)}) async-start(bf16[64,16,128]{2,1,0:T(8,128)(2,1)} %bitcast.22), calls=%async_computation.3 | async-start | bytes 524288 | tf_op jit(solution)/shard_map/all_to_all | solution.py:433
  133.1 1.6 %collective-permute-start.24 = (bf16[3,128,256]{2,1,0:T(8,128)(2,1)S(1)}, bf16[3,128,256]{2,1,0:T(8,128)(2,1)S(1)}, u32[]{:S(2)}, u32[]{:S(2)}) collective-permute-start(bf16[3,128,256]{2,1,0:T(8,128)(2,1)S(1)} %pad_maximum_fusion.2), channel_id=1, source_target_pairs={{0,1},{1,0},{2,3},{3,2},{4,5},{5,4},{6,7},{7,6},{8,9},{9,8},{10,11... | collective-permute-start | bytes 589832 | tf_op jit(solution)/shard_map/ppermute | solution.py:366
